TPU v7x, 32 devices: a whole 2x2x4 slice. The times are simulated.
32 devices in a mesh: wall: 8 (over y, x, core), surf: 4 (over z).
Axes of the slice: x: 2, y: 2, z: 4, core: 2. Of those that a mesh axis runs over, the one named last changes fastest.
Arguments:
- state: bfloat16 [512, 162], P(('wall', 'surf')), may hold values from -6 to 6
- source: bfloat16 [512, 162], P(('wall', 'surf')), may hold values from -6 to 6
- face_coef: float32 [512, 4], P(('wall', 'surf')), may hold values from 0.1 to 0.5
- neighbour: int32 [512, 4], P(('wall', 'surf')), may hold values from 0 to 47
- lift: bfloat16 [162, 162], replicated, may hold values from -0.5 to 0.5
- elem_slot: int32 [16, 32], P('wall', 'surf'), may hold values from 0 to 15, as said below
- line_len: int32 [32], P('surf'), may hold values from 8 to 16
- dinv: bfloat16 [16, 32, 162, 162], P('wall', 'surf'), may hold values from -0.3 to 1.2
- lower: bfloat16 [16, 32, 162, 162], P('wall', 'surf'), may hold values from -1.4 to 0.4
- upper: bfloat16 [16, 32, 162, 162], P('wall', 'surf'), may hold values from -0.4 to 1.4
Outputs:
- solution: float32 [16, 32, 162], P('wall', 'surf')
Inputs may be any that keep to these rules, and one draw needn't show every extreme that they name: `elem_slot`: on each device the entries form a permutation of its 16 slots.
All inputs are finite; a program needn't handle non-finite values.
Results may differ from a plain program's by a relative error of at most 0.0023.
Values may be sent and summed in bfloat16 or wider, within the bound.
No kernel may reach another device: no remote copies, remote signals or barrier semaphores. Data moves between devices by JAX's collectives and lax.ppermute only.
A program may use at most 128 MiB of HBM per device.

v0:
```python
import jax
import jax.numpy as jnp
from jax import lax
from jax.sharding import PartitionSpec as P


def padded(cells, sides, width):
    for axis, dim in sides:
        count = lax.axis_size(axis)
        head = lax.slice_in_dim(cells, 0, width, axis=dim)
        tail = lax.slice_in_dim(cells, cells.shape[dim] - width, cells.shape[dim], axis=dim)
        cells = jnp.concatenate(
            [
                lax.ppermute(tail, axis, [(i, (i + 1) % count) for i in range(count)]),
                cells,
                lax.ppermute(head, axis, [((i + 1) % count, i) for i in range(count)]),
            ],
            axis=dim,
        )
    return cells


def apply_block(matrix, vector):
    return jnp.einsum(
        "lij,lj->li", matrix.astype(jnp.float32), vector, precision=lax.Precision.HIGHEST
    )


def forward_step(carried, items):
    dblock, lblock, rhs_now, act_now = items
    value = act_now[:, None] * apply_block(dblock, rhs_now - apply_block(lblock, carried))
    return (value, value)


def backward_step(carried, items):
    dblock, ublock, y_now, act_now = items
    value = act_now[:, None] * (y_now - apply_block(dblock, apply_block(ublock, carried)))
    return (value, value)


def per_device(state, source, face_coef, neighbour, lift, elem_slot, line_len, dinv, lower, upper):
    slots = state.shape[0]
    extended = padded(state, (("surf", 0),), slots)
    nb_vals = jnp.take(extended, neighbour, axis=0).astype(jnp.float32)
    face_sum = jnp.sum(
        face_coef[:, :, None] * (state.astype(jnp.float32)[:, None, :] - nb_vals), axis=1
    ).astype(jnp.bfloat16)
    residual = source.astype(jnp.float32) - jnp.dot(
        face_sum, lift, preferred_element_type=jnp.float32
    )
    line_rhs = jnp.take(residual, elem_slot, axis=0)
    depth = dinv.shape[0]
    line_count = dinv.shape[1]
    width = dinv.shape[2]
    wall_index = lax.axis_index("wall")
    wall_count = lax.axis_size("wall")
    share = line_count // wall_count
    moved_dinv, moved_lower, moved_upper = (
        lax.all_to_all(dinv, "wall", split_axis=1, concat_axis=0, tiled=True),
        lax.all_to_all(lower, "wall", split_axis=1, concat_axis=0, tiled=True),
        lax.all_to_all(upper, "wall", split_axis=1, concat_axis=0, tiled=True),
    )
    moved_rhs = lax.all_to_all(line_rhs, "wall", split_axis=1, concat_axis=0, tiled=True)
    lengths = lax.dynamic_slice_in_dim(line_len, wall_index * share, share)
    positions = jnp.arange(depth * wall_count, dtype=jnp.int32)
    line_active = (positions[:, None] < lengths[None, :]).astype(jnp.float32)
    zero_lines = jnp.zeros((share, width), jnp.float32)
    _, line_forward = lax.scan(
        forward_step, zero_lines, (moved_dinv, moved_lower, moved_rhs, line_active), unroll=8
    )
    _, line_solution = lax.scan(
        backward_step,
        zero_lines,
        (moved_dinv, moved_upper, line_forward, line_active),
        reverse=True,
        unroll=8,
    )
    solution = lax.all_to_all(line_solution, "wall", split_axis=0, concat_axis=1, tiled=True)
    return solution


def solution(mesh):
    in_specs = (
        P(("wall", "surf"), None),
        P(("wall", "surf"), None),
        P(("wall", "surf"), None),
        P(("wall", "surf"), None),
        P(),
        P("wall", "surf"),
        P("surf"),
        P("wall", "surf", None, None),
        P("wall", "surf", None, None),
        P("wall", "surf", None, None),
    )
    out_specs = P("wall", "surf", None)
    return jax.shard_map(
        per_device, mesh=mesh, in_specs=in_specs, out_specs=out_specs, check_vma=False
    )
```

profile of v0, /device:TPU:1, one launch (start us, length us, event | category | flops | bytes accessed | tf_op | source)
XLA Modules:
  0.0 132.1 jit_solution(18088914985217543344)
XLA Ops:
  0.0 2.1 %collective-permute-start = (bf16[16,162]{1,0:T(8,128)(2,1)}, bf16[16,162]{1,0:T(8,128)(2,1)S(1)}, u32[]{:S(2)}, u32[]{:S(2)}) collective-permute-start(bf16[16,162]{1,0:T(8,128)(2,1)} %param.14), channel_id=1, source_target_pairs={{0,1},{1,2},{2,3},{3,0},{4,5},{5,6},{6,7},{7,4},{8,9},{9,10},{10,1... | collective-permute-start | bytes 15560 | tf_op jit(solution)/shard_map/ppermute | solution.py:14
  2.1 2.1 %collective-permute-start.1 = (bf16[16,162]{1,0:T(8,128)(2,1)}, bf16[16,162]{1,0:T(8,128)(2,1)S(1)}, u32[]{:S(2)}, u32[]{:S(2)}) collective-permute-start(bf16[16,162]{1,0:T(8,128)(2,1)} %param.14), channel_id=1, source_target_pairs={{1,0},{2,1},{3,2},{0,3},{5,4},{6,5},{7,6},{4,7},{9,8},{10,9},{11,1... | collective-permute-start | bytes 15560 | tf_op jit(solution)/shard_map/ppermute | solution.py:16
  7.9 0.8 copy.28
  10.5 0.8 convolution_subtract_fusion
  12.6 4.8 %all-to-all-start.1 = ((f32[2,8,162]{2,0,1:T(2,128)}), f32[2,8,162]{2,0,1:T(2,128)S(1)}, u32[]{:S(2)}, u32[]{:S(2)}) async-start(f32[2,8,162]{2,0,1:T(2,128)} %copy_select_fusion), calls=%async_computation.1 | async-start | bytes 32768 | tf_op jit(solution)/shard_map/all_to_all | solution.py:63
  17.4 2.7 %copy.26 = bf16[2,8,162,162]{3,2,0,1:T(8,128)(2,1)} copy(bf16[2,8,162,162]{3,1,2,0:T(8,128)(2,1)} %param.21) | data formatting | bytes 1679616 | tf_op args[7]
  20.1 1.3 %all-to-all-done.1 = f32[2,8,162]{2,0,1:T(2,128)S(1)} async-done(((f32[2,8,162]{2,0,1:T(2,128)}), f32[2,8,162]{2,0,1:T(2,128)S(1)}, u32[]{:S(2)}, u32[]{:S(2)}) %all-to-all-start.1) | async-done | bytes 10400 | tf_op jit(solution)/shard_map/all_to_all | solution.py:63
  21.4 4.2 %all-to-all-start = ((bf16[2,8,162,162]{3,2,0,1:T(8,128)(2,1)}), bf16[2,8,162,162]{3,2,0,1:T(8,128)(2,1)S(1)}, u32[]{:S(2)}, u32[]{:S(2)}) async-start(bf16[2,8,162,162]{3,2,0,1:T(8,128)(2,1)} %copy.26), calls=%async_computation | async-start | bytes 2752512 | tf_op jit(solution)/shard_map/all_to_all | solution.py:59
  25.6 1.4 %copy.32 = bf16[2,8,162,162]{3,2,0,1:T(8,128)(2,1)} copy(bf16[2,8,162,162]{3,1,2,0:T(8,128)(2,1)S(1)} %copy-done.2) | data formatting | bytes 1679616 | tf_op args[8]
  27.0 14.1 %all-to-all-done = bf16[2,8,162,162]{3,2,0,1:T(8,128)(2,1)S(1)} async-done(((bf16[2,8,162,162]{3,2,0,1:T(8,128)(2,1)}), bf16[2,8,162,162]{3,2,0,1:T(8,128)(2,1)S(1)}, u32[]{:S(2)}, u32[]{:S(2)}) %all-to-all-start) | async-done | bytes 839840 | tf_op jit(solution)/shard_map/all_to_all | solution.py:59
  41.1 7.0 %all-to-all-start.2 = ((bf16[2,8,162,162]{3,2,0,1:T(8,128)(2,1)}), bf16[2,8,162,162]{3,2,0,1:T(8,128)(2,1)S(1)}, u32[]{:S(2)}, u32[]{:S(2)}) async-start(bf16[2,8,162,162]{3,2,0,1:T(8,128)(2,1)} %copy.32), calls=%async_computation.2 | async-start | bytes 2752512 | tf_op jit(solution)/shard_map/all_to_all | solution.py:60
  48.1 2.7 %copy.36 = bf16[2,8,162,162]{3,2,0,1:T(8,128)(2,1)} copy(bf16[2,8,162,162]{3,1,2,0:T(8,128)(2,1)} %param.23) | data formatting | bytes 1679616 | tf_op args[9]
  52.0 11.5 %all-to-all-done.2 = bf16[2,8,162,162]{3,2,0,1:T(8,128)(2,1)S(1)} async-done(((bf16[2,8,162,162]{3,2,0,1:T(8,128)(2,1)}), bf16[2,8,162,162]{3,2,0,1:T(8,128)(2,1)S(1)}, u32[]{:S(2)}, u32[]{:S(2)}) %all-to-all-start.2) | async-done | bytes 839840 | tf_op jit(solution)/shard_map/all_to_all | solution.py:60
  63.5 1.1 copy-done.1
  64.6 7.0 %all-to-all-start.3 = ((bf16[2,8,162,162]{3,2,0,1:T(8,128)(2,1)}), bf16[2,8,162,162]{3,2,0,1:T(8,128)(2,1)S(1)}, u32[]{:S(2)}, u32[]{:S(2)}) async-start(bf16[2,8,162,162]{3,2,0,1:T(8,128)(2,1)} %copy.36), calls=%async_computation.3 | async-start | bytes 2752512 | tf_op jit(solution)/shard_map/all_to_all | solution.py:61
  71.6 33.1 %while.28 = (s32[]{:T(128)}, f32[1,162]{1,0:T(1,128)S(1)}, f32[2,8,1,162]{3,2,1,0:T(1,128)S(1)}, f32[2,8,1]{1,2,0:T(1,128)S(1)}, bf16[2,8,1,162,162]{4,3,2,1,0:T...) while((s32[]{:T(128)}, f32[1,162]{1,0:T(1,128)S(1)}, ...), condition=%wide.region_2.3_spmd, body=%wide.region_1.2_spmd.sunk | while | flops 5041449 | bytes 1473297 | solution.py:68
  71.7 1.0 fusion.167
  72.9 0.8 fusion.169
  74.4 1.0 fusion.170
  76.3 1.0 fusion.172
  77.5 0.8 broadcast_multiply_fusion.18
  78.3 1.0 fusion.174
  79.6 0.8 broadcast_multiply_fusion.19
  80.4 1.0 fusion.176
  81.6 0.8 broadcast_multiply_fusion.20
  82.4 1.0 fusion.178
  84.3 1.0 fusion.180
  86.2 1.0 fusion.182
  88.2 1.0 fusion.167
  89.5 0.8 fusion.169
  90.9 1.0 fusion.170
  92.9 1.0 fusion.172
  94.1 0.8 broadcast_multiply_fusion.18
  94.9 1.0 fusion.174
  96.1 0.8 broadcast_multiply_fusion.19
  96.9 1.0 fusion.176
  98.2 0.8 broadcast_multiply_fusion.20
  99.0 1.0 fusion.178
  100.8 1.0 fusion.180
  102.8 1.0 fusion.182
  104.8 18.7 %while.29 = (s32[]{:T(128)}, f32[1,162]{1,0:T(1,128)S(1)}, f32[2,8,1,162]{3,2,1,0:T(1,128)S(1)}, f32[2,8,1]{1,2,0:T(1,128)S(1)}, f32[2,8,1,162]{3,2,1,0:T(1,128)...) while((s32[]{:T(128)}, f32[1,162]{1,0:T(1,128)S(1)}, ...), condition=%wide.region_4.5_spmd, body=%wide.region_3.4_spmd.sunk | while | flops 5041450 | bytes 1461885 | solution.py:71
  107.0 0.8 subtract_multiply_fusion.17
  109.1 0.7 subtract_multiply_fusion.19
  110.2 0.7 subtract_multiply_fusion.20
  116.3 0.8 subtract_multiply_fusion.17
  118.5 0.7 subtract_multiply_fusion.19
  119.5 0.7 subtract_multiply_fusion.20
  123.5 8.1 %all_to_all.78 = f32[16,1,162]{2,1,0:T(1,128)S(1)} all-to-all(f32[16,1,162]{2,1,0:T(1,128)S(1)} %bitcast.721), channel_id=1, replica_groups=mesh['wall'=8,'surf'=4] {'wall'}, dimensions={0} | all-to-all | bytes 20736 | tf_op jit(solution)/shard_map/all_to_all | solution.py:78
  (166 shorter events, 33.0 us)
Async XLA Ops:
  0.0 10.5 %copy-start = (bf16[162,162]{1,0:T(8,128)(2,1)S(1)}, bf16[162,162]{1,0:T(8,128)(2,1)}, u32[]{:S(2)}) copy-start(bf16[162,162]{1,0:T(8,128)(2,1)} %param.18) | copy-start | bytes 157468
  0.0 8.9 %collective-permute-start = (bf16[16,162]{1,0:T(8,128)(2,1)}, bf16[16,162]{1,0:T(8,128)(2,1)S(1)}, u32[]{:S(2)}, u32[]{:S(2)}) collective-permute-start(bf16[16,162]{1,0:T(8,128)(2,1)} %param.14), channel_id=1, source_target_pairs={{0,1},{1,2},{2,3},{3,0},{4,5},{5,6},{6,7},{7,4},{8,9},{9,10},{10,1... | collective-permute-start | bytes 15560 | tf_op jit(solution)/shard_map/ppermute | solution.py:14
  2.1 6.8 %collective-permute-start.1 = (bf16[16,162]{1,0:T(8,128)(2,1)}, bf16[16,162]{1,0:T(8,128)(2,1)S(1)}, u32[]{:S(2)}, u32[]{:S(2)}) collective-permute-start(bf16[16,162]{1,0:T(8,128)(2,1)} %param.14), channel_id=1, source_target_pairs={{1,0},{2,1},{3,2},{0,3},{5,4},{6,5},{7,6},{4,7},{9,8},{10,9},{11,1... | collective-permute-start | bytes 15560 | tf_op jit(solution)/shard_map/ppermute | solution.py:16
  12.6 8.9 %all-to-all-start.1 = ((f32[2,8,162]{2,0,1:T(2,128)}), f32[2,8,162]{2,0,1:T(2,128)S(1)}, u32[]{:S(2)}, u32[]{:S(2)}) async-start(f32[2,8,162]{2,0,1:T(2,128)} %copy_select_fusion), calls=%async_computation.1 | async-start | bytes 32768 | tf_op jit(solution)/shard_map/all_to_all | solution.py:63
  20.1 5.6 %copy-start.2 = (bf16[2,8,162,162]{3,1,2,0:T(8,128)(2,1)S(1)}, bf16[2,8,162,162]{3,1,2,0:T(8,128)(2,1)}, u32[]{:S(2)}) copy-start(bf16[2,8,162,162]{3,1,2,0:T(8,128)(2,1)} %param.22) | copy-start | bytes 2519428
  21.4 19.6 %all-to-all-start = ((bf16[2,8,162,162]{3,2,0,1:T(8,128)(2,1)}), bf16[2,8,162,162]{3,2,0,1:T(8,128)(2,1)S(1)}, u32[]{:S(2)}, u32[]{:S(2)}) async-start(bf16[2,8,162,162]{3,2,0,1:T(8,128)(2,1)} %copy.26), calls=%async_computation | async-start | bytes 2752512 | tf_op jit(solution)/shard_map/all_to_all | solution.py:59
  41.1 22.4 %all-to-all-start.2 = ((bf16[2,8,162,162]{3,2,0,1:T(8,128)(2,1)}), bf16[2,8,162,162]{3,2,0,1:T(8,128)(2,1)S(1)}, u32[]{:S(2)}, u32[]{:S(2)}) async-start(bf16[2,8,162,162]{3,2,0,1:T(8,128)(2,1)} %copy.32), calls=%async_computation.2 | async-start | bytes 2752512 | tf_op jit(solution)/shard_map/all_to_all | solution.py:60
  48.1 2.7 %copy-start.3 = (s32[8]{0:T(128)S(1)}, s32[8]{0:T(128)}, u32[]{:S(2)}) copy-start(s32[8]{0:T(128)} %param.20) | copy-start | bytes 100
  63.5 1.1 copy-start.1
  64.6 40.2 %all-to-all-start.3 = ((bf16[2,8,162,162]{3,2,0,1:T(8,128)(2,1)}), bf16[2,8,162,162]{3,2,0,1:T(8,128)(2,1)S(1)}, u32[]{:S(2)}, u32[]{:S(2)}) async-start(bf16[2,8,162,162]{3,2,0,1:T(8,128)(2,1)} %copy.36), calls=%async_computation.3 | async-start | bytes 2752512 | tf_op jit(solution)/shard_map/all_to_all | solution.py:61
where the time goes:
time: 134 us; the launch traced here: 132 us
  other arithmetic  28 us (21%)
  starting transfers between devices  27.3 us (20%)
  waiting for transfers between devices  26.9 us (20%)
  matrix products  26.3 us (20%)
  local copies, waits for them, and re-layouts  15 us (11%)
  blocking collectives  8.05 us (6%)
    dot_general x64, matrix products, apply_block(): jnp.einsum('lij,lj->li', matrix.astype(jnp.float32), vector, precision=la...  25.5 us
    all_to_all x1, waiting for transfers between devices, per_device(): lax.all_to_all(dinv, 'wall', split_axis=1, concat_axis=0, tiled=True)  14.1 us
    all_to_all x1, waiting for transfers between devices, per_device(): lax.all_to_all(lower, 'wall', split_axis=1, concat_axis=0, tiled=True)  11.5 us
    mul x16, other arithmetic, forward_step(): act_now[:, None]  11.2 us
    mul x16, other arithmetic, backward_step(): act_now[:, None]  11.1 us
    unnamed x12, local copies, waits for them, and re-layouts  8.58 us
    all_to_all x1, blocking collectives, per_device(): lax.all_to_all(line_solution, 'wall', split_axis=0, concat_axis=1, tiled=...  8.05 us
    all_to_all x1, starting transfers between devices, per_device(): lax.all_to_all(lower, 'wall', split_axis=1, concat_axis=0, tiled=True)  7.01 us
  transfers between devices with their start and end apart: 6, of which 3 were waited for; matrix products, arithmetic and copies ran while one was open for 34% of the time, Pallas kernels for 0%

commit v1 on v0

v1 whole, which is shorter than its diff:
```python
import functools

import jax
import jax.numpy as jnp
from jax import lax
from jax.experimental import pallas as pl
from jax.experimental.pallas import tpu as pltpu
from jax.sharding import PartitionSpec as P

F32 = jnp.float32
BF16 = jnp.bfloat16
ROWS = 8
VMEM = pl.BlockSpec(memory_space=pltpu.VMEM)
SMEM = pl.BlockSpec(memory_space=pltpu.SMEM)
ANY = pl.BlockSpec(memory_space=pl.ANY)


def split2(x):
    high = x.astype(BF16)
    return high, (x - high.astype(F32)).astype(BF16)


def stacked(v):
    return jnp.concatenate(split2(v), axis=0)


def product(x, y):
    dot = functools.partial(jnp.dot, preferred_element_type=F32)
    return dot(x[0], y[0]) + (dot(x[0], y[1]) + dot(x[1], y[0]))


def row_index(width):
    return lax.broadcasted_iota(jnp.int32, (ROWS, width), 0)


def apply_pairs(vector, pair_of, lines):
    rows = row_index(vector.shape[1])
    both = stacked(vector)
    total = jnp.zeros(vector.shape, F32)
    for l in range(lines):
        high, low = pair_of(l)
        first = jnp.dot(both, high, preferred_element_type=F32)
        second = jnp.dot(both, low, preferred_element_type=F32)
        part = first[:ROWS] + first[ROWS:] + second[:ROWS]
        total = jnp.where(rows == l, part, total)
    return total


def apply_rows(vector, matrix_of, lines):
    rows = row_index(vector.shape[1])
    both = stacked(vector)
    total = jnp.zeros(vector.shape, F32)
    for l in range(lines):
        first = lax.dot_general(
            both, matrix_of(l), (((1,), (1,)), ((), ())), preferred_element_type=F32
        )
        total = jnp.where(rows == l, first[:ROWS] + first[ROWS:], total)
    return total


def core_of():
    return lax.rem(lax.axis_index("wall"), 2)


def chip_of():
    return lax.div(lax.axis_index("wall"), 2)


def relayout_kernel(dinv_ref, lower_ref, upper_ref, own_ref, send_ref, scratch):
    half = own_ref.shape[2]
    core = core_of()
    for a, ref in enumerate((dinv_ref, lower_ref, upper_ref)):
        for e in range(own_ref.shape[1]):
            slot = (a * own_ref.shape[1] + e) % 2
            scratch[slot] = ref[e].astype(F32)
            for l in range(half):
                own_ref[a, e, l] = scratch[slot, :, core * half + l, :].astype(BF16)
                send_ref[a, e, l] = scratch[slot, :, (1 - core) * half + l, :].astype(BF16)


def pair_kernel(*refs, first):
    if first:
        raw_ref, q_ref, s_ref, a_ref, c_ref = refs
    else:
        raw_ref, _, _, a_own, c_own, q_ref, s_ref, a_ref, c_ref = refs
    core = core_of()
    place = core if first else 1 - core
    count, lines = raw_ref.shape[1], raw_ref.shape[2]
    for l in range(lines):
        qs, ss = [], []
        for e in range(count):
            for held, ref, source in ((qs, q_ref, 1), (ss, s_ref, 2)):
                block = lax.dot_general(
                    raw_ref[source, e, l],
                    raw_ref[0, e, l],
                    (((0,), (1,)), ((), ())),
                    preferred_element_type=F32,
                )
                pair = split2(block)
                held.append(pair)
                ref[place, e, l, 0] = pair[0]
                ref[place, e, l, 1] = pair[1]
        forward = qs[0]
        for e in range(1, count):
            forward = split2(product(forward, qs[e]))
        backward = ss[count - 1]
        for e in range(count - 2, -1, -1):
            backward = split2(product(backward, ss[e]))
        if not first:
            own = (a_own[l, 0], a_own[l, 1])
            early = [jnp.where(core == 0, x, y) for x, y in zip(own, forward)]
            late = [jnp.where(core == 0, y, x) for x, y in zip(own, forward)]
            forward = split2(product(early, late))
            own = (c_own[l, 0], c_own[l, 1])
            early = [jnp.where(core == 0, x, y) for x, y in zip(own, backward)]
            late = [jnp.where(core == 0, y, x) for x, y in zip(own, backward)]
            backward = split2(product(late, early))
        a_ref[l, 0], a_ref[l, 1] = forward
        c_ref[l, 0], c_ref[l, 1] = backward


def prepare_kernel(
    slot_ref, len_ref, coef_ref, nb_ref, source_ref, weight_ref, rhs_ref, act_ref, *, block
):
    faces, slots = coef_ref.shape
    depth, line_count = slot_ref.shape
    half = line_count // 2
    blocks = half // block
    core, chip = core_of(), chip_of()
    cells = 3 * slots
    k = lax.broadcasted_iota(jnp.int32, (cells, slots), 0)
    e = lax.broadcasted_iota(jnp.int32, (cells, slots), 1)
    weight = jnp.zeros((cells, slots), F32)
    own = jnp.zeros((1, slots), F32)
    for f in range(faces):
        coef = coef_ref[f : f + 1, :]
        own = own + coef
        weight = weight - jnp.where(k == nb_ref[f : f + 1, :], coef, 0.0)
    weight = weight + jnp.where(k == e + slots, own, 0.0)
    count = 2 * depth * blocks * ROWS
    rows = lax.broadcasted_iota(jnp.int32, (count, slots), 0)
    slot = jnp.full((count, slots), -1, jnp.int32)
    for h in range(2):
        first_line = lax.rem(core + h, 2) * half
        for g in range(depth):
            for b in range(blocks):
                for r in range(block):
                    row = ((h * depth + g) * blocks + b) * ROWS + r
                    here = slot_ref[g, first_line + b * block + r]
                    slot = jnp.where(rows == row, here, slot)
    chosen = (slot == lax.broadcasted_iota(jnp.int32, (count, slots), 1)).astype(F32).astype(BF16)
    high, rest = split2(weight)
    rest = weight - high.astype(F32)
    mid, low = split2(rest)
    for i, part in enumerate((high, mid, low)):
        weight_ref[i * count : (i + 1) * count, :] = lax.dot_general(
            chosen, part, (((1,), (1,)), ((), ())), preferred_element_type=F32
        ).astype(BF16)
    rhs_ref[...] = jnp.dot(chosen, source_ref[...], preferred_element_type=F32)
    width = act_ref.shape[2]
    rows = lax.broadcasted_iota(jnp.int32, (blocks * ROWS, width), 0)
    length = jnp.zeros((blocks * ROWS, width), jnp.int32)
    for b in range(blocks):
        for r in range(block):
            here = len_ref[core * half + b * block + r]
            length = jnp.where(rows == b * ROWS + r, here, length)
    for g in range(2 * depth):
        act_ref[g] = (chip * (2 * depth) + g < length).astype(F32)


def residual_kernel(before, state, after, weight, source, lift, own_ref, send_ref):
    cells = jnp.concatenate([before[...], state[...], after[...]], axis=0)
    parts = jnp.dot(weight[...], cells, preferred_element_type=F32)
    count = source.shape[0]
    face_sum = parts[:count] + (parts[count : 2 * count] + parts[2 * count :])
    flux = jnp.dot(face_sum.astype(BF16), lift[...], preferred_element_type=F32)
    rhs = source[...] - flux
    depth, rows, _ = own_ref.shape
    for g in range(depth):
        own_ref[g] = rhs[g * rows : (g + 1) * rows]
        send_ref[g] = rhs[(depth + g) * rows : (depth + g + 1) * rows]


def scaled_kernel(rhs_ref, raw_ref, out_ref):
    for e in range(rhs_ref.shape[0]):
        out_ref[e] = apply_rows(rhs_ref[e], lambda l: raw_ref[0, e, l], raw_ref.shape[2])


def forward_local(scaled, q_ref, act_ref, carried):
    depth, lines = q_ref.shape[1], q_ref.shape[2]
    values = []
    for g in range(2 * depth):
        value = scaled[g]
        if carried is not None:
            value = value - apply_pairs(
                carried, lambda l: (q_ref[g // depth, g % depth, l, 0], q_ref[g // depth, g % depth, l, 1]), lines
            )
        carried = act_ref[g] * value
        values.append(carried)
    return values


def backward_local(values, s_ref, act_ref, carried):
    depth, lines = s_ref.shape[1], s_ref.shape[2]
    solved = [None] * len(values)
    for g in range(2 * depth - 1, -1, -1):
        value = values[g]
        if carried is not None:
            value = value - apply_pairs(
                carried, lambda l: (s_ref[g // depth, g % depth, l, 0], s_ref[g // depth, g % depth, l, 1]), lines
            )
        carried = act_ref[g] * value
        solved[g] = carried
    return solved


def first_kernel(own_ref, rhs_ref, raw_ref, q_ref, act_ref, scaled_ref, b_ref):
    depth = own_ref.shape[0]
    core = core_of()
    own = [own_ref[e] for e in range(depth)]
    other = [
        apply_rows(rhs_ref[e], lambda l: raw_ref[0, e, l], raw_ref.shape[2]) for e in range(depth)
    ]
    scaled = [jnp.where(core == 0, x, y) for x, y in zip(own, other)]
    scaled += [jnp.where(core == 0, y, x) for x, y in zip(own, other)]
    for g in range(2 * depth):
        scaled_ref[g] = scaled[g]
    b_ref[...] = forward_local(scaled, q_ref, act_ref, None)[-1]


def hop_kernel(came_ref, pair_ref, act_ref, local_ref, out_ref, *, chip):
    out_ref[...] = local_ref[...]

    @pl.when(chip_of() == chip)
    def _():
        gone = apply_pairs(
            came_ref[...], lambda l: (pair_ref[l, 0], pair_ref[l, 1]), pair_ref.shape[0]
        )
        out_ref[...] = act_ref[act_ref.shape[0] - 1] * gone + local_ref[...]


def chosen_arrival(refs, chips):
    here = chip_of()
    value = jnp.zeros(refs[0].shape, F32)
    for ref, chip in zip(refs, chips):
        value = jnp.where(here == chip, ref[...], value)
    return value


def turn_kernel(scaled_ref, q_ref, s_ref, act_ref, *refs, chips):
    came, y_ref, d_ref = refs[:-2], refs[-2], refs[-1]
    count = scaled_ref.shape[0]
    carried = chosen_arrival(came, chips)
    values = forward_local([scaled_ref[g] for g in range(count)], q_ref, act_ref, carried)
    for g in range(count):
        y_ref[g] = values[g]
    d_ref[...] = backward_local(values, s_ref, act_ref, None)[0]


def last_kernel(y_ref, s_ref, act_ref, *refs, chips):
    came, own_ref, send_ref = refs[:-2], refs[-2], refs[-1]
    count = y_ref.shape[0]
    depth = count // 2
    core = core_of()
    carried = chosen_arrival(came, chips)
    solved = backward_local([y_ref[g] for g in range(count)], s_ref, act_ref, carried)
    for e in range(depth):
        own_ref[e] = jnp.where(core == 0, solved[e], solved[depth + e])
        send_ref[e] = jnp.where(core == 0, solved[depth + e], solved[e])


def merge_kernel(own_ref, other_ref, out_ref, *, block):
    core = core_of()
    blocks = own_ref.shape[1] // ROWS
    for e in range(out_ref.shape[0]):
        own = [own_ref[e, b * ROWS : b * ROWS + block] for b in range(blocks)]
        other = [other_ref[e, b * ROWS : b * ROWS + block] for b in range(blocks)]
        out_ref[e] = jnp.where(
            core == 0,
            jnp.concatenate(own + other, axis=0),
            jnp.concatenate(other + own, axis=0),
        )


def padded_bytes(shape, dtype):
    size = jnp.dtype(dtype).itemsize
    shape = (1,) * (2 - len(shape)) + tuple(shape)
    rows = -(-shape[-2] // 16) * 16
    columns = -(-shape[-1] // 128) * 128
    total = rows * columns * size
    for extent in shape[:-2]:
        total *= extent
    return total


def run(kernel, operands, outs, blocks=1, scratch=(), aliases=None):
    everything = [(x.shape, x.dtype) for x, _ in operands] + [(s, t) for s, t, _ in outs]
    everything += [(s.shape, s.dtype) for s in scratch]
    limit = sum(padded_bytes(s, t) for s, t in everything)
    if blocks == 1:
        in_specs = [at if isinstance(at, pl.BlockSpec) else VMEM for _, at in operands]
        out_specs = [VMEM for _ in outs]
        grid = ()
    else:

        def spec(shape, at):
            if isinstance(at, pl.BlockSpec):
                return at
            if at is None:
                return pl.BlockSpec(shape, lambda i: (0,) * len(shape))
            size = tuple(n // blocks if axis == at else n for axis, n in enumerate(shape))
            return pl.BlockSpec(size, lambda i: tuple(i if axis == at else 0 for axis in range(len(shape))))

        in_specs = [spec(x.shape, at) for x, at in operands]
        out_specs = [spec(s, at) for s, _, at in outs]
        grid = (blocks,)
        limit = 2 * limit // blocks
    limit = min(limit + limit // 4 + (4 << 20), 60 << 20)
    return pl.pallas_call(
        kernel,
        grid=grid,
        in_specs=in_specs,
        out_specs=out_specs,
        out_shape=[jax.ShapeDtypeStruct(s, t) for s, t, _ in outs],
        scratch_shapes=list(scratch),
        input_output_aliases=aliases or {},
        compiler_params=pltpu.CompilerParams(vmem_limit_bytes=limit),
    )(*[x for x, _ in operands])


def flips(count):
    return [(i, i ^ 1) for i in range(count)]


def hop_pairs(count, start, end, spare):
    target = {i: i ^ 1 for i in range(count)}
    cycle = [start, end] + ([] if spare is None else [spare])
    for here, there in zip(cycle, cycle[1:] + cycle[:1]):
        for core in range(2):
            target[2 * here + core] = 2 * there + core
    return sorted(target.items())


def spare_chip(chips, start, end):
    behind = 2 * start - end
    if 0 <= behind < chips:
        return behind
    ahead = chips - 1 if end > start else 0
    return ahead if ahead not in (start, end) else None


def per_device(state, source, face_coef, neighbour, lift, elem_slot, line_len, dinv, lower, upper):
    wall_count = lax.axis_size("wall")
    surf_count = lax.axis_size("surf")
    chips = wall_count // 2
    depth, line_count, width, _ = dinv.shape
    half = line_count // 2
    block = max(n for n in range(1, ROWS + 1) if half % n == 0)
    blocks = half // block
    rows = blocks * ROWS
    core = lax.rem(lax.axis_index("wall"), 2)

    before = lax.ppermute(state, "surf", [(i, (i + 1) % surf_count) for i in range(surf_count)])
    after = lax.ppermute(state, "surf", [((i + 1) % surf_count, i) for i in range(surf_count)])

    raw_shape = (3, depth, half, width, width)
    if line_count == ROWS:
        turned = [jnp.transpose(x, (0, 2, 1, 3)) for x in (dinv, lower, upper)]
        own, send = run(
            relayout_kernel,
            [(x, None) for x in turned],
            [(raw_shape, BF16, None)] * 2,
            scratch=[pltpu.VMEM((2, width, line_count, width), F32)],
        )
    else:
        every = jnp.stack([dinv, lower, upper])
        own = lax.dynamic_slice_in_dim(every, core * half, half, axis=2)
        send = lax.dynamic_slice_in_dim(every, (1 - core) * half, half, axis=2)
    came = lax.ppermute(send, "wall", flips(wall_count))

    count = 2 * depth * rows
    weight, line_source, act = run(
        functools.partial(prepare_kernel, block=block),
        [
            (elem_slot, SMEM),
            (line_len, SMEM),
            (face_coef.T, None),
            (neighbour.T, None),
            (source, None),
        ],
        [
            ((3 * count, 3 * state.shape[0]), BF16, None),
            ((count, width), F32, None),
            ((2 * depth, rows, width), F32, None),
        ],
    )

    pairs_shape = (2, depth, half, 2, width, width)
    chip_shape = (half, 2, width, width)
    pair_outs = [(pairs_shape, BF16, 2), (pairs_shape, BF16, 2), (chip_shape, BF16, 0), (chip_shape, BF16, 0)]
    q_half, s_half, a_own, c_own = run(
        functools.partial(pair_kernel, first=True), [(own, 2)], pair_outs, blocks
    )
    own_rhs, send_rhs = run(
        residual_kernel,
        [(before, None), (state, None), (after, None), (weight, None), (line_source, None), (lift, None)],
        [((depth, rows, width), F32, None)] * 2,
    )
    came_rhs = lax.ppermute(send_rhs, "wall", flips(wall_count))
    (own_scaled,) = run(
        scaled_kernel, [(own_rhs, 1), (own, 2)], [((depth, rows, width), F32, 1)], blocks
    )
    q, s, a, c = run(
        functools.partial(pair_kernel, first=False),
        [(came, 2), (q_half, ANY), (s_half, ANY), (a_own, 0), (c_own, 0)],
        pair_outs,
        blocks,
        aliases={1: 0, 2: 1},
    )
    scaled, local = run(
        first_kernel,
        [(own_scaled, 1), (came_rhs, 1), (came, 2), (q, 2), (act, 1)],
        [((2 * depth, rows, width), F32, 1), ((rows, width), F32, 0)],
        blocks,
    )

    def hop(came, pair, local, chip):
        (out,) = run(
            functools.partial(hop_kernel, chip=chip),
            [(came, 0), (pair, 0), (act, 1), (local, 0)],
            [((rows, width), F32, 0)],
            blocks,
        )
        return out

    arrivals = []
    for chip in range(chips - 1):
        out = local if chip == 0 else hop(arrivals[-1], a, local, chip)
        pairs = hop_pairs(wall_count, chip, chip + 1, spare_chip(chips, chip, chip + 1))
        arrivals.append(lax.ppermute(out, "wall", pairs))
    y, back = run(
        functools.partial(turn_kernel, chips=list(range(1, chips))),
        [(scaled, 1), (q, 2), (s, 2), (act, 1)] + [(x, 0) for x in arrivals],
        [((2 * depth, rows, width), F32, 1), ((rows, width), F32, 0)],
        blocks,
    )
    arrivals = []
    for chip in range(chips - 1, 0, -1):
        out = back if chip == chips - 1 else hop(arrivals[-1], c, back, chip)
        pairs = hop_pairs(wall_count, chip, chip - 1, spare_chip(chips, chip, chip - 1))
        arrivals.append(lax.ppermute(out, "wall", pairs))
    own_part, send_part = run(
        functools.partial(last_kernel, chips=list(range(chips - 2, -1, -1))),
        [(y, 1), (s, 2), (act, 1)] + [(x, 0) for x in arrivals],
        [((depth, rows, width), F32, 1)] * 2,
        blocks,
    )
    other_part = lax.ppermute(send_part, "wall", flips(wall_count))
    (solution,) = run(
        functools.partial(merge_kernel, block=block),
        [(own_part, None), (other_part, None)],
        [((depth, line_count, width), F32, None)],
    )
    return solution


def solution(mesh):
    in_specs = (
        P(("wall", "surf"), None),
        P(("wall", "surf"), None),
        P(("wall", "surf"), None),
        P(("wall", "surf"), None),
        P(),
        P("wall", "surf"),
        P("surf"),
        P("wall", "surf", None, None),
        P("wall", "surf", None, None),
        P("wall", "surf", None, None),
    )
    out_specs = P("wall", "surf", None)
    return jax.shard_map(
        per_device, mesh=mesh, in_specs=in_specs, out_specs=out_specs, check_vma=False
    )
```

time: 134 us -> 55.5 us (0.41)
  other arithmetic: 28 us -> 0 us
  matrix products: 26.3 us -> 0 us
  Pallas kernels: 0 us -> 19.7 us
  waiting for transfers between devices: 26.9 us -> 11.2 us
  local copies, waits for them, and re-layouts: 15 us -> 5.07 us
  starting transfers between devices: 27.3 us -> 18.4 us
  blocking collectives: 8.05 us -> 0 us
    all_to_all x4 -> x0, waiting for transfers between devices: 26.9 us -> none  [the longest x1 14.1 us: per_device(): lax.all_to_all(dinv, 'wall', split_axis=1, concat_axis=0, tiled=True)]
    dot_general x65 -> x0, matrix products: 26.3 us -> none  [the longest x64 25.5 us: apply_block(): jnp.einsum('lij,lj->li', matrix.astype(jnp.float32), vector, precision=la...]
    all_to_all x4 -> x0, starting transfers between devices: 23.1 us -> none  [the longest x1 7.01 us: per_device(): lax.all_to_all(lower, 'wall', split_axis=1, concat_axis=0, tiled=True)]
    mul x32 -> x0, other arithmetic: 22.3 us -> none  [the longest x16 11.2 us: forward_step(): act_now[:, None]]
    pallas_call x0 -> x14, Pallas kernels: none -> 19.7 us  [run(): pl.pallas_call(kernel, grid=grid, in_specs=in_specs, out_specs=out_specs,...]
    ppermute x2 -> x11, starting transfers between devices: 4.21 us -> 18.4 us  [the longest x6 8.47 us: per_device(): arrivals.append(lax.ppermute(out, 'wall', pairs))]
    ppermute x2 -> x11, waiting for transfers between devices: 0.01 us -> 11.2 us  [the longest x6 10.1 us: per_device(): arrivals.append(lax.ppermute(out, 'wall', pairs))]
    all_to_all x1 -> x0, blocking collectives: 8.05 us -> none  [per_device(): lax.all_to_all(line_solution, 'wall', split_axis=0, concat_axis=1, tiled=...]
  transfers between devices with their start and end apart: 6 -> 11, of which waited for: 3 -> 8; matrix products, arithmetic and copies ran while one was open for 34% -> 1% of each run, Pallas kernels for 0% -> 10%
where the time goes in v1:
time: 55.5 us; the launch traced here: 54.6 us
  Pallas kernels  19.7 us (35%)
  starting transfers between devices  18.4 us (33%)
  waiting for transfers between devices  11.2 us (20%)
  local copies, waits for them, and re-layouts  5.07 us (9%)
    pallas_call x14, Pallas kernels, run(): pl.pallas_call(kernel, grid=grid, in_specs=in_specs, out_specs=out_specs,...  19.7 us
    ppermute x6, waiting for transfers between devices, per_device(): arrivals.append(lax.ppermute(out, 'wall', pairs))  10.1 us
    ppermute x6, starting transfers between devices, per_device(): arrivals.append(lax.ppermute(out, 'wall', pairs))  8.47 us
    ppermute x1, starting transfers between devices, per_device(): other_part = lax.ppermute(send_part, 'wall', flips(wall_count))  4.02 us
    unnamed x20, local copies, waits for them, and re-layouts  4.01 us
    ppermute x1, starting transfers between devices, per_device(): lax.ppermute(state, 'surf', [(i, (i + 1) % surf_count) for i in range(sur...  2.74 us
    ppermute x1, starting transfers between devices, per_device(): lax.ppermute(state, 'surf', [((i + 1) % surf_count, i) for i in range(sur...  2.03 us
  transfers between devices with their start and end apart: 11, of which 8 were waited for; matrix products, arithmetic and copies ran while one was open for 1% of the time, Pallas kernels for 10%

profile of v1, /device:TPU:1, one launch (start us, length us, event | category | flops | bytes accessed | tf_op | source)
XLA Modules:
  0.0 54.6 jit_solution(6595844626381847507)
XLA Ops:
  0.0 1.3 %copy-done = bf16[2,8,162,162]{3,1,2,0:T(8,128)(2,1)S(1)} copy-done((bf16[2,8,162,162]{3,1,2,0:T(8,128)(2,1)S(1)}, bf16[2,8,162,162]{3,1,2,0:T(8,128)(2,1)}, u32[]{:S(2)}) %copy-start) | copy-done | bytes 839832
  1.3 1.3 %copy-done.1 = bf16[2,8,162,162]{3,1,2,0:T(8,128)(2,1)S(1)} copy-done((bf16[2,8,162,162]{3,1,2,0:T(8,128)(2,1)S(1)}, bf16[2,8,162,162]{3,1,2,0:T(8,128)(2,1)}, u32[]{:S(2)}) %copy-start.1) | copy-done | bytes 839832
  2.6 1.3 %copy-done.2 = bf16[2,8,162,162]{3,1,2,0:T(8,128)(2,1)S(1)} copy-done((bf16[2,8,162,162]{3,1,2,0:T(8,128)(2,1)S(1)}, bf16[2,8,162,162]{3,1,2,0:T(8,128)(2,1)}, u32[]{:S(2)}) %copy-start.2) | copy-done | bytes 839832
  4.0 10.6 %shard_map.102 = (bf16[3,2,4,162,162]{4,3,2,1,0:T(8,128)(2,1)S(1)}, bf16[3,2,4,162,162]{4,3,2,1,0:T(8,128)(2,1)S(1)}) custom-call(bf16[2,162,8,162]{3,2,1,0:T(8,128)(2,1)S(1)} %bitcast.5, bf16[2,162,8,162]{3,2,1,0:T(8,128)(2,1)S(1)} %bitcast.6, bf16[2,162,8,162]{3,2,1,0:T(8,128)(2,1)S(1)} %bitcast.7), custom_call_target="tpu_custom_call" | custom-call | tf_op jit(solution)/shard_map/pallas_call | solution.py:319
  14.6 0.0 copy-start.5
  14.6 0.0 copy-start.4
  14.6 0.0 copy-start.6
  14.6 0.0 copy-start.7
  14.6 0.0 copy-start.8
  14.6 0.0 copy-start.9
  14.6 0.0 copy-start.3
  14.7 0.8 %copy.13 = bf16[3,2,4,162,162]{4,2,3,1,0:T(4,128)(2,1)S(1)} copy(bf16[3,2,4,162,162]{4,3,2,1,0:T(8,128)(2,1)S(1)} %get-tuple-element.31) | data formatting | bytes 2519424 | tf_op jit(solution)/shard_map/pallas_call | solution.py:319
  15.4 0.1 collective-permute-start.3
  15.6 0.0 copy-done.5
  15.6 2.7 %collective-permute-start = (bf16[16,162]{1,0:T(8,128)(2,1)S(1)}, bf16[16,162]{1,0:T(8,128)(2,1)S(1)}, u32[]{:S(2)}, u32[]{:S(2)}) collective-permute-start(bf16[16,162]{1,0:T(8,128)(2,1)S(1)} %copy-done.5), channel_id=1, source_target_pairs={{0,1},{1,2},{2,3},{3,0},{4,5},{5,6},{6,7},{7,4},{8,9},{9,10},{10,1... | collective-permute-start | bytes 15560 | tf_op jit(solution)/shard_map/ppermute | solution.py:363
  18.3 2.0 %collective-permute-start.1 = (bf16[16,162]{1,0:T(8,128)(2,1)S(1)}, bf16[16,162]{1,0:T(8,128)(2,1)S(1)}, u32[]{:S(2)}, u32[]{:S(2)}) collective-permute-start(bf16[16,162]{1,0:T(8,128)(2,1)S(1)} %copy-done.5), channel_id=1, source_target_pairs={{1,0},{2,1},{3,2},{0,3},{5,4},{6,5},{7,6},{4,7},{9,8},{10,9},{11,1... | collective-permute-start | bytes 15560 | tf_op jit(solution)/shard_map/ppermute | solution.py:364
  20.3 0.0 copy-done.4
  20.3 0.0 copy-done.6
  20.3 0.0 copy-done.7
  20.4 0.7 %shard_map.100 = (bf16[96,48]{1,0:T(8,128)(2,1)S(1)}, f32[32,162]{1,0:T(8,128)S(1)}, f32[4,8,162]{2,1,0:T(8,128)S(1)}) custom-call(s32[2,8]{1,0:T(2,128)S(1)} %copy-done.8, s32[8]{0:T(128)S(1)} %copy-done.9, f32[4,16]{1,0:T(4,128)S(1)} %bitcast.8, s32[4,16]{1,0:T(4,128)S(1)} %bitcast.9, bf16[16,162]{1,0:T(8,128)(2,1)S(1)} %copy-done.4), custom_call_target="tpu_custom_call" | custom-call | tf_op jit(solution)/shard_map/pallas_call | solution.py:319
  21.1 0.3 collective-permute-done.before
  21.4 0.0 collective-permute-done.1.after
  21.4 0.3 shard_map.101
  21.6 1.0 %collective-permute-start.2 = (f32[2,8,162]{2,1,0:T(8,128)S(1)}, f32[2,8,162]{2,1,0:T(8,128)S(1)}, u32[]{:S(2)}, u32[]{:S(2)}) collective-permute-start(f32[2,8,162]{2,1,0:T(8,128)S(1)} %get-tuple-element.30), channel_id=1, source_target_pairs={{0,4},{4,0},{8,12},{12,8},{16,20},{20,16},{24,28},{28,24},{1,5},{5... | collective-permute-start | bytes 31112 | tf_op jit(solution)/shard_map/ppermute | solution.py:409
  22.7 1.6 %shard_map.104 = (bf16[2,2,4,2,162,162]{5,4,3,2,1,0:T(8,128)(2,1)S(1)}, bf16[2,2,4,2,162,162]{5,4,3,2,1,0:T(8,128)(2,1)S(1)}, bf16[4,2,162,162]{3,2,1,0:T(8,128)(2,1)S(1)}, bf16[4,2,162,162]{3,2,1,0:T(8,128)(2,1)S(1)}) custom-call(bf16[3,2,4,162,162]{4,3,2,1,0:T(8,128)(2,1)S(1)} %get-tuple-element.29.raw_ref.refs_0_), custom_call_target="tpu_custom_call" | custom-call | tf_op jit(solution)/shard_map/pallas_call | solution.py:319
  24.3 0.3 shard_map.103.own_ref
  24.6 0.0 collective-permute-done.3
  24.6 0.3 copy.15.refs_0_.raw_ref
  24.9 2.7 %shard_map.105 = (bf16[2,2,4,2,162,162]{5,4,3,2,1,0:T(8,128)(2,1)S(1)}, bf16[2,2,4,2,162,162]{5,4,3,2,1,0:T(8,128)(2,1)S(1)}, bf16[4,2,162,162]{3,2,1,0:T(8,128)(2,1)S(1)}, bf16[4,2,162,162]{3,2,1,0:T(8,128)(2,1)S(1)}) custom-call(bf16[3,2,4,162,162]{4,3,2,1,0:T(8,128)(2,1)S(1)} %copy.15.refs_0_.raw_ref, ...), custom_call_target="tpu_custom_call", output_to_operand_aliasing={{0}: (1, {}), {1}: (2, {})} | custom-call | tf_op jit(solution)/shard_map/pallas_call | solution.py:319
  27.6 0.0 collective-permute-done.2.rhs_ref
  27.6 0.8 %shard_map.106 = (f32[4,8,162]{2,1,0:T(8,128)S(1)}, f32[8,162]{1,0:T(8,128)S(1)}) custom-call(f32[2,8,162]{2,1,0:T(8,128)S(1)} %shard_map.103.own_ref, f32[2,8,162]{2,1,0:T(8,128)S(1)} %collective-permute-done.2.rhs_ref, bf16[3,2,4,162,162]{4,3,2,1,0:T(8,128)(2,1)S(1)} %copy.15.refs_0_.raw_ref, bf16[2,2,4,2,162,162]{5,4,3,2,1,0:T(8,128)(2,1)S(1)} %get-tuple-element.36.q_ref, ...), custom_call_target="tpu_custom_call" | custom-call | tf_op jit(solution)/shard_map/pallas_call | solution.py:319
  28.4 1.5 %collective-permute-start.4 = (f32[8,162]{1,0:T(8,128)S(1)}, f32[8,162]{1,0:T(8,128)S(1)}, u32[]{:S(2)}, u32[]{:S(2)}) collective-permute-start(f32[8,162]{1,0:T(8,128)S(1)} %get-tuple-element.40.local_ref), channel_id=1, source_target_pairs={{0,8},{4,12},{8,24},{12,28},{16,20},{20,16},{24,0},{28,4},{1,9},{5... | collective-permute-start | bytes 15560 | tf_op jit(solution)/shard_map/ppermute | solution.py:440
  29.9 2.0 %collective-permute-done.4.came_ref.refs_0_ = f32[8,162]{1,0:T(8,128)S(1)} collective-permute-done((f32[8,162]{1,0:T(8,128)S(1)}, f32[8,162]{1,0:T(8,128)S(1)}, u32[]{:S(2)}, u32[]{:S(2)}) %collective-permute-start.4) | collective-permute-done | bytes 5216 | tf_op jit(solution)/shard_map/ppermute | solution.py:440
  31.9 0.8 %collective-permute-start.5 = (f32[8,162]{1,0:T(8,128)S(1)}, f32[8,162]{1,0:T(8,128)S(1)}, u32[]{:S(2)}, u32[]{:S(2)}) collective-permute-start(f32[8,162]{1,0:T(8,128)S(1)} %shard_map.107), channel_id=1, source_target_pairs={{0,8},{4,12},{8,16},{12,20},{16,0},{20,4},{24,28},{28,24},{1,9},{5... | collective-permute-start | bytes 15560 | tf_op jit(solution)/shard_map/ppermute | solution.py:440
  32.6 1.7 %collective-permute-done.5.came_ref.refs_1_ = f32[8,162]{1,0:T(8,128)S(1)} collective-permute-done((f32[8,162]{1,0:T(8,128)S(1)}, f32[8,162]{1,0:T(8,128)S(1)}, u32[]{:S(2)}, u32[]{:S(2)}) %collective-permute-start.5) | collective-permute-done | bytes 5216 | tf_op jit(solution)/shard_map/ppermute | solution.py:440
  34.4 2.3 %collective-permute-start.6 = (f32[8,162]{1,0:T(8,128)S(1)}, f32[8,162]{1,0:T(8,128)S(1)}, u32[]{:S(2)}, u32[]{:S(2)}) collective-permute-start(f32[8,162]{1,0:T(8,128)S(1)} %shard_map.108), channel_id=1, source_target_pairs={{0,4},{4,0},{8,16},{12,20},{16,24},{20,28},{24,8},{28,12},{1,5},{5... | collective-permute-start | bytes 15560 | tf_op jit(solution)/shard_map/ppermute | solution.py:440
  36.7 0.8 %collective-permute-done.6.refs_2_ = f32[8,162]{1,0:T(8,128)S(1)} collective-permute-done((f32[8,162]{1,0:T(8,128)S(1)}, f32[8,162]{1,0:T(8,128)S(1)}, u32[]{:S(2)}, u32[]{:S(2)}) %collective-permute-start.6) | collective-permute-done | bytes 5216 | tf_op jit(solution)/shard_map/ppermute | solution.py:440
  37.5 1.4 %shard_map.109 = (f32[4,8,162]{2,1,0:T(8,128)S(1)}, f32[8,162]{1,0:T(8,128)S(1)}) custom-call(f32[4,8,162]{2,1,0:T(8,128)S(1)} %get-tuple-element.38.scaled_ref, bf16[2,2,4,2,162,162]{5,4,3,2,1,0:T(8,128)(2,1)S(1)} %get-tuple-element.36.q_ref, bf16[2,2,4,2,162,162]{5,4,3,2,1,0:T(8,128)(2,1)S(1)} %get-tuple-element.39.s_ref, ...), custom_call_target="tpu_custom_call" | custom-call | tf_op jit(solution)/shard_map/pallas_call | solution.py:319
  38.9 0.4 collective-permute-start.7
  39.2 2.2 %collective-permute-done.7.came_ref.refs_0_ = f32[8,162]{1,0:T(8,128)S(1)} collective-permute-done((f32[8,162]{1,0:T(8,128)S(1)}, f32[8,162]{1,0:T(8,128)S(1)}, u32[]{:S(2)}, u32[]{:S(2)}) %collective-permute-start.7) | collective-permute-done | bytes 5216 | tf_op jit(solution)/shard_map/ppermute | solution.py:451
  41.4 3.6 %collective-permute-start.8 = (f32[8,162]{1,0:T(8,128)S(1)}, f32[8,162]{1,0:T(8,128)S(1)}, u32[]{:S(2)}, u32[]{:S(2)}) collective-permute-start(f32[8,162]{1,0:T(8,128)S(1)} %shard_map.110), channel_id=1, source_target_pairs={{0,4},{4,0},{8,24},{12,28},{16,8},{20,12},{24,16},{28,20},{1,5},{5... | collective-permute-start | bytes 15560 | tf_op jit(solution)/shard_map/ppermute | solution.py:451
  45.0 0.8 %collective-permute-done.8.came_ref.refs_1_ = f32[8,162]{1,0:T(8,128)S(1)} collective-permute-done((f32[8,162]{1,0:T(8,128)S(1)}, f32[8,162]{1,0:T(8,128)S(1)}, u32[]{:S(2)}, u32[]{:S(2)}) %collective-permute-start.8) | collective-permute-done | bytes 5216 | tf_op jit(solution)/shard_map/ppermute | solution.py:451
  45.8 0.0 collective-permute-start.9
  45.9 2.5 %collective-permute-done.9.refs_2_ = f32[8,162]{1,0:T(8,128)S(1)} collective-permute-done((f32[8,162]{1,0:T(8,128)S(1)}, f32[8,162]{1,0:T(8,128)S(1)}, u32[]{:S(2)}, u32[]{:S(2)}) %collective-permute-start.9) | collective-permute-done | bytes 5216 | tf_op jit(solution)/shard_map/ppermute | solution.py:451
  48.3 0.8 %shard_map.112 = (f32[2,8,162]{2,1,0:T(8,128)S(1)}, f32[2,8,162]{2,1,0:T(8,128)S(1)}) custom-call(f32[4,8,162]{2,1,0:T(8,128)S(1)} %get-tuple-element.42.y_ref, bf16[2,2,4,2,162,162]{5,4,3,2,1,0:T(8,128)(2,1)S(1)} %get-tuple-element.39.s_ref, f32[4,8,162]{2,1,0:T(8,128)S(1)} %get-tuple-element.37.act_ref, ...), custom_call_target="tpu_custom_call" | custom-call | tf_op jit(solution)/shard_map/pallas_call | solution.py:319
  49.1 4.0 %collective-permute-start.10 = (f32[2,8,162]{2,1,0:T(8,128)S(1)}, f32[2,8,162]{2,1,0:T(8,128)S(1)}, u32[]{:S(2)}, u32[]{:S(2)}) collective-permute-start(f32[2,8,162]{2,1,0:T(8,128)S(1)} %get-tuple-element.46), channel_id=1, source_target_pairs={{0,4},{4,0},{8,12},{12,8},{16,20},{20,16},{24,28},{28,24},{1,5},{5... | collective-permute-start | bytes 31112 | tf_op jit(solution)/shard_map/ppermute | solution.py:458
  53.2 0.8 %collective-permute-done.10.other_ref = f32[2,8,162]{2,1,0:T(8,128)S(1)} collective-permute-done((f32[2,8,162]{2,1,0:T(8,128)S(1)}, f32[2,8,162]{2,1,0:T(8,128)S(1)}, u32[]{:S(2)}, u32[]{:S(2)}) %collective-permute-start.10) | collective-permute-done | bytes 10400 | tf_op jit(solution)/shard_map/ppermute | solution.py:458
  54.0 0.6 %shard_map.113 = f32[2,8,162]{2,1,0:T(8,128)} custom-call(f32[2,8,162]{2,1,0:T(8,128)S(1)} %get-tuple-element.45.own_ref, f32[2,8,162]{2,1,0:T(8,128)S(1)} %collective-permute-done.10.other_ref), custom_call_target="tpu_custom_call" | custom-call | tf_op jit(solution)/shard_map/pallas_call | solution.py:319
  (10 shorter events, 0.0 us)
Async XLA Ops:
  0.0 1.3 %copy-start = (bf16[2,8,162,162]{3,1,2,0:T(8,128)(2,1)S(1)}, bf16[2,8,162,162]{3,1,2,0:T(8,128)(2,1)}, u32[]{:S(2)}) copy-start(bf16[2,8,162,162]{3,1,2,0:T(8,128)(2,1)} %param.17) | copy-start | bytes 2519428
  1.3 1.3 %copy-start.1 = (bf16[2,8,162,162]{3,1,2,0:T(8,128)(2,1)S(1)}, bf16[2,8,162,162]{3,1,2,0:T(8,128)(2,1)}, u32[]{:S(2)}) copy-start(bf16[2,8,162,162]{3,1,2,0:T(8,128)(2,1)} %param.18) | copy-start | bytes 2519428
  2.6 1.3 %copy-start.2 = (bf16[2,8,162,162]{3,1,2,0:T(8,128)(2,1)S(1)}, bf16[2,8,162,162]{3,1,2,0:T(8,128)(2,1)}, u32[]{:S(2)}) copy-start(bf16[2,8,162,162]{3,1,2,0:T(8,128)(2,1)} %param.19) | copy-start | bytes 2519428
  14.6 1.0 %copy-start.5 = (bf16[16,162]{1,0:T(8,128)(2,1)S(1)}, bf16[16,162]{1,0:T(8,128)(2,1)}, u32[]{:S(2)}) copy-start(bf16[16,162]{1,0:T(8,128)(2,1)} %state.1) | copy-start | bytes 15556
  14.6 5.8 %copy-start.4 = (bf16[16,162]{1,0:T(8,128)(2,1)S(1)}, bf16[16,162]{1,0:T(8,128)(2,1)}, u32[]{:S(2)}) copy-start(bf16[16,162]{1,0:T(8,128)(2,1)} %source_ref.1) | copy-start | bytes 15556
  14.6 5.7 %copy-start.6 = (f32[16,4]{0,1:T(4,128)S(1)}, f32[16,4]{0,1:T(4,128)}, u32[]{:S(2)}) copy-start(f32[16,4]{0,1:T(4,128)} %param.12) | copy-start | bytes 772
  14.6 5.7 %copy-start.7 = (s32[16,4]{0,1:T(4,128)S(1)}, s32[16,4]{0,1:T(4,128)}, u32[]{:S(2)}) copy-start(s32[16,4]{0,1:T(4,128)} %param.13) | copy-start | bytes 772
  14.6 5.7 %copy-start.8 = (s32[2,8]{1,0:T(2,128)S(1)}, s32[2,8]{1,0:T(2,128)}, u32[]{:S(2)}) copy-start(s32[2,8]{1,0:T(2,128)} %slot_ref.1) | copy-start | bytes 196
  14.6 5.7 %copy-start.9 = (s32[8]{0:T(128)S(1)}, s32[8]{0:T(128)}, u32[]{:S(2)}) copy-start(s32[8]{0:T(128)} %len_ref.1) | copy-start | bytes 100
  14.6 6.7 %copy-start.3 = (bf16[162,162]{1,0:T(8,128)(2,1)S(1)}, bf16[162,162]{1,0:T(8,128)(2,1)}, u32[]{:S(2)}) copy-start(bf16[162,162]{1,0:T(8,128)(2,1)} %lift.1) | copy-start | bytes 157468
  15.4 9.2 %collective-permute-start.3 = (bf16[3,2,4,162,162]{4,2,3,1,0:T(4,128)(2,1)S(1)}, bf16[3,2,4,162,162]{4,2,3,1,0:T(4,128)(2,1)S(1)}, u32[]{:S(2)}, u32[]{:S(2)}) collective-permute-start(bf16[3,2,4,162,162]{4,2,3,1,0:T(4,128)(2,1)S(1)} %copy.13), channel_id=1, source_target_pairs={{0,4},{4,0},{8,12},{12,8},{16,20},{20,16},{24,28},{28,24},{1,5},{5... | collective-permute-start | bytes 3779144 | tf_op jit(solution)/shard_map/ppermute | solution.py:379
  15.6 5.8 %collective-permute-start = (bf16[16,162]{1,0:T(8,128)(2,1)S(1)}, bf16[16,162]{1,0:T(8,128)(2,1)S(1)}, u32[]{:S(2)}, u32[]{:S(2)}) collective-permute-start(bf16[16,162]{1,0:T(8,128)(2,1)S(1)} %copy-done.5), channel_id=1, source_target_pairs={{0,1},{1,2},{2,3},{3,0},{4,5},{5,6},{6,7},{7,4},{8,9},{9,10},{10,1... | collective-permute-start | bytes 15560 | tf_op jit(solution)/shard_map/ppermute | solution.py:363
  18.3 3.1 %collective-permute-start.1 = (bf16[16,162]{1,0:T(8,128)(2,1)S(1)}, bf16[16,162]{1,0:T(8,128)(2,1)S(1)}, u32[]{:S(2)}, u32[]{:S(2)}) collective-permute-start(bf16[16,162]{1,0:T(8,128)(2,1)S(1)} %copy-done.5), channel_id=1, source_target_pairs={{1,0},{2,1},{3,2},{0,3},{5,4},{6,5},{7,6},{4,7},{9,8},{10,9},{11,1... | collective-permute-start | bytes 15560 | tf_op jit(solution)/shard_map/ppermute | solution.py:364
  21.6 6.0 %collective-permute-start.2 = (f32[2,8,162]{2,1,0:T(8,128)S(1)}, f32[2,8,162]{2,1,0:T(8,128)S(1)}, u32[]{:S(2)}, u32[]{:S(2)}) collective-permute-start(f32[2,8,162]{2,1,0:T(8,128)S(1)} %get-tuple-element.30), channel_id=1, source_target_pairs={{0,4},{4,0},{8,12},{12,8},{16,20},{20,16},{24,28},{28,24},{1,5},{5... | collective-permute-start | bytes 31112 | tf_op jit(solution)/shard_map/ppermute | solution.py:409
  28.4 3.5 %collective-permute-start.4 = (f32[8,162]{1,0:T(8,128)S(1)}, f32[8,162]{1,0:T(8,128)S(1)}, u32[]{:S(2)}, u32[]{:S(2)}) collective-permute-start(f32[8,162]{1,0:T(8,128)S(1)} %get-tuple-element.40.local_ref), channel_id=1, source_target_pairs={{0,8},{4,12},{8,24},{12,28},{16,20},{20,16},{24,0},{28,4},{1,9},{5... | collective-permute-start | bytes 15560 | tf_op jit(solution)/shard_map/ppermute | solution.py:440
  31.9 2.5 %collective-permute-start.5 = (f32[8,162]{1,0:T(8,128)S(1)}, f32[8,162]{1,0:T(8,128)S(1)}, u32[]{:S(2)}, u32[]{:S(2)}) collective-permute-start(f32[8,162]{1,0:T(8,128)S(1)} %shard_map.107), channel_id=1, source_target_pairs={{0,8},{4,12},{8,16},{12,20},{16,0},{20,4},{24,28},{28,24},{1,9},{5... | collective-permute-start | bytes 15560 | tf_op jit(solution)/shard_map/ppermute | solution.py:440
  34.4 3.1 %collective-permute-start.6 = (f32[8,162]{1,0:T(8,128)S(1)}, f32[8,162]{1,0:T(8,128)S(1)}, u32[]{:S(2)}, u32[]{:S(2)}) collective-permute-start(f32[8,162]{1,0:T(8,128)S(1)} %shard_map.108), channel_id=1, source_target_pairs={{0,4},{4,0},{8,16},{12,20},{16,24},{20,28},{24,8},{28,12},{1,5},{5... | collective-permute-start | bytes 15560 | tf_op jit(solution)/shard_map/ppermute | solution.py:440
  38.9 2.6 %collective-permute-start.7 = (f32[8,162]{1,0:T(8,128)S(1)}, f32[8,162]{1,0:T(8,128)S(1)}, u32[]{:S(2)}, u32[]{:S(2)}) collective-permute-start(f32[8,162]{1,0:T(8,128)S(1)} %get-tuple-element.43.local_ref), channel_id=1, source_target_pairs={{0,24},{4,28},{8,12},{12,8},{16,0},{20,4},{24,16},{28,20},{1,25},{... | collective-permute-start | bytes 15560 | tf_op jit(solution)/shard_map/ppermute | solution.py:451
  41.4 4.4 %collective-permute-start.8 = (f32[8,162]{1,0:T(8,128)S(1)}, f32[8,162]{1,0:T(8,128)S(1)}, u32[]{:S(2)}, u32[]{:S(2)}) collective-permute-start(f32[8,162]{1,0:T(8,128)S(1)} %shard_map.110), channel_id=1, source_target_pairs={{0,4},{4,0},{8,24},{12,28},{16,8},{20,12},{24,16},{28,20},{1,5},{5... | collective-permute-start | bytes 15560 | tf_op jit(solution)/shard_map/ppermute | solution.py:451
  45.8 2.5 %collective-permute-start.9 = (f32[8,162]{1,0:T(8,128)S(1)}, f32[8,162]{1,0:T(8,128)S(1)}, u32[]{:S(2)}, u32[]{:S(2)}) collective-permute-start(f32[8,162]{1,0:T(8,128)S(1)} %shard_map.111), channel_id=1, source_target_pairs={{0,16},{4,20},{8,0},{12,4},{16,8},{20,12},{24,28},{28,24},{1,17},{... | collective-permute-start | bytes 15560 | tf_op jit(solution)/shard_map/ppermute | solution.py:451
  49.1 4.9 %collective-permute-start.10 = (f32[2,8,162]{2,1,0:T(8,128)S(1)}, f32[2,8,162]{2,1,0:T(8,128)S(1)}, u32[]{:S(2)}, u32[]{:S(2)}) collective-permute-start(f32[2,8,162]{2,1,0:T(8,128)S(1)} %get-tuple-element.46), channel_id=1, source_target_pairs={{0,4},{4,0},{8,12},{12,8},{16,20},{20,16},{24,28},{28,24},{1,5},{5... | collective-permute-start | bytes 31112 | tf_op jit(solution)/shard_map/ppermute | solution.py:458

commit v2 on v1

--- a/solution.py
+++ b/solution.py
@@ -66,16 +66,22 @@
     return lax.div(lax.axis_index("wall"), 2)
 
 
-def relayout_kernel(dinv_ref, lower_ref, upper_ref, own_ref, send_ref, scratch):
-    half = own_ref.shape[2]
+def relayout_kernel(dinv_ref, lower_ref, upper_ref, own_ref, send_ref, landed, arrived):
+    kinds, depth, half = own_ref.shape[:3]
     core = core_of()
-    for a, ref in enumerate((dinv_ref, lower_ref, upper_ref)):
-        for e in range(own_ref.shape[1]):
-            slot = (a * own_ref.shape[1] + e) % 2
-            scratch[slot] = ref[e].astype(F32)
+    copies = [
+        [pltpu.make_async_copy(ref.at[e], landed.at[a, e], arrived.at[a, e]) for e in range(depth)]
+        for a, ref in enumerate((dinv_ref, lower_ref, upper_ref))
+    ]
+    for copy in sum(copies, []):
+        copy.start()
+    for a in range(kinds):
+        for e in range(depth):
+            copies[a][e].wait()
+            turned = jnp.swapaxes(landed[a, e], 0, 1)
             for l in range(half):
-                own_ref[a, e, l] = scratch[slot, :, core * half + l, :].astype(BF16)
-                send_ref[a, e, l] = scratch[slot, :, (1 - core) * half + l, :].astype(BF16)
+                own_ref[a, e, l] = jnp.where(core == 0, turned[l], turned[half + l])
+                send_ref[a, e, l] = jnp.where(core == 0, turned[half + l], turned[l])
 
 
 def pair_kernel(*refs, first):
@@ -295,7 +301,7 @@
 
 def run(kernel, operands, outs, blocks=1, scratch=(), aliases=None):
     everything = [(x.shape, x.dtype) for x, _ in operands] + [(s, t) for s, t, _ in outs]
-    everything += [(s.shape, s.dtype) for s in scratch]
+    everything += [(s.shape, s.dtype) for s in scratch if s.memory_space == pltpu.VMEM]
     limit = sum(padded_bytes(s, t) for s, t in everything)
     if blocks == 1:
         in_specs = [at if isinstance(at, pl.BlockSpec) else VMEM for _, at in operands]
@@ -368,9 +374,12 @@
         turned = [jnp.transpose(x, (0, 2, 1, 3)) for x in (dinv, lower, upper)]
         own, send = run(
             relayout_kernel,
-            [(x, None) for x in turned],
+            [(x, ANY) for x in turned],
             [(raw_shape, BF16, None)] * 2,
-            scratch=[pltpu.VMEM((2, width, line_count, width), F32)],
+            scratch=[
+                pltpu.VMEM((3, depth, width, line_count, width), BF16),
+                pltpu.SemaphoreType.DMA((3, depth)),
+            ],
         )
     else:
         every = jnp.stack([dinv, lower, upper])

time: 55.5 us -> 47.4 us (0.85)
  Pallas kernels: 19.7 us -> 11.7 us
    pallas_call x14, Pallas kernels: 19.7 us -> 11.7 us  [run(): pl.pallas_call(kernel, grid=grid, in_specs=in_specs, out_specs=out_specs,...]
  transfers between devices with their start and end apart: 11 -> 11, of which waited for: 8 -> 8; matrix products, arithmetic and copies ran while one was open for 1% -> 1% of each run, Pallas kernels for 10% -> 12%
where the time goes in v2:
time: 47.4 us; the launch traced here: 46.5 us
  starting transfers between devices  18.4 us (39%)
  Pallas kernels  11.7 us (25%)
  waiting for transfers between devices  11.2 us (24%)
  local copies, waits for them, and re-layouts  5.07 us (11%)
    pallas_call x14, Pallas kernels, run(): pl.pallas_call(kernel, grid=grid, in_specs=in_specs, out_specs=out_specs,...  11.7 us
    ppermute x6, waiting for transfers between devices, per_device(): arrivals.append(lax.ppermute(out, 'wall', pairs))  10.1 us
    ppermute x6, starting transfers between devices, per_device(): arrivals.append(lax.ppermute(out, 'wall', pairs))  8.46 us
    ppermute x1, starting transfers between devices, per_device(): other_part = lax.ppermute(send_part, 'wall', flips(wall_count))  4.02 us
    unnamed x20, local copies, waits for them, and re-layouts  4.01 us
    ppermute x1, starting transfers between devices, per_device(): lax.ppermute(state, 'surf', [(i, (i + 1) % surf_count) for i in range(sur...  2.74 us
    ppermute x1, starting transfers between devices, per_device(): lax.ppermute(state, 'surf', [((i + 1) % surf_count, i) for i in range(sur...  2.03 us
    ppermute x1, starting transfers between devices, per_device(): came_rhs = lax.ppermute(send_rhs, 'wall', flips(wall_count))  1.05 us
  transfers between devices with their start and end apart: 11, of which 8 were waited for; matrix products, arithmetic and copies ran while one was open for 1% of the time, Pallas kernels for 12%

profile of v2, /device:TPU:1, one launch (start us, length us, event | category | flops | bytes accessed | tf_op | source)
XLA Modules:
  0.0 46.5 jit_solution(6742999691349647855)
XLA Ops:
  0.0 1.3 %copy-done = bf16[2,8,162,162]{3,1,2,0:T(8,128)(2,1)S(1)} copy-done((bf16[2,8,162,162]{3,1,2,0:T(8,128)(2,1)S(1)}, bf16[2,8,162,162]{3,1,2,0:T(8,128)(2,1)}, u32[]{:S(2)}) %copy-start) | copy-done | bytes 839832
  1.3 1.3 %copy-done.1 = bf16[2,8,162,162]{3,1,2,0:T(8,128)(2,1)S(1)} copy-done((bf16[2,8,162,162]{3,1,2,0:T(8,128)(2,1)S(1)}, bf16[2,8,162,162]{3,1,2,0:T(8,128)(2,1)}, u32[]{:S(2)}) %copy-start.1) | copy-done | bytes 839832
  2.6 1.3 %copy-done.2 = bf16[2,8,162,162]{3,1,2,0:T(8,128)(2,1)S(1)} copy-done((bf16[2,8,162,162]{3,1,2,0:T(8,128)(2,1)S(1)}, bf16[2,8,162,162]{3,1,2,0:T(8,128)(2,1)}, u32[]{:S(2)}) %copy-start.2) | copy-done | bytes 839832
  4.0 2.5 %shard_map.102 = (bf16[3,2,4,162,162]{4,3,2,1,0:T(8,128)(2,1)S(1)}, bf16[3,2,4,162,162]{4,3,2,1,0:T(8,128)(2,1)S(1)}) custom-call(bf16[2,162,8,162]{3,2,1,0:T(8,128)(2,1)S(1)} %bitcast.5, bf16[2,162,8,162]{3,2,1,0:T(8,128)(2,1)S(1)} %bitcast.6, bf16[2,162,8,162]{3,2,1,0:T(8,128)(2,1)S(1)} %bitcast.7), custom_call_target="tpu_custom_call" | custom-call | tf_op jit(solution)/shard_map/pallas_call | solution.py:325
  6.5 0.0 copy-start.5
  6.5 0.0 copy-start.4
  6.5 0.0 copy-start.6
  6.5 0.0 copy-start.7
  6.5 0.0 copy-start.8
  6.6 0.0 copy-start.9
  6.6 0.0 copy-start.3
  6.6 0.8 %copy.13 = bf16[3,2,4,162,162]{4,2,3,1,0:T(4,128)(2,1)S(1)} copy(bf16[3,2,4,162,162]{4,3,2,1,0:T(8,128)(2,1)S(1)} %get-tuple-element.31) | data formatting | bytes 2519424 | tf_op jit(solution)/shard_map/pallas_call | solution.py:325
  7.4 0.1 collective-permute-start.3
  7.5 0.0 copy-done.5
  7.5 2.7 %collective-permute-start = (bf16[16,162]{1,0:T(8,128)(2,1)S(1)}, bf16[16,162]{1,0:T(8,128)(2,1)S(1)}, u32[]{:S(2)}, u32[]{:S(2)}) collective-permute-start(bf16[16,162]{1,0:T(8,128)(2,1)S(1)} %copy-done.5), channel_id=1, source_target_pairs={{0,1},{1,2},{2,3},{3,0},{4,5},{5,6},{6,7},{7,4},{8,9},{9,10},{10,1... | collective-permute-start | bytes 15560 | tf_op jit(solution)/shard_map/ppermute | solution.py:369
  10.2 2.0 %collective-permute-start.1 = (bf16[16,162]{1,0:T(8,128)(2,1)S(1)}, bf16[16,162]{1,0:T(8,128)(2,1)S(1)}, u32[]{:S(2)}, u32[]{:S(2)}) collective-permute-start(bf16[16,162]{1,0:T(8,128)(2,1)S(1)} %copy-done.5), channel_id=1, source_target_pairs={{1,0},{2,1},{3,2},{0,3},{5,4},{6,5},{7,6},{4,7},{9,8},{10,9},{11,1... | collective-permute-start | bytes 15560 | tf_op jit(solution)/shard_map/ppermute | solution.py:370
  12.3 0.0 copy-done.4
  12.3 0.0 copy-done.7
  12.3 0.7 %shard_map.100 = (bf16[96,48]{1,0:T(8,128)(2,1)S(1)}, f32[32,162]{1,0:T(8,128)S(1)}, f32[4,8,162]{2,1,0:T(8,128)S(1)}) custom-call(s32[2,8]{1,0:T(2,128)S(1)} %copy-done.8, s32[8]{0:T(128)S(1)} %copy-done.9, f32[4,16]{1,0:T(4,128)S(1)} %bitcast.8, s32[4,16]{1,0:T(4,128)S(1)} %bitcast.9, bf16[16,162]{1,0:T(8,128)(2,1)S(1)} %copy-done.4), custom_call_target="tpu_custom_call" | custom-call | tf_op jit(solution)/shard_map/pallas_call | solution.py:325
  13.0 0.3 collective-permute-done.before
  13.3 0.0 collective-permute-done.1.after
  13.3 0.0 copy-done.3
  13.3 0.3 shard_map.101
  13.5 1.0 %collective-permute-start.2 = (f32[2,8,162]{2,1,0:T(8,128)S(1)}, f32[2,8,162]{2,1,0:T(8,128)S(1)}, u32[]{:S(2)}, u32[]{:S(2)}) collective-permute-start(f32[2,8,162]{2,1,0:T(8,128)S(1)} %get-tuple-element.30), channel_id=1, source_target_pairs={{0,4},{4,0},{8,12},{12,8},{16,20},{20,16},{24,28},{28,24},{1,5},{5... | collective-permute-start | bytes 31112 | tf_op jit(solution)/shard_map/ppermute | solution.py:418
  14.6 1.6 %shard_map.104 = (bf16[2,2,4,2,162,162]{5,4,3,2,1,0:T(8,128)(2,1)S(1)}, bf16[2,2,4,2,162,162]{5,4,3,2,1,0:T(8,128)(2,1)S(1)}, bf16[4,2,162,162]{3,2,1,0:T(8,128)(2,1)S(1)}, bf16[4,2,162,162]{3,2,1,0:T(8,128)(2,1)S(1)}) custom-call(bf16[3,2,4,162,162]{4,3,2,1,0:T(8,128)(2,1)S(1)} %get-tuple-element.29.raw_ref.refs_0_), custom_call_target="tpu_custom_call" | custom-call | tf_op jit(solution)/shard_map/pallas_call | solution.py:325
  16.2 0.3 shard_map.103.own_ref
  16.5 0.0 collective-permute-done.3
  16.5 0.3 copy.15.refs_0_.raw_ref
  16.8 2.7 %shard_map.105 = (bf16[2,2,4,2,162,162]{5,4,3,2,1,0:T(8,128)(2,1)S(1)}, bf16[2,2,4,2,162,162]{5,4,3,2,1,0:T(8,128)(2,1)S(1)}, bf16[4,2,162,162]{3,2,1,0:T(8,128)(2,1)S(1)}, bf16[4,2,162,162]{3,2,1,0:T(8,128)(2,1)S(1)}) custom-call(bf16[3,2,4,162,162]{4,3,2,1,0:T(8,128)(2,1)S(1)} %copy.15.refs_0_.raw_ref, ...), custom_call_target="tpu_custom_call", output_to_operand_aliasing={{0}: (1, {}), {1}: (2, {})} | custom-call | tf_op jit(solution)/shard_map/pallas_call | solution.py:325
  19.5 0.0 collective-permute-done.2.rhs_ref
  19.5 0.8 %shard_map.106 = (f32[4,8,162]{2,1,0:T(8,128)S(1)}, f32[8,162]{1,0:T(8,128)S(1)}) custom-call(f32[2,8,162]{2,1,0:T(8,128)S(1)} %shard_map.103.own_ref, f32[2,8,162]{2,1,0:T(8,128)S(1)} %collective-permute-done.2.rhs_ref, bf16[3,2,4,162,162]{4,3,2,1,0:T(8,128)(2,1)S(1)} %copy.15.refs_0_.raw_ref, bf16[2,2,4,2,162,162]{5,4,3,2,1,0:T(8,128)(2,1)S(1)} %get-tuple-element.36.q_ref, ...), custom_call_target="tpu_custom_call" | custom-call | tf_op jit(solution)/shard_map/pallas_call | solution.py:325
  20.3 1.5 %collective-permute-start.4 = (f32[8,162]{1,0:T(8,128)S(1)}, f32[8,162]{1,0:T(8,128)S(1)}, u32[]{:S(2)}, u32[]{:S(2)}) collective-permute-start(f32[8,162]{1,0:T(8,128)S(1)} %get-tuple-element.40.local_ref), channel_id=1, source_target_pairs={{0,8},{4,12},{8,24},{12,28},{16,20},{20,16},{24,0},{28,4},{1,9},{5... | collective-permute-start | bytes 15560 | tf_op jit(solution)/shard_map/ppermute | solution.py:449
  21.8 2.0 %collective-permute-done.4.came_ref.refs_0_ = f32[8,162]{1,0:T(8,128)S(1)} collective-permute-done((f32[8,162]{1,0:T(8,128)S(1)}, f32[8,162]{1,0:T(8,128)S(1)}, u32[]{:S(2)}, u32[]{:S(2)}) %collective-permute-start.4) | collective-permute-done | bytes 5216 | tf_op jit(solution)/shard_map/ppermute | solution.py:449
  23.8 0.7 %collective-permute-start.5 = (f32[8,162]{1,0:T(8,128)S(1)}, f32[8,162]{1,0:T(8,128)S(1)}, u32[]{:S(2)}, u32[]{:S(2)}) collective-permute-start(f32[8,162]{1,0:T(8,128)S(1)} %shard_map.107), channel_id=1, source_target_pairs={{0,8},{4,12},{8,16},{12,20},{16,0},{20,4},{24,28},{28,24},{1,9},{5... | collective-permute-start | bytes 15560 | tf_op jit(solution)/shard_map/ppermute | solution.py:449
  24.5 1.8 %collective-permute-done.5.came_ref.refs_1_ = f32[8,162]{1,0:T(8,128)S(1)} collective-permute-done((f32[8,162]{1,0:T(8,128)S(1)}, f32[8,162]{1,0:T(8,128)S(1)}, u32[]{:S(2)}, u32[]{:S(2)}) %collective-permute-start.5) | collective-permute-done | bytes 5216 | tf_op jit(solution)/shard_map/ppermute | solution.py:449
  26.3 2.3 %collective-permute-start.6 = (f32[8,162]{1,0:T(8,128)S(1)}, f32[8,162]{1,0:T(8,128)S(1)}, u32[]{:S(2)}, u32[]{:S(2)}) collective-permute-start(f32[8,162]{1,0:T(8,128)S(1)} %shard_map.108), channel_id=1, source_target_pairs={{0,4},{4,0},{8,16},{12,20},{16,24},{20,28},{24,8},{28,12},{1,5},{5... | collective-permute-start | bytes 15560 | tf_op jit(solution)/shard_map/ppermute | solution.py:449
  28.6 0.8 %collective-permute-done.6.refs_2_ = f32[8,162]{1,0:T(8,128)S(1)} collective-permute-done((f32[8,162]{1,0:T(8,128)S(1)}, f32[8,162]{1,0:T(8,128)S(1)}, u32[]{:S(2)}, u32[]{:S(2)}) %collective-permute-start.6) | collective-permute-done | bytes 5216 | tf_op jit(solution)/shard_map/ppermute | solution.py:449
  29.4 1.4 %shard_map.109 = (f32[4,8,162]{2,1,0:T(8,128)S(1)}, f32[8,162]{1,0:T(8,128)S(1)}) custom-call(f32[4,8,162]{2,1,0:T(8,128)S(1)} %get-tuple-element.38.scaled_ref, bf16[2,2,4,2,162,162]{5,4,3,2,1,0:T(8,128)(2,1)S(1)} %get-tuple-element.36.q_ref, bf16[2,2,4,2,162,162]{5,4,3,2,1,0:T(8,128)(2,1)S(1)} %get-tuple-element.39.s_ref, ...), custom_call_target="tpu_custom_call" | custom-call | tf_op jit(solution)/shard_map/pallas_call | solution.py:325
  30.8 0.4 collective-permute-start.7
  31.2 2.2 %collective-permute-done.7.came_ref.refs_0_ = f32[8,162]{1,0:T(8,128)S(1)} collective-permute-done((f32[8,162]{1,0:T(8,128)S(1)}, f32[8,162]{1,0:T(8,128)S(1)}, u32[]{:S(2)}, u32[]{:S(2)}) %collective-permute-start.7) | collective-permute-done | bytes 5216 | tf_op jit(solution)/shard_map/ppermute | solution.py:460
  33.3 3.6 %collective-permute-start.8 = (f32[8,162]{1,0:T(8,128)S(1)}, f32[8,162]{1,0:T(8,128)S(1)}, u32[]{:S(2)}, u32[]{:S(2)}) collective-permute-start(f32[8,162]{1,0:T(8,128)S(1)} %shard_map.110), channel_id=1, source_target_pairs={{0,4},{4,0},{8,24},{12,28},{16,8},{20,12},{24,16},{28,20},{1,5},{5... | collective-permute-start | bytes 15560 | tf_op jit(solution)/shard_map/ppermute | solution.py:460
  36.9 0.8 %collective-permute-done.8.came_ref.refs_1_ = f32[8,162]{1,0:T(8,128)S(1)} collective-permute-done((f32[8,162]{1,0:T(8,128)S(1)}, f32[8,162]{1,0:T(8,128)S(1)}, u32[]{:S(2)}, u32[]{:S(2)}) %collective-permute-start.8) | collective-permute-done | bytes 5216 | tf_op jit(solution)/shard_map/ppermute | solution.py:460
  37.8 0.0 collective-permute-start.9
  37.8 2.5 %collective-permute-done.9.refs_2_ = f32[8,162]{1,0:T(8,128)S(1)} collective-permute-done((f32[8,162]{1,0:T(8,128)S(1)}, f32[8,162]{1,0:T(8,128)S(1)}, u32[]{:S(2)}, u32[]{:S(2)}) %collective-permute-start.9) | collective-permute-done | bytes 5216 | tf_op jit(solution)/shard_map/ppermute | solution.py:460
  40.3 0.8 %shard_map.112 = (f32[2,8,162]{2,1,0:T(8,128)S(1)}, f32[2,8,162]{2,1,0:T(8,128)S(1)}) custom-call(f32[4,8,162]{2,1,0:T(8,128)S(1)} %get-tuple-element.42.y_ref, bf16[2,2,4,2,162,162]{5,4,3,2,1,0:T(8,128)(2,1)S(1)} %get-tuple-element.39.s_ref, f32[4,8,162]{2,1,0:T(8,128)S(1)} %get-tuple-element.37.act_ref, ...), custom_call_target="tpu_custom_call" | custom-call | tf_op jit(solution)/shard_map/pallas_call | solution.py:325
  41.0 4.0 %collective-permute-start.10 = (f32[2,8,162]{2,1,0:T(8,128)S(1)}, f32[2,8,162]{2,1,0:T(8,128)S(1)}, u32[]{:S(2)}, u32[]{:S(2)}) collective-permute-start(f32[2,8,162]{2,1,0:T(8,128)S(1)} %get-tuple-element.46), channel_id=1, source_target_pairs={{0,4},{4,0},{8,12},{12,8},{16,20},{20,16},{24,28},{28,24},{1,5},{5... | collective-permute-start | bytes 31112 | tf_op jit(solution)/shard_map/ppermute | solution.py:467
  45.1 0.8 %collective-permute-done.10.other_ref = f32[2,8,162]{2,1,0:T(8,128)S(1)} collective-permute-done((f32[2,8,162]{2,1,0:T(8,128)S(1)}, f32[2,8,162]{2,1,0:T(8,128)S(1)}, u32[]{:S(2)}, u32[]{:S(2)}) %collective-permute-start.10) | collective-permute-done | bytes 10400 | tf_op jit(solution)/shard_map/ppermute | solution.py:467
  45.9 0.6 %shard_map.113 = f32[2,8,162]{2,1,0:T(8,128)} custom-call(f32[2,8,162]{2,1,0:T(8,128)S(1)} %get-tuple-element.45.own_ref, f32[2,8,162]{2,1,0:T(8,128)S(1)} %collective-permute-done.10.other_ref), custom_call_target="tpu_custom_call" | custom-call | tf_op jit(solution)/shard_map/pallas_call | solution.py:325
  (10 shorter events, 0.0 us)
Async XLA Ops:
  0.0 1.3 %copy-start = (bf16[2,8,162,162]{3,1,2,0:T(8,128)(2,1)S(1)}, bf16[2,8,162,162]{3,1,2,0:T(8,128)(2,1)}, u32[]{:S(2)}) copy-start(bf16[2,8,162,162]{3,1,2,0:T(8,128)(2,1)} %param.17) | copy-start | bytes 2519428
  1.3 1.3 %copy-start.1 = (bf16[2,8,162,162]{3,1,2,0:T(8,128)(2,1)S(1)}, bf16[2,8,162,162]{3,1,2,0:T(8,128)(2,1)}, u32[]{:S(2)}) copy-start(bf16[2,8,162,162]{3,1,2,0:T(8,128)(2,1)} %param.18) | copy-start | bytes 2519428
  2.6 1.3 %copy-start.2 = (bf16[2,8,162,162]{3,1,2,0:T(8,128)(2,1)S(1)}, bf16[2,8,162,162]{3,1,2,0:T(8,128)(2,1)}, u32[]{:S(2)}) copy-start(bf16[2,8,162,162]{3,1,2,0:T(8,128)(2,1)} %param.19) | copy-start | bytes 2519428
  6.5 1.0 %copy-start.5 = (bf16[16,162]{1,0:T(8,128)(2,1)S(1)}, bf16[16,162]{1,0:T(8,128)(2,1)}, u32[]{:S(2)}) copy-start(bf16[16,162]{1,0:T(8,128)(2,1)} %state.1) | copy-start | bytes 15556
  6.5 5.8 %copy-start.4 = (bf16[16,162]{1,0:T(8,128)(2,1)S(1)}, bf16[16,162]{1,0:T(8,128)(2,1)}, u32[]{:S(2)}) copy-start(bf16[16,162]{1,0:T(8,128)(2,1)} %source_ref.1) | copy-start | bytes 15556
  6.5 5.7 %copy-start.6 = (f32[16,4]{0,1:T(4,128)S(1)}, f32[16,4]{0,1:T(4,128)}, u32[]{:S(2)}) copy-start(f32[16,4]{0,1:T(4,128)} %param.12) | copy-start | bytes 772
  6.5 5.7 %copy-start.7 = (s32[16,4]{0,1:T(4,128)S(1)}, s32[16,4]{0,1:T(4,128)}, u32[]{:S(2)}) copy-start(s32[16,4]{0,1:T(4,128)} %param.13) | copy-start | bytes 772
  6.5 5.7 %copy-start.8 = (s32[2,8]{1,0:T(2,128)S(1)}, s32[2,8]{1,0:T(2,128)}, u32[]{:S(2)}) copy-start(s32[2,8]{1,0:T(2,128)} %slot_ref.1) | copy-start | bytes 196
  6.6 5.7 %copy-start.9 = (s32[8]{0:T(128)S(1)}, s32[8]{0:T(128)}, u32[]{:S(2)}) copy-start(s32[8]{0:T(128)} %len_ref.1) | copy-start | bytes 100
  6.6 6.7 %copy-start.3 = (bf16[162,162]{1,0:T(8,128)(2,1)S(1)}, bf16[162,162]{1,0:T(8,128)(2,1)}, u32[]{:S(2)}) copy-start(bf16[162,162]{1,0:T(8,128)(2,1)} %lift.1) | copy-start | bytes 157468
  7.4 9.2 %collective-permute-start.3 = (bf16[3,2,4,162,162]{4,2,3,1,0:T(4,128)(2,1)S(1)}, bf16[3,2,4,162,162]{4,2,3,1,0:T(4,128)(2,1)S(1)}, u32[]{:S(2)}, u32[]{:S(2)}) collective-permute-start(bf16[3,2,4,162,162]{4,2,3,1,0:T(4,128)(2,1)S(1)} %copy.13), channel_id=1, source_target_pairs={{0,4},{4,0},{8,12},{12,8},{16,20},{20,16},{24,28},{28,24},{1,5},{5... | collective-permute-start | bytes 3779144 | tf_op jit(solution)/shard_map/ppermute | solution.py:388
  7.5 5.8 %collective-permute-start = (bf16[16,162]{1,0:T(8,128)(2,1)S(1)}, bf16[16,162]{1,0:T(8,128)(2,1)S(1)}, u32[]{:S(2)}, u32[]{:S(2)}) collective-permute-start(bf16[16,162]{1,0:T(8,128)(2,1)S(1)} %copy-done.5), channel_id=1, source_target_pairs={{0,1},{1,2},{2,3},{3,0},{4,5},{5,6},{6,7},{7,4},{8,9},{9,10},{10,1... | collective-permute-start | bytes 15560 | tf_op jit(solution)/shard_map/ppermute | solution.py:369
  10.2 3.1 %collective-permute-start.1 = (bf16[16,162]{1,0:T(8,128)(2,1)S(1)}, bf16[16,162]{1,0:T(8,128)(2,1)S(1)}, u32[]{:S(2)}, u32[]{:S(2)}) collective-permute-start(bf16[16,162]{1,0:T(8,128)(2,1)S(1)} %copy-done.5), channel_id=1, source_target_pairs={{1,0},{2,1},{3,2},{0,3},{5,4},{6,5},{7,6},{4,7},{9,8},{10,9},{11,1... | collective-permute-start | bytes 15560 | tf_op jit(solution)/shard_map/ppermute | solution.py:370
  13.5 6.0 %collective-permute-start.2 = (f32[2,8,162]{2,1,0:T(8,128)S(1)}, f32[2,8,162]{2,1,0:T(8,128)S(1)}, u32[]{:S(2)}, u32[]{:S(2)}) collective-permute-start(f32[2,8,162]{2,1,0:T(8,128)S(1)} %get-tuple-element.30), channel_id=1, source_target_pairs={{0,4},{4,0},{8,12},{12,8},{16,20},{20,16},{24,28},{28,24},{1,5},{5... | collective-permute-start | bytes 31112 | tf_op jit(solution)/shard_map/ppermute | solution.py:418
  20.3 3.5 %collective-permute-start.4 = (f32[8,162]{1,0:T(8,128)S(1)}, f32[8,162]{1,0:T(8,128)S(1)}, u32[]{:S(2)}, u32[]{:S(2)}) collective-permute-start(f32[8,162]{1,0:T(8,128)S(1)} %get-tuple-element.40.local_ref), channel_id=1, source_target_pairs={{0,8},{4,12},{8,24},{12,28},{16,20},{20,16},{24,0},{28,4},{1,9},{5... | collective-permute-start | bytes 15560 | tf_op jit(solution)/shard_map/ppermute | solution.py:449
  23.8 2.5 %collective-permute-start.5 = (f32[8,162]{1,0:T(8,128)S(1)}, f32[8,162]{1,0:T(8,128)S(1)}, u32[]{:S(2)}, u32[]{:S(2)}) collective-permute-start(f32[8,162]{1,0:T(8,128)S(1)} %shard_map.107), channel_id=1, source_target_pairs={{0,8},{4,12},{8,16},{12,20},{16,0},{20,4},{24,28},{28,24},{1,9},{5... | collective-permute-start | bytes 15560 | tf_op jit(solution)/shard_map/ppermute | solution.py:449
  26.3 3.1 %collective-permute-start.6 = (f32[8,162]{1,0:T(8,128)S(1)}, f32[8,162]{1,0:T(8,128)S(1)}, u32[]{:S(2)}, u32[]{:S(2)}) collective-permute-start(f32[8,162]{1,0:T(8,128)S(1)} %shard_map.108), channel_id=1, source_target_pairs={{0,4},{4,0},{8,16},{12,20},{16,24},{20,28},{24,8},{28,12},{1,5},{5... | collective-permute-start | bytes 15560 | tf_op jit(solution)/shard_map/ppermute | solution.py:449
  30.8 2.6 %collective-permute-start.7 = (f32[8,162]{1,0:T(8,128)S(1)}, f32[8,162]{1,0:T(8,128)S(1)}, u32[]{:S(2)}, u32[]{:S(2)}) collective-permute-start(f32[8,162]{1,0:T(8,128)S(1)} %get-tuple-element.43.local_ref), channel_id=1, source_target_pairs={{0,24},{4,28},{8,12},{12,8},{16,0},{20,4},{24,16},{28,20},{1,25},{... | collective-permute-start | bytes 15560 | tf_op jit(solution)/shard_map/ppermute | solution.py:460
  33.3 4.4 %collective-permute-start.8 = (f32[8,162]{1,0:T(8,128)S(1)}, f32[8,162]{1,0:T(8,128)S(1)}, u32[]{:S(2)}, u32[]{:S(2)}) collective-permute-start(f32[8,162]{1,0:T(8,128)S(1)} %shard_map.110), channel_id=1, source_target_pairs={{0,4},{4,0},{8,24},{12,28},{16,8},{20,12},{24,16},{28,20},{1,5},{5... | collective-permute-start | bytes 15560 | tf_op jit(solution)/shard_map/ppermute | solution.py:460
  37.8 2.5 %collective-permute-start.9 = (f32[8,162]{1,0:T(8,128)S(1)}, f32[8,162]{1,0:T(8,128)S(1)}, u32[]{:S(2)}, u32[]{:S(2)}) collective-permute-start(f32[8,162]{1,0:T(8,128)S(1)} %shard_map.111), channel_id=1, source_target_pairs={{0,16},{4,20},{8,0},{12,4},{16,8},{20,12},{24,28},{28,24},{1,17},{... | collective-permute-start | bytes 15560 | tf_op jit(solution)/shard_map/ppermute | solution.py:460
  41.0 4.9 %collective-permute-start.10 = (f32[2,8,162]{2,1,0:T(8,128)S(1)}, f32[2,8,162]{2,1,0:T(8,128)S(1)}, u32[]{:S(2)}, u32[]{:S(2)}) collective-permute-start(f32[2,8,162]{2,1,0:T(8,128)S(1)} %get-tuple-element.46), channel_id=1, source_target_pairs={{0,4},{4,0},{8,12},{12,8},{16,20},{20,16},{24,28},{28,24},{1,5},{5... | collective-permute-start | bytes 31112 | tf_op jit(solution)/shard_map/ppermute | solution.py:467

commit v3 on v0

v3 whole, which is shorter than its diff:
```python
import functools

import jax
import jax.numpy as jnp
from jax import lax
from jax.experimental import pallas as pl
from jax.experimental.pallas import tpu as pltpu
from jax.sharding import PartitionSpec as P

F32 = jnp.float32
BF16 = jnp.bfloat16
TILE = 8
VMEM = pl.BlockSpec(memory_space=pltpu.VMEM)
SMEM = pl.BlockSpec(memory_space=pltpu.SMEM)
HBM = pl.BlockSpec(memory_space=pltpu.HBM)


def split2(x):
    high = x.astype(BF16)
    return high, (x - high.astype(F32)).astype(BF16)


def product(x, y):
    dot = functools.partial(jnp.dot, preferred_element_type=F32)
    return dot(x[0], y[0]) + (dot(x[0], y[1]) + dot(x[1], y[0]))


def apply_pairs(vector, ref, *at):
    count = vector.shape[0]
    rows = lax.broadcasted_iota(jnp.int32, vector.shape, 0)
    both = jnp.concatenate(split2(vector), axis=0)
    total = jnp.zeros(vector.shape, F32)
    for l in range(count):
        first = jnp.dot(both, ref[(*at, l, 0)], preferred_element_type=F32)
        second = jnp.dot(both, ref[(*at, l, 1)], preferred_element_type=F32)
        total = jnp.where(rows == l, first[:count] + first[count:] + second[:count], total)
    return total


def apply_rows(vector, ref, *at):
    count = vector.shape[0]
    rows = lax.broadcasted_iota(jnp.int32, vector.shape, 0)
    both = jnp.concatenate(split2(vector), axis=0)
    total = jnp.zeros(vector.shape, F32)
    for l in range(count):
        first = lax.dot_general(
            both, ref[(*at, l)], (((1,), (1,)), ((), ())), preferred_element_type=F32
        )
        total = jnp.where(rows == l, first[:count] + first[count:], total)
    return total


def core_of():
    return lax.rem(lax.axis_index("wall"), 2)


def chip_of():
    return lax.div(lax.axis_index("wall"), 2)


def relayout_kernel(dinv_ref, lower_ref, upper_ref, raw_ref, landed, arrived):
    kinds, depth, lines = raw_ref.shape[:3]
    copies = [
        [pltpu.make_async_copy(ref.at[e], landed.at[a, e], arrived.at[a, e]) for e in range(depth)]
        for a, ref in enumerate((dinv_ref, lower_ref, upper_ref))
    ]
    for copy in sum(copies, []):
        copy.start()
    for a in range(kinds):
        for e in range(depth):
            copies[a][e].wait()
            turned = jnp.swapaxes(landed[a, e], 0, 1)
            for l in range(lines):
                raw_ref[a, e, l] = turned[l]


def pair_kernel(raw_ref, q_ref, s_ref, own_ref, send_ref):
    core = core_of()
    count, lines = raw_ref.shape[1], raw_ref.shape[2]
    for l in range(lines):
        qs, ss = [], []
        for e in range(count):
            for held, ref, source in ((qs, q_ref, 1), (ss, s_ref, 2)):
                block = lax.dot_general(
                    raw_ref[source, e, l],
                    raw_ref[0, e, l],
                    (((0,), (1,)), ((), ())),
                    preferred_element_type=F32,
                )
                pair = split2(block)
                held.append(pair)
                ref[e, l, 0], ref[e, l, 1] = pair
        forward = qs[0]
        for e in range(1, count):
            forward = split2(product(forward, qs[e]))
        backward = ss[count - 1]
        for e in range(count - 2, -1, -1):
            backward = split2(product(backward, ss[e]))
        if count % 2:
            forward, backward = [[-x for x in pair] for pair in (forward, backward)]
        for i in range(2):
            own_ref[l, i] = jnp.where(core == 0, backward[i], forward[i])
            send_ref[l, i] = jnp.where(core == 0, forward[i], backward[i])


def chip_kernel(got_ref, own_ref, chip_ref):
    for l in range(own_ref.shape[0]):
        pair = split2(product((got_ref[l, 0], got_ref[l, 1]), (own_ref[l, 0], own_ref[l, 1])))
        chip_ref[l, 0], chip_ref[l, 1] = pair


def through_kernel(len_ref, q_ref, s_ref, own_ref, send_ref, out_ref, *, last):
    depth, lines = q_ref.shape[:2]
    first_line = pl.program_id(0) * lines if pl_grid(len_ref, lines) else 0

    @pl.when(chip_of() == last)
    def _():
        core = core_of()
        place = lax.axis_index("wall") * depth
        for l in range(lines):
            length = len_ref[first_line + l]
            active = [(place + g < length).astype(F32) for g in range(depth)]
            whole = [jnp.where(core == 0, send_ref[l, i], own_ref[l, i]) for i in range(2)]
            steps = [(-q_ref[0, l, 0], -q_ref[0, l, 1])]
            for g in range(1, depth - 1):
                steps.append(split2(-product(steps[-1], (q_ref[g, l, 0], q_ref[g, l, 1]))))
            value = active[depth - 1] * (whole[0].astype(F32) + whole[1].astype(F32))
            for g in range(depth - 2, -1, -1):
                reach = steps[g][0].astype(F32) + steps[g][1].astype(F32)
                value = active[g] * (reach - product(split2(value), (s_ref[g, l, 0], s_ref[g, l, 1])))
            out_ref[l, 0], out_ref[l, 1] = split2(value)


def pl_grid(len_ref, lines):
    return len_ref.shape[0] != lines


def prepare_kernel(slot_ref, len_ref, coef_ref, nb_ref, source_ref, weight_ref, rhs_ref, act_ref):
    faces, slots = coef_ref.shape
    depth, lines = slot_ref.shape
    cells = 3 * slots
    k = lax.broadcasted_iota(jnp.int32, (cells, slots), 0)
    e = lax.broadcasted_iota(jnp.int32, (cells, slots), 1)
    weight = jnp.zeros((cells, slots), F32)
    own = jnp.zeros((1, slots), F32)
    for f in range(faces):
        coef = coef_ref[f : f + 1, :]
        own = own + coef
        weight = weight - jnp.where(k == nb_ref[f : f + 1, :], coef, 0.0)
    weight = weight + jnp.where(k == e + slots, own, 0.0)
    count = depth * lines
    rows = lax.broadcasted_iota(jnp.int32, (count, slots), 0)
    slot = jnp.zeros((count, slots), jnp.int32)
    for g in range(depth):
        for l in range(lines):
            slot = jnp.where(rows == g * lines + l, slot_ref[g, l], slot)
    chosen = (slot == lax.broadcasted_iota(jnp.int32, (count, slots), 1)).astype(F32).astype(BF16)
    high = weight.astype(BF16)
    mid, low = split2(weight - high.astype(F32))
    for i, part in enumerate((high, mid, low)):
        weight_ref[i * count : (i + 1) * count, :] = lax.dot_general(
            chosen, part, (((1,), (1,)), ((), ())), preferred_element_type=F32
        ).astype(BF16)
    rhs_ref[...] = jnp.dot(chosen, source_ref[...], preferred_element_type=F32)
    rows = lax.broadcasted_iota(jnp.int32, act_ref.shape[1:], 0)
    length = jnp.zeros(act_ref.shape[1:], jnp.int32)
    for l in range(lines):
        length = jnp.where(rows == l, len_ref[l], length)
    place = lax.axis_index("wall") * depth
    for g in range(depth):
        act_ref[g] = (place + g < length).astype(F32)


def residual_kernel(before, state, after, weight, source, lift, rhs_ref):
    cells = jnp.concatenate([before[...], state[...], after[...]], axis=0)
    parts = jnp.dot(weight[...], cells, preferred_element_type=F32)
    count = source.shape[0]
    face_sum = parts[:count] + (parts[count : 2 * count] + parts[2 * count :])
    flux = jnp.dot(face_sum.astype(BF16), lift[...], preferred_element_type=F32)
    rhs = source[...] - flux
    depth, lines, _ = rhs_ref.shape
    for g in range(depth):
        rhs_ref[g] = rhs[g * lines : (g + 1) * lines]


def forward_local(scaled, q_ref, act_ref, carried):
    values = []
    for g, value in enumerate(scaled):
        if carried is not None:
            value = value - apply_pairs(carried, q_ref, g)
        carried = act_ref[g] * value
        values.append(carried)
    return values


def backward_local(values, s_ref, act_ref, carried):
    solved = [None] * len(values)
    for g in range(len(values) - 1, -1, -1):
        value = values[g]
        if carried is not None:
            value = value - apply_pairs(carried, s_ref, g)
        carried = act_ref[g] * value
        solved[g] = carried
    return solved


def local_kernel(rhs_ref, raw_ref, q_ref, act_ref, scaled_ref, y_ref):
    depth = rhs_ref.shape[0]
    scaled = [apply_rows(rhs_ref[g], raw_ref, 0, g) for g in range(depth)]
    values = forward_local(scaled, q_ref, act_ref, None)
    for g in range(depth):
        scaled_ref[g] = scaled[g]
        y_ref[g] = values[g]


def chip_local_kernel(came_ref, own_ref, act_ref, y_ref, out_ref):
    depth = y_ref.shape[0]
    out_ref[...] = y_ref[depth - 1]

    @pl.when(core_of() == 1)
    def _():
        out_ref[...] = act_ref[depth - 1] * apply_pairs(came_ref[...], own_ref) + y_ref[depth - 1]


def echo_kernel(y_ref, s_ref, act_ref, out_ref):
    depth = y_ref.shape[0]
    out_ref[...] = backward_local([y_ref[g] for g in range(depth)], s_ref, act_ref, None)[0]


def hop_kernel(came_ref, pair_ref, act_ref, local_ref, out_ref, *, chip, core):
    out_ref[...] = local_ref[...]

    @pl.when(jnp.logical_and(chip_of() == chip, core_of() == core))
    def _():
        gone = apply_pairs(came_ref[...], pair_ref)
        out_ref[...] = act_ref[act_ref.shape[0] - 1] * gone + local_ref[...]


def chosen_arrival(refs, chips, like):
    here = chip_of()
    value = jnp.zeros(like, F32)
    for ref, chip in zip(refs, chips):
        value = jnp.where(here == chip, ref[...], value)
    return value


def enter_kernel(echo_ref, *refs, chips):
    out_ref = refs[-1]
    out_ref[0] = chosen_arrival(refs[:-1], chips, echo_ref.shape)
    out_ref[1] = echo_ref[...]


def turn_kernel(
    enter_ref, met_ref, echo_ref, y_ref, act_ref, send_ref, own_ref, own_d, came_d, out_ref, mid_ref, *, last
):
    depth = y_ref.shape[0]
    out_ref[...] = echo_ref[...]
    mid_ref[...] = echo_ref[...]

    @pl.when(jnp.logical_and(chip_of() == last, core_of() == 0))
    def _():
        enter = enter_ref[...]
        leave = act_ref[depth - 1] * apply_pairs(enter, send_ref) + y_ref[depth - 1]
        first = apply_pairs(enter, own_d) + echo_ref[...]
        middle = apply_pairs(leave, came_d) + met_ref[1]
        mid_ref[...] = middle
        out_ref[...] = apply_pairs(middle, own_ref) + first


def inner_kernel(entered_ref, met_ref, got_ref, came_ref, scaled_ref, q_ref, s_ref, act_ref, y_ref, first_ref, flow, *, last):
    depth = scaled_ref.shape[0]

    @pl.when(chip_of() != last)
    def _():
        flow[...] = met_ref[0]

        @pl.when(core_of() == 1)
        def _():
            flow[...] = apply_pairs(entered_ref[0], got_ref) + came_ref[...]

        scaled = [scaled_ref[g] for g in range(depth)]
        values = forward_local(scaled, q_ref, act_ref, flow[...])
        for g in range(depth):
            y_ref[g] = values[g]
        first_ref[...] = backward_local(values, s_ref, act_ref, None)[0]


def inner_chip_kernel(met_ref, first_ref, own_ref, out_ref):
    @pl.when(core_of() == 0)
    def _():
        out_ref[...] = apply_pairs(met_ref[...], own_ref) + first_ref[...]


def leave_kernel(enter_ref, *refs, chips):
    out_ref = refs[-1]
    out_ref[0] = chosen_arrival(refs[:-1], chips, enter_ref.shape)
    out_ref[1] = enter_ref[...]


def middle_kernel(leave_ref, got_ref, met_ref, mid_ref, out_ref, *, last):
    out_ref[...] = mid_ref[...]

    @pl.when(jnp.logical_and(chip_of() != last, core_of() == 0))
    def _():
        out_ref[...] = apply_pairs(leave_ref[0], got_ref) + met_ref[...]


def last_kernel(
    met_ref, middle_ref, enter_ref, came_ref, got_ref, scaled_ref, q_ref, s_ref, act_ref, y_ref, out_ref, flow, held, *, last
):
    depth = y_ref.shape[0]
    core = core_of()
    for g in range(depth):
        held[g] = y_ref[g]

    @pl.when(chip_of() == last)
    def _():
        flow[...] = enter_ref[...]

        @pl.when(core == 1)
        def _():
            flow[...] = apply_pairs(met_ref[1], got_ref) + came_ref[...]

        scaled = [scaled_ref[g] for g in range(depth)]
        for g, value in enumerate(forward_local(scaled, q_ref, act_ref, flow[...])):
            held[g] = value

    carried = jnp.where(core == 0, middle_ref[...], met_ref[0])
    solved = backward_local([held[g] for g in range(depth)], s_ref, act_ref, carried)
    for g in range(depth):
        out_ref[g] = solved[g]


def padded_bytes(shape, dtype):
    size = jnp.dtype(dtype).itemsize
    shape = (1,) * (2 - len(shape)) + tuple(shape)
    total = -(-shape[-2] // 16) * 16 * -(-shape[-1] // 128) * 128 * size
    for extent in shape[:-2]:
        total *= extent
    return total


def run(kernel, operands, outs, blocks=1, scratch=()):
    held = [(x.shape, x.dtype) for x, _ in operands] + [(s, t) for s, t, _ in outs]
    limit = sum(padded_bytes(s, t) for s, t in held)
    if blocks == 1:
        in_specs = [at if isinstance(at, pl.BlockSpec) else VMEM for _, at in operands]
        out_specs = [VMEM for _ in outs]
        grid = ()
    else:

        def spec(shape, at):
            if isinstance(at, pl.BlockSpec):
                return at
            if at is None:
                return pl.BlockSpec(shape, lambda i: (0,) * len(shape))
            size = tuple(n // blocks if axis == at else n for axis, n in enumerate(shape))
            return pl.BlockSpec(size, lambda i: tuple(i if axis == at else 0 for axis in range(len(shape))))

        in_specs = [spec(x.shape, at) for x, at in operands]
        out_specs = [spec(s, at) for s, _, at in outs]
        grid = (blocks,)
        limit = 2 * limit // blocks
    limit += sum(padded_bytes(s.shape, s.dtype) for s in scratch if s.memory_space == pltpu.VMEM)
    limit = min(limit + limit // 4 + (4 << 20), 60 << 20)
    return pl.pallas_call(
        kernel,
        grid=grid,
        in_specs=in_specs,
        out_specs=out_specs,
        out_shape=[jax.ShapeDtypeStruct(s, t) for s, t, _ in outs],
        scratch_shapes=list(scratch),
        compiler_params=pltpu.CompilerParams(vmem_limit_bytes=limit),
    )(*[x for x, _ in operands])


def hop_pairs(count, start, end):
    target = {i: i ^ 1 for i in range(count)}
    target.update({start: end, end: end ^ 1, end ^ 1: start ^ 1, start ^ 1: start})
    return sorted(target.items())


def per_device(state, source, face_coef, neighbour, lift, elem_slot, line_len, dinv, lower, upper):
    wall_count = lax.axis_size("wall")
    surf_count = lax.axis_size("surf")
    chips = wall_count // 2
    last = chips - 1
    depth, lines, width, _ = dinv.shape
    slots = state.shape[0]
    block = TILE if lines % TILE == 0 else lines
    blocks = lines // block
    flips = [(i, i ^ 1) for i in range(wall_count)]
    line_vector = ((lines, width), F32, 0)
    two_vectors = ((2, lines, width), F32, 1)
    element_vectors = ((depth, lines, width), F32, 1)
    line_pairs = ((lines, 2, width, width), BF16, 0)
    element_pairs = ((depth, lines, 2, width, width), BF16, 1)
    flow = pltpu.VMEM((block, width), F32)

    before = lax.ppermute(state, "surf", [(i, (i + 1) % surf_count) for i in range(surf_count)])
    after = lax.ppermute(state, "surf", [((i + 1) % surf_count, i) for i in range(surf_count)])

    raw_shape = (3, depth, lines, width, width)
    if lines == TILE:
        (raw,) = run(
            relayout_kernel,
            [(jnp.transpose(x, (0, 2, 1, 3)), HBM) for x in (dinv, lower, upper)],
            [(raw_shape, BF16, None)],
            scratch=[
                pltpu.VMEM((3, depth, width, lines, width), BF16),
                pltpu.SemaphoreType.DMA((3, depth)),
            ],
        )
    else:
        raw = jnp.stack([dinv, lower, upper])
    q, s, own, send = run(
        pair_kernel, [(raw, 2)], [element_pairs, element_pairs, line_pairs, line_pairs], blocks
    )
    got = lax.ppermute(send, "wall", flips)

    count = depth * lines
    weight, line_source, act = run(
        prepare_kernel,
        [(elem_slot, SMEM), (line_len, SMEM), (face_coef.T, None), (neighbour.T, None), (source, None)],
        [((3 * count, 3 * slots), BF16, None), ((count, width), F32, None), element_vectors],
    )
    (rhs,) = run(
        residual_kernel,
        [(before, None), (state, None), (after, None), (weight, None), (line_source, None), (lift, None)],
        [element_vectors],
    )
    scaled, y_local = run(
        local_kernel,
        [(rhs, 1), (raw, 2), (q, 1), (act, 1)],
        [element_vectors, element_vectors],
        blocks,
    )
    came_y = lax.ppermute(y_local[depth - 1], "wall", flips)
    (chip,) = run(chip_kernel, [(got, 0), (own, 0)], [line_pairs], blocks)
    (y_chip,) = run(
        chip_local_kernel, [(came_y, 0), (own, 0), (act, 1), (y_local, 1)], [line_vector], blocks
    )
    (through,) = run(
        functools.partial(through_kernel, last=last),
        [(line_len, SMEM), (q, 1), (s, 1), (own, 0), (send, 0)],
        [line_pairs],
        blocks,
    )
    came_through = lax.ppermute(through, "wall", flips)
    (echo,) = run(echo_kernel, [(y_local, 1), (s, 1), (act, 1)], [line_vector], blocks)

    def hop(came, local, at, core):
        (out,) = run(
            functools.partial(hop_kernel, chip=at, core=core),
            [(came, 0), (chip, 0), (act, 1), (local, 0)],
            [line_vector],
            blocks,
        )
        return out

    arrivals = []
    for at in range(last):
        if at == last - 1:
            (entered,) = run(
                functools.partial(enter_kernel, chips=list(range(1, last))),
                [(echo, 0)] + [(x, 0) for x in arrivals],
                [two_vectors],
                blocks,
            )
        out = y_chip if at == 0 else hop(arrivals[-1], y_chip, at, 1)
        end = 2 * at + 3 if at + 1 < last else 2 * last
        arrivals.append(lax.ppermute(out, "wall", hop_pairs(wall_count, 2 * at + 1, end)))
    met = lax.ppermute(entered, "wall", flips)
    enter_last = arrivals[-1]
    x_last, x_middle = run(
        functools.partial(turn_kernel, last=last),
        [(enter_last, 0), (met, 1), (echo, 0), (y_local, 1), (act, 1)]
        + [(x, 0) for x in (send, own, through, came_through)],
        [line_vector, line_vector],
        blocks,
    )
    y, first = run(
        functools.partial(inner_kernel, last=last),
        [(entered, 1), (met, 1), (got, 0), (came_y, 0), (scaled, 1), (q, 1), (s, 1), (act, 1)],
        [element_vectors, line_vector],
        blocks,
        [flow],
    )
    arrivals = [lax.ppermute(x_last, "wall", hop_pairs(wall_count, 2 * last, 2 * last - 2))]
    came_first = lax.ppermute(first, "wall", flips)
    (x_chip,) = run(inner_chip_kernel, [(came_first, 0), (first, 0), (own, 0)], [line_vector], blocks)
    for at in range(last - 1, 0, -1):
        out = hop(arrivals[-1], x_chip, at, 0)
        arrivals.append(lax.ppermute(out, "wall", hop_pairs(wall_count, 2 * at, 2 * at - 2)))
    (left,) = run(
        functools.partial(leave_kernel, chips=list(range(last - 1, -1, -1))),
        [(enter_last, 0)] + [(x, 0) for x in arrivals],
        [two_vectors],
        blocks,
    )
    met_left = lax.ppermute(left, "wall", flips)
    (middle,) = run(
        functools.partial(middle_kernel, last=last),
        [(left, 1), (got, 0), (came_first, 0), (x_middle, 0)],
        [line_vector],
        blocks,
    )
    (solution,) = run(
        functools.partial(last_kernel, last=last),
        [(met_left, 1), (middle, 0), (enter_last, 0), (came_y, 0), (got, 0)]
        + [(x, 1) for x in (scaled, q, s, act, y)],
        [element_vectors],
        blocks,
        [flow, pltpu.VMEM((depth, block, width), F32)],
    )
    return solution


def solution(mesh):
    in_specs = (
        P(("wall", "surf"), None),
        P(("wall", "surf"), None),
        P(("wall", "surf"), None),
        P(("wall", "surf"), None),
        P(),
        P("wall", "surf"),
        P("surf"),
        P("wall", "surf", None, None),
        P("wall", "surf", None, None),
        P("wall", "surf", None, None),
    )
    out_specs = P("wall", "surf", None)
    return jax.shard_map(
        per_device, mesh=mesh, in_specs=in_specs, out_specs=out_specs, check_vma=False
    )
```

time: 134 us -> 42.7 us (0.32); the launches traced: 132 us -> 42.2 us
  other arithmetic: 28 us -> 0 us
  matrix products: 26.3 us -> 0 us
  waiting for transfers between devices: 26.9 us -> 5.34 us
  Pallas kernels: 0 us -> 11.5 us
  local copies, waits for them, and re-layouts: 15 us -> 5.53 us
  blocking collectives: 8.05 us -> 0 us
  starting transfers between devices: 27.3 us -> 19.7 us
    all_to_all x4 -> x0, waiting for transfers between devices: 26.9 us -> none  [the longest x1 14.1 us: per_device(): lax.all_to_all(dinv, 'wall', split_axis=1, concat_axis=0, tiled=True)]
    dot_general x65 -> x0, matrix products: 26.3 us -> none  [the longest x64 25.5 us: apply_block(): jnp.einsum('lij,lj->li', matrix.astype(jnp.float32), vector, precision=la...]
    all_to_all x4 -> x0, starting transfers between devices: 23.1 us -> none  [the longest x1 7.01 us: per_device(): lax.all_to_all(lower, 'wall', split_axis=1, concat_axis=0, tiled=True)]
    mul x32 -> x0, other arithmetic: 22.3 us -> none  [the longest x16 11.2 us: forward_step(): act_now[:, None]]
    ppermute x2 -> x14, starting transfers between devices: 4.21 us -> 19.7 us  [the longest x1 5.92 us: per_device(): met_left = lax.ppermute(left, 'wall', flips)]
    pallas_call x0 -> x20, Pallas kernels: none -> 11.5 us  [run(): pl.pallas_call(kernel, grid=grid, in_specs=in_specs, out_specs=out_specs,...]
    all_to_all x1 -> x0, blocking collectives: 8.05 us -> none  [per_device(): lax.all_to_all(line_solution, 'wall', split_axis=0, concat_axis=1, tiled=...]
    ppermute x2 -> x14, waiting for transfers between devices: 0.01 us -> 5.34 us  [the longest x2 1.62 us: per_device(): lax.ppermute(out, 'wall', hop_pairs(wall_count, 2 * at, 2 * at - 2))]
  transfers between devices with their start and end apart: 6 -> 14, of which waited for: 3 -> 9; matrix products, arithmetic and copies ran while one was open for 34% -> 2% of each run, Pallas kernels for 0% -> 11%
where the time goes in v3:
time: 42.7 us; the launch traced here: 42.2 us
  starting transfers between devices  19.7 us (46%)
  Pallas kernels  11.5 us (27%)
  local copies, waits for them, and re-layouts  5.53 us (13%)
  waiting for transfers between devices  5.34 us (13%)
    pallas_call x20, Pallas kernels, run(): pl.pallas_call(kernel, grid=grid, in_specs=in_specs, out_specs=out_specs,...  11.5 us
    ppermute x1, starting transfers between devices, per_device(): met_left = lax.ppermute(left, 'wall', flips)  5.92 us
    unnamed x20, local copies, waits for them, and re-layouts  4.06 us
    ppermute x2, starting transfers between devices, per_device(): lax.ppermute(out, 'wall', hop_pairs(wall_count, 2 * at, 2 * at - 2))  3.57 us
    ppermute x3, starting transfers between devices, per_device(): lax.ppermute(out, 'wall', hop_pairs(wall_count, 2 * at + 1, end))  2.83 us
    ppermute x1, starting transfers between devices, per_device(): lax.ppermute(state, 'surf', [(i, (i + 1) % surf_count) for i in range(sur...  2.4 us
    ppermute x1, starting transfers between devices, per_device(): lax.ppermute(state, 'surf', [((i + 1) % surf_count, i) for i in range(sur...  2.06 us
    ppermute x2, waiting for transfers between devices, per_device(): lax.ppermute(out, 'wall', hop_pairs(wall_count, 2 * at, 2 * at - 2))  1.62 us
  transfers between devices with their start and end apart: 14, of which 9 were waited for; matrix products, arithmetic and copies ran while one was open for 2% of the time, Pallas kernels for 11%

profile of v3, /device:TPU:1, one launch (start us, length us, event | category | flops | bytes accessed | tf_op | source)
XLA Modules:
  0.0 42.2 jit_solution(18011108217010729210)
XLA Ops:
  0.0 1.3 %copy-done = bf16[2,8,162,162]{3,1,2,0:T(8,128)(2,1)S(1)} copy-done((bf16[2,8,162,162]{3,1,2,0:T(8,128)(2,1)S(1)}, bf16[2,8,162,162]{3,1,2,0:T(8,128)(2,1)}, u32[]{:S(2)}) %copy-start) | copy-done | bytes 839832
  1.3 1.3 %copy-done.1 = bf16[2,8,162,162]{3,1,2,0:T(8,128)(2,1)S(1)} copy-done((bf16[2,8,162,162]{3,1,2,0:T(8,128)(2,1)S(1)}, bf16[2,8,162,162]{3,1,2,0:T(8,128)(2,1)}, u32[]{:S(2)}) %copy-start.1) | copy-done | bytes 839832
  2.6 1.3 %copy-done.2 = bf16[2,8,162,162]{3,1,2,0:T(8,128)(2,1)S(1)} copy-done((bf16[2,8,162,162]{3,1,2,0:T(8,128)(2,1)S(1)}, bf16[2,8,162,162]{3,1,2,0:T(8,128)(2,1)}, u32[]{:S(2)}) %copy-start.2) | copy-done | bytes 839832
  4.0 2.4 %shard_map.102.raw_ref = bf16[3,2,8,162,162]{4,3,2,1,0:T(8,128)(2,1)S(1)} custom-call(bf16[2,162,8,162]{3,2,1,0:T(8,128)(2,1)S(1)} %bitcast.7, bf16[2,162,8,162]{3,2,1,0:T(8,128)(2,1)S(1)} %bitcast.8, bf16[2,162,8,162]{3,2,1,0:T(8,128)(2,1)S(1)} %bitcast.9), custom_call_target="tpu_custom_call" | custom-call | tf_op jit(solution)/shard_map/pallas_call | solution.py:366
  6.4 3.2 %shard_map.103 = (bf16[2,8,2,162,162]{4,3,2,1,0:T(8,128)(2,1)S(1)}, bf16[2,8,2,162,162]{4,3,2,1,0:T(8,128)(2,1)S(1)}, bf16[8,2,162,162]{3,2,1,0:T(8,128)(2,1)S(1)}, bf16[8,2,162,162]{3,2,1,0:T(8,128)(2,1)S(1)}) custom-call(bf16[3,2,8,162,162]{4,3,2,1,0:T(8,128)(2,1)S(1)} %shard_map.102.raw_ref), custom_call_target="tpu_custom_call" | custom-call | tf_op jit(solution)/shard_map/pallas_call | solution.py:366
  9.5 0.0 copy-start.6
  9.6 0.5 %copy.11 = bf16[8,2,162,162]{3,0,2,1:T(8,128)(2,1)S(1)} copy(bf16[8,2,162,162]{3,2,1,0:T(8,128)(2,1)S(1)} %get-tuple-element.24.send_ref) | data formatting | bytes 1679616 | tf_op jit(solution)/shard_map/pallas_call | solution.py:366
  10.0 0.1 collective-permute-start.4
  10.1 0.1 copy-done.6
  10.2 0.6 %shard_map.111.own_d = bf16[8,2,162,162]{3,2,1,0:T(8,128)(2,1)S(1)} custom-call(s32[8]{0:T(128)S(1)} %copy-done.6, bf16[2,8,2,162,162]{4,3,2,1,0:T(8,128)(2,1)S(1)} %get-tuple-element.20.q_ref, bf16[2,8,2,162,162]{4,3,2,1,0:T(8,128)(2,1)S(1)} %get-tuple-element.25.s_ref, bf16[8,2,162,162]{3,2,1,0:T(8,128)(2,1)S(1)} %get-tuple-element.23.own_ref, ...), custom_call_target="tpu_custom_call" | custom-call | tf_op jit(solution)/shard_map/pallas_call | solution.py:366
  10.8 0.0 copy-start.4
  10.8 0.0 copy-start.5
  10.8 0.0 copy-start.7
  10.8 0.0 copy-start.8
  10.8 0.0 copy-start.3
  10.8 0.5 %copy.13 = bf16[8,2,162,162]{3,0,2,1:T(8,128)(2,1)S(1)} copy(bf16[8,2,162,162]{3,2,1,0:T(8,128)(2,1)S(1)} %shard_map.111.own_d) | data formatting | bytes 1679616 | tf_op jit(solution)/shard_map/pallas_call | solution.py:366
  11.3 0.5 %collective-permute-start.8 = (bf16[8,2,162,162]{3,0,2,1:T(8,128)(2,1)S(1)}, bf16[8,2,162,162]{3,0,2,1:T(8,128)(2,1)S(1)}, u32[]{:S(2)}, u32[]{:S(2)}) collective-permute-start(bf16[8,2,162,162]{3,0,2,1:T(8,128)(2,1)S(1)} %copy.13), channel_id=1, source_target_pairs={{0,4},{4,0},{8,12},{12,8},{16,20},{20,16},{24,28},{28,24},{1,5},{5... | collective-permute-start | bytes 2519432 | tf_op jit(solution)/shard_map/ppermute | solution.py:449
  11.8 2.4 %collective-permute-start = (bf16[16,162]{1,0:T(8,128)(2,1)S(1)}, bf16[16,162]{1,0:T(8,128)(2,1)S(1)}, u32[]{:S(2)}, u32[]{:S(2)}) collective-permute-start(bf16[16,162]{1,0:T(8,128)(2,1)S(1)} %copy-done.4), channel_id=1, source_target_pairs={{0,1},{1,2},{2,3},{3,0},{4,5},{5,6},{6,7},{7,4},{8,9},{9,10},{10,1... | collective-permute-start | bytes 15560 | tf_op jit(solution)/shard_map/ppermute | solution.py:400
  14.2 2.1 %collective-permute-start.1 = (bf16[16,162]{1,0:T(8,128)(2,1)S(1)}, bf16[16,162]{1,0:T(8,128)(2,1)S(1)}, u32[]{:S(2)}, u32[]{:S(2)}) collective-permute-start(bf16[16,162]{1,0:T(8,128)(2,1)S(1)} %copy-done.4), channel_id=1, source_target_pairs={{1,0},{2,1},{3,2},{0,3},{5,4},{6,5},{7,6},{4,7},{9,8},{10,9},{11,1... | collective-permute-start | bytes 15560 | tf_op jit(solution)/shard_map/ppermute | solution.py:401
  16.2 0.7 %shard_map.100 = (bf16[48,48]{1,0:T(8,128)(2,1)S(1)}, f32[16,162]{1,0:T(8,128)S(1)}, f32[2,8,162]{2,1,0:T(8,128)S(1)}) custom-call(s32[2,8]{1,0:T(2,128)S(1)} %copy-done.9, s32[8]{0:T(128)S(1)} %copy-done.6, f32[4,16]{1,0:T(4,128)S(1)} %bitcast.10, s32[4,16]{1,0:T(4,128)S(1)} %bitcast.11, bf16[16,162]{1,0:T(8,128)(2,1)S(1)} %copy-done.5), custom_call_target="tpu_custom_call" | custom-call | tf_op jit(solution)/shard_map/pallas_call | solution.py:366
  16.9 0.3 collective-permute-done.before
  17.2 0.2 shard_map.101.rhs_ref
  17.5 0.7 %shard_map.104 = (f32[2,8,162]{2,1,0:T(8,128)S(1)}, f32[2,8,162]{2,1,0:T(8,128)S(1)}) custom-call(f32[2,8,162]{2,1,0:T(8,128)S(1)} %shard_map.101.rhs_ref, bf16[3,2,8,162,162]{4,3,2,1,0:T(8,128)(2,1)S(1)} %shard_map.102.raw_ref, bf16[2,8,2,162,162]{4,3,2,1,0:T(8,128)(2,1)S(1)} %get-tuple-element.20.q_ref, f32[2,8,162]{2,1,0:T(8,128)S(1)} %get-tuple-element.21.act_ref), custom_call_target="tpu_custom_call" | custom-call | tf_op jit(solution)/shard_map/pallas_call | solution.py:366
  18.2 1.4 %collective-permute-start.2 = (f32[8,162]{1,0:T(8,128)S(1)}, f32[8,162]{1,0:T(8,128)S(1)}, u32[]{:S(2)}, u32[]{:S(2)}) collective-permute-start(f32[8,162]{1,0:T(8,128)S(1)} %slice_bitcast_fusion), channel_id=1, source_target_pairs={{0,4},{4,0},{8,12},{12,8},{16,20},{20,16},{24,28},{28,24},{1,5},{5... | collective-permute-start | bytes 15560 | tf_op jit(solution)/shard_map/ppermute | solution.py:438
  19.6 0.8 %collective-permute-done.2.came_ref = f32[8,162]{1,0:T(8,128)S(1)} collective-permute-done((f32[8,162]{1,0:T(8,128)S(1)}, f32[8,162]{1,0:T(8,128)S(1)}, u32[]{:S(2)}, u32[]{:S(2)}) %collective-permute-start.2) | collective-permute-done | bytes 5216 | tf_op jit(solution)/shard_map/ppermute | solution.py:438
  20.4 0.3 shard_map.105.local_ref
  20.7 1.4 %collective-permute-start.3 = (f32[8,162]{1,0:T(8,128)S(1)}, f32[8,162]{1,0:T(8,128)S(1)}, u32[]{:S(2)}, u32[]{:S(2)}) collective-permute-start(f32[8,162]{1,0:T(8,128)S(1)} %shard_map.105.local_ref), channel_id=1, source_target_pairs={{0,4},{4,12},{8,0},{12,8},{16,20},{20,16},{24,28},{28,24},{1,5},{5... | collective-permute-start | bytes 15560 | tf_op jit(solution)/shard_map/ppermute | solution.py:472
  22.1 0.3 copy.12.got_ref
  22.4 0.7 %shard_map.106.pair_ref = bf16[8,2,162,162]{3,2,1,0:T(8,128)(2,1)S(1)} custom-call(bf16[8,2,162,162]{3,2,1,0:T(8,128)(2,1)S(1)} %copy.12.got_ref, bf16[8,2,162,162]{3,2,1,0:T(8,128)(2,1)S(1)} %get-tuple-element.23.own_ref), custom_call_target="tpu_custom_call" | custom-call | tf_op jit(solution)/shard_map/pallas_call | solution.py:366
  23.2 1.3 %collective-permute-start.5 = (f32[8,162]{1,0:T(8,128)S(1)}, f32[8,162]{1,0:T(8,128)S(1)}, u32[]{:S(2)}, u32[]{:S(2)}) collective-permute-start(f32[8,162]{1,0:T(8,128)S(1)} %shard_map.107), channel_id=1, source_target_pairs={{0,4},{4,0},{8,12},{12,20},{16,8},{20,16},{24,28},{28,24},{1,5},{5... | collective-permute-start | bytes 15560 | tf_op jit(solution)/shard_map/ppermute | solution.py:472
  24.4 0.3 shard_map.109.echo_ref
  24.7 0.5 %collective-permute-done.5.came_ref.refs_1_ = f32[8,162]{1,0:T(8,128)S(1)} collective-permute-done((f32[8,162]{1,0:T(8,128)S(1)}, f32[8,162]{1,0:T(8,128)S(1)}, u32[]{:S(2)}, u32[]{:S(2)}) %collective-permute-start.5) | collective-permute-done | bytes 5216 | tf_op jit(solution)/shard_map/ppermute | solution.py:472
  25.3 0.3 collective-permute-start.7
  25.6 0.2 collective-permute-start.6
  25.8 0.3 copy.14.came_d
  26.1 0.4 collective-permute-done.7.met_ref
  26.5 1.2 %shard_map.113 = (f32[2,8,162]{2,1,0:T(8,128)S(1)}, f32[8,162]{1,0:T(8,128)S(1)}) custom-call(f32[2,8,162]{2,1,0:T(8,128)S(1)} %shard_map.110.entered_ref, f32[2,8,162]{2,1,0:T(8,128)S(1)} %collective-permute-done.7.met_ref, bf16[8,2,162,162]{3,2,1,0:T(8,128)(2,1)S(1)} %copy.12.got_ref, f32[8,162]{1,0:T(8,128)S(1)} %collective-permute-done.2.came_ref, ...), custom_call_target="tpu_custom_call" | custom-call | tf_op jit(solution)/shard_map/pallas_call | solution.py:366
  27.6 0.1 collective-permute-start.10
  27.8 0.5 %collective-permute-start.9 = (f32[8,162]{1,0:T(8,128)S(1)}, f32[8,162]{1,0:T(8,128)S(1)}, u32[]{:S(2)}, u32[]{:S(2)}) collective-permute-start(f32[8,162]{1,0:T(8,128)S(1)} %get-tuple-element.26), channel_id=1, source_target_pairs={{0,4},{4,0},{8,12},{12,8},{16,20},{20,28},{24,16},{28,24},{1,5},{5... | collective-permute-start | bytes 15560 | tf_op jit(solution)/shard_map/ppermute | solution.py:489
  28.2 0.7 %collective-permute-done.10.met_ref = f32[8,162]{1,0:T(8,128)S(1)} collective-permute-done((f32[8,162]{1,0:T(8,128)S(1)}, f32[8,162]{1,0:T(8,128)S(1)}, u32[]{:S(2)}, u32[]{:S(2)}) %collective-permute-start.10) | collective-permute-done | bytes 5216 | tf_op jit(solution)/shard_map/ppermute | solution.py:490
  28.9 0.2 collective-permute-done.9.came_ref.refs_0_
  29.0 0.4 collective-permute-start.11
  29.4 0.8 %collective-permute-done.11.came_ref.refs_1_ = f32[8,162]{1,0:T(8,128)S(1)} collective-permute-done((f32[8,162]{1,0:T(8,128)S(1)}, f32[8,162]{1,0:T(8,128)S(1)}, u32[]{:S(2)}, u32[]{:S(2)}) %collective-permute-start.11) | collective-permute-done | bytes 5216 | tf_op jit(solution)/shard_map/ppermute | solution.py:494
  30.3 3.2 %collective-permute-start.12 = (f32[8,162]{1,0:T(8,128)S(1)}, f32[8,162]{1,0:T(8,128)S(1)}, u32[]{:S(2)}, u32[]{:S(2)}) collective-permute-start(f32[8,162]{1,0:T(8,128)S(1)} %shard_map.116), channel_id=1, source_target_pairs={{0,4},{4,12},{8,0},{12,8},{16,20},{20,16},{24,28},{28,24},{1,5},{5... | collective-permute-start | bytes 15560 | tf_op jit(solution)/shard_map/ppermute | solution.py:494
  33.5 0.8 %collective-permute-done.12.refs_2_ = f32[8,162]{1,0:T(8,128)S(1)} collective-permute-done((f32[8,162]{1,0:T(8,128)S(1)}, f32[8,162]{1,0:T(8,128)S(1)}, u32[]{:S(2)}, u32[]{:S(2)}) %collective-permute-start.12) | collective-permute-done | bytes 5216 | tf_op jit(solution)/shard_map/ppermute | solution.py:494
  34.3 5.9 %collective-permute-start.13 = (f32[2,8,162]{2,1,0:T(8,128)S(1)}, f32[2,8,162]{2,1,0:T(8,128)S(1)}, u32[]{:S(2)}, u32[]{:S(2)}) collective-permute-start(f32[2,8,162]{2,1,0:T(8,128)S(1)} %shard_map.117.leave_ref), channel_id=1, source_target_pairs={{0,4},{4,0},{8,12},{12,8},{16,20},{20,16},{24,28},{28,24},{1,5},{5... | collective-permute-start | bytes 31112 | tf_op jit(solution)/shard_map/ppermute | solution.py:501
  40.2 0.8 %collective-permute-done.13.met_ref = f32[2,8,162]{2,1,0:T(8,128)S(1)} collective-permute-done((f32[2,8,162]{2,1,0:T(8,128)S(1)}, f32[2,8,162]{2,1,0:T(8,128)S(1)}, u32[]{:S(2)}, u32[]{:S(2)}) %collective-permute-start.13) | collective-permute-done | bytes 10400 | tf_op jit(solution)/shard_map/ppermute | solution.py:501
  41.0 1.2 %shard_map.119 = f32[2,8,162]{2,1,0:T(8,128)} custom-call(f32[2,8,162]{2,1,0:T(8,128)S(1)} %collective-permute-done.13.met_ref, f32[8,162]{1,0:T(8,128)S(1)} %shard_map.118.middle_ref, f32[8,162]{1,0:T(8,128)S(1)} %collective-permute-done.6.enter_ref, f32[8,162]{1,0:T(8,128)S(1)} %collective-permute-done.2.came_ref, ...), custom_call_target="tpu_custom_call" | custom-call | tf_op jit(solution)/shard_map/pallas_call | solution.py:366
  (25 shorter events, 0.1 us)
Async XLA Ops:
  0.0 1.3 %copy-start = (bf16[2,8,162,162]{3,1,2,0:T(8,128)(2,1)S(1)}, bf16[2,8,162,162]{3,1,2,0:T(8,128)(2,1)}, u32[]{:S(2)}) copy-start(bf16[2,8,162,162]{3,1,2,0:T(8,128)(2,1)} %param.17) | copy-start | bytes 2519428
  1.3 1.3 %copy-start.1 = (bf16[2,8,162,162]{3,1,2,0:T(8,128)(2,1)S(1)}, bf16[2,8,162,162]{3,1,2,0:T(8,128)(2,1)}, u32[]{:S(2)}) copy-start(bf16[2,8,162,162]{3,1,2,0:T(8,128)(2,1)} %param.18) | copy-start | bytes 2519428
  2.6 1.3 %copy-start.2 = (bf16[2,8,162,162]{3,1,2,0:T(8,128)(2,1)S(1)}, bf16[2,8,162,162]{3,1,2,0:T(8,128)(2,1)}, u32[]{:S(2)}) copy-start(bf16[2,8,162,162]{3,1,2,0:T(8,128)(2,1)} %param.19) | copy-start | bytes 2519428
  9.5 0.7 %copy-start.6 = (s32[8]{0:T(128)S(1)}, s32[8]{0:T(128)}, u32[]{:S(2)}) copy-start(s32[8]{0:T(128)} %len_ref.3) | copy-start | bytes 100
  10.0 12.1 %collective-permute-start.4 = (bf16[8,2,162,162]{3,0,2,1:T(8,128)(2,1)S(1)}, bf16[8,2,162,162]{3,0,2,1:T(8,128)(2,1)S(1)}, u32[]{:S(2)}, u32[]{:S(2)}) collective-permute-start(bf16[8,2,162,162]{3,0,2,1:T(8,128)(2,1)S(1)} %copy.11), channel_id=1, source_target_pairs={{0,4},{4,0},{8,12},{12,8},{16,20},{20,16},{24,28},{28,24},{1,5},{5... | collective-permute-start | bytes 2519432 | tf_op jit(solution)/shard_map/ppermute | solution.py:419
  10.8 1.0 %copy-start.4 = (bf16[16,162]{1,0:T(8,128)(2,1)S(1)}, bf16[16,162]{1,0:T(8,128)(2,1)}, u32[]{:S(2)}) copy-start(bf16[16,162]{1,0:T(8,128)(2,1)} %state.1) | copy-start | bytes 15556
  10.8 5.5 %copy-start.5 = (bf16[16,162]{1,0:T(8,128)(2,1)S(1)}, bf16[16,162]{1,0:T(8,128)(2,1)}, u32[]{:S(2)}) copy-start(bf16[16,162]{1,0:T(8,128)(2,1)} %source_ref.1) | copy-start | bytes 15556
  10.8 5.4 %copy-start.7 = (f32[16,4]{0,1:T(4,128)S(1)}, f32[16,4]{0,1:T(4,128)}, u32[]{:S(2)}) copy-start(f32[16,4]{0,1:T(4,128)} %param.12) | copy-start | bytes 772
  10.8 5.4 %copy-start.8 = (s32[16,4]{0,1:T(4,128)S(1)}, s32[16,4]{0,1:T(4,128)}, u32[]{:S(2)}) copy-start(s32[16,4]{0,1:T(4,128)} %param.13) | copy-start | bytes 772
  10.8 5.4 %copy-start.9 = (s32[2,8]{1,0:T(2,128)S(1)}, s32[2,8]{1,0:T(2,128)}, u32[]{:S(2)}) copy-start(s32[2,8]{1,0:T(2,128)} %slot_ref.1) | copy-start | bytes 196
  10.8 6.4 %copy-start.3 = (bf16[162,162]{1,0:T(8,128)(2,1)S(1)}, bf16[162,162]{1,0:T(8,128)(2,1)}, u32[]{:S(2)}) copy-start(bf16[162,162]{1,0:T(8,128)(2,1)} %lift.1) | copy-start | bytes 157468
  11.3 14.5 %collective-permute-start.8 = (bf16[8,2,162,162]{3,0,2,1:T(8,128)(2,1)S(1)}, bf16[8,2,162,162]{3,0,2,1:T(8,128)(2,1)S(1)}, u32[]{:S(2)}, u32[]{:S(2)}) collective-permute-start(bf16[8,2,162,162]{3,0,2,1:T(8,128)(2,1)S(1)} %copy.13), channel_id=1, source_target_pairs={{0,4},{4,0},{8,12},{12,8},{16,20},{20,16},{24,28},{28,24},{1,5},{5... | collective-permute-start | bytes 2519432 | tf_op jit(solution)/shard_map/ppermute | solution.py:449
  11.8 5.5 %collective-permute-start = (bf16[16,162]{1,0:T(8,128)(2,1)S(1)}, bf16[16,162]{1,0:T(8,128)(2,1)S(1)}, u32[]{:S(2)}, u32[]{:S(2)}) collective-permute-start(bf16[16,162]{1,0:T(8,128)(2,1)S(1)} %copy-done.4), channel_id=1, source_target_pairs={{0,1},{1,2},{2,3},{3,0},{4,5},{5,6},{6,7},{7,4},{8,9},{9,10},{10,1... | collective-permute-start | bytes 15560 | tf_op jit(solution)/shard_map/ppermute | solution.py:400
  14.2 3.1 %collective-permute-start.1 = (bf16[16,162]{1,0:T(8,128)(2,1)S(1)}, bf16[16,162]{1,0:T(8,128)(2,1)S(1)}, u32[]{:S(2)}, u32[]{:S(2)}) collective-permute-start(bf16[16,162]{1,0:T(8,128)(2,1)S(1)} %copy-done.4), channel_id=1, source_target_pairs={{1,0},{2,1},{3,2},{0,3},{5,4},{6,5},{7,6},{4,7},{9,8},{10,9},{11,1... | collective-permute-start | bytes 15560 | tf_op jit(solution)/shard_map/ppermute | solution.py:401
  18.2 2.2 %collective-permute-start.2 = (f32[8,162]{1,0:T(8,128)S(1)}, f32[8,162]{1,0:T(8,128)S(1)}, u32[]{:S(2)}, u32[]{:S(2)}) collective-permute-start(f32[8,162]{1,0:T(8,128)S(1)} %slice_bitcast_fusion), channel_id=1, source_target_pairs={{0,4},{4,0},{8,12},{12,8},{16,20},{20,16},{24,28},{28,24},{1,5},{5... | collective-permute-start | bytes 15560 | tf_op jit(solution)/shard_map/ppermute | solution.py:438
  20.7 2.4 %collective-permute-start.3 = (f32[8,162]{1,0:T(8,128)S(1)}, f32[8,162]{1,0:T(8,128)S(1)}, u32[]{:S(2)}, u32[]{:S(2)}) collective-permute-start(f32[8,162]{1,0:T(8,128)S(1)} %shard_map.105.local_ref), channel_id=1, source_target_pairs={{0,4},{4,12},{8,0},{12,8},{16,20},{20,16},{24,28},{28,24},{1,5},{5... | collective-permute-start | bytes 15560 | tf_op jit(solution)/shard_map/ppermute | solution.py:472
  23.2 2.1 %collective-permute-start.5 = (f32[8,162]{1,0:T(8,128)S(1)}, f32[8,162]{1,0:T(8,128)S(1)}, u32[]{:S(2)}, u32[]{:S(2)}) collective-permute-start(f32[8,162]{1,0:T(8,128)S(1)} %shard_map.107), channel_id=1, source_target_pairs={{0,4},{4,0},{8,12},{12,20},{16,8},{20,16},{24,28},{28,24},{1,5},{5... | collective-permute-start | bytes 15560 | tf_op jit(solution)/shard_map/ppermute | solution.py:472
  25.3 1.2 %collective-permute-start.7 = (f32[2,8,162]{2,1,0:T(8,128)S(1)}, f32[2,8,162]{2,1,0:T(8,128)S(1)}, u32[]{:S(2)}, u32[]{:S(2)}) collective-permute-start(f32[2,8,162]{2,1,0:T(8,128)S(1)} %shard_map.110.entered_ref), channel_id=1, source_target_pairs={{0,4},{4,0},{8,12},{12,8},{16,20},{20,16},{24,28},{28,24},{1,5},{5... | collective-permute-start | bytes 31112 | tf_op jit(solution)/shard_map/ppermute | solution.py:473
  25.6 2.1 %collective-permute-start.6 = (f32[8,162]{1,0:T(8,128)S(1)}, f32[8,162]{1,0:T(8,128)S(1)}, u32[]{:S(2)}, u32[]{:S(2)}) collective-permute-start(f32[8,162]{1,0:T(8,128)S(1)} %shard_map.108), channel_id=1, source_target_pairs={{0,4},{4,0},{8,12},{12,8},{16,20},{20,24},{24,28},{28,16},{1,5},{5... | collective-permute-start | bytes 15560 | tf_op jit(solution)/shard_map/ppermute | solution.py:472
  27.6 1.2 %collective-permute-start.10 = (f32[8,162]{1,0:T(8,128)S(1)}, f32[8,162]{1,0:T(8,128)S(1)}, u32[]{:S(2)}, u32[]{:S(2)}) collective-permute-start(f32[8,162]{1,0:T(8,128)S(1)} %get-tuple-element.28.first_ref), channel_id=1, source_target_pairs={{0,4},{4,0},{8,12},{12,8},{16,20},{20,16},{24,28},{28,24},{1,5},{5... | collective-permute-start | bytes 15560 | tf_op jit(solution)/shard_map/ppermute | solution.py:490
  27.8 1.3 %collective-permute-start.9 = (f32[8,162]{1,0:T(8,128)S(1)}, f32[8,162]{1,0:T(8,128)S(1)}, u32[]{:S(2)}, u32[]{:S(2)}) collective-permute-start(f32[8,162]{1,0:T(8,128)S(1)} %get-tuple-element.26), channel_id=1, source_target_pairs={{0,4},{4,0},{8,12},{12,8},{16,20},{20,28},{24,16},{28,24},{1,5},{5... | collective-permute-start | bytes 15560 | tf_op jit(solution)/shard_map/ppermute | solution.py:489
  29.0 1.2 %collective-permute-start.11 = (f32[8,162]{1,0:T(8,128)S(1)}, f32[8,162]{1,0:T(8,128)S(1)}, u32[]{:S(2)}, u32[]{:S(2)}) collective-permute-start(f32[8,162]{1,0:T(8,128)S(1)} %shard_map.115), channel_id=1, source_target_pairs={{0,4},{4,0},{8,12},{12,20},{16,8},{20,16},{24,28},{28,24},{1,5},{5... | collective-permute-start | bytes 15560 | tf_op jit(solution)/shard_map/ppermute | solution.py:494
  30.3 4.0 %collective-permute-start.12 = (f32[8,162]{1,0:T(8,128)S(1)}, f32[8,162]{1,0:T(8,128)S(1)}, u32[]{:S(2)}, u32[]{:S(2)}) collective-permute-start(f32[8,162]{1,0:T(8,128)S(1)} %shard_map.116), channel_id=1, source_target_pairs={{0,4},{4,12},{8,0},{12,8},{16,20},{20,16},{24,28},{28,24},{1,5},{5... | collective-permute-start | bytes 15560 | tf_op jit(solution)/shard_map/ppermute | solution.py:494
  34.3 6.8 %collective-permute-start.13 = (f32[2,8,162]{2,1,0:T(8,128)S(1)}, f32[2,8,162]{2,1,0:T(8,128)S(1)}, u32[]{:S(2)}, u32[]{:S(2)}) collective-permute-start(f32[2,8,162]{2,1,0:T(8,128)S(1)} %shard_map.117.leave_ref), channel_id=1, source_target_pairs={{0,4},{4,0},{8,12},{12,8},{16,20},{20,16},{24,28},{28,24},{1,5},{5... | collective-permute-start | bytes 31112 | tf_op jit(solution)/shard_map/ppermute | solution.py:501

commit v4 on v3

v4 whole, which is shorter than its diff:
```python
import functools

import jax
import jax.numpy as jnp
from jax import lax
from jax.experimental import pallas as pl
from jax.experimental.pallas import tpu as pltpu
from jax.sharding import PartitionSpec as P

F32 = jnp.float32
BF16 = jnp.bfloat16
TILE = 8
LANES = 128
VMEM = pl.BlockSpec(memory_space=pltpu.VMEM)
ANY = pl.BlockSpec(memory_space=pl.ANY)
SMEM = pl.BlockSpec(memory_space=pltpu.SMEM)


def split2(x):
    high = x.astype(BF16)
    return high, (x - high.astype(F32)).astype(BF16)


def product(x, y):
    dot = functools.partial(jnp.dot, preferred_element_type=F32)
    return dot(x[0], y[0]) + (dot(x[0], y[1]) + dot(x[1], y[0]))


def room_of(width):
    rows = -(-width // (2 * TILE)) * 2 * TILE
    main = width // LANES * LANES
    return rows, 2 * main + (LANES if width - main <= LANES // 2 else 2 * LANES), main


def pair_at(ref, width, *at):
    if len(ref.shape) > 2:
        return [ref[(*at, i)] for i in range(2)]
    rows, columns, main = room_of(width)
    here = pl.ds(at[0] * rows, width)
    step = (columns - 2 * main) // 2
    if width == main:
        return [ref[here, i * main : (i + 1) * main] for i in range(2)]
    return [
        jnp.concatenate(
            [
                ref[here, i * main : (i + 1) * main],
                ref[here, 2 * main + i * step : 2 * main + i * step + width - main],
            ],
            axis=1,
        )
        for i in range(2)
    ]


def store_pair(ref, pair, *at):
    if len(ref.shape) > 2:
        for i in range(2):
            ref[(*at, i)] = pair[i]
        return
    width = pair[0].shape[0]
    rows, columns, main = room_of(width)
    here = pl.ds(at[0] * rows, width)
    step = (columns - 2 * main) // 2
    for i in range(2):
        ref[here, i * main : (i + 1) * main] = pair[i][:, :main]
        if width > main:
            ref[here, 2 * main + i * step : 2 * main + i * step + width - main] = pair[i][:, main:]


def apply_pairs(vector, ref, *at):
    count = vector.shape[0]
    rows = lax.broadcasted_iota(jnp.int32, vector.shape, 0)
    both = jnp.concatenate(split2(vector), axis=0)
    total = jnp.zeros(vector.shape, F32)
    for l in range(count):
        part, here = ref, l
        if isinstance(ref, (list, tuple)):
            each = count // len(ref)
            part, here = ref[l // each], l % each
        high, low = pair_at(part, vector.shape[1], *at, here)
        first = jnp.dot(both, high, preferred_element_type=F32)
        second = jnp.dot(both, low, preferred_element_type=F32)
        total = jnp.where(rows == l, first[:count] + first[count:] + second[:count], total)
    return total


def apply_rows(vector, ref, *at):
    count = vector.shape[0]
    rows = lax.broadcasted_iota(jnp.int32, vector.shape, 0)
    both = jnp.concatenate(split2(vector), axis=0)
    total = jnp.zeros(vector.shape, F32)
    for l in range(count):
        first = lax.dot_general(
            both, ref[(*at, l)], (((1,), (1,)), ((), ())), preferred_element_type=F32
        )
        total = jnp.where(rows == l, first[:count] + first[count:], total)
    return total


def core_of():
    return lax.rem(lax.axis_index("wall"), 2)


def chip_of():
    return lax.div(lax.axis_index("wall"), 2)


def pair_kernel(raw_ref, *refs, first_chip, **options):
    @pl.when(chip_of() >= first_chip)
    def _():
        make_pairs(raw_ref, *refs[-3:], **options)


def make_pairs(raw_ref, step_ref, whole_ref, sent_ref, *, kind, lines, ascending):
    count = raw_ref.shape[1]
    for l in range(*lines):
        steps = []
        for e in range(count):
            block = lax.dot_general(
                raw_ref[kind, e, l], raw_ref[0, e, l], (((0,), (1,)), ((), ())), preferred_element_type=F32
            )
            steps.append(split2(block))
            store_pair(step_ref, steps[-1], e, l)
        if not ascending:
            steps = steps[::-1]
        whole = steps[0]
        for step in steps[1:]:
            whole = split2(product(whole, step))
        if count % 2:
            whole = [-x for x in whole]
        store_pair(whole_ref, whole, l - lines[0])
        store_pair(sent_ref, whole, l - lines[0])


def chip_kernel(*refs, parts, width, own_first):
    got_refs, own_refs, chip_ref = refs[:parts], refs[parts:-1], refs[-1]

    @pl.when(core_of() == 1)
    def _():
        each = chip_ref.shape[0] // parts
        for l in range(chip_ref.shape[0]):
            pairs = [pair_at(x[l // each], width, l % each) for x in (got_refs, own_refs)]
            store_pair(chip_ref, split2(product(*(pairs[::-1] if own_first else pairs))), l)


def relayout_kernel(*refs, kinds):
    raw_ref, landed, arrived = refs[-3:]
    _, depth, lines = raw_ref.shape[:3]
    copies = [
        pltpu.make_async_copy(ref.at[e], landed.at[a, e], arrived.at[a, e])
        for a, ref in enumerate(refs[:kinds])
        for e in range(depth)
    ]
    for copy in copies:
        copy.start()
    for i, copy in enumerate(copies):
        copy.wait()
        a, e = divmod(i, depth)
        turned = jnp.swapaxes(landed[a, e], 0, 1)
        for l in range(lines):
            raw_ref[a, e, l] = turned[l]


def prepare_kernel(*refs):
    places, (weight_ref, rhs_ref, act_ref, state_ref, lift_ref) = refs[:7], refs[7:12]
    slot_ref, len_ref, coef_ref, nb_ref, source_ref, arrived = refs[12:]
    targets = (slot_ref, len_ref, coef_ref, nb_ref, source_ref, state_ref, lift_ref)
    copies = [
        pltpu.make_async_copy(there, here, arrived.at[i]) for i, (there, here) in enumerate(zip(places, targets))
    ]
    for copy in copies:
        copy.start()
    for copy in copies:
        copy.wait()
    faces, slots = coef_ref.shape
    depth, lines = slot_ref.shape
    cells = 3 * slots
    k = lax.broadcasted_iota(jnp.int32, (cells, slots), 0)
    e = lax.broadcasted_iota(jnp.int32, (cells, slots), 1)
    weight = jnp.zeros((cells, slots), F32)
    own = jnp.zeros((1, slots), F32)
    for f in range(faces):
        coef = coef_ref[f : f + 1, :]
        own = own + coef
        weight = weight - jnp.where(k == nb_ref[f : f + 1, :], coef, 0.0)
    weight = weight + jnp.where(k == e + slots, own, 0.0)
    count = depth * lines
    rows = lax.broadcasted_iota(jnp.int32, (count, slots), 0)
    slot = jnp.zeros((count, slots), jnp.int32)
    for g in range(depth):
        for l in range(lines):
            slot = jnp.where(rows == g * lines + l, slot_ref[g, l], slot)
    chosen = (slot == lax.broadcasted_iota(jnp.int32, (count, slots), 1)).astype(F32).astype(BF16)
    high = weight.astype(BF16)
    mid, low = split2(weight - high.astype(F32))
    for i, part in enumerate((high, mid, low)):
        weight_ref[i * count : (i + 1) * count, :] = lax.dot_general(
            chosen, part, (((1,), (1,)), ((), ())), preferred_element_type=F32
        ).astype(BF16)
    rhs_ref[...] = jnp.dot(chosen, source_ref[...], preferred_element_type=F32)
    rows = lax.broadcasted_iota(jnp.int32, act_ref.shape[1:], 0)
    length = jnp.zeros(act_ref.shape[1:], jnp.int32)
    for l in range(lines):
        length = jnp.where(rows == l, len_ref[l], length)
    place = lax.axis_index("wall") * depth
    for g in range(depth):
        act_ref[g] = (place + g < length).astype(F32)


def residual_kernel(before, state, after, weight, source, lift, rhs_ref):
    cells = jnp.concatenate([before[...], state[...], after[...]], axis=0)
    parts = jnp.dot(weight[...], cells, preferred_element_type=F32)
    count = source.shape[0]
    face_sum = parts[:count] + (parts[count : 2 * count] + parts[2 * count :])
    flux = jnp.dot(face_sum.astype(BF16), lift[...], preferred_element_type=F32)
    rhs = source[...] - flux
    depth, lines, _ = rhs_ref.shape
    for g in range(depth):
        rhs_ref[g] = rhs[g * lines : (g + 1) * lines]


def forward_local(scaled, q_ref, act_ref, carried):
    values = []
    for g, value in enumerate(scaled):
        if carried is not None:
            value = value - apply_pairs(carried, q_ref, g)
        carried = act_ref[g] * value
        values.append(carried)
    return values


def backward_local(values, s_ref, act_ref, carried):
    solved = [None] * len(values)
    for g in range(len(values) - 1, -1, -1):
        value = values[g]
        if carried is not None:
            value = value - apply_pairs(carried, s_ref, g)
        carried = act_ref[g] * value
        solved[g] = carried
    return solved


def local_kernel(rhs_ref, raw_ref, act_ref, scaled_ref, y_ref, leave_ref):
    depth = rhs_ref.shape[0]
    scaled = [apply_rows(rhs_ref[g], raw_ref, 0, g) for g in range(depth)]
    values = raw_steps(scaled, raw_ref, act_ref, None)
    for g in range(depth):
        scaled_ref[g] = scaled[g]
        y_ref[g] = values[g]
    leave_ref[...] = values[-1]


def raw_steps(scaled, raw_ref, act_ref, carried):
    values = []
    for g, value in enumerate(scaled):
        if carried is not None:
            value = value - apply_rows(apply_rows(carried, raw_ref, 1, g), raw_ref, 0, g)
        carried = act_ref[g] * value
        values.append(carried)
    return values


def wall_kernel(came_ref, scaled_ref, raw_ref, act_ref, y_ref, out_ref, leave_ref):
    depth = y_ref.shape[0]
    out_ref[...] = y_ref[...]
    leave_ref[...] = y_ref[depth - 1]

    @pl.when(lax.axis_index("wall") == 1)
    def _():
        values = raw_steps([scaled_ref[g] for g in range(depth)], raw_ref, act_ref, came_ref[...])
        for g in range(depth):
            out_ref[g] = values[g]
        leave_ref[...] = values[-1]


def chip_local_kernel(came_ref, act_ref, y_ref, *refs):
    own_refs, out_ref = refs[:-1], refs[-1]
    depth = y_ref.shape[0]
    out_ref[...] = y_ref[depth - 1]

    @pl.when(jnp.logical_and(core_of() == 1, chip_of() > 0))
    def _():
        out_ref[...] = act_ref[depth - 1] * apply_pairs(came_ref[...], own_refs) + y_ref[depth - 1]


def hop_kernel(came_ref, act_ref, local_ref, *refs, chip):
    pair_refs, out_ref = refs[:-1], refs[-1]
    out_ref[...] = local_ref[...]

    @pl.when(jnp.logical_and(chip_of() == chip, core_of() == 1))
    def _():
        gone = apply_pairs(came_ref[...], pair_refs)
        out_ref[...] = act_ref[act_ref.shape[0] - 1] * gone + local_ref[...]


def early_hop_kernel(came_ref, act_ref, mate_ref, y_ref, *refs, chip, parts):
    got_refs, own_refs, out_ref = refs[:parts], refs[parts : 2 * parts], refs[-1]
    depth = y_ref.shape[0]
    out_ref[...] = came_ref[...]

    @pl.when(jnp.logical_and(chip_of() == chip, core_of() == 1))
    def _():
        middle = apply_pairs(came_ref[...], got_refs) + mate_ref[...]
        out_ref[...] = act_ref[depth - 1] * apply_pairs(middle, own_refs) + y_ref[depth - 1]


def chosen_arrival(refs, chips, like):
    here = chip_of()
    value = jnp.zeros(like, F32)
    for ref, chip in zip(refs, chips):
        value = jnp.where(here == chip, ref[...], value)
    return value


def choose_kernel(*refs, chips):
    refs[-1][...] = chosen_arrival(refs[:-1], chips, refs[-1].shape)


def inner_kernel(
    direct_ref, met_ref, came_ref, scaled_ref, q_ref, s_ref, act_ref, wall_ref, *refs, on_last, last, parts
):
    got_refs = refs[:parts]
    y_ref, first_ref, flow = refs[-3:]
    depth = scaled_ref.shape[0]
    here = chip_of()

    @pl.when(here == last if on_last else jnp.logical_and(here > 0, here != last))
    def _():
        flow[...] = met_ref[...]

        @pl.when(core_of() == 1)
        def _():
            flow[...] = apply_pairs(direct_ref[...], got_refs) + came_ref[...]

        values = forward_local([scaled_ref[g] for g in range(depth)], q_ref, act_ref, flow[...])
        for g in range(depth):
            y_ref[g] = values[g]

    if not on_last:

        @pl.when(here == 0)
        def _():
            y_ref[...] = wall_ref[...]

    @pl.when(here == last if on_last else here != last)
    def _():
        first_ref[...] = backward_local([y_ref[g] for g in range(depth)], s_ref, act_ref, None)[0]


def reach_kernel(first_ref, got_ref, out_ref):
    @pl.when(core_of() == 1)
    def _():
        out_ref[...] = apply_pairs(first_ref[...], got_ref)


def add_kernel(x_ref, y_ref, out_ref):
    out_ref[...] = x_ref[...] + y_ref[...]


def leave_kernel(own_ref, first_ref, *refs, chips):
    came_ref, out_ref = refs[-2:]
    came_ref[...] = chosen_arrival(refs[:-2], chips, came_ref.shape)
    out_ref[...] = first_ref[...]

    @pl.when(core_of() == 1)
    def _():
        out_ref[...] = apply_pairs(came_ref[...], own_ref) + first_ref[...]


def last_kernel(beyond_ref, met_ref, s_ref, act_ref, y_ref, out_ref):
    depth = y_ref.shape[0]
    carried = jnp.where(core_of() == 0, met_ref[...], beyond_ref[...])
    solved = backward_local([y_ref[g] for g in range(depth)], s_ref, act_ref, carried)
    for g in range(depth):
        out_ref[g] = solved[g]


def padded_bytes(shape, dtype):
    size = jnp.dtype(dtype).itemsize
    shape = (1,) * (2 - len(shape)) + tuple(shape)
    total = -(-shape[-2] // 16) * 16 * -(-shape[-1] // 128) * 128 * size
    for extent in shape[:-2]:
        total *= extent
    return total


def run(kernel, operands, outs, blocks=1, scratch=(), aliases=None):
    held = [(x.shape, x.dtype) for x, _ in operands] + [(s, t) for s, t, _ in outs]
    limit = sum(padded_bytes(s, t) for s, t in held)
    if blocks == 1:
        in_specs = [at if isinstance(at, pl.BlockSpec) else VMEM for _, at in operands]
        out_specs = [VMEM for _ in outs]
        grid = ()
    else:

        def spec(shape, at):
            if isinstance(at, pl.BlockSpec):
                return at
            if at is None:
                return pl.BlockSpec(shape, lambda i: (0,) * len(shape))
            size = tuple(n // blocks if axis == at else n for axis, n in enumerate(shape))
            return pl.BlockSpec(size, lambda i: tuple(i if axis == at else 0 for axis in range(len(shape))))

        in_specs = [spec(x.shape, at) for x, at in operands]
        out_specs = [spec(s, at) for s, _, at in outs]
        grid = (blocks,)
        limit = 2 * limit // blocks
    limit += sum(padded_bytes(s.shape, s.dtype) for s in scratch if s.memory_space == pltpu.VMEM)
    limit = min(limit + (2 << 20), 60 << 20)
    return pl.pallas_call(
        kernel,
        grid=grid,
        in_specs=in_specs,
        out_specs=out_specs,
        out_shape=[jax.ShapeDtypeStruct(s, t) for s, t, _ in outs],
        scratch_shapes=list(scratch),
        input_output_aliases=aliases or {},
        compiler_params=pltpu.CompilerParams(vmem_limit_bytes=limit),
        cost_estimate=pl.CostEstimate(flops=1, bytes_accessed=1, transcendentals=0),
    )(*[x for x, _ in operands])


def hop_pairs(count, start, end, core=1):
    start, end = 2 * start + 1, 2 * end + core
    target = {i: i ^ 1 for i in range(count)}
    target.update({start: end, end: end ^ 1, end ^ 1: start ^ 1, start ^ 1: start})
    return sorted(target.items())


def in_hbm(value):
    return pltpu.with_memory_space_constraint(value, pltpu.HBM)


def after(value, *others):
    return lax.optimization_barrier((value, *others))[0]


def per_device(state, source, face_coef, neighbour, lift, elem_slot, line_len, dinv, lower, upper):
    wall_count = lax.axis_size("wall")
    surf_count = lax.axis_size("surf")
    last = wall_count // 2 - 1
    depth, lines, width, _ = dinv.shape
    slots = state.shape[0]
    block = TILE if lines % TILE == 0 else lines
    blocks = lines // block
    parts = 2 if blocks == 1 and lines % 2 == 0 else 1
    room, columns, _ = room_of(width)
    line_vector = ((lines, width), F32, 0)
    element_vectors = ((depth, lines, width), F32, 1)
    line_sent = ((lines * room, columns), BF16, 0)
    line_pairs = ((lines, 2, width, width), BF16, 0)
    part_sent = ((lines // parts * room, columns), BF16, 0)
    part_pairs = ((lines // parts, 2, width, width), BF16, 0)
    element_pairs = ((depth, lines, 2, width, width), BF16, 1)

    def mates(value):
        return lax.ppermute(value, "wall", [(i, i ^ 1) for i in range(wall_count)])

    count = depth * lines
    rows = lax.broadcasted_iota(jnp.int32, (count, slots), 0)
    slot = jnp.zeros((count, slots), jnp.int32)
    for g in range(depth):
        for l in range(lines):
            slot = jnp.where(rows == g * lines + l, slot_ref[g, l], slot)
    chosen = (slot == lax.broadcasted_iota(jnp.int32, (count, slots), 1)).astype(F32).astype(BF16)
    high = weight.astype(BF16)
    mid, low = split2(weight - high.astype(F32))
    for i, part in enumerate((high, mid, low)):
        weight_ref[i * count : (i + 1) * count, :] = lax.dot_general(
            chosen, part, (((1,), (1,)), ((), ())), preferred_element_type=F32
        ).astype(BF16)
    rhs_ref[...] = jnp.dot(chosen, source_ref[...], preferred_element_type=F32)
    rows = lax.broadcasted_iota(jnp.int32, act_ref.shape[1:], 0)
    length = jnp.zeros(act_ref.shape[1:], jnp.int32)
    for l in range(lines):
        length = jnp.where(rows == l, len_ref[l], length)
    place = lax.axis_index("wall") * depth
    for g in range(depth):
        act_ref[g] = (place + g < length).astype(F32)


def residual_kernel(before, state, after, weight, source, lift, rhs_ref):
    cells = jnp.concatenate([before[...], state[...], after[...]], axis=0)
    parts = jnp.dot(weight[...], cells, preferred_element_type=F32)
    count = source.shape[0]
    face_sum = parts[:count] + (parts[count : 2 * count] + parts[2 * count :])
    flux = jnp.dot(face_sum.astype(BF16), lift[...], preferred_element_type=F32)
    rhs = source[...] - flux
    depth, lines, _ = rhs_ref.shape
    for g in range(depth):
        rhs_ref[g] = rhs[g * lines : (g + 1) * lines]


def forward_local(scaled, q_ref, act_ref, carried):
    values = []
    for g, value in enumerate(scaled):
        if carried is not None:
            value = value - apply_pairs(carried, q_ref, g)
        carried = act_ref[g] * value
        values.append(carried)
    return values


def backward_local(values, s_ref, act_ref, carried):
    solved = [None] * len(values)
    for g in range(len(values) - 1, -1, -1):
        value = values[g]
        if carried is not None:
            value = value - apply_pairs(carried, s_ref, g)
        carried = act_ref[g] * value
        solved[g] = carried
    return solved


def local_kernel(rhs_ref, raw_ref, act_ref, scaled_ref, y_ref, leave_ref):
    depth = rhs_ref.shape[0]
    scaled = [apply_rows(rhs_ref[g], raw_ref, 0, g) for g in range(depth)]
    values = raw_steps(scaled, raw_ref, act_ref, None)
    for g in range(depth):
        scaled_ref[g] = scaled[g]
        y_ref[g] = values[g]
    leave_ref[...] = values[-1]


def raw_steps(scaled, raw_ref, act_ref, carried):
    values = []
    for g, value in enumerate(scaled):
        if carried is not None:
            value = value - apply_rows(apply_rows(carried, raw_ref, 1, g), raw_ref, 0, g)
        carried = act_ref[g] * value
        values.append(carried)
    return values


def wall_kernel(came_ref, scaled_ref, raw_ref, act_ref, y_ref, out_ref, leave_ref):
    depth = y_ref.shape[0]
    out_ref[...] = y_ref[...]
    leave_ref[...] = y_ref[depth - 1]

    @pl.when(lax.axis_index("wall") == 1)
    def _():
        values = raw_steps([scaled_ref[g] for g in range(depth)], raw_ref, act_ref, came_ref[...])
        for g in range(depth):
            out_ref[g] = values[g]
        leave_ref[...] = values[-1]


def chip_local_kernel(came_ref, act_ref, y_ref, *refs):
    own_refs, out_ref = refs[:-1], refs[-1]
    depth = y_ref.shape[0]
    out_ref[...] = y_ref[depth - 1]

    @pl.when(jnp.logical_and(core_of() == 1, chip_of() > 0))
    def _():
        out_ref[...] = act_ref[depth - 1] * apply_pairs(came_ref[...], own_refs) + y_ref[depth - 1]


def hop_kernel(came_ref, act_ref, local_ref, *refs, chip):
    pair_refs, out_ref = refs[:-1], refs[-1]
    out_ref[...] = local_ref[...]

    @pl.when(jnp.logical_and(chip_of() == chip, core_of() == 1))
    def _():
        gone = apply_pairs(came_ref[...], pair_refs)
        out_ref[...] = act_ref[act_ref.shape[0] - 1] * gone + local_ref[...]


def chosen_arrival(refs, chips, like):
    here = chip_of()
    value = jnp.zeros(like, F32)
    for ref, chip in zip(refs, chips):
        value = jnp.where(here == chip, ref[...], value)
    return value


def choose_kernel(*refs, chips):
    refs[-1][...] = chosen_arrival(refs[:-1], chips, refs[-1].shape)


def inner_kernel(
    direct_ref, met_ref, came_ref, scaled_ref, q_ref, s_ref, act_ref, wall_ref, *refs, on_last, last, parts
):
    got_refs = refs[:parts]
    y_ref, first_ref, flow = refs[-3:]
    depth = scaled_ref.shape[0]
    here = chip_of()

    @pl.when(here == last if on_last else jnp.logical_and(here > 0, here != last))
    def _():
        flow[...] = met_ref[...]

        @pl.when(core_of() == 1)
        def _():
            flow[...] = apply_pairs(direct_ref[...], got_refs) + came_ref[...]

        values = forward_local([scaled_ref[g] for g in range(depth)], q_ref, act_ref, flow[...])
        for g in range(depth):
            y_ref[g] = values[g]

    if not on_last:

        @pl.when(here == 0)
        def _():
            y_ref[...] = wall_ref[...]

    @pl.when(here == last if on_last else here != last)
    def _():
        first_ref[...] = backward_local([y_ref[g] for g in range(depth)], s_ref, act_ref, None)[0]


def reach_kernel(first_ref, got_ref, out_ref):
    @pl.when(core_of() == 1)
    def _():
        out_ref[...] = apply_pairs(first_ref[...], got_ref)


def add_kernel(x_ref, y_ref, out_ref):
    out_ref[...] = x_ref[...] + y_ref[...]


def leave_kernel(own_ref, first_ref, *refs, chips):
    came_ref, out_ref = refs[-2:]
    came_ref[...] = chosen_arrival(refs[:-2], chips, came_ref.shape)
    out_ref[...] = first_ref[...]

    @pl.when(core_of() == 1)
    def _():
        out_ref[...] = apply_pairs(came_ref[...], own_ref) + first_ref[...]


def last_kernel(beyond_ref, met_ref, s_ref, act_ref, y_ref, out_ref):
    depth = y_ref.shape[0]
    carried = jnp.where(core_of() == 0, met_ref[...], beyond_ref[...])
    solved = backward_local([y_ref[g] for g in range(depth)], s_ref, act_ref, carried)
    for g in range(depth):
        out_ref[g] = solved[g]


def padded_bytes(shape, dtype):
    size = jnp.dtype(dtype).itemsize
    shape = (1,) * (2 - len(shape)) + tuple(shape)
    total = -(-shape[-2] // 16) * 16 * -(-shape[-1] // 128) * 128 * size
    for extent in shape[:-2]:
        total *= extent
    return total


def run(kernel, operands, outs, blocks=1, scratch=(), aliases=None):
    held = [(x.shape, x.dtype) for x, _ in operands] + [(s, t) for s, t, _ in outs]
    limit = sum(padded_bytes(s, t) for s, t in held)
    if blocks == 1:
        in_specs = [at if isinstance(at, pl.BlockSpec) else VMEM for _, at in operands]
        out_specs = [VMEM for _ in outs]
        grid = ()
    else:

        def spec(shape, at):
            if isinstance(at, pl.BlockSpec):
                return at
            if at is None:
                return pl.BlockSpec(shape, lambda i: (0,) * len(shape))
            size = tuple(n // blocks if axis == at else n for axis, n in enumerate(shape))
            return pl.BlockSpec(size, lambda i: tuple(i if axis == at else 0 for axis in range(len(shape))))

        in_specs = [spec(x.shape, at) for x, at in operands]
        out_specs = [spec(s, at) for s, _, at in outs]
        grid = (blocks,)
        limit = 2 * limit // blocks
    limit += sum(padded_bytes(s.shape, s.dtype) for s in scratch if s.memory_space == pltpu.VMEM)
    limit = min(limit + (2 << 20), 60 << 20)
    return pl.pallas_call(
        kernel,
        grid=grid,
        in_specs=in_specs,
        out_specs=out_specs,
        out_shape=[jax.ShapeDtypeStruct(s, t) for s, t, _ in outs],
        scratch_shapes=list(scratch),
        input_output_aliases=aliases or {},
        compiler_params=pltpu.CompilerParams(vmem_limit_bytes=limit),
        cost_estimate=pl.CostEstimate(flops=1, bytes_accessed=1, transcendentals=0),
    )(*[x for x, _ in operands])


def hop_pairs(count, start, end, core=1):
    start, end = 2 * start + 1, 2 * end + core
    target = {i: i ^ 1 for i in range(count)}
    target.update({start: end, end: end ^ 1, end ^ 1: start ^ 1, start ^ 1: start})
    return sorted(target.items())


def in_hbm(value):
    return pltpu.with_memory_space_constraint(value, pltpu.HBM)


def after(value, *others):
    return lax.optimization_barrier((value, *others))[0]


def per_device(state, source, face_coef, neighbour, lift, elem_slot, line_len, dinv, lower, upper):
    wall_count = lax.axis_size("wall")
    surf_count = lax.axis_size("surf")
    last = wall_count // 2 - 1
    depth, lines, width, _ = dinv.shape
    slots = state.shape[0]
    block = TILE if lines % TILE == 0 else lines
    blocks = lines // block
    parts = 2 if blocks == 1 and lines % 2 == 0 else 1
    room, columns, _ = room_of(width)
    line_vector = ((lines, width), F32, 0)
    element_vectors = ((depth, lines, width), F32, 1)
    line_sent = ((lines * room, columns), BF16, 0)
    line_pairs = ((lines, 2, width, width), BF16, 0)
    part_sent = ((lines // parts * room, columns), BF16, 0)
    part_pairs = ((lines // parts, 2, width, width), BF16, 0)
    element_pairs = ((depth, lines, 2, width, width), BF16, 1)

    def mates(value):
        return lax.ppermute(value, "wall", [(i, i ^ 1) for i in range(wall_count)])

    def relaid(arrays, *others):
        if lines != TILE:
            return jnp.stack(arrays)
        shape = (len(arrays), depth, lines, width, width)
        return run(
            functools.partial(relayout_kernel, kinds=len(arrays)),
            [(in_hbm(jnp.transpose(x, (0, 2, 1, 3))), ANY) for x in arrays] + [(x, None) for x in others],
            [(shape, BF16, None)],
            scratch=[
                pltpu.VMEM((len(arrays), depth, width, lines, width), BF16),
                pltpu.SemaphoreType.DMA((len(arrays), depth)),
            ],
        )[0]

    count = depth * lines
    small = (elem_slot, line_len, face_coef.T, neighbour.T, source)
    weight, line_source, act, near_state, near_lift = run(
        prepare_kernel,
        [(in_hbm(x), ANY) for x in (*small, state, lift)],
        [
            ((3 * count, 3 * slots), BF16, None),
            ((count, width), F32, None),
            element_vectors,
            (state.shape, BF16, None),
            (lift.shape, BF16, None),
        ],
        scratch=[(pltpu.SMEM if i < 2 else pltpu.VMEM)(x.shape, x.dtype) for i, x in enumerate(small)]
        + [pltpu.SemaphoreType.DMA((len(small) + 2,))],
    )
    before = lax.ppermute(state, "surf", [(i, (i + 1) % surf_count) for i in range(surf_count)])
    beyond = lax.ppermute(state, "surf", [((i + 1) % surf_count, i) for i in range(surf_count)])
    (rhs,) = run(
        residual_kernel,
        [(x, None) for x in (before, near_state, beyond, weight, line_source, near_lift)],
        [element_vectors],
    )
    blocks_in = (dinv, lower, upper)
    if lines == TILE:
        (raw,) = run(
            functools.partial(relayout_kernel, kinds=3),
            [(in_hbm(jnp.transpose(x, (0, 2, 1, 3))), ANY) for x in blocks_in]
            + [(x, None) for x in (before, beyond, weight)],
            [((3, depth, lines, width, width), BF16, None)],
            scratch=[
                pltpu.VMEM((3, depth, width, lines, width), BF16),
                pltpu.SemaphoreType.DMA((3, depth)),
            ],
        )
    else:
        raw = jnp.stack(blocks_in)
    scaled, y_local, y_leave = run(
        local_kernel,
        [(rhs, 1), (raw, 2), (act, 1)],
        [element_vectors, element_vectors, line_vector],
        blocks,
    )
    came_y = mates(y_leave)
    wall_y, wall_leave = run(
        wall_kernel,
        [(came_y, 0), (scaled, 1), (raw, 2), (act, 1), (y_local, 1)],
        [element_vectors, line_vector],
        blocks,
    )
    arrivals = [lax.ppermute(wall_leave, "wall", hop_pairs(wall_count, 0, 1))]
    a, got_a, q = [], [], None
    for part in range(parts):
        each = block // parts
        q, whole, sent = run(
            functools.partial(
                pair_kernel, first_chip=1, kind=1, lines=(part * each, part * each + each), ascending=True
            ),
            [(after(raw, wall_leave if part else y_leave), 2)] + ([] if q is None else [(q, ANY)]),
            [element_pairs, part_pairs, part_sent],
            blocks,
            aliases={} if q is None else {1: 0},
        )
        a.append(whole)
        got_a.append(mates(after(sent, got_a[-1] if part else came_y)))
    s, c, sent_c = run(
        functools.partial(pair_kernel, first_chip=0, kind=2, lines=(0, block), ascending=False),
        [(after(raw, a[-1], wall_leave), 2)],
        [element_pairs, line_pairs, line_sent],
        blocks,
    )
    got_c = mates(after(sent_c, arrivals[0],got_a[-1]))

    def hop(came, pairs, local, at):
        (out,) = run(
            functools.partial(hop_kernel, chip=at),
            [(came, 0), (act, 1), (local, 0)] + [(x, 0) for x in pairs],
            [line_vector],
            blocks,
        )
        return out

    out = wall_leave
    for at in range(1, last):
        if at == 1:
            (out,) = run(
                functools.partial(early_hop_kernel, chip=at, parts=parts),
                [(arrivals[-1], 0), (act, 1), (came_y, 0), (y_local, 1)] + [(x, 0) for x in got_a + a],
                [line_vector],
                blocks,
            )
            (chip_a,) = run(
                functools.partial(chip_kernel, parts=parts, width=width, own_first=False),
                [(after(x, out) if i == 0 else x, 0) for i, x in enumerate(got_a + a)],
                [line_pairs],
                blocks,
            )
            (y_chip,) = run(
                chip_local_kernel,
                [(after(came_y, out), 0), (act, 1), (y_local, 1)] + [(x, 0) for x in a],
                [line_vector],
                blocks,
            )
        else:
            out = hop(arrivals[-1], [chip_a], y_chip, at)
        arrivals.append(lax.ppermute(out, "wall", hop_pairs(wall_count, at, at + 1)))
    direct = lax.ppermute(out, "wall", hop_pairs(wall_count, last - 1, last, 0))

    def inner(on_last, entered, met, held=()):
        return run(
            functools.partial(inner_kernel, on_last=on_last, last=last, parts=parts),
            [(entered, 0), (met, 0), (came_y, 0)]
            + [(x, 1) for x in (scaled, q, s, act, wall_y)]
            + [(x, 0) for x in got_a]
            + [(x, ANY) for x in held],
            [element_vectors, line_vector],
            blocks,
            [pltpu.VMEM((block, width), F32)],
            {8 + parts: 0, 9 + parts: 1} if held else {},
        )

    def chosen(arrived, chips):
        return run(
            functools.partial(choose_kernel, chips=chips), [(x, 0) for x in arrived], [line_vector], blocks
        )[0]

    chips = list(range(1, last))
    entered = chosen(arrivals[:-1], chips)
    held = inner(False, after(entered, out), mates(entered))
    y, first = inner(True, arrivals[-1], direct, held)
    came_first = mates(first)
    (reach,) = run(reach_kernel, [(first, 0), (got_c, 0)], [line_vector], blocks)
    (x_chip,) = run(add_kernel, [(reach, 0), (came_first, 0)], [line_vector], blocks)
    arrived = [lax.ppermute(x_chip, "wall", hop_pairs(wall_count, last, last - 1))]
    (chip_c,) = run(
        functools.partial(chip_kernel, parts=1, width=width, own_first=True),
        [(after(got_c, x_chip), 0), (c, 0)],
        [line_pairs],
        blocks,
    )
    for at in range(last - 1, 0, -1):
        out = hop(arrived[-1], [chip_c], x_chip, at)
        arrived.append(lax.ppermute(out, "wall", hop_pairs(wall_count, at, at - 1)))
    beyond, left = run(
        functools.partial(leave_kernel, chips=list(range(last - 1, -1, -1))),
        [(x, 0) for x in (c, first, *arrived)],
        [line_vector, line_vector],
        blocks,
    )
    met_left = mates(left)
    (solution,) = run(
        last_kernel, [(beyond, 0), (met_left, 0)] + [(x, 1) for x in (s, act, y)], [element_vectors], blocks
    )
    return solution


def solution(mesh):
    in_specs = (
        P(("wall", "surf"), None),
        P(("wall", "surf"), None),
        P(("wall", "surf"), None),
        P(("wall", "surf"), None),
        P(),
        P("wall", "surf"),
        P("surf"),
        P("wall", "surf", None, None),
        P("wall", "surf", None, None),
        P("wall", "surf", None, None),
    )
    out_specs = P("wall", "surf", None)
    return jax.shard_map(
        per_device, mesh=mesh, in_specs=in_specs, out_specs=out_specs, check_vma=False
    )
```

time: 42.7 us -> 36.7 us (0.86)
  starting transfers between devices: 19.7 us -> 11.1 us
  waiting for transfers between devices: 5.34 us -> 13.9 us
  local copies, waits for them, and re-layouts: 5.53 us -> 0 us
    ppermute x12 -> x14, waiting for transfers between devices: 5.05 us -> 13.8 us  [the longest x2 8.22 us: per_device(): arrived.append(lax.ppermute(out, 'wall', hop_pairs(wall_count, at, at - 1)))]
    ppermute x12 -> x14, starting transfers between devices: 15.2 us -> 6.97 us  [the longest x7 3.81 us: mates(): return lax.ppermute(value, 'wall', [(i, i ^ 1) for i in range(wall_count)])]
    unnamed x20 -> x0, local copies, waits for them, and re-layouts: 4.06 us -> none
    pallas_call x2 -> x0, local copies, waits for them, and re-layouts: 0.93 us -> none  [run(): pl.pallas_call(kernel, grid=grid, in_specs=in_specs, out_specs=out_specs,...]
    ppermute x2 -> x0, local copies, waits for them, and re-layouts: 0.54 us -> none  [the longest x1 0.27 us: per_device(): got = lax.ppermute(send, 'wall', flips)]
    pallas_call x20 -> x22, Pallas kernels: 11.5 us -> 11.3 us  [run(): pl.pallas_call(kernel, grid=grid, in_specs=in_specs, out_specs=out_specs,...]
  transfers between devices with their start and end apart: 14 -> 16, of which waited for: 9 -> 11; matrix products, arithmetic and copies ran while one was open for 2% -> 0% of each run, Pallas kernels for 11% -> 17%
where the time goes in v4:
time: 36.7 us; the launch traced here: 36.4 us
  waiting for transfers between devices  13.9 us (38%)
  Pallas kernels  11.3 us (31%)
  starting transfers between devices  11.1 us (30%)
    pallas_call x22, Pallas kernels, run(): pl.pallas_call(kernel, grid=grid, in_specs=in_specs, out_specs=out_specs,...  11.3 us
    ppermute x2, waiting for transfers between devices, per_device(): arrived.append(lax.ppermute(out, 'wall', hop_pairs(wall_count, at, at - 1)))  8.22 us
    ppermute x7, starting transfers between devices, mates(): return lax.ppermute(value, 'wall', [(i, i ^ 1) for i in range(wall_count)])  3.81 us
    ppermute x7, waiting for transfers between devices, mates(): return lax.ppermute(value, 'wall', [(i, i ^ 1) for i in range(wall_count)])  2.78 us
    ppermute x2, waiting for transfers between devices, per_device(): lax.ppermute(out, 'wall', hop_pairs(wall_count, at, at + 1))  2.4 us
    ppermute x1, starting transfers between devices, per_device(): lax.ppermute(state, 'surf', [(i, (i + 1) % surf_count) for i in range(sur...  2.13 us
    ppermute x1, starting transfers between devices, per_device(): lax.ppermute(state, 'surf', [((i + 1) % surf_count, i) for i in range(sur...  2.03 us
    ppermute x1, starting transfers between devices, per_device(): arrivals = [lax.ppermute(wall_leave, 'wall', hop_pairs(wall_count, 0, 1))]  1.5 us
  transfers between devices with their start and end apart: 16, of which 11 were waited for; matrix products, arithmetic and copies ran while one was open for 0% of the time, Pallas kernels for 17%

profile of v4, /device:TPU:1, one launch (start us, length us, event | category | flops | bytes accessed | tf_op | source)
XLA Modules:
  0.0 36.4 jit_solution(9023028277443087900)
XLA Ops:
  0.0 2.1 %collective-permute-start = (bf16[16,162]{1,0:T(8,128)(2,1)}, bf16[16,162]{1,0:T(8,128)(2,1)S(1)}, u32[]{:S(2)}, u32[]{:S(2)}) collective-permute-start(bf16[16,162]{1,0:T(8,128)(2,1)} %refs_5_.1), channel_id=1, source_target_pairs={{0,1},{1,2},{2,3},{3,0},{4,5},{5,6},{6,7},{7,4},{8,9},{9,10},{10,1... | collective-permute-start | bytes 15560 | tf_op jit(solution)/shard_map/ppermute | solution.py:749
  2.1 2.0 %collective-permute-start.1 = (bf16[16,162]{1,0:T(8,128)(2,1)}, bf16[16,162]{1,0:T(8,128)(2,1)S(1)}, u32[]{:S(2)}, u32[]{:S(2)}) collective-permute-start(bf16[16,162]{1,0:T(8,128)(2,1)} %refs_5_.1), channel_id=1, source_target_pairs={{1,0},{2,1},{3,2},{0,3},{5,4},{6,5},{7,6},{4,7},{9,8},{10,9},{11,1... | collective-permute-start | bytes 15560 | tf_op jit(solution)/shard_map/ppermute | solution.py:750
  4.2 1.2 %shard_map.100 = (bf16[48,48]{1,0:T(8,128)(2,1)S(1)}, f32[16,162]{1,0:T(8,128)S(1)}, f32[2,8,162]{2,1,0:T(8,128)S(1)}, bf16[16,162]{1,0:T(8,128)(2,1)S(1)}, bf16[162,162]{1,0:T(8,128)(2,1)S(1)}) custom-call(s32[2,8]{1,0:T(2,128)} %refs_0_.1, s32[8]{0:T(128)} %refs_1_.1, f32[4,16]{1,0:T(4,128)} %bitcast.8, s32[4,16]{1,0:T(4,128)} %bitcast.9, ...), custom_call_target="tpu_custom_call" | custom-call | flops 1 | bytes 1 | tf_op jit(solution)/shard_map/pallas_call | solution.py:671
  5.3 0.1 collective-permute-done.refs_3_.before
  5.4 0.0 collective-permute-done.1.refs_4_.after
  5.4 0.2 shard_map.102.rhs_ref
  5.7 2.3 %shard_map.101.raw_ref = bf16[3,2,8,162,162]{4,3,2,1,0:T(8,128)(2,1)S(1)} custom-call(bf16[2,162,8,162]{3,2,1,0:T(8,128)(2,1)} %bitcast.5, bf16[2,162,8,162]{3,2,1,0:T(8,128)(2,1)} %bitcast.6, bf16[2,162,8,162]{3,2,1,0:T(8,128)(2,1)} %bitcast.7, bf16[16,162]{1,0:T(8,128)(2,1)S(1)} %collective-permute-done.refs_3_.before, ...), custom_call_target="tpu_custom_call" | custom-call | flops 1 | bytes 1 | tf_op jit(solution)/shard_map/pallas_call | solution.py:671
  8.0 0.9 %shard_map.103 = (f32[2,8,162]{2,1,0:T(8,128)S(1)}, f32[2,8,162]{2,1,0:T(8,128)S(1)}, f32[8,162]{1,0:T(8,128)S(1)}) custom-call(f32[2,8,162]{2,1,0:T(8,128)S(1)} %shard_map.102.rhs_ref, bf16[3,2,8,162,162]{4,3,2,1,0:T(8,128)(2,1)S(1)} %shard_map.101.raw_ref, f32[2,8,162]{2,1,0:T(8,128)S(1)} %get-tuple-element.44.act_ref), custom_call_target="tpu_custom_call" | custom-call | flops 1 | bytes 1 | tf_op jit(solution)/shard_map/pallas_call | solution.py:671
  8.9 1.7 %collective-permute-start.2 = (f32[8,162]{1,0:T(8,128)S(1)}, f32[8,162]{1,0:T(8,128)S(1)}, u32[]{:S(2)}, u32[]{:S(2)}) collective-permute-start(f32[8,162]{1,0:T(8,128)S(1)} %get-tuple-element.45), channel_id=1, source_target_pairs={{0,4},{4,0},{8,12},{12,8},{16,20},{20,16},{24,28},{28,24},{1,5},{5... | collective-permute-start | bytes 15560 | tf_op jit(solution)/shard_map/ppermute | solution.py:718
  10.6 0.8 %collective-permute-done.2.came_ref.mate_ref = f32[8,162]{1,0:T(8,128)S(1)} collective-permute-done((f32[8,162]{1,0:T(8,128)S(1)}, f32[8,162]{1,0:T(8,128)S(1)}, u32[]{:S(2)}, u32[]{:S(2)}) %collective-permute-start.2) | collective-permute-done | bytes 5216 | tf_op jit(solution)/shard_map/ppermute | solution.py:718
  11.4 0.3 collective-permute-start.4
  11.8 1.1 %shard_map.104 = (f32[2,8,162]{2,1,0:T(8,128)S(1)}, f32[8,162]{1,0:T(8,128)S(1)}) custom-call(f32[8,162]{1,0:T(8,128)S(1)} %collective-permute-done.2.came_ref.mate_ref, f32[2,8,162]{2,1,0:T(8,128)S(1)} %get-tuple-element.46.scaled_ref, bf16[3,2,8,162,162]{4,3,2,1,0:T(8,128)(2,1)S(1)} %shard_map.101.raw_ref, f32[2,8,162]{2,1,0:T(8,128)S(1)} %get-tuple-element.44.act_ref, ...), custom_call_target="tpu_custom_call" | custom-call | flops 1 | bytes 1 | tf_op jit(solution)/shard_map/pallas_call | solution.py:671
  12.9 0.5 %collective-permute-done.4.refs_0_ = bf16[704,384]{1,0:T(8,128)(2,1)S(1)} collective-permute-done((bf16[704,384]{1,0:T(8,128)(2,1)S(1)}, bf16[704,384]{1,0:T(8,128)(2,1)S(1)}, u32[]{:S(2)}, u32[]{:S(2)}) %collective-permute-start.4) | collective-permute-done | bytes 540704 | tf_op jit(solution)/shard_map/ppermute | solution.py:718
  13.4 0.3 collective-permute-start.5
  13.7 1.5 %collective-permute-start.3 = (f32[8,162]{1,0:T(8,128)S(1)}, f32[8,162]{1,0:T(8,128)S(1)}, u32[]{:S(2)}, u32[]{:S(2)}) collective-permute-start(f32[8,162]{1,0:T(8,128)S(1)} %get-tuple-element.48), channel_id=1, source_target_pairs={{0,4},{4,12},{8,0},{12,8},{16,20},{20,16},{24,28},{28,24},{1,5},{5... | collective-permute-start | bytes 15560 | tf_op jit(solution)/shard_map/ppermute | solution.py:783
  15.2 1.8 %shard_map.107 = (bf16[2,8,2,162,162]{4,3,2,1,0:T(8,128)(2,1)S(1)}, bf16[8,2,162,162]{3,2,1,0:T(8,128)(2,1)S(1)}, bf16[1408,384]{1,0:T(8,128)(2,1)S(1)}) custom-call(bf16[3,2,8,162,162]{4,3,2,1,0:T(8,128)(2,1)S(1)} %shard_map.101.raw_ref), custom_call_target="tpu_custom_call" | custom-call | flops 1 | bytes 1 | tf_op jit(solution)/shard_map/pallas_call | solution.py:671
  17.0 0.0 collective-permute-done.3.came_ref.refs_0_
  17.0 0.0 collective-permute-done.5.refs_1_
  17.0 0.5 %collective-permute-start.10 = (bf16[1408,384]{1,0:T(8,128)(2,1)S(1)}, bf16[1408,384]{1,0:T(8,128)(2,1)S(1)}, u32[]{:S(2)}, u32[]{:S(2)}) collective-permute-start(bf16[1408,384]{1,0:T(8,128)(2,1)S(1)} %get-tuple-element.70), channel_id=1, source_target_pairs={{0,4},{4,0},{8,12},{12,8},{16,20},{20,16},{24,28},{28,24},{1,5},{5... | collective-permute-start | bytes 3244040 | tf_op jit(solution)/shard_map/ppermute | solution.py:718
  17.5 0.1 collective-permute-start.6
  17.6 2.2 %collective-permute-done.6.came_ref.refs_1_ = f32[8,162]{1,0:T(8,128)S(1)} collective-permute-done((f32[8,162]{1,0:T(8,128)S(1)}, f32[8,162]{1,0:T(8,128)S(1)}, u32[]{:S(2)}, u32[]{:S(2)}) %collective-permute-start.6) | collective-permute-done | bytes 5216 | tf_op jit(solution)/shard_map/ppermute | solution.py:838
  19.9 0.4 %collective-permute-start.9 = (f32[8,162]{1,0:T(8,128)S(1)}, f32[8,162]{1,0:T(8,128)S(1)}, u32[]{:S(2)}, u32[]{:S(2)}) collective-permute-start(f32[8,162]{1,0:T(8,128)S(1)} %shard_map.112.direct_ref), channel_id=1, source_target_pairs={{0,4},{4,0},{8,12},{12,8},{16,20},{20,16},{24,28},{28,24},{1,5},{5... | collective-permute-start | bytes 15560 | tf_op jit(solution)/shard_map/ppermute | solution.py:718
  20.2 0.8 %shard_map.110.refs_0_ = bf16[8,2,162,162]{3,2,1,0:T(8,128)(2,1)S(1)} custom-call(bf16[704,384]{1,0:T(8,128)(2,1)S(1)} %collective-permute-done.4.refs_0_, bf16[704,384]{1,0:T(8,128)(2,1)S(1)} %collective-permute-done.5.refs_1_, bf16[4,2,162,162]{3,2,1,0:T(8,128)(2,1)S(1)} %get-tuple-element.59.refs_2_.refs_0_, ...), custom_call_target="tpu_custom_call" | custom-call | flops 1 | bytes 1 | tf_op jit(solution)/shard_map/pallas_call | solution.py:671
  21.0 0.1 collective-permute-start.8
  21.1 0.5 %collective-permute-start.7 = (f32[8,162]{1,0:T(8,128)S(1)}, f32[8,162]{1,0:T(8,128)S(1)}, u32[]{:S(2)}, u32[]{:S(2)}) collective-permute-start(f32[8,162]{1,0:T(8,128)S(1)} %shard_map.111), channel_id=1, source_target_pairs={{0,4},{4,0},{8,12},{12,8},{16,20},{20,28},{24,16},{28,24},{1,5},{5... | collective-permute-start | bytes 15560 | tf_op jit(solution)/shard_map/ppermute | solution.py:838
  21.6 0.0 collective-permute-done.9.met_ref
  21.6 0.3 shard_map.113
  21.9 0.4 collective-permute-done.8.met_ref
  22.3 0.2 collective-permute-done.7.direct_ref
  22.4 0.3 collective-permute-start.11
  22.8 0.0 collective-permute-done.10.got_ref.refs_0_
  22.8 0.4 shard_map.115.x_ref
  23.1 0.5 %collective-permute-done.11.y_ref = f32[8,162]{1,0:T(8,128)S(1)} collective-permute-done((f32[8,162]{1,0:T(8,128)S(1)}, f32[8,162]{1,0:T(8,128)S(1)}, u32[]{:S(2)}, u32[]{:S(2)}) %collective-permute-start.11) | collective-permute-done | bytes 5216 | tf_op jit(solution)/shard_map/ppermute | solution.py:718
  23.6 0.3 collective-permute-start.12
  24.0 0.8 %shard_map.117.refs_0_ = bf16[8,2,162,162]{3,2,1,0:T(8,128)(2,1)S(1)} custom-call(bf16[1408,384]{1,0:T(8,128)(2,1)S(1)} %collective-permute-done.10.got_ref.refs_0_, bf16[8,2,162,162]{3,2,1,0:T(8,128)(2,1)S(1)} %get-tuple-element.54.refs_1_.own_ref), custom_call_target="tpu_custom_call" | custom-call | flops 1 | bytes 1 | tf_op jit(solution)/shard_map/pallas_call | solution.py:671
  24.7 0.1 collective-permute-done.12.came_ref.refs_0_
  24.8 0.3 collective-permute-start.13
  25.1 0.9 %collective-permute-done.13.came_ref.refs_1_ = f32[8,162]{1,0:T(8,128)S(1)} collective-permute-done((f32[8,162]{1,0:T(8,128)S(1)}, f32[8,162]{1,0:T(8,128)S(1)}, u32[]{:S(2)}, u32[]{:S(2)}) %collective-permute-start.13) | collective-permute-done | bytes 5216 | tf_op jit(solution)/shard_map/ppermute | solution.py:875
  26.0 0.3 collective-permute-start.14
  26.3 7.4 %collective-permute-done.14.refs_2_ = f32[8,162]{1,0:T(8,128)S(1)} collective-permute-done((f32[8,162]{1,0:T(8,128)S(1)}, f32[8,162]{1,0:T(8,128)S(1)}, u32[]{:S(2)}, u32[]{:S(2)}) %collective-permute-start.14) | collective-permute-done | bytes 5216 | tf_op jit(solution)/shard_map/ppermute | solution.py:875
  33.7 0.3 shard_map.120
  34.0 0.3 collective-permute-start.15
  34.2 1.0 %collective-permute-done.15.met_ref = f32[8,162]{1,0:T(8,128)S(1)} collective-permute-done((f32[8,162]{1,0:T(8,128)S(1)}, f32[8,162]{1,0:T(8,128)S(1)}, u32[]{:S(2)}, u32[]{:S(2)}) %collective-permute-start.15) | collective-permute-done | bytes 5216 | tf_op jit(solution)/shard_map/ppermute | solution.py:718
  35.2 1.2 %shard_map.121 = f32[2,8,162]{2,1,0:T(8,128)} custom-call(f32[8,162]{1,0:T(8,128)S(1)} %get-tuple-element.72.beyond_ref, f32[8,162]{1,0:T(8,128)S(1)} %collective-permute-done.15.met_ref, bf16[2,8,2,162,162]{4,3,2,1,0:T(8,128)(2,1)S(1)} %get-tuple-element.63.s_ref, f32[2,8,162]{2,1,0:T(8,128)S(1)} %get-tuple-element.44.act_ref, ...), custom_call_target="tpu_custom_call" | custom-call | flops 1 | bytes 1 | tf_op jit(solution)/shard_map/pallas_call | solution.py:671
  (10 shorter events, 0.0 us)
Async XLA Ops:
  0.0 5.4 %collective-permute-start = (bf16[16,162]{1,0:T(8,128)(2,1)}, bf16[16,162]{1,0:T(8,128)(2,1)S(1)}, u32[]{:S(2)}, u32[]{:S(2)}) collective-permute-start(bf16[16,162]{1,0:T(8,128)(2,1)} %refs_5_.1), channel_id=1, source_target_pairs={{0,1},{1,2},{2,3},{3,0},{4,5},{5,6},{6,7},{7,4},{8,9},{9,10},{10,1... | collective-permute-start | bytes 15560 | tf_op jit(solution)/shard_map/ppermute | solution.py:749
  2.1 3.3 %collective-permute-start.1 = (bf16[16,162]{1,0:T(8,128)(2,1)}, bf16[16,162]{1,0:T(8,128)(2,1)S(1)}, u32[]{:S(2)}, u32[]{:S(2)}) collective-permute-start(bf16[16,162]{1,0:T(8,128)(2,1)} %refs_5_.1), channel_id=1, source_target_pairs={{1,0},{2,1},{3,2},{0,3},{5,4},{6,5},{7,6},{4,7},{9,8},{10,9},{11,1... | collective-permute-start | bytes 15560 | tf_op jit(solution)/shard_map/ppermute | solution.py:750
  8.9 2.5 %collective-permute-start.2 = (f32[8,162]{1,0:T(8,128)S(1)}, f32[8,162]{1,0:T(8,128)S(1)}, u32[]{:S(2)}, u32[]{:S(2)}) collective-permute-start(f32[8,162]{1,0:T(8,128)S(1)} %get-tuple-element.45), channel_id=1, source_target_pairs={{0,4},{4,0},{8,12},{12,8},{16,20},{20,16},{24,28},{28,24},{1,5},{5... | collective-permute-start | bytes 15560 | tf_op jit(solution)/shard_map/ppermute | solution.py:718
  11.4 1.9 %collective-permute-start.4 = (bf16[704,384]{1,0:T(8,128)(2,1)S(1)}, bf16[704,384]{1,0:T(8,128)(2,1)S(1)}, u32[]{:S(2)}, u32[]{:S(2)}) collective-permute-start(bf16[704,384]{1,0:T(8,128)(2,1)S(1)} %get-tuple-element.56), channel_id=1, source_target_pairs={{0,4},{4,0},{8,12},{12,8},{16,20},{20,16},{24,28},{28,24},{1,5},{5... | collective-permute-start | bytes 1622024 | tf_op jit(solution)/shard_map/ppermute | solution.py:718
  13.4 3.7 %collective-permute-start.5 = (bf16[704,384]{1,0:T(8,128)(2,1)S(1)}, bf16[704,384]{1,0:T(8,128)(2,1)S(1)}, u32[]{:S(2)}, u32[]{:S(2)}) collective-permute-start(bf16[704,384]{1,0:T(8,128)(2,1)S(1)} %get-tuple-element.58), channel_id=1, source_target_pairs={{0,4},{4,0},{8,12},{12,8},{16,20},{20,16},{24,28},{28,24},{1,5},{5... | collective-permute-start | bytes 1622024 | tf_op jit(solution)/shard_map/ppermute | solution.py:718
  13.7 3.3 %collective-permute-start.3 = (f32[8,162]{1,0:T(8,128)S(1)}, f32[8,162]{1,0:T(8,128)S(1)}, u32[]{:S(2)}, u32[]{:S(2)}) collective-permute-start(f32[8,162]{1,0:T(8,128)S(1)} %get-tuple-element.48), channel_id=1, source_target_pairs={{0,4},{4,12},{8,0},{12,8},{16,20},{20,16},{24,28},{28,24},{1,5},{5... | collective-permute-start | bytes 15560 | tf_op jit(solution)/shard_map/ppermute | solution.py:783
  17.0 5.7 %collective-permute-start.10 = (bf16[1408,384]{1,0:T(8,128)(2,1)S(1)}, bf16[1408,384]{1,0:T(8,128)(2,1)S(1)}, u32[]{:S(2)}, u32[]{:S(2)}) collective-permute-start(bf16[1408,384]{1,0:T(8,128)(2,1)S(1)} %get-tuple-element.70), channel_id=1, source_target_pairs={{0,4},{4,0},{8,12},{12,8},{16,20},{20,16},{24,28},{28,24},{1,5},{5... | collective-permute-start | bytes 3244040 | tf_op jit(solution)/shard_map/ppermute | solution.py:718
  17.5 2.3 %collective-permute-start.6 = (f32[8,162]{1,0:T(8,128)S(1)}, f32[8,162]{1,0:T(8,128)S(1)}, u32[]{:S(2)}, u32[]{:S(2)}) collective-permute-start(f32[8,162]{1,0:T(8,128)S(1)} %shard_map.108), channel_id=1, source_target_pairs={{0,4},{4,0},{8,12},{12,20},{16,8},{20,16},{24,28},{28,24},{1,5},{5... | collective-permute-start | bytes 15560 | tf_op jit(solution)/shard_map/ppermute | solution.py:838
  19.9 1.7 %collective-permute-start.9 = (f32[8,162]{1,0:T(8,128)S(1)}, f32[8,162]{1,0:T(8,128)S(1)}, u32[]{:S(2)}, u32[]{:S(2)}) collective-permute-start(f32[8,162]{1,0:T(8,128)S(1)} %shard_map.112.direct_ref), channel_id=1, source_target_pairs={{0,4},{4,0},{8,12},{12,8},{16,20},{20,16},{24,28},{28,24},{1,5},{5... | collective-permute-start | bytes 15560 | tf_op jit(solution)/shard_map/ppermute | solution.py:718
  21.0 1.2 %collective-permute-start.8 = (f32[8,162]{1,0:T(8,128)S(1)}, f32[8,162]{1,0:T(8,128)S(1)}, u32[]{:S(2)}, u32[]{:S(2)}) collective-permute-start(f32[8,162]{1,0:T(8,128)S(1)} %shard_map.111), channel_id=1, source_target_pairs={{0,4},{4,0},{8,12},{12,8},{16,20},{20,24},{24,28},{28,16},{1,5},{5... | collective-permute-start | bytes 15560 | tf_op jit(solution)/shard_map/ppermute | solution.py:839
  21.1 1.3 %collective-permute-start.7 = (f32[8,162]{1,0:T(8,128)S(1)}, f32[8,162]{1,0:T(8,128)S(1)}, u32[]{:S(2)}, u32[]{:S(2)}) collective-permute-start(f32[8,162]{1,0:T(8,128)S(1)} %shard_map.111), channel_id=1, source_target_pairs={{0,4},{4,0},{8,12},{12,8},{16,20},{20,28},{24,16},{28,24},{1,5},{5... | collective-permute-start | bytes 15560 | tf_op jit(solution)/shard_map/ppermute | solution.py:838
  22.4 1.2 %collective-permute-start.11 = (f32[8,162]{1,0:T(8,128)S(1)}, f32[8,162]{1,0:T(8,128)S(1)}, u32[]{:S(2)}, u32[]{:S(2)}) collective-permute-start(f32[8,162]{1,0:T(8,128)S(1)} %get-tuple-element.68.first_ref), channel_id=1, source_target_pairs={{0,4},{4,0},{8,12},{12,8},{16,20},{20,16},{24,28},{28,24},{1,5},{5... | collective-permute-start | bytes 15560 | tf_op jit(solution)/shard_map/ppermute | solution.py:718
  23.6 1.2 %collective-permute-start.12 = (f32[8,162]{1,0:T(8,128)S(1)}, f32[8,162]{1,0:T(8,128)S(1)}, u32[]{:S(2)}, u32[]{:S(2)}) collective-permute-start(f32[8,162]{1,0:T(8,128)S(1)} %shard_map.116.local_ref), channel_id=1, source_target_pairs={{0,4},{4,0},{8,12},{12,8},{16,24},{20,16},{24,28},{28,20},{1,5},{5... | collective-permute-start | bytes 15560 | tf_op jit(solution)/shard_map/ppermute | solution.py:866
  24.8 1.2 %collective-permute-start.13 = (f32[8,162]{1,0:T(8,128)S(1)}, f32[8,162]{1,0:T(8,128)S(1)}, u32[]{:S(2)}, u32[]{:S(2)}) collective-permute-start(f32[8,162]{1,0:T(8,128)S(1)} %shard_map.118), channel_id=1, source_target_pairs={{0,4},{4,0},{8,16},{12,8},{16,20},{20,12},{24,28},{28,24},{1,5},{5... | collective-permute-start | bytes 15560 | tf_op jit(solution)/shard_map/ppermute | solution.py:875
  26.0 7.7 %collective-permute-start.14 = (f32[8,162]{1,0:T(8,128)S(1)}, f32[8,162]{1,0:T(8,128)S(1)}, u32[]{:S(2)}, u32[]{:S(2)}) collective-permute-start(f32[8,162]{1,0:T(8,128)S(1)} %shard_map.119), channel_id=1, source_target_pairs={{0,8},{4,0},{8,12},{12,4},{16,20},{20,16},{24,28},{28,24},{1,9},{5... | collective-permute-start | bytes 15560 | tf_op jit(solution)/shard_map/ppermute | solution.py:875
  34.0 1.2 %collective-permute-start.15 = (f32[8,162]{1,0:T(8,128)S(1)}, f32[8,162]{1,0:T(8,128)S(1)}, u32[]{:S(2)}, u32[]{:S(2)}) collective-permute-start(f32[8,162]{1,0:T(8,128)S(1)} %get-tuple-element.73), channel_id=1, source_target_pairs={{0,4},{4,0},{8,12},{12,8},{16,20},{20,16},{24,28},{28,24},{1,5},{5... | collective-permute-start | bytes 15560 | tf_op jit(solution)/shard_map/ppermute | solution.py:718

commit v5 on v4

--- a/solution.py
+++ b/solution.py
@@ -105,19 +105,38 @@
     return lax.div(lax.axis_index("wall"), 2)
 
 
-def pair_kernel(raw_ref, *refs, first_chip, **options):
+def pair_kernel(raw_ref, *refs, first_chip, fetch, turn, **options):
+    if fetch:
+        next_ref, landed, arrived = refs[0], refs[4], refs[-1]
+        copies = [
+            pltpu.make_async_copy(next_ref.at[e], landed.at[0, e], arrived.at[e]) for e in range(next_ref.shape[0])
+        ]
+        for copy in copies:
+            copy.start()
+        refs = refs[1:4]
+    other_ref = raw_ref
+    if turn:
+        other_ref = refs[-1]
+        for e in range(raw_ref.shape[1]):
+            turn_blocks(refs[0], 0, e, other_ref)
+        refs = refs[1:4]
+
     @pl.when(chip_of() >= first_chip)
     def _():
-        make_pairs(raw_ref, *refs[-3:], **options)
-
-
-def make_pairs(raw_ref, step_ref, whole_ref, sent_ref, *, kind, lines, ascending):
+        make_pairs(raw_ref, other_ref, *refs[-3:], **options)
+
+    if fetch:
+        for copy in copies:
+            copy.wait()
+
+
+def make_pairs(raw_ref, other_ref, step_ref, whole_ref, sent_ref, *, kind, lines, ascending):
     count = raw_ref.shape[1]
     for l in range(*lines):
         steps = []
         for e in range(count):
             block = lax.dot_general(
-                raw_ref[kind, e, l], raw_ref[0, e, l], (((0,), (1,)), ((), ())), preferred_element_type=F32
+                other_ref[kind, e, l], raw_ref[0, e, l], (((0,), (1,)), ((), ())), preferred_element_type=F32
             )
             steps.append(split2(block))
             store_pair(step_ref, steps[-1], e, l)
@@ -143,9 +162,15 @@
             store_pair(chip_ref, split2(product(*(pairs[::-1] if own_first else pairs))), l)
 
 
+def turn_blocks(landed_ref, a, e, raw_ref):
+    turned = jnp.swapaxes(landed_ref[a, e], 0, 1)
+    for l in range(raw_ref.shape[2]):
+        raw_ref[a, e, l] = turned[l]
+
+
 def relayout_kernel(*refs, kinds):
     raw_ref, landed, arrived = refs[-3:]
-    _, depth, lines = raw_ref.shape[:3]
+    depth = raw_ref.shape[1]
     copies = [
         pltpu.make_async_copy(ref.at[e], landed.at[a, e], arrived.at[a, e])
         for a, ref in enumerate(refs[:kinds])
@@ -155,10 +180,7 @@
         copy.start()
     for i, copy in enumerate(copies):
         copy.wait()
-        a, e = divmod(i, depth)
-        turned = jnp.swapaxes(landed[a, e], 0, 1)
-        for l in range(lines):
-            raw_ref[a, e, l] = turned[l]
+        turn_blocks(landed, *divmod(i, depth), raw_ref)
 
 
 def prepare_kernel(*refs):
@@ -283,9 +305,43 @@
         out_ref[...] = act_ref[depth - 1] * apply_pairs(came_ref[...], own_refs) + y_ref[depth - 1]
 
 
-def hop_kernel(came_ref, act_ref, local_ref, *refs, chip):
+def three_terms(x):
+    high = x.astype(BF16)
+    return high, *split2(x - high.astype(F32))
+
+
+def through_kernel(act_ref, q_ref, s_ref, y_ref, *refs, parts):
+    whole_refs, (out_ref, sent_ref, echo_ref) = refs[:parts], refs[parts:]
+    depth, lines, _, _, width = q_ref.shape
+    main, below = width // LANES * LANES, lines * room_of(width)[0]
+    echo = backward_local([y_ref[g] for g in range(depth)], s_ref, act_ref, None)[0]
+    echo_ref[...] = echo
+    for i, term in enumerate(three_terms(echo)):
+        sent_ref[below + 2 * TILE * i : below + 2 * TILE * i + lines, :main] = term[:, :main]
+        if width > main:
+            sent_ref[below + 2 * TILE * i : below + 2 * TILE * i + lines, main:width] = term[:, main:]
+
+    @pl.when(chip_of() > 0)
+    def _():
+        for l in range(lines):
+            active = [act_ref[g, l : l + 1, :] for g in range(depth)]
+            steps = [[-x for x in pair_at(q_ref, width, 0, l)]]
+            for g in range(1, depth - 1):
+                steps.append(split2(-product(steps[-1], pair_at(q_ref, width, g, l))))
+            each = lines // parts
+            high, low = pair_at(whole_refs[l // each], width, l % each)
+            value = active[depth - 1] * (high.astype(F32) + low.astype(F32))
+            for g in range(depth - 2, -1, -1):
+                reach = steps[g][0].astype(F32) + steps[g][1].astype(F32)
+                value = active[g] * (reach - product(split2(value), pair_at(s_ref, width, g, l)))
+            pair = split2(value)
+            store_pair(out_ref, pair, l)
+            store_pair(sent_ref, pair, l)
+
+
+def hop_kernel(came_ref, act_ref, local_ref, idle_ref, *refs, chip):
     pair_refs, out_ref = refs[:-1], refs[-1]
-    out_ref[...] = local_ref[...]
+    out_ref[...] = idle_ref[...]
 
     @pl.when(jnp.logical_and(chip_of() == chip, core_of() == 1))
     def _():
@@ -316,45 +372,58 @@
     refs[-1][...] = chosen_arrival(refs[:-1], chips, refs[-1].shape)
 
 
-def inner_kernel(
-    direct_ref, met_ref, came_ref, scaled_ref, q_ref, s_ref, act_ref, wall_ref, *refs, on_last, last, parts
-):
-    got_refs = refs[:parts]
-    y_ref, first_ref, flow = refs[-3:]
+def turn_kernel(enter_ref, came_ref, echo_ref, got_c, got_d, own_d, *refs, parts, chips, fill):
+    got_refs, (enter_y, mid_ref, out_ref) = refs[:parts], refs[-3:]
+    inside = jnp.logical_and(chip_of() >= chips[0], chip_of() < chips[1])
+    if fill:
+
+        @pl.when(jnp.logical_not(inside))
+        def _():
+            enter_y[...] = enter_ref[...]
+            mid_ref[...] = echo_ref[...]
+            out_ref[...] = echo_ref[...]
+
+    @pl.when(jnp.logical_and(inside, core_of() == 1))
+    def _():
+        enter = enter_ref[...]
+        leave = apply_pairs(enter, got_refs) + came_ref[...]
+        middle = apply_pairs(leave, own_d) + echo_ref[...]
+        lines, width = enter.shape
+        below = lines * room_of(width)[0]
+        first = apply_pairs(enter, got_d)
+        for i in range(3):
+            first = first + got_d[below + 2 * TILE * i : below + 2 * TILE * i + lines, :width].astype(F32)
+        enter_y[...] = leave
+        mid_ref[...] = middle
+        out_ref[...] = apply_pairs(middle, got_c) + first
+
+
+def send_kernel(x_ref, enter_ref, out_ref, *, last):
+    out_ref[...] = jnp.where(chip_of() == last, x_ref[...], enter_ref[...])
+
+
+def steps_kernel(flow_ref, scaled_ref, q_ref, act_ref, wall_ref, *refs, late):
+    y_ref = refs[-1]
     depth = scaled_ref.shape[0]
-    here = chip_of()
-
-    @pl.when(here == last if on_last else jnp.logical_and(here > 0, here != last))
-    def _():
-        flow[...] = met_ref[...]
-
-        @pl.when(core_of() == 1)
-        def _():
-            flow[...] = apply_pairs(direct_ref[...], got_refs) + came_ref[...]
-
-        values = forward_local([scaled_ref[g] for g in range(depth)], q_ref, act_ref, flow[...])
-        for g in range(depth):
-            y_ref[g] = values[g]
-
-    if not on_last:
+    here, core = chip_of(), core_of()
+    if late:
+        inside = jnp.logical_and(core == 0, here > 1)
+    else:
+        inside = jnp.logical_and(here > 0, jnp.logical_or(core == 1, here == 1))
 
         @pl.when(here == 0)
         def _():
             y_ref[...] = wall_ref[...]
 
-    @pl.when(here == last if on_last else here != last)
-    def _():
-        first_ref[...] = backward_local([y_ref[g] for g in range(depth)], s_ref, act_ref, None)[0]
-
-
-def reach_kernel(first_ref, got_ref, out_ref):
-    @pl.when(core_of() == 1)
-    def _():
-        out_ref[...] = apply_pairs(first_ref[...], got_ref)
-
-
-def add_kernel(x_ref, y_ref, out_ref):
-    out_ref[...] = x_ref[...] + y_ref[...]
+    @pl.when(inside)
+    def _():
+        values = forward_local([scaled_ref[g] for g in range(depth)], q_ref, act_ref, flow_ref[...])
+        for g in range(depth):
+            y_ref[g] = values[g]
+
+
+def entry_kernel(own_ref, came_ref, out_ref):
+    out_ref[...] = jnp.where(core_of() == 1, own_ref[...], came_ref[...])
 
 
 def leave_kernel(own_ref, first_ref, *refs, chips):
@@ -420,8 +489,8 @@
     )(*[x for x, _ in operands])
 
 
-def hop_pairs(count, start, end, core=1):
-    start, end = 2 * start + 1, 2 * end + core
+def hop_pairs(count, start, end):
+    start, end = 2 * start + 1, 2 * end + 1
     target = {i: i ^ 1 for i in range(count)}
     target.update({start: end, end: end ^ 1, end ^ 1: start ^ 1, start ^ 1: start})
     return sorted(target.items())
@@ -443,272 +512,12 @@
     slots = state.shape[0]
     block = TILE if lines % TILE == 0 else lines
     blocks = lines // block
-    parts = 2 if blocks == 1 and lines % 2 == 0 else 1
+    parts = 1
     room, columns, _ = room_of(width)
     line_vector = ((lines, width), F32, 0)
     element_vectors = ((depth, lines, width), F32, 1)
     line_sent = ((lines * room, columns), BF16, 0)
-    line_pairs = ((lines, 2, width, width), BF16, 0)
-    part_sent = ((lines // parts * room, columns), BF16, 0)
-    part_pairs = ((lines // parts, 2, width, width), BF16, 0)
-    element_pairs = ((depth, lines, 2, width, width), BF16, 1)
-
-    def mates(value):
-        return lax.ppermute(value, "wall", [(i, i ^ 1) for i in range(wall_count)])
-
-    count = depth * lines
-    rows = lax.broadcasted_iota(jnp.int32, (count, slots), 0)
-    slot = jnp.zeros((count, slots), jnp.int32)
-    for g in range(depth):
-        for l in range(lines):
-            slot = jnp.where(rows == g * lines + l, slot_ref[g, l], slot)
-    chosen = (slot == lax.broadcasted_iota(jnp.int32, (count, slots), 1)).astype(F32).astype(BF16)
-    high = weight.astype(BF16)
-    mid, low = split2(weight - high.astype(F32))
-    for i, part in enumerate((high, mid, low)):
-        weight_ref[i * count : (i + 1) * count, :] = lax.dot_general(
-            chosen, part, (((1,), (1,)), ((), ())), preferred_element_type=F32
-        ).astype(BF16)
-    rhs_ref[...] = jnp.dot(chosen, source_ref[...], preferred_element_type=F32)
-    rows = lax.broadcasted_iota(jnp.int32, act_ref.shape[1:], 0)
-    length = jnp.zeros(act_ref.shape[1:], jnp.int32)
-    for l in range(lines):
-        length = jnp.where(rows == l, len_ref[l], length)
-    place = lax.axis_index("wall") * depth
-    for g in range(depth):
-        act_ref[g] = (place + g < length).astype(F32)
-
-
-def residual_kernel(before, state, after, weight, source, lift, rhs_ref):
-    cells = jnp.concatenate([before[...], state[...], after[...]], axis=0)
-    parts = jnp.dot(weight[...], cells, preferred_element_type=F32)
-    count = source.shape[0]
-    face_sum = parts[:count] + (parts[count : 2 * count] + parts[2 * count :])
-    flux = jnp.dot(face_sum.astype(BF16), lift[...], preferred_element_type=F32)
-    rhs = source[...] - flux
-    depth, lines, _ = rhs_ref.shape
-    for g in range(depth):
-        rhs_ref[g] = rhs[g * lines : (g + 1) * lines]
-
-
-def forward_local(scaled, q_ref, act_ref, carried):
-    values = []
-    for g, value in enumerate(scaled):
-        if carried is not None:
-            value = value - apply_pairs(carried, q_ref, g)
-        carried = act_ref[g] * value
-        values.append(carried)
-    return values
-
-
-def backward_local(values, s_ref, act_ref, carried):
-    solved = [None] * len(values)
-    for g in range(len(values) - 1, -1, -1):
-        value = values[g]
-        if carried is not None:
-            value = value - apply_pairs(carried, s_ref, g)
-        carried = act_ref[g] * value
-        solved[g] = carried
-    return solved
-
-
-def local_kernel(rhs_ref, raw_ref, act_ref, scaled_ref, y_ref, leave_ref):
-    depth = rhs_ref.shape[0]
-    scaled = [apply_rows(rhs_ref[g], raw_ref, 0, g) for g in range(depth)]
-    values = raw_steps(scaled, raw_ref, act_ref, None)
-    for g in range(depth):
-        scaled_ref[g] = scaled[g]
-        y_ref[g] = values[g]
-    leave_ref[...] = values[-1]
-
-
-def raw_steps(scaled, raw_ref, act_ref, carried):
-    values = []
-    for g, value in enumerate(scaled):
-        if carried is not None:
-            value = value - apply_rows(apply_rows(carried, raw_ref, 1, g), raw_ref, 0, g)
-        carried = act_ref[g] * value
-        values.append(carried)
-    return values
-
-
-def wall_kernel(came_ref, scaled_ref, raw_ref, act_ref, y_ref, out_ref, leave_ref):
-    depth = y_ref.shape[0]
-    out_ref[...] = y_ref[...]
-    leave_ref[...] = y_ref[depth - 1]
-
-    @pl.when(lax.axis_index("wall") == 1)
-    def _():
-        values = raw_steps([scaled_ref[g] for g in range(depth)], raw_ref, act_ref, came_ref[...])
-        for g in range(depth):
-            out_ref[g] = values[g]
-        leave_ref[...] = values[-1]
-
-
-def chip_local_kernel(came_ref, act_ref, y_ref, *refs):
-    own_refs, out_ref = refs[:-1], refs[-1]
-    depth = y_ref.shape[0]
-    out_ref[...] = y_ref[depth - 1]
-
-    @pl.when(jnp.logical_and(core_of() == 1, chip_of() > 0))
-    def _():
-        out_ref[...] = act_ref[depth - 1] * apply_pairs(came_ref[...], own_refs) + y_ref[depth - 1]
-
-
-def hop_kernel(came_ref, act_ref, local_ref, *refs, chip):
-    pair_refs, out_ref = refs[:-1], refs[-1]
-    out_ref[...] = local_ref[...]
-
-    @pl.when(jnp.logical_and(chip_of() == chip, core_of() == 1))
-    def _():
-        gone = apply_pairs(came_ref[...], pair_refs)
-        out_ref[...] = act_ref[act_ref.shape[0] - 1] * gone + local_ref[...]
-
-
-def chosen_arrival(refs, chips, like):
-    here = chip_of()
-    value = jnp.zeros(like, F32)
-    for ref, chip in zip(refs, chips):
-        value = jnp.where(here == chip, ref[...], value)
-    return value
-
-
-def choose_kernel(*refs, chips):
-    refs[-1][...] = chosen_arrival(refs[:-1], chips, refs[-1].shape)
-
-
-def inner_kernel(
-    direct_ref, met_ref, came_ref, scaled_ref, q_ref, s_ref, act_ref, wall_ref, *refs, on_last, last, parts
-):
-    got_refs = refs[:parts]
-    y_ref, first_ref, flow = refs[-3:]
-    depth = scaled_ref.shape[0]
-    here = chip_of()
-
-    @pl.when(here == last if on_last else jnp.logical_and(here > 0, here != last))
-    def _():
-        flow[...] = met_ref[...]
-
-        @pl.when(core_of() == 1)
-        def _():
-            flow[...] = apply_pairs(direct_ref[...], got_refs) + came_ref[...]
-
-        values = forward_local([scaled_ref[g] for g in range(depth)], q_ref, act_ref, flow[...])
-        for g in range(depth):
-            y_ref[g] = values[g]
-
-    if not on_last:
-
-        @pl.when(here == 0)
-        def _():
-            y_ref[...] = wall_ref[...]
-
-    @pl.when(here == last if on_last else here != last)
-    def _():
-        first_ref[...] = backward_local([y_ref[g] for g in range(depth)], s_ref, act_ref, None)[0]
-
-
-def reach_kernel(first_ref, got_ref, out_ref):
-    @pl.when(core_of() == 1)
-    def _():
-        out_ref[...] = apply_pairs(first_ref[...], got_ref)
-
-
-def add_kernel(x_ref, y_ref, out_ref):
-    out_ref[...] = x_ref[...] + y_ref[...]
-
-
-def leave_kernel(own_ref, first_ref, *refs, chips):
-    came_ref, out_ref = refs[-2:]
-    came_ref[...] = chosen_arrival(refs[:-2], chips, came_ref.shape)
-    out_ref[...] = first_ref[...]
-
-    @pl.when(core_of() == 1)
-    def _():
-        out_ref[...] = apply_pairs(came_ref[...], own_ref) + first_ref[...]
-
-
-def last_kernel(beyond_ref, met_ref, s_ref, act_ref, y_ref, out_ref):
-    depth = y_ref.shape[0]
-    carried = jnp.where(core_of() == 0, met_ref[...], beyond_ref[...])
-    solved = backward_local([y_ref[g] for g in range(depth)], s_ref, act_ref, carried)
-    for g in range(depth):
-        out_ref[g] = solved[g]
-
-
-def padded_bytes(shape, dtype):
-    size = jnp.dtype(dtype).itemsize
-    shape = (1,) * (2 - len(shape)) + tuple(shape)
-    total = -(-shape[-2] // 16) * 16 * -(-shape[-1] // 128) * 128 * size
-    for extent in shape[:-2]:
-        total *= extent
-    return total
-
-
-def run(kernel, operands, outs, blocks=1, scratch=(), aliases=None):
-    held = [(x.shape, x.dtype) for x, _ in operands] + [(s, t) for s, t, _ in outs]
-    limit = sum(padded_bytes(s, t) for s, t in held)
-    if blocks == 1:
-        in_specs = [at if isinstance(at, pl.BlockSpec) else VMEM for _, at in operands]
-        out_specs = [VMEM for _ in outs]
-        grid = ()
-    else:
-
-        def spec(shape, at):
-            if isinstance(at, pl.BlockSpec):
-                return at
-            if at is None:
-                return pl.BlockSpec(shape, lambda i: (0,) * len(shape))
-            size = tuple(n // blocks if axis == at else n for axis, n in enumerate(shape))
-            return pl.BlockSpec(size, lambda i: tuple(i if axis == at else 0 for axis in range(len(shape))))
-
-        in_specs = [spec(x.shape, at) for x, at in operands]
-        out_specs = [spec(s, at) for s, _, at in outs]
-        grid = (blocks,)
-        limit = 2 * limit // blocks
-    limit += sum(padded_bytes(s.shape, s.dtype) for s in scratch if s.memory_space == pltpu.VMEM)
-    limit = min(limit + (2 << 20), 60 << 20)
-    return pl.pallas_call(
-        kernel,
-        grid=grid,
-        in_specs=in_specs,
-        out_specs=out_specs,
-        out_shape=[jax.ShapeDtypeStruct(s, t) for s, t, _ in outs],
-        scratch_shapes=list(scratch),
-        input_output_aliases=aliases or {},
-        compiler_params=pltpu.CompilerParams(vmem_limit_bytes=limit),
-        cost_estimate=pl.CostEstimate(flops=1, bytes_accessed=1, transcendentals=0),
-    )(*[x for x, _ in operands])
-
-
-def hop_pairs(count, start, end, core=1):
-    start, end = 2 * start + 1, 2 * end + core
-    target = {i: i ^ 1 for i in range(count)}
-    target.update({start: end, end: end ^ 1, end ^ 1: start ^ 1, start ^ 1: start})
-    return sorted(target.items())
-
-
-def in_hbm(value):
-    return pltpu.with_memory_space_constraint(value, pltpu.HBM)
-
-
-def after(value, *others):
-    return lax.optimization_barrier((value, *others))[0]
-
-
-def per_device(state, source, face_coef, neighbour, lift, elem_slot, line_len, dinv, lower, upper):
-    wall_count = lax.axis_size("wall")
-    surf_count = lax.axis_size("surf")
-    last = wall_count // 2 - 1
-    depth, lines, width, _ = dinv.shape
-    slots = state.shape[0]
-    block = TILE if lines % TILE == 0 else lines
-    blocks = lines // block
-    parts = 2 if blocks == 1 and lines % 2 == 0 else 1
-    room, columns, _ = room_of(width)
-    line_vector = ((lines, width), F32, 0)
-    element_vectors = ((depth, lines, width), F32, 1)
-    line_sent = ((lines * room, columns), BF16, 0)
+    vector_sent = ((lines * room + 6 * TILE * blocks, columns), BF16, 0)
     line_pairs = ((lines, 2, width, width), BF16, 0)
     part_sent = ((lines // parts * room, columns), BF16, 0)
     part_pairs = ((lines // parts, 2, width, width), BF16, 0)
@@ -753,20 +562,20 @@
         [(x, None) for x in (before, near_state, beyond, weight, line_source, near_lift)],
         [element_vectors],
     )
-    blocks_in = (dinv, lower, upper)
-    if lines == TILE:
+    in_place = lines == TILE
+    if in_place:
+        blocks_in = [in_hbm(jnp.transpose(x, (0, 2, 1, 3))) for x in (dinv, lower, upper)]
         (raw,) = run(
-            functools.partial(relayout_kernel, kinds=3),
-            [(in_hbm(jnp.transpose(x, (0, 2, 1, 3))), ANY) for x in blocks_in]
-            + [(x, None) for x in (before, beyond, weight)],
-            [((3, depth, lines, width, width), BF16, None)],
+            functools.partial(relayout_kernel, kinds=2),
+            [(x, ANY) for x in blocks_in[:2]] + [(x, None) for x in (before, weight)],
+            [((2, depth, lines, width, width), BF16, None)],
             scratch=[
-                pltpu.VMEM((3, depth, width, lines, width), BF16),
-                pltpu.SemaphoreType.DMA((3, depth)),
+                pltpu.VMEM((2, depth, width, lines, width), BF16),
+                pltpu.SemaphoreType.DMA((2, depth)),
             ],
         )
     else:
-        raw = jnp.stack(blocks_in)
+        raw = jnp.stack([dinv, lower, upper])
     scaled, y_local, y_leave = run(
         local_kernel,
         [(rhs, 1), (raw, 2), (act, 1)],
@@ -781,32 +590,37 @@
         blocks,
     )
     arrivals = [lax.ppermute(wall_leave, "wall", hop_pairs(wall_count, 0, 1))]
-    a, got_a, q = [], [], None
-    for part in range(parts):
-        each = block // parts
-        q, whole, sent = run(
-            functools.partial(
-                pair_kernel, first_chip=1, kind=1, lines=(part * each, part * each + each), ascending=True
-            ),
-            [(after(raw, wall_leave if part else y_leave), 2)] + ([] if q is None else [(q, ANY)]),
-            [element_pairs, part_pairs, part_sent],
-            blocks,
-            aliases={} if q is None else {1: 0},
-        )
-        a.append(whole)
-        got_a.append(mates(after(sent, got_a[-1] if part else came_y)))
+    q, *rest = run(
+        functools.partial(
+            pair_kernel, first_chip=1, fetch=in_place, turn=False, kind=1, lines=(0, block), ascending=True
+        ),
+        [(after(raw, y_leave), 2)] + ([(blocks_in[2], ANY)] if in_place else []),
+        [element_pairs, line_pairs, line_sent] + ([((1, *blocks_in[2].shape), BF16, None)] if in_place else []),
+        blocks,
+        [pltpu.SemaphoreType.DMA((depth,))] if in_place else [],
+    )
+    a, got_a = [rest[0]], [mates(after(rest[1], came_y))]
     s, c, sent_c = run(
-        functools.partial(pair_kernel, first_chip=0, kind=2, lines=(0, block), ascending=False),
-        [(after(raw, a[-1], wall_leave), 2)],
+        functools.partial(
+            pair_kernel,
+            first_chip=0,
+            fetch=False,
+            turn=in_place,
+            kind=0 if in_place else 2,
+            lines=(0, block),
+            ascending=False,
+        ),
+        [(after(raw, a[-1], wall_leave), 2)] + ([(rest[2], None)] if in_place else []),
         [element_pairs, line_pairs, line_sent],
         blocks,
+        [pltpu.VMEM((1, depth, lines, width, width), BF16)] if in_place else [],
     )
     got_c = mates(after(sent_c, arrivals[0],got_a[-1]))
 
-    def hop(came, pairs, local, at):
+    def hop(came, pairs, local, idle, at):
         (out,) = run(
             functools.partial(hop_kernel, chip=at),
-            [(came, 0), (act, 1), (local, 0)] + [(x, 0) for x in pairs],
+            [(came, 0), (act, 1), (local, 0), (idle, 0)] + [(x, 0) for x in pairs],
             [line_vector],
             blocks,
         )
@@ -833,49 +647,70 @@
                 [line_vector],
                 blocks,
             )
+            through, sent_d, echo = run(
+                functools.partial(through_kernel, parts=parts),
+                [(act, 1), (after(q, out, chip_a, y_chip), 1), (s, 1), (wall_y, 1)] + [(x, 0) for x in a],
+                [line_pairs, vector_sent, line_vector],
+                blocks,
+            )
         else:
-            out = hop(arrivals[-1], [chip_a], y_chip, at)
+            out = hop(arrivals[-1], [chip_a], y_chip, y_chip, at)
         arrivals.append(lax.ppermute(out, "wall", hop_pairs(wall_count, at, at + 1)))
-    direct = lax.ppermute(out, "wall", hop_pairs(wall_count, last - 1, last, 0))
-
-    def inner(on_last, entered, met, held=()):
-        return run(
-            functools.partial(inner_kernel, on_last=on_last, last=last, parts=parts),
-            [(entered, 0), (met, 0), (came_y, 0)]
-            + [(x, 1) for x in (scaled, q, s, act, wall_y)]
-            + [(x, 0) for x in got_a]
-            + [(x, ANY) for x in held],
-            [element_vectors, line_vector],
-            blocks,
-            [pltpu.VMEM((block, width), F32)],
-            {8 + parts: 0, 9 + parts: 1} if held else {},
-        )
+        if at == 1:
+            got_d = mates(after(sent_d, got_c, arrivals[-1]))
 
     def chosen(arrived, chips):
         return run(
             functools.partial(choose_kernel, chips=chips), [(x, 0) for x in arrived], [line_vector], blocks
         )[0]
 
-    chips = list(range(1, last))
-    entered = chosen(arrivals[:-1], chips)
-    held = inner(False, after(entered, out), mates(entered))
-    y, first = inner(True, arrivals[-1], direct, held)
-    came_first = mates(first)
-    (reach,) = run(reach_kernel, [(first, 0), (got_c, 0)], [line_vector], blocks)
-    (x_chip,) = run(add_kernel, [(reach, 0), (came_first, 0)], [line_vector], blocks)
-    arrived = [lax.ppermute(x_chip, "wall", hop_pairs(wall_count, last, last - 1))]
+    def turn(first_chip, end_chip, entered, held=()):
+        return run(
+            functools.partial(turn_kernel, parts=parts, chips=(first_chip, end_chip), fill=not held),
+            [(x, 0) for x in (entered, came_y, echo, got_c, got_d, through, *got_a)]
+            + [(x, ANY) for x in held],
+            [line_vector] * 3,
+            blocks,
+            aliases={6 + parts + i: i for i in range(3)} if held else {},
+        )
+
+    def steps(late, flow, held=()):
+        return run(
+            functools.partial(steps_kernel, late=late),
+            [(flow, 0)] + [(x, 1) for x in (scaled, q, act, wall_y)] + [(x, ANY) for x in held],
+            [element_vectors],
+            blocks,
+            aliases={5: 0} if held else {},
+        )
+
+    entered = chosen(arrivals[:-1], list(range(1, last)))
+    held = turn(last - 1, last, after(entered, out))
+    arrivals[-1] = after(arrivals[-1], held[0])
+    held = turn(last, last + 1, arrivals[-1], held)
+    x_chip = held[-1]
+    entered = chosen(arrivals, list(range(1, last + 1)))
+    (out,) = run(functools.partial(send_kernel, last=last), [(x_chip, 0), (entered, 0)], [line_vector], blocks)
+    arrived = [lax.ppermute(out, "wall", hop_pairs(wall_count, last, last - 1))]
     (chip_c,) = run(
         functools.partial(chip_kernel, parts=1, width=width, own_first=True),
         [(after(got_c, x_chip), 0), (c, 0)],
         [line_pairs],
         blocks,
     )
+    y = ()
     for at in range(last - 1, 0, -1):
-        out = hop(arrived[-1], [chip_c], x_chip, at)
+        came = arrived[-1]
+        if at == 1:
+            enter_y, middle, x_chip = turn(1, last - 1, after(entered, out), held)
+            (flow,) = run(entry_kernel, [(enter_y, 0), (after(arrived[0], out), 0)], [line_vector], blocks)
+            y = steps(False, flow)
+            came = after(came, *y)
+        out = hop(came, [chip_c], x_chip, entered, at)
         arrived.append(lax.ppermute(out, "wall", hop_pairs(wall_count, at, at - 1)))
+    (y,) = steps(True, arrived[-1], y)
     beyond, left = run(
         functools.partial(leave_kernel, chips=list(range(last - 1, -1, -1))),
-        [(x, 0) for x in (c, first, *arrived)],
+        [(x, 0) for x in (c, middle, *arrived)],
         [line_vector, line_vector],
         blocks,
     )

time: 36.7 us -> 33.4 us (0.910)
  starting transfers between devices: 11.1 us -> 8.61 us
  waiting for transfers between devices: 13.9 us -> 12.1 us
  Pallas kernels: 11.3 us -> 12.2 us
    ppermute x7 -> x5, starting transfers between devices: 3.81 us -> 2.15 us  [mates(): return lax.ppermute(value, 'wall', [(i, i ^ 1) for i in range(wall_count)])]
    ppermute x2, waiting for transfers between devices: 2.4 us -> 1.09 us  [per_device(): lax.ppermute(out, 'wall', hop_pairs(wall_count, at, at + 1))]
    ppermute x2, waiting for transfers between devices: 8.22 us -> 7.24 us  [per_device(): arrived.append(lax.ppermute(out, 'wall', hop_pairs(wall_count, at, at - 1)))]
    pallas_call x22 -> x26, Pallas kernels: 11.3 us -> 12.2 us  [run(): pl.pallas_call(kernel, grid=grid, in_specs=in_specs, out_specs=out_specs,...]
    ppermute x7 -> x5, waiting for transfers between devices: 2.78 us -> 3.38 us  [mates(): return lax.ppermute(value, 'wall', [(i, i ^ 1) for i in range(wall_count)])]
    ppermute x1, starting transfers between devices: 1.5 us -> 1.02 us  [per_device(): arrivals = [lax.ppermute(wall_leave, 'wall', hop_pairs(wall_count, 0, 1))]]
  transfers between devices with their start and end apart: 16 -> 13, of which waited for: 11 -> 7; matrix products, arithmetic and copies ran while one was open for 0% -> 0% of each run, Pallas kernels for 17% -> 29%
where the time goes in v5:
time: 33.4 us; the launch traced here: 33 us
  Pallas kernels  12.2 us (37%)
  waiting for transfers between devices  12.1 us (36%)
  starting transfers between devices  8.61 us (26%)
    pallas_call x26, Pallas kernels, run(): pl.pallas_call(kernel, grid=grid, in_specs=in_specs, out_specs=out_specs,...  12.2 us
    ppermute x2, waiting for transfers between devices, per_device(): arrived.append(lax.ppermute(out, 'wall', hop_pairs(wall_count, at, at - 1)))  7.24 us
    ppermute x5, waiting for transfers between devices, mates(): return lax.ppermute(value, 'wall', [(i, i ^ 1) for i in range(wall_count)])  3.38 us
    ppermute x5, starting transfers between devices, mates(): return lax.ppermute(value, 'wall', [(i, i ^ 1) for i in range(wall_count)])  2.15 us
    ppermute x1, starting transfers between devices, per_device(): lax.ppermute(state, 'surf', [(i, (i + 1) % surf_count) for i in range(sur...  2.13 us
    ppermute x1, starting transfers between devices, per_device(): lax.ppermute(state, 'surf', [((i + 1) % surf_count, i) for i in range(sur...  2.03 us
    ppermute x2, waiting for transfers between devices, per_device(): lax.ppermute(out, 'wall', hop_pairs(wall_count, at, at + 1))  1.09 us
    ppermute x1, starting transfers between devices, per_device(): arrivals = [lax.ppermute(wall_leave, 'wall', hop_pairs(wall_count, 0, 1))]  1.02 us
  transfers between devices with their start and end apart: 13, of which 7 were waited for; matrix products, arithmetic and copies ran while one was open for 0% of the time, Pallas kernels for 29%

profile of v5, /device:TPU:1, one launch (start us, length us, event | category | flops | bytes accessed | tf_op | source)
XLA Modules:
  0.0 33.0 jit_solution(666491656310839370)
XLA Ops:
  0.0 2.1 %collective-permute-start = (bf16[16,162]{1,0:T(8,128)(2,1)}, bf16[16,162]{1,0:T(8,128)(2,1)S(1)}, u32[]{:S(2)}, u32[]{:S(2)}) collective-permute-start(bf16[16,162]{1,0:T(8,128)(2,1)} %refs_5_.1), channel_id=1, source_target_pairs={{0,1},{1,2},{2,3},{3,0},{4,5},{5,6},{6,7},{7,4},{8,9},{9,10},{10,1... | collective-permute-start | bytes 15560 | tf_op jit(solution)/shard_map/ppermute | solution.py:558
  2.1 2.0 %collective-permute-start.1 = (bf16[16,162]{1,0:T(8,128)(2,1)}, bf16[16,162]{1,0:T(8,128)(2,1)S(1)}, u32[]{:S(2)}, u32[]{:S(2)}) collective-permute-start(bf16[16,162]{1,0:T(8,128)(2,1)} %refs_5_.1), channel_id=1, source_target_pairs={{1,0},{2,1},{3,2},{0,3},{5,4},{6,5},{7,6},{4,7},{9,8},{10,9},{11,1... | collective-permute-start | bytes 15560 | tf_op jit(solution)/shard_map/ppermute | solution.py:559
  4.2 1.2 %shard_map.100 = (bf16[48,48]{1,0:T(8,128)(2,1)S(1)}, f32[16,162]{1,0:T(8,128)S(1)}, f32[2,8,162]{2,1,0:T(8,128)S(1)}, bf16[16,162]{1,0:T(8,128)(2,1)S(1)}, bf16[162,162]{1,0:T(8,128)(2,1)S(1)}) custom-call(s32[2,8]{1,0:T(2,128)} %refs_0_.1, s32[8]{0:T(128)} %refs_1_.1, f32[4,16]{1,0:T(4,128)} %bitcast.8, s32[4,16]{1,0:T(4,128)} %bitcast.9, ...), custom_call_target="tpu_custom_call" | custom-call | flops 1 | bytes 1 | tf_op jit(solution)/shard_map/pallas_call | solution.py:479
  5.3 0.1 collective-permute-done.refs_2_.before
  5.4 1.9 %shard_map.101.raw_ref = bf16[2,2,8,162,162]{4,3,2,1,0:T(8,128)(2,1)S(1)} custom-call(bf16[2,162,8,162]{3,2,1,0:T(8,128)(2,1)} %bitcast.5, bf16[2,162,8,162]{3,2,1,0:T(8,128)(2,1)} %bitcast.6, bf16[16,162]{1,0:T(8,128)(2,1)S(1)} %collective-permute-done.refs_2_.before, bf16[48,48]{1,0:T(8,128)(2,1)S(1)} %get-tuple-element.50.refs_3_.weight), custom_call_target="tpu_custom_call" | custom-call | flops 1 | bytes 1 | tf_op jit(solution)/shard_map/pallas_call | solution.py:479
  7.3 0.0 collective-permute-done.1.after
  7.3 0.2 shard_map.102.rhs_ref
  7.6 0.9 %shard_map.103 = (f32[2,8,162]{2,1,0:T(8,128)S(1)}, f32[2,8,162]{2,1,0:T(8,128)S(1)}, f32[8,162]{1,0:T(8,128)S(1)}) custom-call(f32[2,8,162]{2,1,0:T(8,128)S(1)} %shard_map.102.rhs_ref, bf16[2,2,8,162,162]{4,3,2,1,0:T(8,128)(2,1)S(1)} %shard_map.101.raw_ref, f32[2,8,162]{2,1,0:T(8,128)S(1)} %get-tuple-element.54.act_ref), custom_call_target="tpu_custom_call" | custom-call | flops 1 | bytes 1 | tf_op jit(solution)/shard_map/pallas_call | solution.py:479
  8.5 1.7 %collective-permute-start.2 = (f32[8,162]{1,0:T(8,128)S(1)}, f32[8,162]{1,0:T(8,128)S(1)}, u32[]{:S(2)}, u32[]{:S(2)}) collective-permute-start(f32[8,162]{1,0:T(8,128)S(1)} %get-tuple-element.55), channel_id=1, source_target_pairs={{0,4},{4,0},{8,12},{12,8},{16,20},{20,16},{24,28},{28,24},{1,5},{5... | collective-permute-start | bytes 15560 | tf_op jit(solution)/shard_map/ppermute | solution.py:527
  10.2 1.3 %shard_map.104 = (bf16[2,8,2,162,162]{4,3,2,1,0:T(8,128)(2,1)S(1)}, bf16[8,2,162,162]{3,2,1,0:T(8,128)(2,1)S(1)}, bf16[1408,384]{1,0:T(8,128)(2,1)S(1)}, bf16[1,2,162,8,162]{4,3,2,1,0:T(8,128)(2,1)S(1)}) custom-call(bf16[2,2,8,162,162]{4,3,2,1,0:T(8,128)(2,1)S(1)} %shard_map.101.raw_ref, bf16[2,162,8,162]{3,2,1,0:T(8,128)(2,1)} %bitcast.7), custom_call_target="tpu_custom_call" | custom-call | flops 1 | bytes 1 | tf_op jit(solution)/shard_map/pallas_call | solution.py:479
  11.5 0.0 collective-permute-done.2.came_ref.mate_ref
  11.5 0.1 collective-permute-start.4
  11.6 1.1 %shard_map.105 = (f32[2,8,162]{2,1,0:T(8,128)S(1)}, f32[8,162]{1,0:T(8,128)S(1)}) custom-call(f32[8,162]{1,0:T(8,128)S(1)} %collective-permute-done.2.came_ref.mate_ref, f32[2,8,162]{2,1,0:T(8,128)S(1)} %get-tuple-element.58.scaled_ref, bf16[2,2,8,162,162]{4,3,2,1,0:T(8,128)(2,1)S(1)} %shard_map.101.raw_ref, f32[2,8,162]{2,1,0:T(8,128)S(1)} %get-tuple-element.54.act_ref, ...), custom_call_target="tpu_custom_call" | custom-call | flops 1 | bytes 1 | tf_op jit(solution)/shard_map/pallas_call | solution.py:479
  12.7 1.0 %collective-permute-start.3 = (f32[8,162]{1,0:T(8,128)S(1)}, f32[8,162]{1,0:T(8,128)S(1)}, u32[]{:S(2)}, u32[]{:S(2)}) collective-permute-start(f32[8,162]{1,0:T(8,128)S(1)} %get-tuple-element.60), channel_id=1, source_target_pairs={{0,4},{4,12},{8,0},{12,8},{16,20},{20,16},{24,28},{28,24},{1,5},{5... | collective-permute-start | bytes 15560 | tf_op jit(solution)/shard_map/ppermute | solution.py:592
  13.7 2.1 %shard_map.106 = (bf16[2,8,2,162,162]{4,3,2,1,0:T(8,128)(2,1)S(1)}, bf16[8,2,162,162]{3,2,1,0:T(8,128)(2,1)S(1)}, bf16[1408,384]{1,0:T(8,128)(2,1)S(1)}) custom-call(bf16[2,2,8,162,162]{4,3,2,1,0:T(8,128)(2,1)S(1)} %shard_map.101.raw_ref, bf16[1,2,162,8,162]{4,3,2,1,0:T(8,128)(2,1)S(1)} %get-tuple-element.62.refs_0_), custom_call_target="tpu_custom_call" | custom-call | flops 1 | bytes 1 | tf_op jit(solution)/shard_map/pallas_call | solution.py:479
  15.8 0.0 collective-permute-done.3.came_ref.refs_0_
  15.8 0.0 collective-permute-done.4.refs_0_
  15.8 0.2 collective-permute-start.7
  16.0 0.4 %collective-permute-start.5 = (f32[8,162]{1,0:T(8,128)S(1)}, f32[8,162]{1,0:T(8,128)S(1)}, u32[]{:S(2)}, u32[]{:S(2)}) collective-permute-start(f32[8,162]{1,0:T(8,128)S(1)} %shard_map.107), channel_id=1, source_target_pairs={{0,4},{4,0},{8,12},{12,20},{16,8},{20,16},{24,28},{28,24},{1,5},{5... | collective-permute-start | bytes 15560 | tf_op jit(solution)/shard_map/ppermute | solution.py:658
  16.4 0.8 %shard_map.109.refs_0_ = bf16[8,2,162,162]{3,2,1,0:T(8,128)(2,1)S(1)} custom-call(bf16[1408,384]{1,0:T(8,128)(2,1)S(1)} %collective-permute-done.4.refs_0_, bf16[8,2,162,162]{3,2,1,0:T(8,128)(2,1)S(1)} %get-tuple-element.57.refs_1_.refs_0_), custom_call_target="tpu_custom_call" | custom-call | flops 1 | bytes 1 | tf_op jit(solution)/shard_map/pallas_call | solution.py:479
  17.2 0.3 shard_map.112
  17.5 1.1 %collective-permute-done.5.came_ref.refs_1_ = f32[8,162]{1,0:T(8,128)S(1)} collective-permute-done((f32[8,162]{1,0:T(8,128)S(1)}, f32[8,162]{1,0:T(8,128)S(1)}, u32[]{:S(2)}, u32[]{:S(2)}) %collective-permute-start.5) | collective-permute-done | bytes 5216 | tf_op jit(solution)/shard_map/ppermute | solution.py:658
  18.6 0.0 collective-permute-done.7.got_c.refs_0_
  18.6 0.1 collective-permute-start.8
  18.8 0.4 %collective-permute-start.6 = (f32[8,162]{1,0:T(8,128)S(1)}, f32[8,162]{1,0:T(8,128)S(1)}, u32[]{:S(2)}, u32[]{:S(2)}) collective-permute-start(f32[8,162]{1,0:T(8,128)S(1)} %shard_map.110), channel_id=1, source_target_pairs={{0,4},{4,0},{8,12},{12,8},{16,20},{20,28},{24,16},{28,24},{1,5},{5... | collective-permute-start | bytes 15560 | tf_op jit(solution)/shard_map/ppermute | solution.py:658
  19.1 2.2 %collective-permute-done.8.got_d = bf16[1456,384]{1,0:T(8,128)(2,1)S(1)} collective-permute-done((bf16[1456,384]{1,0:T(8,128)(2,1)S(1)}, bf16[1456,384]{1,0:T(8,128)(2,1)S(1)}, u32[]{:S(2)}, u32[]{:S(2)}) %collective-permute-start.8) | collective-permute-done | bytes 1118240 | tf_op jit(solution)/shard_map/ppermute | solution.py:527
  21.4 0.0 collective-permute-done.6.refs_2_.enter_ref
  21.5 0.2 collective-permute-start.9
  21.7 0.8 %shard_map.117.refs_0_ = bf16[8,2,162,162]{3,2,1,0:T(8,128)(2,1)S(1)} custom-call(bf16[1408,384]{1,0:T(8,128)(2,1)S(1)} %collective-permute-done.7.got_c.refs_0_, bf16[8,2,162,162]{3,2,1,0:T(8,128)(2,1)S(1)} %get-tuple-element.63.refs_1_.own_ref), custom_call_target="tpu_custom_call" | custom-call | flops 1 | bytes 1 | tf_op jit(solution)/shard_map/pallas_call | solution.py:479
  22.4 0.3 collective-permute-done.9.came_ref.refs_0_
  22.7 0.2 collective-permute-start.10
  22.9 1.0 %collective-permute-done.10.came_ref.refs_1_ = f32[8,162]{1,0:T(8,128)S(1)} collective-permute-done((f32[8,162]{1,0:T(8,128)S(1)}, f32[8,162]{1,0:T(8,128)S(1)}, u32[]{:S(2)}, u32[]{:S(2)}) %collective-permute-start.10) | collective-permute-done | bytes 5216 | tf_op jit(solution)/shard_map/ppermute | solution.py:709
  23.9 0.2 collective-permute-start.11
  24.0 6.3 %collective-permute-done.11.refs_2_.flow_ref = f32[8,162]{1,0:T(8,128)S(1)} collective-permute-done((f32[8,162]{1,0:T(8,128)S(1)}, f32[8,162]{1,0:T(8,128)S(1)}, u32[]{:S(2)}, u32[]{:S(2)}) %collective-permute-start.11) | collective-permute-done | bytes 5216 | tf_op jit(solution)/shard_map/ppermute | solution.py:709
  30.3 0.3 shard_map.123
  30.6 0.1 collective-permute-start.12
  30.7 1.1 %collective-permute-done.12.met_ref = f32[8,162]{1,0:T(8,128)S(1)} collective-permute-done((f32[8,162]{1,0:T(8,128)S(1)}, f32[8,162]{1,0:T(8,128)S(1)}, u32[]{:S(2)}, u32[]{:S(2)}) %collective-permute-start.12) | collective-permute-done | bytes 5216 | tf_op jit(solution)/shard_map/ppermute | solution.py:527
  31.8 1.2 %shard_map.125 = f32[2,8,162]{2,1,0:T(8,128)} custom-call(f32[8,162]{1,0:T(8,128)S(1)} %get-tuple-element.93.beyond_ref, f32[8,162]{1,0:T(8,128)S(1)} %collective-permute-done.12.met_ref, bf16[2,8,2,162,162]{4,3,2,1,0:T(8,128)(2,1)S(1)} %get-tuple-element.71.s_ref, f32[2,8,162]{2,1,0:T(8,128)S(1)} %get-tuple-element.54.act_ref, ...), custom_call_target="tpu_custom_call" | custom-call | flops 1 | bytes 1 | tf_op jit(solution)/shard_map/pallas_call | solution.py:479
  (14 shorter events, 0.1 us)
Async XLA Ops:
  0.0 5.4 %collective-permute-start = (bf16[16,162]{1,0:T(8,128)(2,1)}, bf16[16,162]{1,0:T(8,128)(2,1)S(1)}, u32[]{:S(2)}, u32[]{:S(2)}) collective-permute-start(bf16[16,162]{1,0:T(8,128)(2,1)} %refs_5_.1), channel_id=1, source_target_pairs={{0,1},{1,2},{2,3},{3,0},{4,5},{5,6},{6,7},{7,4},{8,9},{9,10},{10,1... | collective-permute-start | bytes 15560 | tf_op jit(solution)/shard_map/ppermute | solution.py:558
  2.1 5.2 %collective-permute-start.1 = (bf16[16,162]{1,0:T(8,128)(2,1)}, bf16[16,162]{1,0:T(8,128)(2,1)S(1)}, u32[]{:S(2)}, u32[]{:S(2)}) collective-permute-start(bf16[16,162]{1,0:T(8,128)(2,1)} %refs_5_.1), channel_id=1, source_target_pairs={{1,0},{2,1},{3,2},{0,3},{5,4},{6,5},{7,6},{4,7},{9,8},{10,9},{11,1... | collective-permute-start | bytes 15560 | tf_op jit(solution)/shard_map/ppermute | solution.py:559
  8.5 3.0 %collective-permute-start.2 = (f32[8,162]{1,0:T(8,128)S(1)}, f32[8,162]{1,0:T(8,128)S(1)}, u32[]{:S(2)}, u32[]{:S(2)}) collective-permute-start(f32[8,162]{1,0:T(8,128)S(1)} %get-tuple-element.55), channel_id=1, source_target_pairs={{0,4},{4,0},{8,12},{12,8},{16,20},{20,16},{24,28},{28,24},{1,5},{5... | collective-permute-start | bytes 15560 | tf_op jit(solution)/shard_map/ppermute | solution.py:527
  11.5 4.3 %collective-permute-start.4 = (bf16[1408,384]{1,0:T(8,128)(2,1)S(1)}, bf16[1408,384]{1,0:T(8,128)(2,1)S(1)}, u32[]{:S(2)}, u32[]{:S(2)}) collective-permute-start(bf16[1408,384]{1,0:T(8,128)(2,1)S(1)} %get-tuple-element.65), channel_id=1, source_target_pairs={{0,4},{4,0},{8,12},{12,8},{16,20},{20,16},{24,28},{28,24},{1,5},{5... | collective-permute-start | bytes 3244040 | tf_op jit(solution)/shard_map/ppermute | solution.py:527
  12.7 3.2 %collective-permute-start.3 = (f32[8,162]{1,0:T(8,128)S(1)}, f32[8,162]{1,0:T(8,128)S(1)}, u32[]{:S(2)}, u32[]{:S(2)}) collective-permute-start(f32[8,162]{1,0:T(8,128)S(1)} %get-tuple-element.60), channel_id=1, source_target_pairs={{0,4},{4,12},{8,0},{12,8},{16,20},{20,16},{24,28},{28,24},{1,5},{5... | collective-permute-start | bytes 15560 | tf_op jit(solution)/shard_map/ppermute | solution.py:592
  15.8 2.8 %collective-permute-start.7 = (bf16[1408,384]{1,0:T(8,128)(2,1)S(1)}, bf16[1408,384]{1,0:T(8,128)(2,1)S(1)}, u32[]{:S(2)}, u32[]{:S(2)}) collective-permute-start(bf16[1408,384]{1,0:T(8,128)(2,1)S(1)} %get-tuple-element.75), channel_id=1, source_target_pairs={{0,4},{4,0},{8,12},{12,8},{16,20},{20,16},{24,28},{28,24},{1,5},{5... | collective-permute-start | bytes 3244040 | tf_op jit(solution)/shard_map/ppermute | solution.py:527
  16.0 2.6 %collective-permute-start.5 = (f32[8,162]{1,0:T(8,128)S(1)}, f32[8,162]{1,0:T(8,128)S(1)}, u32[]{:S(2)}, u32[]{:S(2)}) collective-permute-start(f32[8,162]{1,0:T(8,128)S(1)} %shard_map.107), channel_id=1, source_target_pairs={{0,4},{4,0},{8,12},{12,20},{16,8},{20,16},{24,28},{28,24},{1,5},{5... | collective-permute-start | bytes 15560 | tf_op jit(solution)/shard_map/ppermute | solution.py:658
  18.6 2.8 %collective-permute-start.8 = (bf16[1456,384]{1,0:T(8,128)(2,1)S(1)}, bf16[1456,384]{1,0:T(8,128)(2,1)S(1)}, u32[]{:S(2)}, u32[]{:S(2)}) collective-permute-start(bf16[1456,384]{1,0:T(8,128)(2,1)S(1)} %get-tuple-element.77), channel_id=1, source_target_pairs={{0,4},{4,0},{8,12},{12,8},{16,20},{20,16},{24,28},{28,24},{1,5},{5... | collective-permute-start | bytes 3354632 | tf_op jit(solution)/shard_map/ppermute | solution.py:527
  18.8 2.6 %collective-permute-start.6 = (f32[8,162]{1,0:T(8,128)S(1)}, f32[8,162]{1,0:T(8,128)S(1)}, u32[]{:S(2)}, u32[]{:S(2)}) collective-permute-start(f32[8,162]{1,0:T(8,128)S(1)} %shard_map.110), channel_id=1, source_target_pairs={{0,4},{4,0},{8,12},{12,8},{16,20},{20,28},{24,16},{28,24},{1,5},{5... | collective-permute-start | bytes 15560 | tf_op jit(solution)/shard_map/ppermute | solution.py:658
  21.5 1.2 %collective-permute-start.9 = (f32[8,162]{1,0:T(8,128)S(1)}, f32[8,162]{1,0:T(8,128)S(1)}, u32[]{:S(2)}, u32[]{:S(2)}) collective-permute-start(f32[8,162]{1,0:T(8,128)S(1)} %shard_map.116), channel_id=1, source_target_pairs={{0,4},{4,0},{8,12},{12,8},{16,24},{20,16},{24,28},{28,20},{1,5},{5... | collective-permute-start | bytes 15560 | tf_op jit(solution)/shard_map/ppermute | solution.py:693
  22.7 1.2 %collective-permute-start.10 = (f32[8,162]{1,0:T(8,128)S(1)}, f32[8,162]{1,0:T(8,128)S(1)}, u32[]{:S(2)}, u32[]{:S(2)}) collective-permute-start(f32[8,162]{1,0:T(8,128)S(1)} %shard_map.118), channel_id=1, source_target_pairs={{0,4},{4,0},{8,16},{12,8},{16,20},{20,12},{24,28},{28,24},{1,5},{5... | collective-permute-start | bytes 15560 | tf_op jit(solution)/shard_map/ppermute | solution.py:709
  23.9 6.4 %collective-permute-start.11 = (f32[8,162]{1,0:T(8,128)S(1)}, f32[8,162]{1,0:T(8,128)S(1)}, u32[]{:S(2)}, u32[]{:S(2)}) collective-permute-start(f32[8,162]{1,0:T(8,128)S(1)} %shard_map.122), channel_id=1, source_target_pairs={{0,8},{4,0},{8,12},{12,4},{16,20},{20,16},{24,28},{28,24},{1,9},{5... | collective-permute-start | bytes 15560 | tf_op jit(solution)/shard_map/ppermute | solution.py:709
  30.6 1.2 %collective-permute-start.12 = (f32[8,162]{1,0:T(8,128)S(1)}, f32[8,162]{1,0:T(8,128)S(1)}, u32[]{:S(2)}, u32[]{:S(2)}) collective-permute-start(f32[8,162]{1,0:T(8,128)S(1)} %get-tuple-element.94), channel_id=1, source_target_pairs={{0,4},{4,0},{8,12},{12,8},{16,20},{20,16},{24,28},{28,24},{1,5},{5... | collective-permute-start | bytes 15560 | tf_op jit(solution)/shard_map/ppermute | solution.py:527

commit v6 on v5

--- a/solution.py
+++ b/solution.py
@@ -105,6 +105,11 @@
     return lax.div(lax.axis_index("wall"), 2)
 
 
+def between(chips, core):
+    inside = jnp.logical_and(chip_of() >= chips[0], chip_of() < chips[1])
+    return jnp.logical_and(inside, core_of() == core)
+
+
 def pair_kernel(raw_ref, *refs, first_chip, fetch, turn, **options):
     if fetch:
         next_ref, landed, arrived = refs[0], refs[4], refs[-1]
@@ -131,30 +136,28 @@
 
 
 def make_pairs(raw_ref, other_ref, step_ref, whole_ref, sent_ref, *, kind, lines, ascending):
-    count = raw_ref.shape[1]
+    count, width = raw_ref.shape[1], raw_ref.shape[3]
     for l in range(*lines):
-        steps = []
         for e in range(count):
             block = lax.dot_general(
                 other_ref[kind, e, l], raw_ref[0, e, l], (((0,), (1,)), ((), ())), preferred_element_type=F32
             )
-            steps.append(split2(block))
-            store_pair(step_ref, steps[-1], e, l)
-        if not ascending:
-            steps = steps[::-1]
-        whole = steps[0]
-        for step in steps[1:]:
-            whole = split2(product(whole, step))
+            store_pair(step_ref, split2(block), e, l)
+    order = list(range(count)) if ascending else list(range(count))[::-1]
+    for l in range(*lines):
+        whole = pair_at(step_ref, width, order[0], l)
+        for e in order[1:]:
+            whole = split2(product(whole, pair_at(step_ref, width, e, l)))
         if count % 2:
             whole = [-x for x in whole]
         store_pair(whole_ref, whole, l - lines[0])
         store_pair(sent_ref, whole, l - lines[0])
 
 
-def chip_kernel(*refs, parts, width, own_first):
+def chip_kernel(*refs, parts, width, own_first, chips):
     got_refs, own_refs, chip_ref = refs[:parts], refs[parts:-1], refs[-1]
 
-    @pl.when(core_of() == 1)
+    @pl.when(between(chips, 1))
     def _():
         each = chip_ref.shape[0] // parts
         for l in range(chip_ref.shape[0]):
@@ -168,29 +171,23 @@
         raw_ref[a, e, l] = turned[l]
 
 
-def relayout_kernel(*refs, kinds):
-    raw_ref, landed, arrived = refs[-3:]
-    depth = raw_ref.shape[1]
-    copies = [
-        pltpu.make_async_copy(ref.at[e], landed.at[a, e], arrived.at[a, e])
-        for a, ref in enumerate(refs[:kinds])
-        for e in range(depth)
-    ]
-    for copy in copies:
-        copy.start()
-    for i, copy in enumerate(copies):
-        copy.wait()
-        turn_blocks(landed, *divmod(i, depth), raw_ref)
-
-
-def prepare_kernel(*refs):
-    places, (weight_ref, rhs_ref, act_ref, state_ref, lift_ref) = refs[:7], refs[7:12]
-    slot_ref, len_ref, coef_ref, nb_ref, source_ref, arrived = refs[12:]
+def prepare_kernel(*refs, taken):
+    blocks = refs[7 : 7 + taken]
+    places, (weight_ref, rhs_ref, act_ref, state_ref, lift_ref) = refs[:7], refs[7 + taken : 12 + taken]
+    slot_ref, len_ref, coef_ref, nb_ref, source_ref, arrived = refs[12 + taken + (taken > 0) :][:6]
     targets = (slot_ref, len_ref, coef_ref, nb_ref, source_ref, state_ref, lift_ref)
     copies = [
         pltpu.make_async_copy(there, here, arrived.at[i]) for i, (there, here) in enumerate(zip(places, targets))
     ]
-    for copy in copies:
+    block_copies = []
+    if taken:
+        raw_ref, landed, landed_at = refs[12 + taken], refs[-2], refs[-1]
+        block_copies = [
+            pltpu.make_async_copy(ref.at[e], landed.at[a, e], landed_at.at[a, e])
+            for a, ref in enumerate(blocks)
+            for e in range(landed.shape[1])
+        ]
+    for copy in copies + block_copies:
         copy.start()
     for copy in copies:
         copy.wait()
@@ -227,6 +224,9 @@
     place = lax.axis_index("wall") * depth
     for g in range(depth):
         act_ref[g] = (place + g < length).astype(F32)
+    for i, copy in enumerate(block_copies):
+        copy.wait()
+        turn_blocks(landed, *divmod(i, landed.shape[1]), raw_ref)
 
 
 def residual_kernel(before, state, after, weight, source, lift, rhs_ref):
@@ -295,12 +295,12 @@
         leave_ref[...] = values[-1]
 
 
-def chip_local_kernel(came_ref, act_ref, y_ref, *refs):
+def chip_local_kernel(came_ref, act_ref, y_ref, *refs, chips):
     own_refs, out_ref = refs[:-1], refs[-1]
     depth = y_ref.shape[0]
     out_ref[...] = y_ref[depth - 1]
 
-    @pl.when(jnp.logical_and(core_of() == 1, chip_of() > 0))
+    @pl.when(between(chips, 1))
     def _():
         out_ref[...] = act_ref[depth - 1] * apply_pairs(came_ref[...], own_refs) + y_ref[depth - 1]
 
@@ -329,12 +329,15 @@
             for g in range(1, depth - 1):
                 steps.append(split2(-product(steps[-1], pair_at(q_ref, width, g, l))))
             each = lines // parts
-            high, low = pair_at(whole_refs[l // each], width, l % each)
-            value = active[depth - 1] * (high.astype(F32) + low.astype(F32))
+            value = [
+                (active[depth - 1] * x.astype(F32)).astype(BF16)
+                for x in pair_at(whole_refs[l // each], width, l % each)
+            ]
             for g in range(depth - 2, -1, -1):
                 reach = steps[g][0].astype(F32) + steps[g][1].astype(F32)
-                value = active[g] * (reach - product(split2(value), pair_at(s_ref, width, g, l)))
-            pair = split2(value)
+                total = active[g] * (reach - product(value, pair_at(s_ref, width, g, l)))
+                value = split2(total)
+            pair = value
             store_pair(out_ref, pair, l)
             store_pair(sent_ref, pair, l)
 
@@ -431,15 +434,30 @@
     came_ref[...] = chosen_arrival(refs[:-2], chips, came_ref.shape)
     out_ref[...] = first_ref[...]
 
-    @pl.when(core_of() == 1)
+    @pl.when(jnp.logical_and(core_of() == 1, chip_of() > 0))
     def _():
         out_ref[...] = apply_pairs(came_ref[...], own_ref) + first_ref[...]
 
 
-def last_kernel(beyond_ref, met_ref, s_ref, act_ref, y_ref, out_ref):
+def wall_middle_kernel(came_ref, got_c, got_d, out_ref):
+    @pl.when(lax.axis_index("wall") == 0)
+    def _():
+        lines, width = came_ref.shape
+        below = lines * room_of(width)[0]
+        value = apply_pairs(came_ref[...], got_c)
+        for i in range(3):
+            value = value + got_d[below + 2 * TILE * i : below + 2 * TILE * i + lines, :width].astype(F32)
+        out_ref[...] = value
+
+
+def last_kernel(beyond_ref, met_ref, middle_ref, wall_ref, s_ref, act_ref, y_ref, out_ref):
     depth = y_ref.shape[0]
-    carried = jnp.where(core_of() == 0, met_ref[...], beyond_ref[...])
-    solved = backward_local([y_ref[g] for g in range(depth)], s_ref, act_ref, carried)
+    core, chip = core_of(), chip_of()
+    first = jnp.where(chip == 0, middle_ref[...], met_ref[...])
+    second = jnp.where(chip == 0, wall_ref[...], beyond_ref[...])
+    solved = backward_local(
+        [y_ref[g] for g in range(depth)], s_ref, act_ref, jnp.where(core == 0, first, second)
+    )
     for g in range(depth):
         out_ref[g] = solved[g]
 
@@ -489,10 +507,13 @@
     )(*[x for x, _ in operands])
 
 
-def hop_pairs(count, start, end):
-    start, end = 2 * start + 1, 2 * end + 1
+def hop_pairs(count, start, end, core=1, relay=None):
+    start, end = 2 * start + 1, 2 * end + core
     target = {i: i ^ 1 for i in range(count)}
-    target.update({start: end, end: end ^ 1, end ^ 1: start ^ 1, start ^ 1: start})
+    cycle = [start, end, end ^ 1, start ^ 1]
+    if relay is not None:
+        cycle[3:3] = [2 * relay, 2 * relay + 1]
+    target.update(zip(cycle, cycle[1:] + cycle[:1]))
     return sorted(target.items())
 
 
@@ -542,18 +563,26 @@
 
     count = depth * lines
     small = (elem_slot, line_len, face_coef.T, neighbour.T, source)
-    weight, line_source, act, near_state, near_lift = run(
-        prepare_kernel,
-        [(in_hbm(x), ANY) for x in (*small, state, lift)],
+    in_place = lines == TILE
+    blocks_in = [in_hbm(jnp.transpose(x, (0, 2, 1, 3))) for x in (dinv, lower, upper)] if in_place else []
+    weight, line_source, act, near_state, near_lift, *landed = run(
+        functools.partial(prepare_kernel, taken=2 if in_place else 0),
+        [(in_hbm(x), ANY) for x in (*small, state, lift)] + [(x, ANY) for x in blocks_in[:2]],
         [
             ((3 * count, 3 * slots), BF16, None),
             ((count, width), F32, None),
             element_vectors,
             (state.shape, BF16, None),
             (lift.shape, BF16, None),
-        ],
+        ]
+        + ([((2, depth, lines, width, width), BF16, None)] if in_place else []),
         scratch=[(pltpu.SMEM if i < 2 else pltpu.VMEM)(x.shape, x.dtype) for i, x in enumerate(small)]
-        + [pltpu.SemaphoreType.DMA((len(small) + 2,))],
+        + [pltpu.SemaphoreType.DMA((len(small) + 2,))]
+        + (
+            [pltpu.VMEM((2, depth, width, lines, width), BF16), pltpu.SemaphoreType.DMA((2, depth))]
+            if in_place
+            else []
+        ),
     )
     before = lax.ppermute(state, "surf", [(i, (i + 1) % surf_count) for i in range(surf_count)])
     beyond = lax.ppermute(state, "surf", [((i + 1) % surf_count, i) for i in range(surf_count)])
@@ -562,20 +591,7 @@
         [(x, None) for x in (before, near_state, beyond, weight, line_source, near_lift)],
         [element_vectors],
     )
-    in_place = lines == TILE
-    if in_place:
-        blocks_in = [in_hbm(jnp.transpose(x, (0, 2, 1, 3))) for x in (dinv, lower, upper)]
-        (raw,) = run(
-            functools.partial(relayout_kernel, kinds=2),
-            [(x, ANY) for x in blocks_in[:2]] + [(x, None) for x in (before, weight)],
-            [((2, depth, lines, width, width), BF16, None)],
-            scratch=[
-                pltpu.VMEM((2, depth, width, lines, width), BF16),
-                pltpu.SemaphoreType.DMA((2, depth)),
-            ],
-        )
-    else:
-        raw = jnp.stack([dinv, lower, upper])
+    raw = landed[0] if in_place else jnp.stack([dinv, lower, upper])
     scaled, y_local, y_leave = run(
         local_kernel,
         [(rhs, 1), (raw, 2), (act, 1)],
@@ -636,13 +652,13 @@
                 blocks,
             )
             (chip_a,) = run(
-                functools.partial(chip_kernel, parts=parts, width=width, own_first=False),
+                functools.partial(chip_kernel, parts=parts, width=width, own_first=False, chips=(2, last)),
                 [(after(x, out) if i == 0 else x, 0) for i, x in enumerate(got_a + a)],
                 [line_pairs],
                 blocks,
             )
             (y_chip,) = run(
-                chip_local_kernel,
+                functools.partial(chip_local_kernel, chips=(2, last)),
                 [(after(came_y, out), 0), (act, 1), (y_local, 1)] + [(x, 0) for x in a],
                 [line_vector],
                 blocks,
@@ -655,7 +671,8 @@
             )
         else:
             out = hop(arrivals[-1], [chip_a], y_chip, y_chip, at)
-        arrivals.append(lax.ppermute(out, "wall", hop_pairs(wall_count, at, at + 1)))
+        pairs = hop_pairs(wall_count, at, at + 1, relay={1: 0}.get(at))
+        arrivals.append(lax.ppermute(out, "wall", pairs))
         if at == 1:
             got_d = mates(after(sent_d, got_c, arrivals[-1]))
 
@@ -683,20 +700,20 @@
             aliases={5: 0} if held else {},
         )
 
-    entered = chosen(arrivals[:-1], list(range(1, last)))
-    held = turn(last - 1, last, after(entered, out))
-    arrivals[-1] = after(arrivals[-1], held[0])
-    held = turn(last, last + 1, arrivals[-1], held)
+    (chip_c,) = run(
+        functools.partial(chip_kernel, parts=1, width=width, own_first=True, chips=(1, last)),
+        [(after(got_c, out), 0), (c, 0)],
+        [line_pairs],
+        blocks,
+    )
+    arrivals[-1] = after(arrivals[-1], chip_c)
+    held = turn(last, last + 1, arrivals[-1])
+    entered = chosen(arrivals, list(range(1, last + 1)))
     x_chip = held[-1]
-    entered = chosen(arrivals, list(range(1, last + 1)))
     (out,) = run(functools.partial(send_kernel, last=last), [(x_chip, 0), (entered, 0)], [line_vector], blocks)
     arrived = [lax.ppermute(out, "wall", hop_pairs(wall_count, last, last - 1))]
-    (chip_c,) = run(
-        functools.partial(chip_kernel, parts=1, width=width, own_first=True),
-        [(after(got_c, x_chip), 0), (c, 0)],
-        [line_pairs],
-        blocks,
-    )
+    held = turn(last - 1, last, after(entered, out), held)
+    x_chip = held[-1]
     y = ()
     for at in range(last - 1, 0, -1):
         came = arrived[-1]
@@ -706,17 +723,24 @@
             y = steps(False, flow)
             came = after(came, *y)
         out = hop(came, [chip_c], x_chip, entered, at)
-        arrived.append(lax.ppermute(out, "wall", hop_pairs(wall_count, at, at - 1)))
-    (y,) = steps(True, arrived[-1], y)
+        arrived.append(lax.ppermute(out, "wall", hop_pairs(wall_count, at, at - 1, int(at > 1), {}.get(at))))
+    wall = lax.ppermute(out, "wall", hop_pairs(wall_count, 1, 0))
     beyond, left = run(
-        functools.partial(leave_kernel, chips=list(range(last - 1, -1, -1))),
-        [(x, 0) for x in (c, middle, *arrived)],
+        functools.partial(leave_kernel, chips=list(range(last - 1, 0, -1))),
+        [(x, 0) for x in (c, middle, *arrived[:-1])],
         [line_vector, line_vector],
         blocks,
     )
-    met_left = mates(left)
+    met_left = mates(after(left, out))
+    (y,) = steps(True, arrived[-1], y)
+    (wall_middle,) = run(
+        wall_middle_kernel, [(after(arrived[-1], wall), 0), (got_c, 0), (got_d, 0)], [line_vector], blocks
+    )
     (solution,) = run(
-        last_kernel, [(beyond, 0), (met_left, 0)] + [(x, 1) for x in (s, act, y)], [element_vectors], blocks
+        last_kernel,
+        [(beyond, 0), (met_left, 0), (wall_middle, 0), (wall, 0)] + [(x, 1) for x in (s, act, y)],
+        [element_vectors],
+        blocks,
     )
     return solution
 

time: 33.4 us -> 30.4 us (0.910)
  waiting for transfers between devices: 12.1 us -> 7.23 us
  starting transfers between devices: 8.61 us -> 13.4 us
  Pallas kernels: 12.2 us -> 9.48 us
    ppermute x4 -> x5, starting transfers between devices: 1.1 us -> 4.41 us  [the longest x2 3.8 us: per_device(): lax.ppermute(out, 'wall', hop_pairs(wall_count, at, at - 1, int(at > 1),...]
    ppermute x5, waiting for transfers between devices: 3.38 us -> 0.13 us  [mates(): return lax.ppermute(value, 'wall', [(i, i ^ 1) for i in range(wall_count)])]
    pallas_call x26 -> x25, Pallas kernels: 12.2 us -> 9.48 us  [run(): pl.pallas_call(kernel, grid=grid, in_specs=in_specs, out_specs=out_specs,...]
    ppermute x4 -> x5, waiting for transfers between devices: 8.34 us -> 6.26 us  [the longest x2 3.68 us: per_device(): arrivals.append(lax.ppermute(out, 'wall', pairs))]
    ppermute x5, starting transfers between devices: 2.15 us -> 3.86 us  [mates(): return lax.ppermute(value, 'wall', [(i, i ^ 1) for i in range(wall_count)])]
    ppermute x1, waiting for transfers between devices: 0.27 us -> 0.83 us  [per_device(): arrived = [lax.ppermute(out, 'wall', hop_pairs(wall_count, last, last - 1))]]
    ppermute x1, starting transfers between devices: 1.02 us -> 0.59 us  [per_device(): arrivals = [lax.ppermute(wall_leave, 'wall', hop_pairs(wall_count, 0, 1))]]
  transfers between devices with their start and end apart: 13 -> 14, of which waited for: 7 -> 7; matrix products, arithmetic and copies ran while one was open for 0% -> 0% of each run, Pallas kernels for 29% -> 23%
where the time goes in v6:
time: 30.4 us; the launch traced here: 30.3 us
  starting transfers between devices  13.4 us (44%)
  Pallas kernels  9.48 us (31%)
  waiting for transfers between devices  7.23 us (24%)
    pallas_call x25, Pallas kernels, run(): pl.pallas_call(kernel, grid=grid, in_specs=in_specs, out_specs=out_specs,...  9.48 us
    ppermute x5, starting transfers between devices, mates(): return lax.ppermute(value, 'wall', [(i, i ^ 1) for i in range(wall_count)])  3.86 us
    ppermute x2, starting transfers between devices, per_device(): lax.ppermute(out, 'wall', hop_pairs(wall_count, at, at - 1, int(at > 1),...  3.8 us
    ppermute x2, waiting for transfers between devices, per_device(): arrivals.append(lax.ppermute(out, 'wall', pairs))  3.68 us
    ppermute x1, starting transfers between devices, per_device(): lax.ppermute(state, 'surf', [(i, (i + 1) % surf_count) for i in range(sur...  2.13 us
    ppermute x1, starting transfers between devices, per_device(): lax.ppermute(state, 'surf', [((i + 1) % surf_count, i) for i in range(sur...  2.03 us
    ppermute x1, waiting for transfers between devices, per_device(): wall = lax.ppermute(out, 'wall', hop_pairs(wall_count, 1, 0))  1.71 us
    ppermute x2, waiting for transfers between devices, per_device(): lax.ppermute(out, 'wall', hop_pairs(wall_count, at, at - 1, int(at > 1),...  0.88 us
  transfers between devices with their start and end apart: 14, of which 7 were waited for; matrix products, arithmetic and copies ran while one was open for 0% of the time, Pallas kernels for 23%

profile of v6, /device:TPU:1, one launch (start us, length us, event | category | flops | bytes accessed | tf_op | source)
XLA Modules:
  0.0 30.3 jit_solution(6076529478044147333)
XLA Ops:
  0.0 2.1 %collective-permute-start = (bf16[16,162]{1,0:T(8,128)(2,1)}, bf16[16,162]{1,0:T(8,128)(2,1)S(1)}, u32[]{:S(2)}, u32[]{:S(2)}) collective-permute-start(bf16[16,162]{1,0:T(8,128)(2,1)} %refs_5_.1), channel_id=1, source_target_pairs={{0,1},{1,2},{2,3},{3,0},{4,5},{5,6},{6,7},{7,4},{8,9},{9,10},{10,1... | collective-permute-start | bytes 15560 | tf_op jit(solution)/shard_map/ppermute | solution.py:587
  2.1 2.0 %collective-permute-start.1 = (bf16[16,162]{1,0:T(8,128)(2,1)}, bf16[16,162]{1,0:T(8,128)(2,1)S(1)}, u32[]{:S(2)}, u32[]{:S(2)}) collective-permute-start(bf16[16,162]{1,0:T(8,128)(2,1)} %refs_5_.1), channel_id=1, source_target_pairs={{1,0},{2,1},{3,2},{0,3},{5,4},{6,5},{7,6},{4,7},{9,8},{10,9},{11,1... | collective-permute-start | bytes 15560 | tf_op jit(solution)/shard_map/ppermute | solution.py:588
  4.2 2.5 %shard_map.100 = (bf16[48,48]{1,0:T(8,128)(2,1)S(1)}, f32[16,162]{1,0:T(8,128)S(1)}, f32[2,8,162]{2,1,0:T(8,128)S(1)}, bf16[16,162]{1,0:T(8,128)(2,1)S(1)}, bf16...) custom-call(s32[2,8]{1,0:T(2,128)} %refs_0_.1, s32[8]{0:T(128)} %refs_1_.1, f32[4,16]{1,0:T(4,128)} %bitcast.8, ...), custom_call_target="tpu_custom_call" | custom-call | flops 1 | bytes 1 | tf_op jit(solution)/shard_map/pallas_call | solution.py:497
  6.7 0.0 collective-permute-done.before
  6.7 0.0 collective-permute-done.1.after
  6.7 0.2 shard_map.101.rhs_ref
  6.9 0.9 %shard_map.102 = (f32[2,8,162]{2,1,0:T(8,128)S(1)}, f32[2,8,162]{2,1,0:T(8,128)S(1)}, f32[8,162]{1,0:T(8,128)S(1)}) custom-call(f32[2,8,162]{2,1,0:T(8,128)S(1)} %shard_map.101.rhs_ref, bf16[2,2,8,162,162]{4,3,2,1,0:T(8,128)(2,1)S(1)} %get-tuple-element.65.raw_ref, f32[2,8,162]{2,1,0:T(8,128)S(1)} %get-tuple-element.58.act_ref), custom_call_target="tpu_custom_call" | custom-call | flops 1 | bytes 1 | tf_op jit(solution)/shard_map/pallas_call | solution.py:497
  7.9 1.0 %collective-permute-start.2 = (f32[8,162]{1,0:T(8,128)S(1)}, f32[8,162]{1,0:T(8,128)S(1)}, u32[]{:S(2)}, u32[]{:S(2)}) collective-permute-start(f32[8,162]{1,0:T(8,128)S(1)} %get-tuple-element.59), channel_id=1, source_target_pairs={{0,4},{4,0},{8,12},{12,8},{16,20},{20,16},{24,28},{28,24},{1,5},{5... | collective-permute-start | bytes 15560 | tf_op jit(solution)/shard_map/ppermute | solution.py:548
  8.9 1.3 %shard_map.103 = (bf16[2,8,2,162,162]{4,3,2,1,0:T(8,128)(2,1)S(1)}, bf16[8,2,162,162]{3,2,1,0:T(8,128)(2,1)S(1)}, bf16[1408,384]{1,0:T(8,128)(2,1)S(1)}, bf16[1,2,162,8,162]{4,3,2,1,0:T(8,128)(2,1)S(1)}) custom-call(bf16[2,2,8,162,162]{4,3,2,1,0:T(8,128)(2,1)S(1)} %get-tuple-element.65.raw_ref, bf16[2,162,8,162]{3,2,1,0:T(8,128)(2,1)} %bitcast.7), custom_call_target="tpu_custom_call" | custom-call | flops 1 | bytes 1 | tf_op jit(solution)/shard_map/pallas_call | solution.py:497
  10.2 0.0 collective-permute-done.2.came_ref.mate_ref
  10.2 0.1 collective-permute-start.4
  10.3 1.1 %shard_map.104 = (f32[2,8,162]{2,1,0:T(8,128)S(1)}, f32[8,162]{1,0:T(8,128)S(1)}) custom-call(f32[8,162]{1,0:T(8,128)S(1)} %collective-permute-done.2.came_ref.mate_ref, f32[2,8,162]{2,1,0:T(8,128)S(1)} %get-tuple-element.62.scaled_ref, bf16[2,2,8,162,162]{4,3,2,1,0:T(8,128)(2,1)S(1)} %get-tuple-element.65.raw_ref, ...), custom_call_target="tpu_custom_call" | custom-call | flops 1 | bytes 1 | tf_op jit(solution)/shard_map/pallas_call | solution.py:497
  11.4 0.6 %collective-permute-start.3 = (f32[8,162]{1,0:T(8,128)S(1)}, f32[8,162]{1,0:T(8,128)S(1)}, u32[]{:S(2)}, u32[]{:S(2)}) collective-permute-start(f32[8,162]{1,0:T(8,128)S(1)} %get-tuple-element.64), channel_id=1, source_target_pairs={{0,4},{4,12},{8,0},{12,8},{16,20},{20,16},{24,28},{28,24},{1,5},{5... | collective-permute-start | bytes 15560 | tf_op jit(solution)/shard_map/ppermute | solution.py:608
  12.0 1.8 %shard_map.105 = (bf16[2,8,2,162,162]{4,3,2,1,0:T(8,128)(2,1)S(1)}, bf16[8,2,162,162]{3,2,1,0:T(8,128)(2,1)S(1)}, bf16[1408,384]{1,0:T(8,128)(2,1)S(1)}) custom-call(bf16[2,2,8,162,162]{4,3,2,1,0:T(8,128)(2,1)S(1)} %get-tuple-element.65.raw_ref, bf16[1,2,162,8,162]{4,3,2,1,0:T(8,128)(2,1)S(1)} %get-tuple-element.66.refs_0_), custom_call_target="tpu_custom_call" | custom-call | flops 1 | bytes 1 | tf_op jit(solution)/shard_map/pallas_call | solution.py:497
  13.8 0.0 collective-permute-done.3.came_ref.refs_0_
  13.8 0.0 collective-permute-done.4.refs_0_
  13.8 0.6 %collective-permute-start.7 = (bf16[1408,384]{1,0:T(8,128)(2,1)S(1)}, bf16[1408,384]{1,0:T(8,128)(2,1)S(1)}, u32[]{:S(2)}, u32[]{:S(2)}) collective-permute-start(bf16[1408,384]{1,0:T(8,128)(2,1)S(1)} %get-tuple-element.73), channel_id=1, source_target_pairs={{0,4},{4,0},{8,12},{12,8},{16,20},{20,16},{24,28},{28,24},{1,5},{5... | collective-permute-start | bytes 3244040 | tf_op jit(solution)/shard_map/ppermute | solution.py:548
  14.4 0.5 %collective-permute-start.5 = (f32[8,162]{1,0:T(8,128)S(1)}, f32[8,162]{1,0:T(8,128)S(1)}, u32[]{:S(2)}, u32[]{:S(2)}) collective-permute-start(f32[8,162]{1,0:T(8,128)S(1)} %shard_map.106), channel_id=1, source_target_pairs={{0,4},{4,8},{8,12},{12,20},{16,0},{20,16},{24,28},{28,24},{1,5},{5... | collective-permute-start | bytes 15560 | tf_op jit(solution)/shard_map/ppermute | solution.py:675
  15.0 0.3 %shard_map.112 = (bf16[8,2,162,162]{3,2,1,0:T(8,128)(2,1)S(1)}, bf16[1456,384]{1,0:T(8,128)(2,1)S(1)}, f32[8,162]{1,0:T(8,128)S(1)}) custom-call(f32[2,8,162]{2,1,0:T(8,128)S(1)} %get-tuple-element.58.act_ref, bf16[2,8,2,162,162]{4,3,2,1,0:T(8,128)(2,1)S(1)} %get-tuple-element.77.q_ref, bf16[2,8,2,162,162]{4,3,2,1,0:T(8,128)(2,1)S(1)} %get-tuple-element.78.s_ref, ...), custom_call_target="tpu_custom_call" | custom-call | flops 1 | bytes 1 | tf_op jit(solution)/shard_map/pallas_call | solution.py:497
  15.3 1.4 %collective-permute-done.5.came_ref.refs_1_ = f32[8,162]{1,0:T(8,128)S(1)} collective-permute-done((f32[8,162]{1,0:T(8,128)S(1)}, f32[8,162]{1,0:T(8,128)S(1)}, u32[]{:S(2)}, u32[]{:S(2)}) %collective-permute-start.5) | collective-permute-done | bytes 5216 | tf_op jit(solution)/shard_map/ppermute | solution.py:675
  16.7 0.1 collective-permute-done.7.refs_0_.got_c
  16.8 1.4 %collective-permute-start.8 = (bf16[1456,384]{1,0:T(8,128)(2,1)S(1)}, bf16[1456,384]{1,0:T(8,128)(2,1)S(1)}, u32[]{:S(2)}, u32[]{:S(2)}) collective-permute-start(bf16[1456,384]{1,0:T(8,128)(2,1)S(1)} %get-tuple-element.82), channel_id=1, source_target_pairs={{0,4},{4,0},{8,12},{12,8},{16,20},{20,16},{24,28},{28,24},{1,5},{5... | collective-permute-start | bytes 3354632 | tf_op jit(solution)/shard_map/ppermute | solution.py:548
  18.2 0.1 collective-permute-start.6
  18.3 2.3 %collective-permute-done.6.refs_2_.enter_ref = f32[8,162]{1,0:T(8,128)S(1)} collective-permute-done((f32[8,162]{1,0:T(8,128)S(1)}, f32[8,162]{1,0:T(8,128)S(1)}, u32[]{:S(2)}, u32[]{:S(2)}) %collective-permute-start.6) | collective-permute-done | bytes 5216 | tf_op jit(solution)/shard_map/ppermute | solution.py:675
  20.6 0.0 collective-permute-done.8.got_d
  20.7 0.4 %collective-permute-start.9 = (f32[8,162]{1,0:T(8,128)S(1)}, f32[8,162]{1,0:T(8,128)S(1)}, u32[]{:S(2)}, u32[]{:S(2)}) collective-permute-start(f32[8,162]{1,0:T(8,128)S(1)} %shard_map.114), channel_id=1, source_target_pairs={{0,4},{4,0},{8,12},{12,8},{16,24},{20,16},{24,28},{28,20},{1,5},{5... | collective-permute-start | bytes 15560 | tf_op jit(solution)/shard_map/ppermute | solution.py:714
  21.1 0.8 %collective-permute-done.9.came_ref.refs_0_ = f32[8,162]{1,0:T(8,128)S(1)} collective-permute-done((f32[8,162]{1,0:T(8,128)S(1)}, f32[8,162]{1,0:T(8,128)S(1)}, u32[]{:S(2)}, u32[]{:S(2)}) %collective-permute-start.9) | collective-permute-done | bytes 5216 | tf_op jit(solution)/shard_map/ppermute | solution.py:714
  21.9 0.3 %collective-permute-start.10 = (f32[8,162]{1,0:T(8,128)S(1)}, f32[8,162]{1,0:T(8,128)S(1)}, u32[]{:S(2)}, u32[]{:S(2)}) collective-permute-start(f32[8,162]{1,0:T(8,128)S(1)} %shard_map.116), channel_id=1, source_target_pairs={{0,4},{4,0},{8,16},{12,8},{16,20},{20,12},{24,28},{28,24},{1,5},{5... | collective-permute-start | bytes 15560 | tf_op jit(solution)/shard_map/ppermute | solution.py:726
  22.3 0.8 %collective-permute-done.10.refs_1_.came_ref = f32[8,162]{1,0:T(8,128)S(1)} collective-permute-done((f32[8,162]{1,0:T(8,128)S(1)}, f32[8,162]{1,0:T(8,128)S(1)}, u32[]{:S(2)}, u32[]{:S(2)}) %collective-permute-start.10) | collective-permute-done | bytes 5216 | tf_op jit(solution)/shard_map/ppermute | solution.py:726
  23.1 3.5 %collective-permute-start.12 = (f32[8,162]{1,0:T(8,128)S(1)}, f32[8,162]{1,0:T(8,128)S(1)}, u32[]{:S(2)}, u32[]{:S(2)}) collective-permute-start(f32[8,162]{1,0:T(8,128)S(1)} %shard_map.121), channel_id=1, source_target_pairs={{0,4},{4,8},{8,12},{12,0},{16,20},{20,16},{24,28},{28,24},{1,5},{5... | collective-permute-start | bytes 15560 | tf_op jit(solution)/shard_map/ppermute | solution.py:726
  26.5 0.0 collective-permute-start.13
  26.6 0.7 %collective-permute-start.11 = (f32[8,162]{1,0:T(8,128)S(1)}, f32[8,162]{1,0:T(8,128)S(1)}, u32[]{:S(2)}, u32[]{:S(2)}) collective-permute-start(f32[8,162]{1,0:T(8,128)S(1)} %get-tuple-element.99), channel_id=1, source_target_pairs={{0,4},{4,0},{8,12},{12,8},{16,20},{20,16},{24,28},{28,24},{1,5},{5... | collective-permute-start | bytes 15560 | tf_op jit(solution)/shard_map/ppermute | solution.py:548
  27.3 0.1 collective-permute-done.12.came_ref.flow_ref
  27.3 1.7 %collective-permute-done.13.wall_ref = f32[8,162]{1,0:T(8,128)S(1)} collective-permute-done((f32[8,162]{1,0:T(8,128)S(1)}, f32[8,162]{1,0:T(8,128)S(1)}, u32[]{:S(2)}, u32[]{:S(2)}) %collective-permute-start.13) | collective-permute-done | bytes 5216 | tf_op jit(solution)/shard_map/ppermute | solution.py:727
  29.0 0.0 collective-permute-done.11.met_ref
  29.1 1.2 %shard_map.124 = f32[2,8,162]{2,1,0:T(8,128)} custom-call(f32[8,162]{1,0:T(8,128)S(1)} %get-tuple-element.93.beyond_ref, f32[8,162]{1,0:T(8,128)S(1)} %collective-permute-done.11.met_ref, f32[8,162]{1,0:T(8,128)S(1)} %shard_map.122.middle_ref, f32[8,162]{1,0:T(8,128)S(1)} %collective-permute-done.13.wall_ref, ...), custom_call_target="tpu_custom_call" | custom-call | flops 1 | bytes 1 | tf_op jit(solution)/shard_map/pallas_call | solution.py:497
  (17 shorter events, 0.1 us)
Async XLA Ops:
  0.0 6.7 %collective-permute-start = (bf16[16,162]{1,0:T(8,128)(2,1)}, bf16[16,162]{1,0:T(8,128)(2,1)S(1)}, u32[]{:S(2)}, u32[]{:S(2)}) collective-permute-start(bf16[16,162]{1,0:T(8,128)(2,1)} %refs_5_.1), channel_id=1, source_target_pairs={{0,1},{1,2},{2,3},{3,0},{4,5},{5,6},{6,7},{7,4},{8,9},{9,10},{10,1... | collective-permute-start | bytes 15560 | tf_op jit(solution)/shard_map/ppermute | solution.py:587
  2.1 4.6 %collective-permute-start.1 = (bf16[16,162]{1,0:T(8,128)(2,1)}, bf16[16,162]{1,0:T(8,128)(2,1)S(1)}, u32[]{:S(2)}, u32[]{:S(2)}) collective-permute-start(bf16[16,162]{1,0:T(8,128)(2,1)} %refs_5_.1), channel_id=1, source_target_pairs={{1,0},{2,1},{3,2},{0,3},{5,4},{6,5},{7,6},{4,7},{9,8},{10,9},{11,1... | collective-permute-start | bytes 15560 | tf_op jit(solution)/shard_map/ppermute | solution.py:588
  7.9 2.3 %collective-permute-start.2 = (f32[8,162]{1,0:T(8,128)S(1)}, f32[8,162]{1,0:T(8,128)S(1)}, u32[]{:S(2)}, u32[]{:S(2)}) collective-permute-start(f32[8,162]{1,0:T(8,128)S(1)} %get-tuple-element.59), channel_id=1, source_target_pairs={{0,4},{4,0},{8,12},{12,8},{16,20},{20,16},{24,28},{28,24},{1,5},{5... | collective-permute-start | bytes 15560 | tf_op jit(solution)/shard_map/ppermute | solution.py:548
  10.2 3.6 %collective-permute-start.4 = (bf16[1408,384]{1,0:T(8,128)(2,1)S(1)}, bf16[1408,384]{1,0:T(8,128)(2,1)S(1)}, u32[]{:S(2)}, u32[]{:S(2)}) collective-permute-start(bf16[1408,384]{1,0:T(8,128)(2,1)S(1)} %get-tuple-element.69), channel_id=1, source_target_pairs={{0,4},{4,0},{8,12},{12,8},{16,20},{20,16},{24,28},{28,24},{1,5},{5... | collective-permute-start | bytes 3244040 | tf_op jit(solution)/shard_map/ppermute | solution.py:548
  11.4 2.4 %collective-permute-start.3 = (f32[8,162]{1,0:T(8,128)S(1)}, f32[8,162]{1,0:T(8,128)S(1)}, u32[]{:S(2)}, u32[]{:S(2)}) collective-permute-start(f32[8,162]{1,0:T(8,128)S(1)} %get-tuple-element.64), channel_id=1, source_target_pairs={{0,4},{4,12},{8,0},{12,8},{16,20},{20,16},{24,28},{28,24},{1,5},{5... | collective-permute-start | bytes 15560 | tf_op jit(solution)/shard_map/ppermute | solution.py:608
  13.8 3.0 %collective-permute-start.7 = (bf16[1408,384]{1,0:T(8,128)(2,1)S(1)}, bf16[1408,384]{1,0:T(8,128)(2,1)S(1)}, u32[]{:S(2)}, u32[]{:S(2)}) collective-permute-start(bf16[1408,384]{1,0:T(8,128)(2,1)S(1)} %get-tuple-element.73), channel_id=1, source_target_pairs={{0,4},{4,0},{8,12},{12,8},{16,20},{20,16},{24,28},{28,24},{1,5},{5... | collective-permute-start | bytes 3244040 | tf_op jit(solution)/shard_map/ppermute | solution.py:548
  14.4 2.2 %collective-permute-start.5 = (f32[8,162]{1,0:T(8,128)S(1)}, f32[8,162]{1,0:T(8,128)S(1)}, u32[]{:S(2)}, u32[]{:S(2)}) collective-permute-start(f32[8,162]{1,0:T(8,128)S(1)} %shard_map.106), channel_id=1, source_target_pairs={{0,4},{4,8},{8,12},{12,20},{16,0},{20,16},{24,28},{28,24},{1,5},{5... | collective-permute-start | bytes 15560 | tf_op jit(solution)/shard_map/ppermute | solution.py:675
  16.8 3.8 %collective-permute-start.8 = (bf16[1456,384]{1,0:T(8,128)(2,1)S(1)}, bf16[1456,384]{1,0:T(8,128)(2,1)S(1)}, u32[]{:S(2)}, u32[]{:S(2)}) collective-permute-start(bf16[1456,384]{1,0:T(8,128)(2,1)S(1)} %get-tuple-element.82), channel_id=1, source_target_pairs={{0,4},{4,0},{8,12},{12,8},{16,20},{20,16},{24,28},{28,24},{1,5},{5... | collective-permute-start | bytes 3354632 | tf_op jit(solution)/shard_map/ppermute | solution.py:548
  18.2 2.4 %collective-permute-start.6 = (f32[8,162]{1,0:T(8,128)S(1)}, f32[8,162]{1,0:T(8,128)S(1)}, u32[]{:S(2)}, u32[]{:S(2)}) collective-permute-start(f32[8,162]{1,0:T(8,128)S(1)} %shard_map.109), channel_id=1, source_target_pairs={{0,4},{4,0},{8,12},{12,8},{16,20},{20,28},{24,16},{28,24},{1,5},{5... | collective-permute-start | bytes 15560 | tf_op jit(solution)/shard_map/ppermute | solution.py:675
  20.7 1.3 %collective-permute-start.9 = (f32[8,162]{1,0:T(8,128)S(1)}, f32[8,162]{1,0:T(8,128)S(1)}, u32[]{:S(2)}, u32[]{:S(2)}) collective-permute-start(f32[8,162]{1,0:T(8,128)S(1)} %shard_map.114), channel_id=1, source_target_pairs={{0,4},{4,0},{8,12},{12,8},{16,24},{20,16},{24,28},{28,20},{1,5},{5... | collective-permute-start | bytes 15560 | tf_op jit(solution)/shard_map/ppermute | solution.py:714
  21.9 1.2 %collective-permute-start.10 = (f32[8,162]{1,0:T(8,128)S(1)}, f32[8,162]{1,0:T(8,128)S(1)}, u32[]{:S(2)}, u32[]{:S(2)}) collective-permute-start(f32[8,162]{1,0:T(8,128)S(1)} %shard_map.116), channel_id=1, source_target_pairs={{0,4},{4,0},{8,16},{12,8},{16,20},{20,12},{24,28},{28,24},{1,5},{5... | collective-permute-start | bytes 15560 | tf_op jit(solution)/shard_map/ppermute | solution.py:726
  23.1 4.3 %collective-permute-start.12 = (f32[8,162]{1,0:T(8,128)S(1)}, f32[8,162]{1,0:T(8,128)S(1)}, u32[]{:S(2)}, u32[]{:S(2)}) collective-permute-start(f32[8,162]{1,0:T(8,128)S(1)} %shard_map.121), channel_id=1, source_target_pairs={{0,4},{4,8},{8,12},{12,0},{16,20},{20,16},{24,28},{28,24},{1,5},{5... | collective-permute-start | bytes 15560 | tf_op jit(solution)/shard_map/ppermute | solution.py:726
  26.5 2.5 %collective-permute-start.13 = (f32[8,162]{1,0:T(8,128)S(1)}, f32[8,162]{1,0:T(8,128)S(1)}, u32[]{:S(2)}, u32[]{:S(2)}) collective-permute-start(f32[8,162]{1,0:T(8,128)S(1)} %shard_map.121), channel_id=1, source_target_pairs={{0,8},{4,0},{8,12},{12,4},{16,20},{20,16},{24,28},{28,24},{1,9},{5... | collective-permute-start | bytes 15560 | tf_op jit(solution)/shard_map/ppermute | solution.py:727
  26.6 2.5 %collective-permute-start.11 = (f32[8,162]{1,0:T(8,128)S(1)}, f32[8,162]{1,0:T(8,128)S(1)}, u32[]{:S(2)}, u32[]{:S(2)}) collective-permute-start(f32[8,162]{1,0:T(8,128)S(1)} %get-tuple-element.99), channel_id=1, source_target_pairs={{0,4},{4,0},{8,12},{12,8},{16,20},{20,16},{24,28},{28,24},{1,5},{5... | collective-permute-start | bytes 15560 | tf_op jit(solution)/shard_map/ppermute | solution.py:548

commit v7 on v6

--- a/solution.py
+++ b/solution.py
@@ -112,35 +112,40 @@
 
 def pair_kernel(raw_ref, *refs, first_chip, fetch, turn, **options):
     if fetch:
-        next_ref, landed, arrived = refs[0], refs[4], refs[-1]
+        next_ref, landed_ref, *outs, landed, turned_ref, arrived = refs
         copies = [
             pltpu.make_async_copy(next_ref.at[e], landed.at[0, e], arrived.at[e]) for e in range(next_ref.shape[0])
         ]
         for copy in copies:
             copy.start()
-        refs = refs[1:4]
-    other_ref = raw_ref
-    if turn:
-        other_ref = refs[-1]
+        turn_blocks(landed_ref, 0, 0, turned_ref)
+    elif turn:
+        landed_ref, *outs, turned_ref = refs
         for e in range(raw_ref.shape[1]):
-            turn_blocks(refs[0], 0, e, other_ref)
-        refs = refs[1:4]
+            turn_blocks(landed_ref, 0, e, turned_ref)
+    else:
+        outs = refs
+
+    def other(e, l):
+        if turn or (fetch and e == 0):
+            return turned_ref[0, e, l]
+        return raw_ref[options["kind"], e, l]
 
     @pl.when(chip_of() >= first_chip)
     def _():
-        make_pairs(raw_ref, other_ref, *refs[-3:], **options)
+        make_pairs(raw_ref, other, *outs, lines=options["lines"], ascending=options["ascending"])
 
     if fetch:
         for copy in copies:
             copy.wait()
 
 
-def make_pairs(raw_ref, other_ref, step_ref, whole_ref, sent_ref, *, kind, lines, ascending):
+def make_pairs(raw_ref, other, step_ref, whole_ref, sent_ref, *, lines, ascending):
     count, width = raw_ref.shape[1], raw_ref.shape[3]
     for l in range(*lines):
         for e in range(count):
             block = lax.dot_general(
-                other_ref[kind, e, l], raw_ref[0, e, l], (((0,), (1,)), ((), ())), preferred_element_type=F32
+                other(e, l), raw_ref[0, e, l], (((0,), (1,)), ((), ())), preferred_element_type=F32
             )
             store_pair(step_ref, split2(block), e, l)
     order = list(range(count)) if ascending else list(range(count))[::-1]
@@ -182,10 +187,9 @@
     block_copies = []
     if taken:
         raw_ref, landed, landed_at = refs[12 + taken], refs[-2], refs[-1]
+        places_in = [(a, e) for a in range(taken) for e in range(landed.shape[1]) if (a, e) != (1, 0)]
         block_copies = [
-            pltpu.make_async_copy(ref.at[e], landed.at[a, e], landed_at.at[a, e])
-            for a, ref in enumerate(blocks)
-            for e in range(landed.shape[1])
+            pltpu.make_async_copy(blocks[a].at[e], landed.at[a, e], landed_at.at[a, e]) for a, e in places_in
         ]
     for copy in copies + block_copies:
         copy.start()
@@ -226,19 +230,23 @@
         act_ref[g] = (place + g < length).astype(F32)
     for i, copy in enumerate(block_copies):
         copy.wait()
-        turn_blocks(landed, *divmod(i, landed.shape[1]), raw_ref)
-
-
-def residual_kernel(before, state, after, weight, source, lift, rhs_ref):
+        turn_blocks(landed, *places_in[i], raw_ref)
+
+
+def residual(before, state, after, weight, source, lift, depth):
     cells = jnp.concatenate([before[...], state[...], after[...]], axis=0)
     parts = jnp.dot(weight[...], cells, preferred_element_type=F32)
     count = source.shape[0]
     face_sum = parts[:count] + (parts[count : 2 * count] + parts[2 * count :])
     flux = jnp.dot(face_sum.astype(BF16), lift[...], preferred_element_type=F32)
     rhs = source[...] - flux
-    depth, lines, _ = rhs_ref.shape
-    for g in range(depth):
-        rhs_ref[g] = rhs[g * lines : (g + 1) * lines]
+    lines = count // depth
+    return [rhs[g * lines : (g + 1) * lines] for g in range(depth)]
+
+
+def residual_kernel(before, state, after, weight, source, lift, rhs_ref):
+    for g, rhs in enumerate(residual(before, state, after, weight, source, lift, rhs_ref.shape[0])):
+        rhs_ref[g] = rhs
 
 
 def forward_local(scaled, q_ref, act_ref, carried):
@@ -262,34 +270,47 @@
     return solved
 
 
-def local_kernel(rhs_ref, raw_ref, act_ref, scaled_ref, y_ref, leave_ref):
-    depth = rhs_ref.shape[0]
-    scaled = [apply_rows(rhs_ref[g], raw_ref, 0, g) for g in range(depth)]
-    values = raw_steps(scaled, raw_ref, act_ref, None)
+def local_kernel(*refs, merged):
+    if merged:
+        *cells, raw_ref, act_ref, lower_in, scaled_ref, y_ref, leave_ref, landed_ref, arrived = refs
+        copy = pltpu.make_async_copy(lower_in.at[0], landed_ref.at[0, 0], arrived)
+        copy.start()
+        rhs = residual(*cells, scaled_ref.shape[0])
+    else:
+        rhs_ref, raw_ref, act_ref, scaled_ref, y_ref, leave_ref = refs
+        rhs = [rhs_ref[g] for g in range(rhs_ref.shape[0])]
+    depth = len(rhs)
+    scaled = [apply_rows(rhs[g], raw_ref, 0, g) for g in range(depth)]
+    values = raw_steps(scaled, raw_ref, None, act_ref, None)
     for g in range(depth):
         scaled_ref[g] = scaled[g]
         y_ref[g] = values[g]
     leave_ref[...] = values[-1]
-
-
-def raw_steps(scaled, raw_ref, act_ref, carried):
+    if merged:
+        copy.wait()
+
+
+def raw_steps(scaled, raw_ref, first_ref, act_ref, carried):
     values = []
     for g, value in enumerate(scaled):
         if carried is not None:
-            value = value - apply_rows(apply_rows(carried, raw_ref, 1, g), raw_ref, 0, g)
+            at = (first_ref, 0, 0) if first_ref is not None and g == 0 else (raw_ref, 1, g)
+            value = value - apply_rows(apply_rows(carried, *at), raw_ref, 0, g)
         carried = act_ref[g] * value
         values.append(carried)
     return values
 
 
-def wall_kernel(came_ref, scaled_ref, raw_ref, act_ref, y_ref, out_ref, leave_ref):
+def wall_kernel(came_ref, scaled_ref, raw_ref, act_ref, y_ref, *refs):
+    out_ref, leave_ref = refs[-2:]
+    first_ref = refs[0] if len(refs) > 2 else None
     depth = y_ref.shape[0]
     out_ref[...] = y_ref[...]
     leave_ref[...] = y_ref[depth - 1]
 
     @pl.when(lax.axis_index("wall") == 1)
     def _():
-        values = raw_steps([scaled_ref[g] for g in range(depth)], raw_ref, act_ref, came_ref[...])
+        values = raw_steps([scaled_ref[g] for g in range(depth)], raw_ref, first_ref, act_ref, came_ref[...])
         for g in range(depth):
             out_ref[g] = values[g]
         leave_ref[...] = values[-1]
@@ -378,6 +399,9 @@
 def turn_kernel(enter_ref, came_ref, echo_ref, got_c, got_d, own_d, *refs, parts, chips, fill):
     got_refs, (enter_y, mid_ref, out_ref) = refs[:parts], refs[-3:]
     inside = jnp.logical_and(chip_of() >= chips[0], chip_of() < chips[1])
+    if not fill:
+        for held, ref in zip(refs[parts:], refs[-3:]):
+            ref[...] = held[...]
     if fill:
 
         @pl.when(jnp.logical_not(inside))
@@ -405,18 +429,14 @@
     out_ref[...] = jnp.where(chip_of() == last, x_ref[...], enter_ref[...])
 
 
-def steps_kernel(flow_ref, scaled_ref, q_ref, act_ref, wall_ref, *refs, late):
-    y_ref = refs[-1]
+def steps_kernel(flow_ref, scaled_ref, q_ref, act_ref, held_ref, y_ref, *, late):
     depth = scaled_ref.shape[0]
     here, core = chip_of(), core_of()
+    y_ref[...] = held_ref[...]
     if late:
         inside = jnp.logical_and(core == 0, here > 1)
     else:
         inside = jnp.logical_and(here > 0, jnp.logical_or(core == 1, here == 1))
-
-        @pl.when(here == 0)
-        def _():
-            y_ref[...] = wall_ref[...]
 
     @pl.when(inside)
     def _():
@@ -586,45 +606,48 @@
     )
     before = lax.ppermute(state, "surf", [(i, (i + 1) % surf_count) for i in range(surf_count)])
     beyond = lax.ppermute(state, "surf", [((i + 1) % surf_count, i) for i in range(surf_count)])
-    (rhs,) = run(
-        residual_kernel,
-        [(x, None) for x in (before, near_state, beyond, weight, line_source, near_lift)],
-        [element_vectors],
-    )
+    cells = [(x, None) for x in (before, near_state, beyond, weight, line_source, near_lift)]
     raw = landed[0] if in_place else jnp.stack([dinv, lower, upper])
-    scaled, y_local, y_leave = run(
-        local_kernel,
-        [(rhs, 1), (raw, 2), (act, 1)],
-        [element_vectors, element_vectors, line_vector],
-        blocks,
-    )
+    vectors = [element_vectors, element_vectors, line_vector]
+    if in_place:
+        scaled, y_local, y_leave, first_lower = run(
+            functools.partial(local_kernel, merged=True),
+            cells + [(raw, None), (act, None), (blocks_in[1], ANY)],
+            vectors + [((1, 1, width, lines, width), BF16, None)],
+            scratch=[pltpu.SemaphoreType.DMA(())],
+        )
+    else:
+        (rhs,) = run(residual_kernel, cells, [element_vectors])
+        scaled, y_local, y_leave = run(
+            functools.partial(local_kernel, merged=False), [(rhs, 1), (raw, 2), (act, 1)], vectors, blocks
+        )
     came_y = mates(y_leave)
-    wall_y, wall_leave = run(
-        wall_kernel,
-        [(came_y, 0), (scaled, 1), (raw, 2), (act, 1), (y_local, 1)],
-        [element_vectors, line_vector],
-        blocks,
-    )
-    arrivals = [lax.ppermute(wall_leave, "wall", hop_pairs(wall_count, 0, 1))]
     q, *rest = run(
         functools.partial(
             pair_kernel, first_chip=1, fetch=in_place, turn=False, kind=1, lines=(0, block), ascending=True
         ),
-        [(after(raw, y_leave), 2)] + ([(blocks_in[2], ANY)] if in_place else []),
-        [element_pairs, line_pairs, line_sent] + ([((1, *blocks_in[2].shape), BF16, None)] if in_place else []),
+        [(after(raw, y_leave), 2)]
+        + ([(blocks_in[2], ANY), (first_lower, None)] if in_place else []),
+        [element_pairs, line_pairs, line_sent]
+        + (
+            [((1, depth, width, lines, width), BF16, None), ((1, 1, lines, width, width), BF16, None)]
+            if in_place
+            else []
+        ),
         blocks,
         [pltpu.SemaphoreType.DMA((depth,))] if in_place else [],
     )
+    wall_y, wall_leave = run(
+        wall_kernel,
+        [(came_y, 0), (scaled, 1), (raw, 2), (act, 1), (y_local, 1)] + [(x, 2) for x in rest[3:]],
+        [element_vectors, line_vector],
+        blocks,
+    )
+    arrivals = [lax.ppermute(wall_leave, "wall", hop_pairs(wall_count, 0, 1))]
     a, got_a = [rest[0]], [mates(after(rest[1], came_y))]
     s, c, sent_c = run(
         functools.partial(
-            pair_kernel,
-            first_chip=0,
-            fetch=False,
-            turn=in_place,
-            kind=0 if in_place else 2,
-            lines=(0, block),
-            ascending=False,
+            pair_kernel, first_chip=0, fetch=False, turn=in_place, kind=2, lines=(0, block), ascending=False
         ),
         [(after(raw, a[-1], wall_leave), 2)] + ([(rest[2], None)] if in_place else []),
         [element_pairs, line_pairs, line_sent],
@@ -685,19 +708,17 @@
         return run(
             functools.partial(turn_kernel, parts=parts, chips=(first_chip, end_chip), fill=not held),
             [(x, 0) for x in (entered, came_y, echo, got_c, got_d, through, *got_a)]
-            + [(x, ANY) for x in held],
+            + [(x, 0) for x in held],
             [line_vector] * 3,
             blocks,
-            aliases={6 + parts + i: i for i in range(3)} if held else {},
         )
 
-    def steps(late, flow, held=()):
+    def steps(late, flow, held):
         return run(
             functools.partial(steps_kernel, late=late),
-            [(flow, 0)] + [(x, 1) for x in (scaled, q, act, wall_y)] + [(x, ANY) for x in held],
+            [(flow, 0)] + [(x, 1) for x in (scaled, q, act, held)],
             [element_vectors],
             blocks,
-            aliases={5: 0} if held else {},
         )
 
     (chip_c,) = run(
@@ -714,16 +735,18 @@
     arrived = [lax.ppermute(out, "wall", hop_pairs(wall_count, last, last - 1))]
     held = turn(last - 1, last, after(entered, out), held)
     x_chip = held[-1]
-    y = ()
+    enter_y, middle, _ = held
+    y = wall_y
     for at in range(last - 1, 0, -1):
         came = arrived[-1]
+        if at == last - 2:
+            enter_y, middle, x_chip = turn(1, last - 1, after(entered, out), held)
         if at == 1:
-            enter_y, middle, x_chip = turn(1, last - 1, after(entered, out), held)
             (flow,) = run(entry_kernel, [(enter_y, 0), (after(arrived[0], out), 0)], [line_vector], blocks)
-            y = steps(False, flow)
-            came = after(came, *y)
+            (y,) = steps(False, flow, wall_y)
+            came = after(came, y)
         out = hop(came, [chip_c], x_chip, entered, at)
-        arrived.append(lax.ppermute(out, "wall", hop_pairs(wall_count, at, at - 1, int(at > 1), {}.get(at))))
+        arrived.append(lax.ppermute(out, "wall", hop_pairs(wall_count, at, at - 1, int(at > 1))))
     wall = lax.ppermute(out, "wall", hop_pairs(wall_count, 1, 0))
     beyond, left = run(
         functools.partial(leave_kernel, chips=list(range(last - 1, 0, -1))),

time: 30.4 us -> 30.3 us (level)
  starting transfers between devices: 13.4 us -> 13.8 us
  Pallas kernels: 9.48 us -> 9.16 us
    pallas_call x25 -> x24, Pallas kernels: 9.48 us -> 9.16 us  [run(): pl.pallas_call(kernel, grid=grid, in_specs=in_specs, out_specs=out_specs,...]
  transfers between devices with their start and end apart: 14 -> 14, of which waited for: 7 -> 6; matrix products, arithmetic and copies ran while one was open for 0% -> 0% of each run, Pallas kernels for 23% -> 22%
where the time goes in v7:
time: 30.3 us; the launch traced here: 30.1 us
  starting transfers between devices  13.8 us (46%)
  Pallas kernels  9.16 us (30%)
  waiting for transfers between devices  7.05 us (23%)
    pallas_call x24, Pallas kernels, run(): pl.pallas_call(kernel, grid=grid, in_specs=in_specs, out_specs=out_specs,...  9.16 us
    ppermute x2, starting transfers between devices, per_device(): lax.ppermute(out, 'wall', hop_pairs(wall_count, at, at - 1, int(at > 1)))  3.93 us
    ppermute x5, starting transfers between devices, mates(): return lax.ppermute(value, 'wall', [(i, i ^ 1) for i in range(wall_count)])  3.72 us
    ppermute x2, waiting for transfers between devices, per_device(): arrivals.append(lax.ppermute(out, 'wall', pairs))  3.64 us
    ppermute x1, starting transfers between devices, per_device(): lax.ppermute(state, 'surf', [(i, (i + 1) % surf_count) for i in range(sur...  2.13 us
    ppermute x1, starting transfers between devices, per_device(): lax.ppermute(state, 'surf', [((i + 1) % surf_count, i) for i in range(sur...  2.03 us
    ppermute x1, waiting for transfers between devices, per_device(): wall = lax.ppermute(out, 'wall', hop_pairs(wall_count, 1, 0))  1.7 us
    ppermute x2, waiting for transfers between devices, per_device(): lax.ppermute(out, 'wall', hop_pairs(wall_count, at, at - 1, int(at > 1)))  0.85 us
  transfers between devices with their start and end apart: 14, of which 6 were waited for; matrix products, arithmetic and copies ran while one was open for 0% of the time, Pallas kernels for 22%

profile of v7, /device:TPU:1, one launch (start us, length us, event | category | flops | bytes accessed | tf_op | source)
XLA Modules:
  0.0 30.1 jit_solution(17439635244261291995)
XLA Ops:
  0.0 2.1 %collective-permute-start = (bf16[16,162]{1,0:T(8,128)(2,1)}, bf16[16,162]{1,0:T(8,128)(2,1)S(1)}, u32[]{:S(2)}, u32[]{:S(2)}) collective-permute-start(bf16[16,162]{1,0:T(8,128)(2,1)} %refs_5_.1), channel_id=1, source_target_pairs={{0,1},{1,2},{2,3},{3,0},{4,5},{5,6},{6,7},{7,4},{8,9},{9,10},{10,1... | collective-permute-start | bytes 15560 | tf_op jit(solution)/shard_map/ppermute | solution.py:607
  2.1 2.0 %collective-permute-start.1 = (bf16[16,162]{1,0:T(8,128)(2,1)}, bf16[16,162]{1,0:T(8,128)(2,1)S(1)}, u32[]{:S(2)}, u32[]{:S(2)}) collective-permute-start(bf16[16,162]{1,0:T(8,128)(2,1)} %refs_5_.1), channel_id=1, source_target_pairs={{1,0},{2,1},{3,2},{0,3},{5,4},{6,5},{7,6},{4,7},{9,8},{10,9},{11,1... | collective-permute-start | bytes 15560 | tf_op jit(solution)/shard_map/ppermute | solution.py:608
  4.2 2.1 %shard_map.100 = (bf16[48,48]{1,0:T(8,128)(2,1)S(1)}, f32[16,162]{1,0:T(8,128)S(1)}, f32[2,8,162]{2,1,0:T(8,128)S(1)}, bf16[16,162]{1,0:T(8,128)(2,1)S(1)}, bf16...) custom-call(s32[2,8]{1,0:T(2,128)} %refs_0_.1, s32[8]{0:T(128)} %refs_1_.1, f32[4,16]{1,0:T(4,128)} %bitcast.9, ...), custom_call_target="tpu_custom_call" | custom-call | flops 1 | bytes 1 | tf_op jit(solution)/shard_map/pallas_call | solution.py:517
  6.3 0.0 collective-permute-done.refs_0_
  6.3 0.0 collective-permute-done.1.refs_2_
  6.3 1.2 %shard_map.101 = (f32[2,8,162]{2,1,0:T(8,128)S(1)}, f32[2,8,162]{2,1,0:T(8,128)S(1)}, f32[8,162]{1,0:T(8,128)S(1)}, bf16[1,1,162,8,162]{4,3,2,1,0:T(8,128)(2,1)S(1)}) custom-call(bf16[16,162]{1,0:T(8,128)(2,1)S(1)} %collective-permute-done.refs_0_, bf16[16,162]{1,0:T(8,128)(2,1)S(1)} %get-tuple-element.56.refs_1_, ...), custom_call_target="tpu_custom_call" | custom-call | flops 1 | bytes 1 | tf_op jit(solution)/shard_map/pallas_call | solution.py:517
  7.5 1.0 %collective-permute-start.2 = (f32[8,162]{1,0:T(8,128)S(1)}, f32[8,162]{1,0:T(8,128)S(1)}, u32[]{:S(2)}, u32[]{:S(2)}) collective-permute-start(f32[8,162]{1,0:T(8,128)S(1)} %get-tuple-element.61), channel_id=1, source_target_pairs={{0,4},{4,0},{8,12},{12,8},{16,20},{20,16},{24,28},{28,24},{1,5},{5... | collective-permute-start | bytes 15560 | tf_op jit(solution)/shard_map/ppermute | solution.py:568
  8.5 1.3 %shard_map.102 = (bf16[2,8,2,162,162]{4,3,2,1,0:T(8,128)(2,1)S(1)}, bf16[8,2,162,162]{3,2,1,0:T(8,128)(2,1)S(1)}, bf16[1408,384]{1,0:T(8,128)(2,1)S(1)}, bf16[1,...) custom-call(bf16[2,2,8,162,162]{4,3,2,1,0:T(8,128)(2,1)S(1)} %get-tuple-element.69.refs_6_.raw_ref, ...), custom_call_target="tpu_custom_call" | custom-call | flops 1 | bytes 1 | tf_op jit(solution)/shard_map/pallas_call | solution.py:517
  9.8 0.0 collective-permute-done.2.came_ref.mate_ref
  9.8 0.1 collective-permute-start.4
  9.9 1.1 %shard_map.103 = (f32[2,8,162]{2,1,0:T(8,128)S(1)}, f32[8,162]{1,0:T(8,128)S(1)}) custom-call(f32[8,162]{1,0:T(8,128)S(1)} %collective-permute-done.2.came_ref.mate_ref, f32[2,8,162]{2,1,0:T(8,128)S(1)} %get-tuple-element.65.scaled_ref, bf16[2,2,8,162,162]{4,3,2,1,0:T(8,128)(2,1)S(1)} %get-tuple-element.69.refs_6_.raw_ref, ...), custom_call_target="tpu_custom_call" | custom-call | flops 1 | bytes 1 | tf_op jit(solution)/shard_map/pallas_call | solution.py:517
  11.0 0.8 %collective-permute-start.3 = (f32[8,162]{1,0:T(8,128)S(1)}, f32[8,162]{1,0:T(8,128)S(1)}, u32[]{:S(2)}, u32[]{:S(2)}) collective-permute-start(f32[8,162]{1,0:T(8,128)S(1)} %get-tuple-element.68), channel_id=1, source_target_pairs={{0,4},{4,12},{8,0},{12,8},{16,20},{20,16},{24,28},{28,24},{1,5},{5... | collective-permute-start | bytes 15560 | tf_op jit(solution)/shard_map/ppermute | solution.py:646
  11.8 1.8 %shard_map.104 = (bf16[2,8,2,162,162]{4,3,2,1,0:T(8,128)(2,1)S(1)}, bf16[8,2,162,162]{3,2,1,0:T(8,128)(2,1)S(1)}, bf16[1408,384]{1,0:T(8,128)(2,1)S(1)}) custom-call(bf16[2,2,8,162,162]{4,3,2,1,0:T(8,128)(2,1)S(1)} %get-tuple-element.69.refs_6_.raw_ref, bf16[1,2,162,8,162]{4,3,2,1,0:T(8,128)(2,1)S(1)} %get-tuple-element.70.refs_0_), custom_call_target="tpu_custom_call" | custom-call | flops 1 | bytes 1 | tf_op jit(solution)/shard_map/pallas_call | solution.py:517
  13.6 0.0 collective-permute-done.3.came_ref.refs_0_
  13.6 0.0 collective-permute-done.4.refs_0_
  13.7 0.5 %collective-permute-start.7 = (bf16[1408,384]{1,0:T(8,128)(2,1)S(1)}, bf16[1408,384]{1,0:T(8,128)(2,1)S(1)}, u32[]{:S(2)}, u32[]{:S(2)}) collective-permute-start(bf16[1408,384]{1,0:T(8,128)(2,1)S(1)} %get-tuple-element.77), channel_id=1, source_target_pairs={{0,4},{4,0},{8,12},{12,8},{16,20},{20,16},{24,28},{28,24},{1,5},{5... | collective-permute-start | bytes 3244040 | tf_op jit(solution)/shard_map/ppermute | solution.py:568
  14.1 0.7 %collective-permute-start.5 = (f32[8,162]{1,0:T(8,128)S(1)}, f32[8,162]{1,0:T(8,128)S(1)}, u32[]{:S(2)}, u32[]{:S(2)}) collective-permute-start(f32[8,162]{1,0:T(8,128)S(1)} %shard_map.105), channel_id=1, source_target_pairs={{0,4},{4,8},{8,12},{12,20},{16,0},{20,16},{24,28},{28,24},{1,5},{5... | collective-permute-start | bytes 15560 | tf_op jit(solution)/shard_map/ppermute | solution.py:698
  14.8 0.3 %shard_map.111 = (bf16[8,2,162,162]{3,2,1,0:T(8,128)(2,1)S(1)}, bf16[1456,384]{1,0:T(8,128)(2,1)S(1)}, f32[8,162]{1,0:T(8,128)S(1)}) custom-call(f32[2,8,162]{2,1,0:T(8,128)S(1)} %get-tuple-element.60.refs_7_.act_ref, bf16[2,8,2,162,162]{4,3,2,1,0:T(8,128)(2,1)S(1)} %get-tuple-element.81.q_ref, bf16[2,8,2,162,162]{4,3,2,1,0:T(8,128)(2,1)S(1)} %get-tuple-element.82.s_ref, ...), custom_call_target="tpu_custom_call" | custom-call | flops 1 | bytes 1 | tf_op jit(solution)/shard_map/pallas_call | solution.py:517
  15.1 1.3 %collective-permute-done.5.came_ref.refs_1_ = f32[8,162]{1,0:T(8,128)S(1)} collective-permute-done((f32[8,162]{1,0:T(8,128)S(1)}, f32[8,162]{1,0:T(8,128)S(1)}, u32[]{:S(2)}, u32[]{:S(2)}) %collective-permute-start.5) | collective-permute-done | bytes 5216 | tf_op jit(solution)/shard_map/ppermute | solution.py:698
  16.4 0.0 collective-permute-done.7.refs_0_.got_c
  16.5 1.4 %collective-permute-start.8 = (bf16[1456,384]{1,0:T(8,128)(2,1)S(1)}, bf16[1456,384]{1,0:T(8,128)(2,1)S(1)}, u32[]{:S(2)}, u32[]{:S(2)}) collective-permute-start(bf16[1456,384]{1,0:T(8,128)(2,1)S(1)} %get-tuple-element.86), channel_id=1, source_target_pairs={{0,4},{4,0},{8,12},{12,8},{16,20},{20,16},{24,28},{28,24},{1,5},{5... | collective-permute-start | bytes 3354632 | tf_op jit(solution)/shard_map/ppermute | solution.py:568
  17.9 0.1 collective-permute-start.6
  18.0 2.3 %collective-permute-done.6.refs_2_.enter_ref = f32[8,162]{1,0:T(8,128)S(1)} collective-permute-done((f32[8,162]{1,0:T(8,128)S(1)}, f32[8,162]{1,0:T(8,128)S(1)}, u32[]{:S(2)}, u32[]{:S(2)}) %collective-permute-start.6) | collective-permute-done | bytes 5216 | tf_op jit(solution)/shard_map/ppermute | solution.py:698
  20.3 0.0 collective-permute-done.8.got_d
  20.4 0.4 %collective-permute-start.9 = (f32[8,162]{1,0:T(8,128)S(1)}, f32[8,162]{1,0:T(8,128)S(1)}, u32[]{:S(2)}, u32[]{:S(2)}) collective-permute-start(f32[8,162]{1,0:T(8,128)S(1)} %shard_map.113), channel_id=1, source_target_pairs={{0,4},{4,0},{8,12},{12,8},{16,24},{20,16},{24,28},{28,20},{1,5},{5... | collective-permute-start | bytes 15560 | tf_op jit(solution)/shard_map/ppermute | solution.py:735
  20.8 0.8 %collective-permute-done.9.came_ref.refs_0_ = f32[8,162]{1,0:T(8,128)S(1)} collective-permute-done((f32[8,162]{1,0:T(8,128)S(1)}, f32[8,162]{1,0:T(8,128)S(1)}, u32[]{:S(2)}, u32[]{:S(2)}) %collective-permute-start.9) | collective-permute-done | bytes 5216 | tf_op jit(solution)/shard_map/ppermute | solution.py:735
  21.6 0.3 %collective-permute-start.10 = (f32[8,162]{1,0:T(8,128)S(1)}, f32[8,162]{1,0:T(8,128)S(1)}, u32[]{:S(2)}, u32[]{:S(2)}) collective-permute-start(f32[8,162]{1,0:T(8,128)S(1)} %shard_map.115), channel_id=1, source_target_pairs={{0,4},{4,0},{8,16},{12,8},{16,20},{20,12},{24,28},{28,24},{1,5},{5... | collective-permute-start | bytes 15560 | tf_op jit(solution)/shard_map/ppermute | solution.py:749
  22.0 0.8 %collective-permute-done.10.refs_1_.came_ref = f32[8,162]{1,0:T(8,128)S(1)} collective-permute-done((f32[8,162]{1,0:T(8,128)S(1)}, f32[8,162]{1,0:T(8,128)S(1)}, u32[]{:S(2)}, u32[]{:S(2)}) %collective-permute-start.10) | collective-permute-done | bytes 5216 | tf_op jit(solution)/shard_map/ppermute | solution.py:749
  22.8 3.6 %collective-permute-start.12 = (f32[8,162]{1,0:T(8,128)S(1)}, f32[8,162]{1,0:T(8,128)S(1)}, u32[]{:S(2)}, u32[]{:S(2)}) collective-permute-start(f32[8,162]{1,0:T(8,128)S(1)} %shard_map.120), channel_id=1, source_target_pairs={{0,4},{4,8},{8,12},{12,0},{16,20},{20,16},{24,28},{28,24},{1,5},{5... | collective-permute-start | bytes 15560 | tf_op jit(solution)/shard_map/ppermute | solution.py:749
  26.4 0.0 collective-permute-start.13
  26.4 0.7 %collective-permute-start.11 = (f32[8,162]{1,0:T(8,128)S(1)}, f32[8,162]{1,0:T(8,128)S(1)}, u32[]{:S(2)}, u32[]{:S(2)}) collective-permute-start(f32[8,162]{1,0:T(8,128)S(1)} %get-tuple-element.103), channel_id=1, source_target_pairs={{0,4},{4,0},{8,12},{12,8},{16,20},{20,16},{24,28},{28,24},{1,5},{5... | collective-permute-start | bytes 15560 | tf_op jit(solution)/shard_map/ppermute | solution.py:568
  27.1 0.1 collective-permute-done.12.came_ref.flow_ref
  27.2 1.7 %collective-permute-done.13.wall_ref = f32[8,162]{1,0:T(8,128)S(1)} collective-permute-done((f32[8,162]{1,0:T(8,128)S(1)}, f32[8,162]{1,0:T(8,128)S(1)}, u32[]{:S(2)}, u32[]{:S(2)}) %collective-permute-start.13) | collective-permute-done | bytes 5216 | tf_op jit(solution)/shard_map/ppermute | solution.py:750
  28.9 0.0 collective-permute-done.11.met_ref
  28.9 1.2 %shard_map.123 = f32[2,8,162]{2,1,0:T(8,128)} custom-call(f32[8,162]{1,0:T(8,128)S(1)} %get-tuple-element.97.beyond_ref, f32[8,162]{1,0:T(8,128)S(1)} %collective-permute-done.11.met_ref, f32[8,162]{1,0:T(8,128)S(1)} %shard_map.121.middle_ref, f32[8,162]{1,0:T(8,128)S(1)} %collective-permute-done.13.wall_ref, ...), custom_call_target="tpu_custom_call" | custom-call | flops 1 | bytes 1 | tf_op jit(solution)/shard_map/pallas_call | solution.py:517
  (17 shorter events, 0.1 us)
Async XLA Ops:
  0.0 6.3 %collective-permute-start = (bf16[16,162]{1,0:T(8,128)(2,1)}, bf16[16,162]{1,0:T(8,128)(2,1)S(1)}, u32[]{:S(2)}, u32[]{:S(2)}) collective-permute-start(bf16[16,162]{1,0:T(8,128)(2,1)} %refs_5_.1), channel_id=1, source_target_pairs={{0,1},{1,2},{2,3},{3,0},{4,5},{5,6},{6,7},{7,4},{8,9},{9,10},{10,1... | collective-permute-start | bytes 15560 | tf_op jit(solution)/shard_map/ppermute | solution.py:607
  2.1 4.2 %collective-permute-start.1 = (bf16[16,162]{1,0:T(8,128)(2,1)}, bf16[16,162]{1,0:T(8,128)(2,1)S(1)}, u32[]{:S(2)}, u32[]{:S(2)}) collective-permute-start(bf16[16,162]{1,0:T(8,128)(2,1)} %refs_5_.1), channel_id=1, source_target_pairs={{1,0},{2,1},{3,2},{0,3},{5,4},{6,5},{7,6},{4,7},{9,8},{10,9},{11,1... | collective-permute-start | bytes 15560 | tf_op jit(solution)/shard_map/ppermute | solution.py:608
  7.5 2.3 %collective-permute-start.2 = (f32[8,162]{1,0:T(8,128)S(1)}, f32[8,162]{1,0:T(8,128)S(1)}, u32[]{:S(2)}, u32[]{:S(2)}) collective-permute-start(f32[8,162]{1,0:T(8,128)S(1)} %get-tuple-element.61), channel_id=1, source_target_pairs={{0,4},{4,0},{8,12},{12,8},{16,20},{20,16},{24,28},{28,24},{1,5},{5... | collective-permute-start | bytes 15560 | tf_op jit(solution)/shard_map/ppermute | solution.py:568
  9.8 3.8 %collective-permute-start.4 = (bf16[1408,384]{1,0:T(8,128)(2,1)S(1)}, bf16[1408,384]{1,0:T(8,128)(2,1)S(1)}, u32[]{:S(2)}, u32[]{:S(2)}) collective-permute-start(bf16[1408,384]{1,0:T(8,128)(2,1)S(1)} %get-tuple-element.73), channel_id=1, source_target_pairs={{0,4},{4,0},{8,12},{12,8},{16,20},{20,16},{24,28},{28,24},{1,5},{5... | collective-permute-start | bytes 3244040 | tf_op jit(solution)/shard_map/ppermute | solution.py:568
  11.0 2.6 %collective-permute-start.3 = (f32[8,162]{1,0:T(8,128)S(1)}, f32[8,162]{1,0:T(8,128)S(1)}, u32[]{:S(2)}, u32[]{:S(2)}) collective-permute-start(f32[8,162]{1,0:T(8,128)S(1)} %get-tuple-element.68), channel_id=1, source_target_pairs={{0,4},{4,12},{8,0},{12,8},{16,20},{20,16},{24,28},{28,24},{1,5},{5... | collective-permute-start | bytes 15560 | tf_op jit(solution)/shard_map/ppermute | solution.py:646
  13.7 2.8 %collective-permute-start.7 = (bf16[1408,384]{1,0:T(8,128)(2,1)S(1)}, bf16[1408,384]{1,0:T(8,128)(2,1)S(1)}, u32[]{:S(2)}, u32[]{:S(2)}) collective-permute-start(bf16[1408,384]{1,0:T(8,128)(2,1)S(1)} %get-tuple-element.77), channel_id=1, source_target_pairs={{0,4},{4,0},{8,12},{12,8},{16,20},{20,16},{24,28},{28,24},{1,5},{5... | collective-permute-start | bytes 3244040 | tf_op jit(solution)/shard_map/ppermute | solution.py:568
  14.1 2.3 %collective-permute-start.5 = (f32[8,162]{1,0:T(8,128)S(1)}, f32[8,162]{1,0:T(8,128)S(1)}, u32[]{:S(2)}, u32[]{:S(2)}) collective-permute-start(f32[8,162]{1,0:T(8,128)S(1)} %shard_map.105), channel_id=1, source_target_pairs={{0,4},{4,8},{8,12},{12,20},{16,0},{20,16},{24,28},{28,24},{1,5},{5... | collective-permute-start | bytes 15560 | tf_op jit(solution)/shard_map/ppermute | solution.py:698
  16.5 3.8 %collective-permute-start.8 = (bf16[1456,384]{1,0:T(8,128)(2,1)S(1)}, bf16[1456,384]{1,0:T(8,128)(2,1)S(1)}, u32[]{:S(2)}, u32[]{:S(2)}) collective-permute-start(bf16[1456,384]{1,0:T(8,128)(2,1)S(1)} %get-tuple-element.86), channel_id=1, source_target_pairs={{0,4},{4,0},{8,12},{12,8},{16,20},{20,16},{24,28},{28,24},{1,5},{5... | collective-permute-start | bytes 3354632 | tf_op jit(solution)/shard_map/ppermute | solution.py:568
  17.9 2.4 %collective-permute-start.6 = (f32[8,162]{1,0:T(8,128)S(1)}, f32[8,162]{1,0:T(8,128)S(1)}, u32[]{:S(2)}, u32[]{:S(2)}) collective-permute-start(f32[8,162]{1,0:T(8,128)S(1)} %shard_map.108), channel_id=1, source_target_pairs={{0,4},{4,0},{8,12},{12,8},{16,20},{20,28},{24,16},{28,24},{1,5},{5... | collective-permute-start | bytes 15560 | tf_op jit(solution)/shard_map/ppermute | solution.py:698
  20.4 1.3 %collective-permute-start.9 = (f32[8,162]{1,0:T(8,128)S(1)}, f32[8,162]{1,0:T(8,128)S(1)}, u32[]{:S(2)}, u32[]{:S(2)}) collective-permute-start(f32[8,162]{1,0:T(8,128)S(1)} %shard_map.113), channel_id=1, source_target_pairs={{0,4},{4,0},{8,12},{12,8},{16,24},{20,16},{24,28},{28,20},{1,5},{5... | collective-permute-start | bytes 15560 | tf_op jit(solution)/shard_map/ppermute | solution.py:735
  21.6 1.2 %collective-permute-start.10 = (f32[8,162]{1,0:T(8,128)S(1)}, f32[8,162]{1,0:T(8,128)S(1)}, u32[]{:S(2)}, u32[]{:S(2)}) collective-permute-start(f32[8,162]{1,0:T(8,128)S(1)} %shard_map.115), channel_id=1, source_target_pairs={{0,4},{4,0},{8,16},{12,8},{16,20},{20,12},{24,28},{28,24},{1,5},{5... | collective-permute-start | bytes 15560 | tf_op jit(solution)/shard_map/ppermute | solution.py:749
  22.8 4.4 %collective-permute-start.12 = (f32[8,162]{1,0:T(8,128)S(1)}, f32[8,162]{1,0:T(8,128)S(1)}, u32[]{:S(2)}, u32[]{:S(2)}) collective-permute-start(f32[8,162]{1,0:T(8,128)S(1)} %shard_map.120), channel_id=1, source_target_pairs={{0,4},{4,8},{8,12},{12,0},{16,20},{20,16},{24,28},{28,24},{1,5},{5... | collective-permute-start | bytes 15560 | tf_op jit(solution)/shard_map/ppermute | solution.py:749
  26.4 2.5 %collective-permute-start.13 = (f32[8,162]{1,0:T(8,128)S(1)}, f32[8,162]{1,0:T(8,128)S(1)}, u32[]{:S(2)}, u32[]{:S(2)}) collective-permute-start(f32[8,162]{1,0:T(8,128)S(1)} %shard_map.120), channel_id=1, source_target_pairs={{0,8},{4,0},{8,12},{12,4},{16,20},{20,16},{24,28},{28,24},{1,9},{5... | collective-permute-start | bytes 15560 | tf_op jit(solution)/shard_map/ppermute | solution.py:750
  26.4 2.5 %collective-permute-start.11 = (f32[8,162]{1,0:T(8,128)S(1)}, f32[8,162]{1,0:T(8,128)S(1)}, u32[]{:S(2)}, u32[]{:S(2)}) collective-permute-start(f32[8,162]{1,0:T(8,128)S(1)} %get-tuple-element.103), channel_id=1, source_target_pairs={{0,4},{4,0},{8,12},{12,8},{16,20},{20,16},{24,28},{28,24},{1,5},{5... | collective-permute-start | bytes 15560 | tf_op jit(solution)/shard_map/ppermute | solution.py:568

commit v8 on v7

--- a/solution.py
+++ b/solution.py
@@ -233,6 +233,10 @@
         turn_blocks(landed, *places_in[i], raw_ref)
 
 
+def copy_kernel(here, _, there):
+    there[...] = here[...]
+
+
 def residual(before, state, after, weight, source, lift, depth):
     cells = jnp.concatenate([before[...], state[...], after[...]], axis=0)
     parts = jnp.dot(weight[...], cells, preferred_element_type=F32)
@@ -491,7 +495,7 @@
     return total
 
 
-def run(kernel, operands, outs, blocks=1, scratch=(), aliases=None):
+def run(kernel, operands, outs, blocks=1, scratch=()):
     held = [(x.shape, x.dtype) for x, _ in operands] + [(s, t) for s, t, _ in outs]
     limit = sum(padded_bytes(s, t) for s, t in held)
     if blocks == 1:
@@ -521,7 +525,6 @@
         out_specs=out_specs,
         out_shape=[jax.ShapeDtypeStruct(s, t) for s, t, _ in outs],
         scratch_shapes=list(scratch),
-        input_output_aliases=aliases or {},
         compiler_params=pltpu.CompilerParams(vmem_limit_bytes=limit),
         cost_estimate=pl.CostEstimate(flops=1, bytes_accessed=1, transcendentals=0),
     )(*[x for x, _ in operands])
@@ -606,6 +609,7 @@
     )
     before = lax.ppermute(state, "surf", [(i, (i + 1) % surf_count) for i in range(surf_count)])
     beyond = lax.ppermute(state, "surf", [((i + 1) % surf_count, i) for i in range(surf_count)])
+    (before,) = run(copy_kernel, [(before, None), (weight, None)], [(state.shape, BF16, None)])
     cells = [(x, None) for x in (before, near_state, beyond, weight, line_source, near_lift)]
     raw = landed[0] if in_place else jnp.stack([dinv, lower, upper])
     vectors = [element_vectors, element_vectors, line_vector]
@@ -694,7 +698,7 @@
             )
         else:
             out = hop(arrivals[-1], [chip_a], y_chip, y_chip, at)
-        pairs = hop_pairs(wall_count, at, at + 1, relay={1: 0}.get(at))
+        pairs = hop_pairs(wall_count, at, at + 1, relay=0 if at == 1 else None)
         arrivals.append(lax.ppermute(out, "wall", pairs))
         if at == 1:
             got_d = mates(after(sent_d, got_c, arrivals[-1]))
@@ -757,7 +761,7 @@
     met_left = mates(after(left, out))
     (y,) = steps(True, arrived[-1], y)
     (wall_middle,) = run(
-        wall_middle_kernel, [(after(arrived[-1], wall), 0), (got_c, 0), (got_d, 0)], [line_vector], blocks
+        wall_middle_kernel, [(after(arrived[-1], wall, y), 0), (got_c, 0), (got_d, 0)], [line_vector], blocks
     )
     (solution,) = run(
         last_kernel,

time: 30.3 us -> 30.3 us (level)
    pallas_call x24 -> x25, Pallas kernels: 9.16 us -> 9.16 us  [run(): pl.pallas_call(kernel, grid=grid, in_specs=in_specs, out_specs=out_specs,...]
where the time goes in v8:
time: 30.3 us; the launch traced here: 30.1 us
  starting transfers between devices  13.8 us (46%)
  Pallas kernels  9.16 us (30%)
  waiting for transfers between devices  7.05 us (23%)
    pallas_call x25, Pallas kernels, run(): pl.pallas_call(kernel, grid=grid, in_specs=in_specs, out_specs=out_specs,...  9.16 us
    ppermute x2, starting transfers between devices, per_device(): lax.ppermute(out, 'wall', hop_pairs(wall_count, at, at - 1, int(at > 1)))  3.92 us
    ppermute x5, starting transfers between devices, mates(): return lax.ppermute(value, 'wall', [(i, i ^ 1) for i in range(wall_count)])  3.72 us
    ppermute x2, waiting for transfers between devices, per_device(): arrivals.append(lax.ppermute(out, 'wall', pairs))  3.64 us
    ppermute x1, starting transfers between devices, per_device(): lax.ppermute(state, 'surf', [(i, (i + 1) % surf_count) for i in range(sur...  2.13 us
    ppermute x1, starting transfers between devices, per_device(): lax.ppermute(state, 'surf', [((i + 1) % surf_count, i) for i in range(sur...  2.03 us
    ppermute x1, waiting for transfers between devices, per_device(): wall = lax.ppermute(out, 'wall', hop_pairs(wall_count, 1, 0))  1.7 us
    ppermute x2, waiting for transfers between devices, per_device(): lax.ppermute(out, 'wall', hop_pairs(wall_count, at, at - 1, int(at > 1)))  0.85 us
  transfers between devices with their start and end apart: 14, of which 6 were waited for; matrix products, arithmetic and copies ran while one was open for 0% of the time, Pallas kernels for 22%

profile of v8, /device:TPU:1, one launch (start us, length us, event | category | flops | bytes accessed | tf_op | source)
XLA Modules:
  0.0 30.1 jit_solution(8163485497687210718)
XLA Ops:
  0.0 2.1 %collective-permute-start = (bf16[16,162]{1,0:T(8,128)(2,1)}, bf16[16,162]{1,0:T(8,128)(2,1)S(1)}, u32[]{:S(2)}, u32[]{:S(2)}) collective-permute-start(bf16[16,162]{1,0:T(8,128)(2,1)} %refs_5_.1), channel_id=1, source_target_pairs={{0,1},{1,2},{2,3},{3,0},{4,5},{5,6},{6,7},{7,4},{8,9},{9,10},{10,1... | collective-permute-start | bytes 15560 | tf_op jit(solution)/shard_map/ppermute | solution.py:610
  2.1 2.0 %collective-permute-start.1 = (bf16[16,162]{1,0:T(8,128)(2,1)}, bf16[16,162]{1,0:T(8,128)(2,1)S(1)}, u32[]{:S(2)}, u32[]{:S(2)}) collective-permute-start(bf16[16,162]{1,0:T(8,128)(2,1)} %refs_5_.1), channel_id=1, source_target_pairs={{1,0},{2,1},{3,2},{0,3},{5,4},{6,5},{7,6},{4,7},{9,8},{10,9},{11,1... | collective-permute-start | bytes 15560 | tf_op jit(solution)/shard_map/ppermute | solution.py:611
  4.2 2.1 %shard_map.100 = (bf16[48,48]{1,0:T(8,128)(2,1)S(1)}, f32[16,162]{1,0:T(8,128)S(1)}, f32[2,8,162]{2,1,0:T(8,128)S(1)}, bf16[16,162]{1,0:T(8,128)(2,1)S(1)}, bf16...) custom-call(s32[2,8]{1,0:T(2,128)} %refs_0_.1, s32[8]{0:T(128)} %refs_1_.1, f32[4,16]{1,0:T(4,128)} %bitcast.9, ...), custom_call_target="tpu_custom_call" | custom-call | flops 1 | bytes 1 | tf_op jit(solution)/shard_map/pallas_call | solution.py:521
  6.3 0.0 collective-permute-done.here
  6.3 0.0 collective-permute-done.1.refs_2_
  6.3 1.2 %shard_map.102 = (f32[2,8,162]{2,1,0:T(8,128)S(1)}, f32[2,8,162]{2,1,0:T(8,128)S(1)}, f32[8,162]{1,0:T(8,128)S(1)}, bf16[1,1,162,8,162]{4,3,2,1,0:T(8,128)(2,1)S(1)}) custom-call(bf16[16,162]{1,0:T(8,128)(2,1)S(1)} %shard_map.101.refs_0_, bf16[16,162]{1,0:T(8,128)(2,1)S(1)} %get-tuple-element.57.refs_1_, bf16[16,162]{1,0:T(8,128)(2,1)S(1)} %collective-permute-done.1.refs_2_, ...), custom_call_target="tpu_custom_call" | custom-call | flops 1 | bytes 1 | tf_op jit(solution)/shard_map/pallas_call | solution.py:521
  7.5 1.0 %collective-permute-start.2 = (f32[8,162]{1,0:T(8,128)S(1)}, f32[8,162]{1,0:T(8,128)S(1)}, u32[]{:S(2)}, u32[]{:S(2)}) collective-permute-start(f32[8,162]{1,0:T(8,128)S(1)} %get-tuple-element.61), channel_id=1, source_target_pairs={{0,4},{4,0},{8,12},{12,8},{16,20},{20,16},{24,28},{28,24},{1,5},{5... | collective-permute-start | bytes 15560 | tf_op jit(solution)/shard_map/ppermute | solution.py:571
  8.5 1.3 %shard_map.103 = (bf16[2,8,2,162,162]{4,3,2,1,0:T(8,128)(2,1)S(1)}, bf16[8,2,162,162]{3,2,1,0:T(8,128)(2,1)S(1)}, bf16[1408,384]{1,0:T(8,128)(2,1)S(1)}, bf16[1,...) custom-call(bf16[2,2,8,162,162]{4,3,2,1,0:T(8,128)(2,1)S(1)} %get-tuple-element.69.refs_6_.raw_ref, ...), custom_call_target="tpu_custom_call" | custom-call | flops 1 | bytes 1 | tf_op jit(solution)/shard_map/pallas_call | solution.py:521
  9.8 0.0 collective-permute-done.2.came_ref.mate_ref
  9.9 0.1 collective-permute-start.4
  9.9 1.1 %shard_map.104 = (f32[2,8,162]{2,1,0:T(8,128)S(1)}, f32[8,162]{1,0:T(8,128)S(1)}) custom-call(f32[8,162]{1,0:T(8,128)S(1)} %collective-permute-done.2.came_ref.mate_ref, f32[2,8,162]{2,1,0:T(8,128)S(1)} %get-tuple-element.65.scaled_ref, bf16[2,2,8,162,162]{4,3,2,1,0:T(8,128)(2,1)S(1)} %get-tuple-element.69.refs_6_.raw_ref, ...), custom_call_target="tpu_custom_call" | custom-call | flops 1 | bytes 1 | tf_op jit(solution)/shard_map/pallas_call | solution.py:521
  11.0 0.8 %collective-permute-start.3 = (f32[8,162]{1,0:T(8,128)S(1)}, f32[8,162]{1,0:T(8,128)S(1)}, u32[]{:S(2)}, u32[]{:S(2)}) collective-permute-start(f32[8,162]{1,0:T(8,128)S(1)} %get-tuple-element.68), channel_id=1, source_target_pairs={{0,4},{4,12},{8,0},{12,8},{16,20},{20,16},{24,28},{28,24},{1,5},{5... | collective-permute-start | bytes 15560 | tf_op jit(solution)/shard_map/ppermute | solution.py:650
  11.8 1.8 %shard_map.105 = (bf16[2,8,2,162,162]{4,3,2,1,0:T(8,128)(2,1)S(1)}, bf16[8,2,162,162]{3,2,1,0:T(8,128)(2,1)S(1)}, bf16[1408,384]{1,0:T(8,128)(2,1)S(1)}) custom-call(bf16[2,2,8,162,162]{4,3,2,1,0:T(8,128)(2,1)S(1)} %get-tuple-element.69.refs_6_.raw_ref, bf16[1,2,162,8,162]{4,3,2,1,0:T(8,128)(2,1)S(1)} %get-tuple-element.70.refs_0_), custom_call_target="tpu_custom_call" | custom-call | flops 1 | bytes 1 | tf_op jit(solution)/shard_map/pallas_call | solution.py:521
  13.6 0.0 collective-permute-done.3.came_ref.refs_0_
  13.7 0.0 collective-permute-done.4.refs_0_
  13.7 0.5 %collective-permute-start.7 = (bf16[1408,384]{1,0:T(8,128)(2,1)S(1)}, bf16[1408,384]{1,0:T(8,128)(2,1)S(1)}, u32[]{:S(2)}, u32[]{:S(2)}) collective-permute-start(bf16[1408,384]{1,0:T(8,128)(2,1)S(1)} %get-tuple-element.77), channel_id=1, source_target_pairs={{0,4},{4,0},{8,12},{12,8},{16,20},{20,16},{24,28},{28,24},{1,5},{5... | collective-permute-start | bytes 3244040 | tf_op jit(solution)/shard_map/ppermute | solution.py:571
  14.1 0.7 %collective-permute-start.5 = (f32[8,162]{1,0:T(8,128)S(1)}, f32[8,162]{1,0:T(8,128)S(1)}, u32[]{:S(2)}, u32[]{:S(2)}) collective-permute-start(f32[8,162]{1,0:T(8,128)S(1)} %shard_map.106), channel_id=1, source_target_pairs={{0,4},{4,8},{8,12},{12,20},{16,0},{20,16},{24,28},{28,24},{1,5},{5... | collective-permute-start | bytes 15560 | tf_op jit(solution)/shard_map/ppermute | solution.py:702
  14.8 0.3 %shard_map.112 = (bf16[8,2,162,162]{3,2,1,0:T(8,128)(2,1)S(1)}, bf16[1456,384]{1,0:T(8,128)(2,1)S(1)}, f32[8,162]{1,0:T(8,128)S(1)}) custom-call(f32[2,8,162]{2,1,0:T(8,128)S(1)} %get-tuple-element.60.refs_7_.act_ref, bf16[2,8,2,162,162]{4,3,2,1,0:T(8,128)(2,1)S(1)} %get-tuple-element.81.q_ref, bf16[2,8,2,162,162]{4,3,2,1,0:T(8,128)(2,1)S(1)} %get-tuple-element.82.s_ref, ...), custom_call_target="tpu_custom_call" | custom-call | flops 1 | bytes 1 | tf_op jit(solution)/shard_map/pallas_call | solution.py:521
  15.1 1.3 %collective-permute-done.5.came_ref.refs_1_ = f32[8,162]{1,0:T(8,128)S(1)} collective-permute-done((f32[8,162]{1,0:T(8,128)S(1)}, f32[8,162]{1,0:T(8,128)S(1)}, u32[]{:S(2)}, u32[]{:S(2)}) %collective-permute-start.5) | collective-permute-done | bytes 5216 | tf_op jit(solution)/shard_map/ppermute | solution.py:702
  16.5 0.0 collective-permute-done.7.refs_0_.got_c
  16.5 1.4 %collective-permute-start.8 = (bf16[1456,384]{1,0:T(8,128)(2,1)S(1)}, bf16[1456,384]{1,0:T(8,128)(2,1)S(1)}, u32[]{:S(2)}, u32[]{:S(2)}) collective-permute-start(bf16[1456,384]{1,0:T(8,128)(2,1)S(1)} %get-tuple-element.86), channel_id=1, source_target_pairs={{0,4},{4,0},{8,12},{12,8},{16,20},{20,16},{24,28},{28,24},{1,5},{5... | collective-permute-start | bytes 3354632 | tf_op jit(solution)/shard_map/ppermute | solution.py:571
  17.9 0.1 collective-permute-start.6
  18.0 2.3 %collective-permute-done.6.refs_2_.enter_ref = f32[8,162]{1,0:T(8,128)S(1)} collective-permute-done((f32[8,162]{1,0:T(8,128)S(1)}, f32[8,162]{1,0:T(8,128)S(1)}, u32[]{:S(2)}, u32[]{:S(2)}) %collective-permute-start.6) | collective-permute-done | bytes 5216 | tf_op jit(solution)/shard_map/ppermute | solution.py:702
  20.3 0.0 collective-permute-done.8.got_d
  20.4 0.4 %collective-permute-start.9 = (f32[8,162]{1,0:T(8,128)S(1)}, f32[8,162]{1,0:T(8,128)S(1)}, u32[]{:S(2)}, u32[]{:S(2)}) collective-permute-start(f32[8,162]{1,0:T(8,128)S(1)} %shard_map.114), channel_id=1, source_target_pairs={{0,4},{4,0},{8,12},{12,8},{16,24},{20,16},{24,28},{28,20},{1,5},{5... | collective-permute-start | bytes 15560 | tf_op jit(solution)/shard_map/ppermute | solution.py:739
  20.8 0.8 %collective-permute-done.9.came_ref.refs_0_ = f32[8,162]{1,0:T(8,128)S(1)} collective-permute-done((f32[8,162]{1,0:T(8,128)S(1)}, f32[8,162]{1,0:T(8,128)S(1)}, u32[]{:S(2)}, u32[]{:S(2)}) %collective-permute-start.9) | collective-permute-done | bytes 5216 | tf_op jit(solution)/shard_map/ppermute | solution.py:739
  21.6 0.3 %collective-permute-start.10 = (f32[8,162]{1,0:T(8,128)S(1)}, f32[8,162]{1,0:T(8,128)S(1)}, u32[]{:S(2)}, u32[]{:S(2)}) collective-permute-start(f32[8,162]{1,0:T(8,128)S(1)} %shard_map.116), channel_id=1, source_target_pairs={{0,4},{4,0},{8,16},{12,8},{16,20},{20,12},{24,28},{28,24},{1,5},{5... | collective-permute-start | bytes 15560 | tf_op jit(solution)/shard_map/ppermute | solution.py:753
  22.0 0.8 %collective-permute-done.10.refs_1_.came_ref = f32[8,162]{1,0:T(8,128)S(1)} collective-permute-done((f32[8,162]{1,0:T(8,128)S(1)}, f32[8,162]{1,0:T(8,128)S(1)}, u32[]{:S(2)}, u32[]{:S(2)}) %collective-permute-start.10) | collective-permute-done | bytes 5216 | tf_op jit(solution)/shard_map/ppermute | solution.py:753
  22.8 3.6 %collective-permute-start.12 = (f32[8,162]{1,0:T(8,128)S(1)}, f32[8,162]{1,0:T(8,128)S(1)}, u32[]{:S(2)}, u32[]{:S(2)}) collective-permute-start(f32[8,162]{1,0:T(8,128)S(1)} %shard_map.121), channel_id=1, source_target_pairs={{0,4},{4,8},{8,12},{12,0},{16,20},{20,16},{24,28},{28,24},{1,5},{5... | collective-permute-start | bytes 15560 | tf_op jit(solution)/shard_map/ppermute | solution.py:753
  26.4 0.0 collective-permute-start.13
  26.4 0.7 %collective-permute-start.11 = (f32[8,162]{1,0:T(8,128)S(1)}, f32[8,162]{1,0:T(8,128)S(1)}, u32[]{:S(2)}, u32[]{:S(2)}) collective-permute-start(f32[8,162]{1,0:T(8,128)S(1)} %get-tuple-element.103), channel_id=1, source_target_pairs={{0,4},{4,0},{8,12},{12,8},{16,20},{20,16},{24,28},{28,24},{1,5},{5... | collective-permute-start | bytes 15560 | tf_op jit(solution)/shard_map/ppermute | solution.py:571
  27.1 0.1 collective-permute-done.12.flow_ref.came_ref
  27.2 1.7 %collective-permute-done.13.wall_ref = f32[8,162]{1,0:T(8,128)S(1)} collective-permute-done((f32[8,162]{1,0:T(8,128)S(1)}, f32[8,162]{1,0:T(8,128)S(1)}, u32[]{:S(2)}, u32[]{:S(2)}) %collective-permute-start.13) | collective-permute-done | bytes 5216 | tf_op jit(solution)/shard_map/ppermute | solution.py:754
  28.9 0.0 collective-permute-done.11.met_ref
  28.9 1.2 %shard_map.124 = f32[2,8,162]{2,1,0:T(8,128)} custom-call(f32[8,162]{1,0:T(8,128)S(1)} %get-tuple-element.97.beyond_ref, f32[8,162]{1,0:T(8,128)S(1)} %collective-permute-done.11.met_ref, f32[8,162]{1,0:T(8,128)S(1)} %shard_map.123.middle_ref, f32[8,162]{1,0:T(8,128)S(1)} %collective-permute-done.13.wall_ref, ...), custom_call_target="tpu_custom_call" | custom-call | flops 1 | bytes 1 | tf_op jit(solution)/shard_map/pallas_call | solution.py:521
  (18 shorter events, 0.1 us)
Async XLA Ops:
  0.0 6.3 %collective-permute-start = (bf16[16,162]{1,0:T(8,128)(2,1)}, bf16[16,162]{1,0:T(8,128)(2,1)S(1)}, u32[]{:S(2)}, u32[]{:S(2)}) collective-permute-start(bf16[16,162]{1,0:T(8,128)(2,1)} %refs_5_.1), channel_id=1, source_target_pairs={{0,1},{1,2},{2,3},{3,0},{4,5},{5,6},{6,7},{7,4},{8,9},{9,10},{10,1... | collective-permute-start | bytes 15560 | tf_op jit(solution)/shard_map/ppermute | solution.py:610
  2.1 4.2 %collective-permute-start.1 = (bf16[16,162]{1,0:T(8,128)(2,1)}, bf16[16,162]{1,0:T(8,128)(2,1)S(1)}, u32[]{:S(2)}, u32[]{:S(2)}) collective-permute-start(bf16[16,162]{1,0:T(8,128)(2,1)} %refs_5_.1), channel_id=1, source_target_pairs={{1,0},{2,1},{3,2},{0,3},{5,4},{6,5},{7,6},{4,7},{9,8},{10,9},{11,1... | collective-permute-start | bytes 15560 | tf_op jit(solution)/shard_map/ppermute | solution.py:611
  7.5 2.3 %collective-permute-start.2 = (f32[8,162]{1,0:T(8,128)S(1)}, f32[8,162]{1,0:T(8,128)S(1)}, u32[]{:S(2)}, u32[]{:S(2)}) collective-permute-start(f32[8,162]{1,0:T(8,128)S(1)} %get-tuple-element.61), channel_id=1, source_target_pairs={{0,4},{4,0},{8,12},{12,8},{16,20},{20,16},{24,28},{28,24},{1,5},{5... | collective-permute-start | bytes 15560 | tf_op jit(solution)/shard_map/ppermute | solution.py:571
  9.9 3.8 %collective-permute-start.4 = (bf16[1408,384]{1,0:T(8,128)(2,1)S(1)}, bf16[1408,384]{1,0:T(8,128)(2,1)S(1)}, u32[]{:S(2)}, u32[]{:S(2)}) collective-permute-start(bf16[1408,384]{1,0:T(8,128)(2,1)S(1)} %get-tuple-element.73), channel_id=1, source_target_pairs={{0,4},{4,0},{8,12},{12,8},{16,20},{20,16},{24,28},{28,24},{1,5},{5... | collective-permute-start | bytes 3244040 | tf_op jit(solution)/shard_map/ppermute | solution.py:571
  11.0 2.6 %collective-permute-start.3 = (f32[8,162]{1,0:T(8,128)S(1)}, f32[8,162]{1,0:T(8,128)S(1)}, u32[]{:S(2)}, u32[]{:S(2)}) collective-permute-start(f32[8,162]{1,0:T(8,128)S(1)} %get-tuple-element.68), channel_id=1, source_target_pairs={{0,4},{4,12},{8,0},{12,8},{16,20},{20,16},{24,28},{28,24},{1,5},{5... | collective-permute-start | bytes 15560 | tf_op jit(solution)/shard_map/ppermute | solution.py:650
  13.7 2.8 %collective-permute-start.7 = (bf16[1408,384]{1,0:T(8,128)(2,1)S(1)}, bf16[1408,384]{1,0:T(8,128)(2,1)S(1)}, u32[]{:S(2)}, u32[]{:S(2)}) collective-permute-start(bf16[1408,384]{1,0:T(8,128)(2,1)S(1)} %get-tuple-element.77), channel_id=1, source_target_pairs={{0,4},{4,0},{8,12},{12,8},{16,20},{20,16},{24,28},{28,24},{1,5},{5... | collective-permute-start | bytes 3244040 | tf_op jit(solution)/shard_map/ppermute | solution.py:571
  14.1 2.3 %collective-permute-start.5 = (f32[8,162]{1,0:T(8,128)S(1)}, f32[8,162]{1,0:T(8,128)S(1)}, u32[]{:S(2)}, u32[]{:S(2)}) collective-permute-start(f32[8,162]{1,0:T(8,128)S(1)} %shard_map.106), channel_id=1, source_target_pairs={{0,4},{4,8},{8,12},{12,20},{16,0},{20,16},{24,28},{28,24},{1,5},{5... | collective-permute-start | bytes 15560 | tf_op jit(solution)/shard_map/ppermute | solution.py:702
  16.5 3.8 %collective-permute-start.8 = (bf16[1456,384]{1,0:T(8,128)(2,1)S(1)}, bf16[1456,384]{1,0:T(8,128)(2,1)S(1)}, u32[]{:S(2)}, u32[]{:S(2)}) collective-permute-start(bf16[1456,384]{1,0:T(8,128)(2,1)S(1)} %get-tuple-element.86), channel_id=1, source_target_pairs={{0,4},{4,0},{8,12},{12,8},{16,20},{20,16},{24,28},{28,24},{1,5},{5... | collective-permute-start | bytes 3354632 | tf_op jit(solution)/shard_map/ppermute | solution.py:571
  17.9 2.4 %collective-permute-start.6 = (f32[8,162]{1,0:T(8,128)S(1)}, f32[8,162]{1,0:T(8,128)S(1)}, u32[]{:S(2)}, u32[]{:S(2)}) collective-permute-start(f32[8,162]{1,0:T(8,128)S(1)} %shard_map.109), channel_id=1, source_target_pairs={{0,4},{4,0},{8,12},{12,8},{16,20},{20,28},{24,16},{28,24},{1,5},{5... | collective-permute-start | bytes 15560 | tf_op jit(solution)/shard_map/ppermute | solution.py:702
  20.4 1.3 %collective-permute-start.9 = (f32[8,162]{1,0:T(8,128)S(1)}, f32[8,162]{1,0:T(8,128)S(1)}, u32[]{:S(2)}, u32[]{:S(2)}) collective-permute-start(f32[8,162]{1,0:T(8,128)S(1)} %shard_map.114), channel_id=1, source_target_pairs={{0,4},{4,0},{8,12},{12,8},{16,24},{20,16},{24,28},{28,20},{1,5},{5... | collective-permute-start | bytes 15560 | tf_op jit(solution)/shard_map/ppermute | solution.py:739
  21.6 1.2 %collective-permute-start.10 = (f32[8,162]{1,0:T(8,128)S(1)}, f32[8,162]{1,0:T(8,128)S(1)}, u32[]{:S(2)}, u32[]{:S(2)}) collective-permute-start(f32[8,162]{1,0:T(8,128)S(1)} %shard_map.116), channel_id=1, source_target_pairs={{0,4},{4,0},{8,16},{12,8},{16,20},{20,12},{24,28},{28,24},{1,5},{5... | collective-permute-start | bytes 15560 | tf_op jit(solution)/shard_map/ppermute | solution.py:753
  22.8 4.4 %collective-permute-start.12 = (f32[8,162]{1,0:T(8,128)S(1)}, f32[8,162]{1,0:T(8,128)S(1)}, u32[]{:S(2)}, u32[]{:S(2)}) collective-permute-start(f32[8,162]{1,0:T(8,128)S(1)} %shard_map.121), channel_id=1, source_target_pairs={{0,4},{4,8},{8,12},{12,0},{16,20},{20,16},{24,28},{28,24},{1,5},{5... | collective-permute-start | bytes 15560 | tf_op jit(solution)/shard_map/ppermute | solution.py:753
  26.4 2.5 %collective-permute-start.13 = (f32[8,162]{1,0:T(8,128)S(1)}, f32[8,162]{1,0:T(8,128)S(1)}, u32[]{:S(2)}, u32[]{:S(2)}) collective-permute-start(f32[8,162]{1,0:T(8,128)S(1)} %shard_map.121), channel_id=1, source_target_pairs={{0,8},{4,0},{8,12},{12,4},{16,20},{20,16},{24,28},{28,24},{1,9},{5... | collective-permute-start | bytes 15560 | tf_op jit(solution)/shard_map/ppermute | solution.py:754
  26.4 2.5 %collective-permute-start.11 = (f32[8,162]{1,0:T(8,128)S(1)}, f32[8,162]{1,0:T(8,128)S(1)}, u32[]{:S(2)}, u32[]{:S(2)}) collective-permute-start(f32[8,162]{1,0:T(8,128)S(1)} %get-tuple-element.103), channel_id=1, source_target_pairs={{0,4},{4,0},{8,12},{12,8},{16,20},{20,16},{24,28},{28,24},{1,5},{5... | collective-permute-start | bytes 15560 | tf_op jit(solution)/shard_map/ppermute | solution.py:571

commit v9 on v8

--- a/solution.py
+++ b/solution.py
@@ -474,16 +474,26 @@
         out_ref[...] = value
 
 
-def last_kernel(beyond_ref, met_ref, middle_ref, wall_ref, s_ref, act_ref, y_ref, out_ref):
+def last_kernel(beyond_ref, met_ref, middle_ref, wall_ref, whole_ref, echo_ref, s_ref, act_ref, y_ref, out_ref):
     depth = y_ref.shape[0]
     core, chip = core_of(), chip_of()
     first = jnp.where(chip == 0, middle_ref[...], met_ref[...])
     second = jnp.where(chip == 0, wall_ref[...], beyond_ref[...])
-    solved = backward_local(
-        [y_ref[g] for g in range(depth)], s_ref, act_ref, jnp.where(core == 0, first, second)
-    )
-    for g in range(depth):
-        out_ref[g] = solved[g]
+    carried = jnp.where(core == 0, first, second)
+
+    @pl.when(chip == 0)
+    def _():
+        out_ref[0] = apply_pairs(carried, whole_ref) + echo_ref[...]
+        value = carried
+        for g in range(depth - 1, 0, -1):
+            value = act_ref[g] * (y_ref[g] - apply_pairs(value, s_ref, g))
+            out_ref[g] = value
+
+    @pl.when(chip > 0)
+    def _():
+        solved = backward_local([y_ref[g] for g in range(depth)], s_ref, act_ref, carried)
+        for g in range(depth):
+            out_ref[g] = solved[g]
 
 
 def padded_bytes(shape, dtype):
@@ -765,7 +775,7 @@
     )
     (solution,) = run(
         last_kernel,
-        [(beyond, 0), (met_left, 0), (wall_middle, 0), (wall, 0)] + [(x, 1) for x in (s, act, y)],
+        [(x, 0) for x in (beyond, met_left, wall_middle, wall, c, echo)] + [(x, 1) for x in (s, act, y)],
         [element_vectors],
         blocks,
     )

time: 30.3 us -> 30.2 us (level)
  transfers between devices with their start and end apart: 14 -> 14, of which waited for: 6 -> 6; matrix products, arithmetic and copies ran while one was open for 0% -> 0% of each run, Pallas kernels for 22% -> 23%
where the time goes in v9:
time: 30.2 us; the launch traced here: 30 us
  starting transfers between devices  13.8 us (46%)
  Pallas kernels  9.24 us (31%)
  waiting for transfers between devices  6.87 us (23%)
    pallas_call x25, Pallas kernels, run(): pl.pallas_call(kernel, grid=grid, in_specs=in_specs, out_specs=out_specs,...  9.24 us
    ppermute x2, starting transfers between devices, per_device(): lax.ppermute(out, 'wall', hop_pairs(wall_count, at, at - 1, int(at > 1)))  3.93 us
    ppermute x5, starting transfers between devices, mates(): return lax.ppermute(value, 'wall', [(i, i ^ 1) for i in range(wall_count)])  3.72 us
    ppermute x2, waiting for transfers between devices, per_device(): arrivals.append(lax.ppermute(out, 'wall', pairs))  3.64 us
    ppermute x1, starting transfers between devices, per_device(): lax.ppermute(state, 'surf', [(i, (i + 1) % surf_count) for i in range(sur...  2.13 us
    ppermute x1, starting transfers between devices, per_device(): lax.ppermute(state, 'surf', [((i + 1) % surf_count, i) for i in range(sur...  2.03 us
    ppermute x1, waiting for transfers between devices, per_device(): wall = lax.ppermute(out, 'wall', hop_pairs(wall_count, 1, 0))  1.7 us
    ppermute x1, waiting for transfers between devices, per_device(): arrived = [lax.ppermute(out, 'wall', hop_pairs(wall_count, last, last - 1))]  0.82 us
  transfers between devices with their start and end apart: 14, of which 6 were waited for; matrix products, arithmetic and copies ran while one was open for 0% of the time, Pallas kernels for 23%

profile of v9, /device:TPU:1, one launch (start us, length us, event | category | flops | bytes accessed | tf_op | source)
XLA Modules:
  0.0 30.0 jit_solution(10469189334242236417)
XLA Ops:
  0.0 2.1 %collective-permute-start = (bf16[16,162]{1,0:T(8,128)(2,1)}, bf16[16,162]{1,0:T(8,128)(2,1)S(1)}, u32[]{:S(2)}, u32[]{:S(2)}) collective-permute-start(bf16[16,162]{1,0:T(8,128)(2,1)} %refs_5_.1), channel_id=1, source_target_pairs={{0,1},{1,2},{2,3},{3,0},{4,5},{5,6},{6,7},{7,4},{8,9},{9,10},{10,1... | collective-permute-start | bytes 15560 | tf_op jit(solution)/shard_map/ppermute | solution.py:620
  2.1 2.0 %collective-permute-start.1 = (bf16[16,162]{1,0:T(8,128)(2,1)}, bf16[16,162]{1,0:T(8,128)(2,1)S(1)}, u32[]{:S(2)}, u32[]{:S(2)}) collective-permute-start(bf16[16,162]{1,0:T(8,128)(2,1)} %refs_5_.1), channel_id=1, source_target_pairs={{1,0},{2,1},{3,2},{0,3},{5,4},{6,5},{7,6},{4,7},{9,8},{10,9},{11,1... | collective-permute-start | bytes 15560 | tf_op jit(solution)/shard_map/ppermute | solution.py:621
  4.2 2.1 %shard_map.100 = (bf16[48,48]{1,0:T(8,128)(2,1)S(1)}, f32[16,162]{1,0:T(8,128)S(1)}, f32[2,8,162]{2,1,0:T(8,128)S(1)}, bf16[16,162]{1,0:T(8,128)(2,1)S(1)}, bf16...) custom-call(s32[2,8]{1,0:T(2,128)} %refs_0_.1, s32[8]{0:T(128)} %refs_1_.1, f32[4,16]{1,0:T(4,128)} %bitcast.9, ...), custom_call_target="tpu_custom_call" | custom-call | flops 1 | bytes 1 | tf_op jit(solution)/shard_map/pallas_call | solution.py:531
  6.3 0.0 collective-permute-done.here
  6.3 0.0 collective-permute-done.1.refs_2_
  6.3 1.2 %shard_map.102 = (f32[2,8,162]{2,1,0:T(8,128)S(1)}, f32[2,8,162]{2,1,0:T(8,128)S(1)}, f32[8,162]{1,0:T(8,128)S(1)}, bf16[1,1,162,8,162]{4,3,2,1,0:T(8,128)(2,1)S(1)}) custom-call(bf16[16,162]{1,0:T(8,128)(2,1)S(1)} %shard_map.101.refs_0_, bf16[16,162]{1,0:T(8,128)(2,1)S(1)} %get-tuple-element.57.refs_1_, bf16[16,162]{1,0:T(8,128)(2,1)S(1)} %collective-permute-done.1.refs_2_, ...), custom_call_target="tpu_custom_call" | custom-call | flops 1 | bytes 1 | tf_op jit(solution)/shard_map/pallas_call | solution.py:531
  7.5 1.0 %collective-permute-start.2 = (f32[8,162]{1,0:T(8,128)S(1)}, f32[8,162]{1,0:T(8,128)S(1)}, u32[]{:S(2)}, u32[]{:S(2)}) collective-permute-start(f32[8,162]{1,0:T(8,128)S(1)} %get-tuple-element.61), channel_id=1, source_target_pairs={{0,4},{4,0},{8,12},{12,8},{16,20},{20,16},{24,28},{28,24},{1,5},{5... | collective-permute-start | bytes 15560 | tf_op jit(solution)/shard_map/ppermute | solution.py:581
  8.5 1.3 %shard_map.103 = (bf16[2,8,2,162,162]{4,3,2,1,0:T(8,128)(2,1)S(1)}, bf16[8,2,162,162]{3,2,1,0:T(8,128)(2,1)S(1)}, bf16[1408,384]{1,0:T(8,128)(2,1)S(1)}, bf16[1,...) custom-call(bf16[2,2,8,162,162]{4,3,2,1,0:T(8,128)(2,1)S(1)} %get-tuple-element.69.refs_6_.raw_ref, ...), custom_call_target="tpu_custom_call" | custom-call | flops 1 | bytes 1 | tf_op jit(solution)/shard_map/pallas_call | solution.py:531
  9.8 0.0 collective-permute-done.2.came_ref.mate_ref
  9.9 0.1 collective-permute-start.4
  9.9 1.1 %shard_map.104 = (f32[2,8,162]{2,1,0:T(8,128)S(1)}, f32[8,162]{1,0:T(8,128)S(1)}) custom-call(f32[8,162]{1,0:T(8,128)S(1)} %collective-permute-done.2.came_ref.mate_ref, f32[2,8,162]{2,1,0:T(8,128)S(1)} %get-tuple-element.65.scaled_ref, bf16[2,2,8,162,162]{4,3,2,1,0:T(8,128)(2,1)S(1)} %get-tuple-element.69.refs_6_.raw_ref, ...), custom_call_target="tpu_custom_call" | custom-call | flops 1 | bytes 1 | tf_op jit(solution)/shard_map/pallas_call | solution.py:531
  11.0 0.8 %collective-permute-start.3 = (f32[8,162]{1,0:T(8,128)S(1)}, f32[8,162]{1,0:T(8,128)S(1)}, u32[]{:S(2)}, u32[]{:S(2)}) collective-permute-start(f32[8,162]{1,0:T(8,128)S(1)} %get-tuple-element.68), channel_id=1, source_target_pairs={{0,4},{4,12},{8,0},{12,8},{16,20},{20,16},{24,28},{28,24},{1,5},{5... | collective-permute-start | bytes 15560 | tf_op jit(solution)/shard_map/ppermute | solution.py:660
  11.8 1.8 %shard_map.105 = (bf16[2,8,2,162,162]{4,3,2,1,0:T(8,128)(2,1)S(1)}, bf16[8,2,162,162]{3,2,1,0:T(8,128)(2,1)S(1)}, bf16[1408,384]{1,0:T(8,128)(2,1)S(1)}) custom-call(bf16[2,2,8,162,162]{4,3,2,1,0:T(8,128)(2,1)S(1)} %get-tuple-element.69.refs_6_.raw_ref, bf16[1,2,162,8,162]{4,3,2,1,0:T(8,128)(2,1)S(1)} %get-tuple-element.70.refs_0_), custom_call_target="tpu_custom_call" | custom-call | flops 1 | bytes 1 | tf_op jit(solution)/shard_map/pallas_call | solution.py:531
  13.7 0.0 collective-permute-done.3.came_ref.refs_0_
  13.7 0.0 collective-permute-done.4.refs_0_
  13.7 0.5 %collective-permute-start.7 = (bf16[1408,384]{1,0:T(8,128)(2,1)S(1)}, bf16[1408,384]{1,0:T(8,128)(2,1)S(1)}, u32[]{:S(2)}, u32[]{:S(2)}) collective-permute-start(bf16[1408,384]{1,0:T(8,128)(2,1)S(1)} %get-tuple-element.77), channel_id=1, source_target_pairs={{0,4},{4,0},{8,12},{12,8},{16,20},{20,16},{24,28},{28,24},{1,5},{5... | collective-permute-start | bytes 3244040 | tf_op jit(solution)/shard_map/ppermute | solution.py:581
  14.1 0.7 %collective-permute-start.5 = (f32[8,162]{1,0:T(8,128)S(1)}, f32[8,162]{1,0:T(8,128)S(1)}, u32[]{:S(2)}, u32[]{:S(2)}) collective-permute-start(f32[8,162]{1,0:T(8,128)S(1)} %shard_map.106), channel_id=1, source_target_pairs={{0,4},{4,8},{8,12},{12,20},{16,0},{20,16},{24,28},{28,24},{1,5},{5... | collective-permute-start | bytes 15560 | tf_op jit(solution)/shard_map/ppermute | solution.py:712
  14.8 0.3 %shard_map.112 = (bf16[8,2,162,162]{3,2,1,0:T(8,128)(2,1)S(1)}, bf16[1456,384]{1,0:T(8,128)(2,1)S(1)}, f32[8,162]{1,0:T(8,128)S(1)}) custom-call(f32[2,8,162]{2,1,0:T(8,128)S(1)} %get-tuple-element.60.refs_7_.act_ref, bf16[2,8,2,162,162]{4,3,2,1,0:T(8,128)(2,1)S(1)} %get-tuple-element.81.q_ref, bf16[2,8,2,162,162]{4,3,2,1,0:T(8,128)(2,1)S(1)} %get-tuple-element.82.s_ref, ...), custom_call_target="tpu_custom_call" | custom-call | flops 1 | bytes 1 | tf_op jit(solution)/shard_map/pallas_call | solution.py:531
  15.1 1.3 %collective-permute-done.5.came_ref.refs_1_ = f32[8,162]{1,0:T(8,128)S(1)} collective-permute-done((f32[8,162]{1,0:T(8,128)S(1)}, f32[8,162]{1,0:T(8,128)S(1)}, u32[]{:S(2)}, u32[]{:S(2)}) %collective-permute-start.5) | collective-permute-done | bytes 5216 | tf_op jit(solution)/shard_map/ppermute | solution.py:712
  16.5 0.0 collective-permute-done.7.refs_0_.got_c
  16.5 1.4 %collective-permute-start.8 = (bf16[1456,384]{1,0:T(8,128)(2,1)S(1)}, bf16[1456,384]{1,0:T(8,128)(2,1)S(1)}, u32[]{:S(2)}, u32[]{:S(2)}) collective-permute-start(bf16[1456,384]{1,0:T(8,128)(2,1)S(1)} %get-tuple-element.86), channel_id=1, source_target_pairs={{0,4},{4,0},{8,12},{12,8},{16,20},{20,16},{24,28},{28,24},{1,5},{5... | collective-permute-start | bytes 3354632 | tf_op jit(solution)/shard_map/ppermute | solution.py:581
  17.9 0.1 collective-permute-start.6
  18.0 2.3 %collective-permute-done.6.refs_2_.enter_ref = f32[8,162]{1,0:T(8,128)S(1)} collective-permute-done((f32[8,162]{1,0:T(8,128)S(1)}, f32[8,162]{1,0:T(8,128)S(1)}, u32[]{:S(2)}, u32[]{:S(2)}) %collective-permute-start.6) | collective-permute-done | bytes 5216 | tf_op jit(solution)/shard_map/ppermute | solution.py:712
  20.3 0.0 collective-permute-done.8.got_d
  20.4 0.4 %collective-permute-start.9 = (f32[8,162]{1,0:T(8,128)S(1)}, f32[8,162]{1,0:T(8,128)S(1)}, u32[]{:S(2)}, u32[]{:S(2)}) collective-permute-start(f32[8,162]{1,0:T(8,128)S(1)} %shard_map.114), channel_id=1, source_target_pairs={{0,4},{4,0},{8,12},{12,8},{16,24},{20,16},{24,28},{28,20},{1,5},{5... | collective-permute-start | bytes 15560 | tf_op jit(solution)/shard_map/ppermute | solution.py:749
  20.8 0.8 %collective-permute-done.9.came_ref.refs_0_ = f32[8,162]{1,0:T(8,128)S(1)} collective-permute-done((f32[8,162]{1,0:T(8,128)S(1)}, f32[8,162]{1,0:T(8,128)S(1)}, u32[]{:S(2)}, u32[]{:S(2)}) %collective-permute-start.9) | collective-permute-done | bytes 5216 | tf_op jit(solution)/shard_map/ppermute | solution.py:749
  21.6 0.3 %collective-permute-start.10 = (f32[8,162]{1,0:T(8,128)S(1)}, f32[8,162]{1,0:T(8,128)S(1)}, u32[]{:S(2)}, u32[]{:S(2)}) collective-permute-start(f32[8,162]{1,0:T(8,128)S(1)} %shard_map.116), channel_id=1, source_target_pairs={{0,4},{4,0},{8,16},{12,8},{16,20},{20,12},{24,28},{28,24},{1,5},{5... | collective-permute-start | bytes 15560 | tf_op jit(solution)/shard_map/ppermute | solution.py:763
  22.0 0.2 shard_map.120.held_ref
  22.2 0.6 %collective-permute-done.10.refs_1_.came_ref = f32[8,162]{1,0:T(8,128)S(1)} collective-permute-done((f32[8,162]{1,0:T(8,128)S(1)}, f32[8,162]{1,0:T(8,128)S(1)}, u32[]{:S(2)}, u32[]{:S(2)}) %collective-permute-start.10) | collective-permute-done | bytes 5216 | tf_op jit(solution)/shard_map/ppermute | solution.py:763
  22.8 3.6 %collective-permute-start.12 = (f32[8,162]{1,0:T(8,128)S(1)}, f32[8,162]{1,0:T(8,128)S(1)}, u32[]{:S(2)}, u32[]{:S(2)}) collective-permute-start(f32[8,162]{1,0:T(8,128)S(1)} %shard_map.121), channel_id=1, source_target_pairs={{0,4},{4,8},{8,12},{12,0},{16,20},{20,16},{24,28},{28,24},{1,5},{5... | collective-permute-start | bytes 15560 | tf_op jit(solution)/shard_map/ppermute | solution.py:763
  26.4 0.0 collective-permute-start.13
  26.4 0.7 %collective-permute-start.11 = (f32[8,162]{1,0:T(8,128)S(1)}, f32[8,162]{1,0:T(8,128)S(1)}, u32[]{:S(2)}, u32[]{:S(2)}) collective-permute-start(f32[8,162]{1,0:T(8,128)S(1)} %get-tuple-element.103), channel_id=1, source_target_pairs={{0,4},{4,0},{8,12},{12,8},{16,20},{20,16},{24,28},{28,24},{1,5},{5... | collective-permute-start | bytes 15560 | tf_op jit(solution)/shard_map/ppermute | solution.py:581
  27.1 0.1 collective-permute-done.12.flow_ref.came_ref
  27.2 1.7 %collective-permute-done.13.wall_ref = f32[8,162]{1,0:T(8,128)S(1)} collective-permute-done((f32[8,162]{1,0:T(8,128)S(1)}, f32[8,162]{1,0:T(8,128)S(1)}, u32[]{:S(2)}, u32[]{:S(2)}) %collective-permute-start.13) | collective-permute-done | bytes 5216 | tf_op jit(solution)/shard_map/ppermute | solution.py:764
  28.9 0.0 collective-permute-done.11.met_ref
  28.9 1.1 %shard_map.124 = f32[2,8,162]{2,1,0:T(8,128)} custom-call(f32[8,162]{1,0:T(8,128)S(1)} %get-tuple-element.97.beyond_ref, f32[8,162]{1,0:T(8,128)S(1)} %collective-permute-done.11.met_ref, f32[8,162]{1,0:T(8,128)S(1)} %shard_map.123.middle_ref, f32[8,162]{1,0:T(8,128)S(1)} %collective-permute-done.13.wall_ref, ...), custom_call_target="tpu_custom_call" | custom-call | flops 1 | bytes 1 | tf_op jit(solution)/shard_map/pallas_call | solution.py:531
  (17 shorter events, 0.1 us)
Async XLA Ops:
  0.0 6.3 %collective-permute-start = (bf16[16,162]{1,0:T(8,128)(2,1)}, bf16[16,162]{1,0:T(8,128)(2,1)S(1)}, u32[]{:S(2)}, u32[]{:S(2)}) collective-permute-start(bf16[16,162]{1,0:T(8,128)(2,1)} %refs_5_.1), channel_id=1, source_target_pairs={{0,1},{1,2},{2,3},{3,0},{4,5},{5,6},{6,7},{7,4},{8,9},{9,10},{10,1... | collective-permute-start | bytes 15560 | tf_op jit(solution)/shard_map/ppermute | solution.py:620
  2.1 4.2 %collective-permute-start.1 = (bf16[16,162]{1,0:T(8,128)(2,1)}, bf16[16,162]{1,0:T(8,128)(2,1)S(1)}, u32[]{:S(2)}, u32[]{:S(2)}) collective-permute-start(bf16[16,162]{1,0:T(8,128)(2,1)} %refs_5_.1), channel_id=1, source_target_pairs={{1,0},{2,1},{3,2},{0,3},{5,4},{6,5},{7,6},{4,7},{9,8},{10,9},{11,1... | collective-permute-start | bytes 15560 | tf_op jit(solution)/shard_map/ppermute | solution.py:621
  7.5 2.3 %collective-permute-start.2 = (f32[8,162]{1,0:T(8,128)S(1)}, f32[8,162]{1,0:T(8,128)S(1)}, u32[]{:S(2)}, u32[]{:S(2)}) collective-permute-start(f32[8,162]{1,0:T(8,128)S(1)} %get-tuple-element.61), channel_id=1, source_target_pairs={{0,4},{4,0},{8,12},{12,8},{16,20},{20,16},{24,28},{28,24},{1,5},{5... | collective-permute-start | bytes 15560 | tf_op jit(solution)/shard_map/ppermute | solution.py:581
  9.9 3.8 %collective-permute-start.4 = (bf16[1408,384]{1,0:T(8,128)(2,1)S(1)}, bf16[1408,384]{1,0:T(8,128)(2,1)S(1)}, u32[]{:S(2)}, u32[]{:S(2)}) collective-permute-start(bf16[1408,384]{1,0:T(8,128)(2,1)S(1)} %get-tuple-element.73), channel_id=1, source_target_pairs={{0,4},{4,0},{8,12},{12,8},{16,20},{20,16},{24,28},{28,24},{1,5},{5... | collective-permute-start | bytes 3244040 | tf_op jit(solution)/shard_map/ppermute | solution.py:581
  11.0 2.6 %collective-permute-start.3 = (f32[8,162]{1,0:T(8,128)S(1)}, f32[8,162]{1,0:T(8,128)S(1)}, u32[]{:S(2)}, u32[]{:S(2)}) collective-permute-start(f32[8,162]{1,0:T(8,128)S(1)} %get-tuple-element.68), channel_id=1, source_target_pairs={{0,4},{4,12},{8,0},{12,8},{16,20},{20,16},{24,28},{28,24},{1,5},{5... | collective-permute-start | bytes 15560 | tf_op jit(solution)/shard_map/ppermute | solution.py:660
  13.7 2.8 %collective-permute-start.7 = (bf16[1408,384]{1,0:T(8,128)(2,1)S(1)}, bf16[1408,384]{1,0:T(8,128)(2,1)S(1)}, u32[]{:S(2)}, u32[]{:S(2)}) collective-permute-start(bf16[1408,384]{1,0:T(8,128)(2,1)S(1)} %get-tuple-element.77), channel_id=1, source_target_pairs={{0,4},{4,0},{8,12},{12,8},{16,20},{20,16},{24,28},{28,24},{1,5},{5... | collective-permute-start | bytes 3244040 | tf_op jit(solution)/shard_map/ppermute | solution.py:581
  14.1 2.3 %collective-permute-start.5 = (f32[8,162]{1,0:T(8,128)S(1)}, f32[8,162]{1,0:T(8,128)S(1)}, u32[]{:S(2)}, u32[]{:S(2)}) collective-permute-start(f32[8,162]{1,0:T(8,128)S(1)} %shard_map.106), channel_id=1, source_target_pairs={{0,4},{4,8},{8,12},{12,20},{16,0},{20,16},{24,28},{28,24},{1,5},{5... | collective-permute-start | bytes 15560 | tf_op jit(solution)/shard_map/ppermute | solution.py:712
  16.5 3.8 %collective-permute-start.8 = (bf16[1456,384]{1,0:T(8,128)(2,1)S(1)}, bf16[1456,384]{1,0:T(8,128)(2,1)S(1)}, u32[]{:S(2)}, u32[]{:S(2)}) collective-permute-start(bf16[1456,384]{1,0:T(8,128)(2,1)S(1)} %get-tuple-element.86), channel_id=1, source_target_pairs={{0,4},{4,0},{8,12},{12,8},{16,20},{20,16},{24,28},{28,24},{1,5},{5... | collective-permute-start | bytes 3354632 | tf_op jit(solution)/shard_map/ppermute | solution.py:581
  17.9 2.4 %collective-permute-start.6 = (f32[8,162]{1,0:T(8,128)S(1)}, f32[8,162]{1,0:T(8,128)S(1)}, u32[]{:S(2)}, u32[]{:S(2)}) collective-permute-start(f32[8,162]{1,0:T(8,128)S(1)} %shard_map.109), channel_id=1, source_target_pairs={{0,4},{4,0},{8,12},{12,8},{16,20},{20,28},{24,16},{28,24},{1,5},{5... | collective-permute-start | bytes 15560 | tf_op jit(solution)/shard_map/ppermute | solution.py:712
  20.4 1.3 %collective-permute-start.9 = (f32[8,162]{1,0:T(8,128)S(1)}, f32[8,162]{1,0:T(8,128)S(1)}, u32[]{:S(2)}, u32[]{:S(2)}) collective-permute-start(f32[8,162]{1,0:T(8,128)S(1)} %shard_map.114), channel_id=1, source_target_pairs={{0,4},{4,0},{8,12},{12,8},{16,24},{20,16},{24,28},{28,20},{1,5},{5... | collective-permute-start | bytes 15560 | tf_op jit(solution)/shard_map/ppermute | solution.py:749
  21.6 1.2 %collective-permute-start.10 = (f32[8,162]{1,0:T(8,128)S(1)}, f32[8,162]{1,0:T(8,128)S(1)}, u32[]{:S(2)}, u32[]{:S(2)}) collective-permute-start(f32[8,162]{1,0:T(8,128)S(1)} %shard_map.116), channel_id=1, source_target_pairs={{0,4},{4,0},{8,16},{12,8},{16,20},{20,12},{24,28},{28,24},{1,5},{5... | collective-permute-start | bytes 15560 | tf_op jit(solution)/shard_map/ppermute | solution.py:763
  22.8 4.4 %collective-permute-start.12 = (f32[8,162]{1,0:T(8,128)S(1)}, f32[8,162]{1,0:T(8,128)S(1)}, u32[]{:S(2)}, u32[]{:S(2)}) collective-permute-start(f32[8,162]{1,0:T(8,128)S(1)} %shard_map.121), channel_id=1, source_target_pairs={{0,4},{4,8},{8,12},{12,0},{16,20},{20,16},{24,28},{28,24},{1,5},{5... | collective-permute-start | bytes 15560 | tf_op jit(solution)/shard_map/ppermute | solution.py:763
  26.4 2.5 %collective-permute-start.13 = (f32[8,162]{1,0:T(8,128)S(1)}, f32[8,162]{1,0:T(8,128)S(1)}, u32[]{:S(2)}, u32[]{:S(2)}) collective-permute-start(f32[8,162]{1,0:T(8,128)S(1)} %shard_map.121), channel_id=1, source_target_pairs={{0,8},{4,0},{8,12},{12,4},{16,20},{20,16},{24,28},{28,24},{1,9},{5... | collective-permute-start | bytes 15560 | tf_op jit(solution)/shard_map/ppermute | solution.py:764
  26.4 2.5 %collective-permute-start.11 = (f32[8,162]{1,0:T(8,128)S(1)}, f32[8,162]{1,0:T(8,128)S(1)}, u32[]{:S(2)}, u32[]{:S(2)}) collective-permute-start(f32[8,162]{1,0:T(8,128)S(1)} %get-tuple-element.103), channel_id=1, source_target_pairs={{0,4},{4,0},{8,12},{12,8},{16,20},{20,16},{24,28},{28,24},{1,5},{5... | collective-permute-start | bytes 15560 | tf_op jit(solution)/shard_map/ppermute | solution.py:581

commit v10 on v9

--- a/solution.py
+++ b/solution.py
@@ -22,8 +22,9 @@
 
 
 def product(x, y):
-    dot = functools.partial(jnp.dot, preferred_element_type=F32)
-    return dot(x[0], y[0]) + (dot(x[0], y[1]) + dot(x[1], y[0]))
+    left = jnp.concatenate([x[0], x[0], x[1]], axis=1)
+    right = jnp.concatenate([y[0], y[1], y[0]], axis=0)
+    return jnp.dot(left, right, preferred_element_type=F32)
 
 
 def room_of(width):

time: 30.2 us -> 30.2 us (level)
  transfers between devices with their start and end apart: 14 -> 14, of which waited for: 6 -> 7; matrix products, arithmetic and copies ran while one was open for 0% -> 0% of each run, Pallas kernels for 23% -> 22%
where the time goes in v10:
time: 30.2 us; the launch traced here: 30 us
  starting transfers between devices  13.8 us (46%)
  Pallas kernels  9.01 us (30%)
  waiting for transfers between devices  7.05 us (23%)
    pallas_call x25, Pallas kernels, run(): pl.pallas_call(kernel, grid=grid, in_specs=in_specs, out_specs=out_specs,...  9.01 us
    ppermute x2, starting transfers between devices, per_device(): lax.ppermute(out, 'wall', hop_pairs(wall_count, at, at - 1, int(at > 1)))  3.96 us
    ppermute x5, starting transfers between devices, mates(): return lax.ppermute(value, 'wall', [(i, i ^ 1) for i in range(wall_count)])  3.74 us
    ppermute x2, waiting for transfers between devices, per_device(): arrivals.append(lax.ppermute(out, 'wall', pairs))  3.59 us
    ppermute x1, starting transfers between devices, per_device(): lax.ppermute(state, 'surf', [(i, (i + 1) % surf_count) for i in range(sur...  2.13 us
    ppermute x1, starting transfers between devices, per_device(): lax.ppermute(state, 'surf', [((i + 1) % surf_count, i) for i in range(sur...  2.03 us
    ppermute x1, waiting for transfers between devices, per_device(): wall = lax.ppermute(out, 'wall', hop_pairs(wall_count, 1, 0))  1.7 us
    ppermute x2, waiting for transfers between devices, per_device(): lax.ppermute(out, 'wall', hop_pairs(wall_count, at, at - 1, int(at > 1)))  0.85 us
  transfers between devices with their start and end apart: 14, of which 7 were waited for; matrix products, arithmetic and copies ran while one was open for 0% of the time, Pallas kernels for 22%

profile of v10, /device:TPU:1, one launch (start us, length us, event | category | flops | bytes accessed | tf_op | source)
XLA Modules:
  0.0 30.0 jit_solution(18146466234487475833)
XLA Ops:
  0.0 2.1 %collective-permute-start = (bf16[16,162]{1,0:T(8,128)(2,1)}, bf16[16,162]{1,0:T(8,128)(2,1)S(1)}, u32[]{:S(2)}, u32[]{:S(2)}) collective-permute-start(bf16[16,162]{1,0:T(8,128)(2,1)} %refs_5_.1), channel_id=1, source_target_pairs={{0,1},{1,2},{2,3},{3,0},{4,5},{5,6},{6,7},{7,4},{8,9},{9,10},{10,1... | collective-permute-start | bytes 15560 | tf_op jit(solution)/shard_map/ppermute | solution.py:621
  2.1 2.0 %collective-permute-start.1 = (bf16[16,162]{1,0:T(8,128)(2,1)}, bf16[16,162]{1,0:T(8,128)(2,1)S(1)}, u32[]{:S(2)}, u32[]{:S(2)}) collective-permute-start(bf16[16,162]{1,0:T(8,128)(2,1)} %refs_5_.1), channel_id=1, source_target_pairs={{1,0},{2,1},{3,2},{0,3},{5,4},{6,5},{7,6},{4,7},{9,8},{10,9},{11,1... | collective-permute-start | bytes 15560 | tf_op jit(solution)/shard_map/ppermute | solution.py:622
  4.2 2.1 %shard_map.100 = (bf16[48,48]{1,0:T(8,128)(2,1)S(1)}, f32[16,162]{1,0:T(8,128)S(1)}, f32[2,8,162]{2,1,0:T(8,128)S(1)}, bf16[16,162]{1,0:T(8,128)(2,1)S(1)}, bf16...) custom-call(s32[2,8]{1,0:T(2,128)} %refs_0_.1, s32[8]{0:T(128)} %refs_1_.1, f32[4,16]{1,0:T(4,128)} %bitcast.9, ...), custom_call_target="tpu_custom_call" | custom-call | flops 1 | bytes 1 | tf_op jit(solution)/shard_map/pallas_call | solution.py:532
  6.3 0.0 collective-permute-done.here
  6.3 0.0 collective-permute-done.1.refs_2_
  6.3 1.2 %shard_map.102 = (f32[2,8,162]{2,1,0:T(8,128)S(1)}, f32[2,8,162]{2,1,0:T(8,128)S(1)}, f32[8,162]{1,0:T(8,128)S(1)}, bf16[1,1,162,8,162]{4,3,2,1,0:T(8,128)(2,1)S(1)}) custom-call(bf16[16,162]{1,0:T(8,128)(2,1)S(1)} %shard_map.101.refs_0_, bf16[16,162]{1,0:T(8,128)(2,1)S(1)} %get-tuple-element.57.refs_1_, bf16[16,162]{1,0:T(8,128)(2,1)S(1)} %collective-permute-done.1.refs_2_, ...), custom_call_target="tpu_custom_call" | custom-call | flops 1 | bytes 1 | tf_op jit(solution)/shard_map/pallas_call | solution.py:532
  7.5 1.0 %collective-permute-start.2 = (f32[8,162]{1,0:T(8,128)S(1)}, f32[8,162]{1,0:T(8,128)S(1)}, u32[]{:S(2)}, u32[]{:S(2)}) collective-permute-start(f32[8,162]{1,0:T(8,128)S(1)} %get-tuple-element.61), channel_id=1, source_target_pairs={{0,4},{4,0},{8,12},{12,8},{16,20},{20,16},{24,28},{28,24},{1,5},{5... | collective-permute-start | bytes 15560 | tf_op jit(solution)/shard_map/ppermute | solution.py:582
  8.5 1.3 %shard_map.103 = (bf16[2,8,2,162,162]{4,3,2,1,0:T(8,128)(2,1)S(1)}, bf16[8,2,162,162]{3,2,1,0:T(8,128)(2,1)S(1)}, bf16[1408,384]{1,0:T(8,128)(2,1)S(1)}, bf16[1,...) custom-call(bf16[2,2,8,162,162]{4,3,2,1,0:T(8,128)(2,1)S(1)} %get-tuple-element.69.refs_6_.raw_ref, ...), custom_call_target="tpu_custom_call" | custom-call | flops 1 | bytes 1 | tf_op jit(solution)/shard_map/pallas_call | solution.py:532
  9.8 0.0 collective-permute-done.2.came_ref.mate_ref
  9.9 0.1 collective-permute-start.4
  9.9 1.1 %shard_map.104 = (f32[2,8,162]{2,1,0:T(8,128)S(1)}, f32[8,162]{1,0:T(8,128)S(1)}) custom-call(f32[8,162]{1,0:T(8,128)S(1)} %collective-permute-done.2.came_ref.mate_ref, f32[2,8,162]{2,1,0:T(8,128)S(1)} %get-tuple-element.65.scaled_ref, bf16[2,2,8,162,162]{4,3,2,1,0:T(8,128)(2,1)S(1)} %get-tuple-element.69.refs_6_.raw_ref, ...), custom_call_target="tpu_custom_call" | custom-call | flops 1 | bytes 1 | tf_op jit(solution)/shard_map/pallas_call | solution.py:532
  11.0 0.8 %collective-permute-start.3 = (f32[8,162]{1,0:T(8,128)S(1)}, f32[8,162]{1,0:T(8,128)S(1)}, u32[]{:S(2)}, u32[]{:S(2)}) collective-permute-start(f32[8,162]{1,0:T(8,128)S(1)} %get-tuple-element.68), channel_id=1, source_target_pairs={{0,4},{4,12},{8,0},{12,8},{16,20},{20,16},{24,28},{28,24},{1,5},{5... | collective-permute-start | bytes 15560 | tf_op jit(solution)/shard_map/ppermute | solution.py:661
  11.8 1.8 %shard_map.105 = (bf16[2,8,2,162,162]{4,3,2,1,0:T(8,128)(2,1)S(1)}, bf16[8,2,162,162]{3,2,1,0:T(8,128)(2,1)S(1)}, bf16[1408,384]{1,0:T(8,128)(2,1)S(1)}) custom-call(bf16[2,2,8,162,162]{4,3,2,1,0:T(8,128)(2,1)S(1)} %get-tuple-element.69.refs_6_.raw_ref, bf16[1,2,162,8,162]{4,3,2,1,0:T(8,128)(2,1)S(1)} %get-tuple-element.70.refs_0_), custom_call_target="tpu_custom_call" | custom-call | flops 1 | bytes 1 | tf_op jit(solution)/shard_map/pallas_call | solution.py:532
  13.6 0.0 collective-permute-done.3.came_ref.refs_0_
  13.6 0.0 collective-permute-done.4.refs_0_
  13.6 0.5 %collective-permute-start.7 = (bf16[1408,384]{1,0:T(8,128)(2,1)S(1)}, bf16[1408,384]{1,0:T(8,128)(2,1)S(1)}, u32[]{:S(2)}, u32[]{:S(2)}) collective-permute-start(bf16[1408,384]{1,0:T(8,128)(2,1)S(1)} %get-tuple-element.77), channel_id=1, source_target_pairs={{0,4},{4,0},{8,12},{12,8},{16,20},{20,16},{24,28},{28,24},{1,5},{5... | collective-permute-start | bytes 3244040 | tf_op jit(solution)/shard_map/ppermute | solution.py:582
  14.2 0.7 %collective-permute-start.5 = (f32[8,162]{1,0:T(8,128)S(1)}, f32[8,162]{1,0:T(8,128)S(1)}, u32[]{:S(2)}, u32[]{:S(2)}) collective-permute-start(f32[8,162]{1,0:T(8,128)S(1)} %shard_map.106), channel_id=1, source_target_pairs={{0,4},{4,8},{8,12},{12,20},{16,0},{20,16},{24,28},{28,24},{1,5},{5... | collective-permute-start | bytes 15560 | tf_op jit(solution)/shard_map/ppermute | solution.py:713
  14.8 0.3 %shard_map.112 = (bf16[8,2,162,162]{3,2,1,0:T(8,128)(2,1)S(1)}, bf16[1456,384]{1,0:T(8,128)(2,1)S(1)}, f32[8,162]{1,0:T(8,128)S(1)}) custom-call(f32[2,8,162]{2,1,0:T(8,128)S(1)} %get-tuple-element.60.refs_7_.act_ref, bf16[2,8,2,162,162]{4,3,2,1,0:T(8,128)(2,1)S(1)} %get-tuple-element.81.q_ref, bf16[2,8,2,162,162]{4,3,2,1,0:T(8,128)(2,1)S(1)} %get-tuple-element.82.s_ref, ...), custom_call_target="tpu_custom_call" | custom-call | flops 1 | bytes 1 | tf_op jit(solution)/shard_map/pallas_call | solution.py:532
  15.2 1.3 %collective-permute-done.5.came_ref.refs_1_ = f32[8,162]{1,0:T(8,128)S(1)} collective-permute-done((f32[8,162]{1,0:T(8,128)S(1)}, f32[8,162]{1,0:T(8,128)S(1)}, u32[]{:S(2)}, u32[]{:S(2)}) %collective-permute-start.5) | collective-permute-done | bytes 5216 | tf_op jit(solution)/shard_map/ppermute | solution.py:713
  16.4 0.1 collective-permute-done.7.refs_0_.got_c
  16.5 1.4 %collective-permute-start.8 = (bf16[1456,384]{1,0:T(8,128)(2,1)S(1)}, bf16[1456,384]{1,0:T(8,128)(2,1)S(1)}, u32[]{:S(2)}, u32[]{:S(2)}) collective-permute-start(bf16[1456,384]{1,0:T(8,128)(2,1)S(1)} %get-tuple-element.86), channel_id=1, source_target_pairs={{0,4},{4,0},{8,12},{12,8},{16,20},{20,16},{24,28},{28,24},{1,5},{5... | collective-permute-start | bytes 3354632 | tf_op jit(solution)/shard_map/ppermute | solution.py:582
  17.9 0.1 collective-permute-start.6
  18.0 2.3 %collective-permute-done.6.refs_2_.enter_ref = f32[8,162]{1,0:T(8,128)S(1)} collective-permute-done((f32[8,162]{1,0:T(8,128)S(1)}, f32[8,162]{1,0:T(8,128)S(1)}, u32[]{:S(2)}, u32[]{:S(2)}) %collective-permute-start.6) | collective-permute-done | bytes 5216 | tf_op jit(solution)/shard_map/ppermute | solution.py:713
  20.3 0.0 collective-permute-done.8.got_d
  20.4 0.4 %collective-permute-start.9 = (f32[8,162]{1,0:T(8,128)S(1)}, f32[8,162]{1,0:T(8,128)S(1)}, u32[]{:S(2)}, u32[]{:S(2)}) collective-permute-start(f32[8,162]{1,0:T(8,128)S(1)} %shard_map.114), channel_id=1, source_target_pairs={{0,4},{4,0},{8,12},{12,8},{16,24},{20,16},{24,28},{28,20},{1,5},{5... | collective-permute-start | bytes 15560 | tf_op jit(solution)/shard_map/ppermute | solution.py:750
  20.8 0.8 %collective-permute-done.9.came_ref.refs_0_ = f32[8,162]{1,0:T(8,128)S(1)} collective-permute-done((f32[8,162]{1,0:T(8,128)S(1)}, f32[8,162]{1,0:T(8,128)S(1)}, u32[]{:S(2)}, u32[]{:S(2)}) %collective-permute-start.9) | collective-permute-done | bytes 5216 | tf_op jit(solution)/shard_map/ppermute | solution.py:750
  21.6 0.3 %collective-permute-start.10 = (f32[8,162]{1,0:T(8,128)S(1)}, f32[8,162]{1,0:T(8,128)S(1)}, u32[]{:S(2)}, u32[]{:S(2)}) collective-permute-start(f32[8,162]{1,0:T(8,128)S(1)} %shard_map.116), channel_id=1, source_target_pairs={{0,4},{4,0},{8,16},{12,8},{16,20},{20,12},{24,28},{28,24},{1,5},{5... | collective-permute-start | bytes 15560 | tf_op jit(solution)/shard_map/ppermute | solution.py:764
  22.0 0.8 %collective-permute-done.10.refs_1_.came_ref = f32[8,162]{1,0:T(8,128)S(1)} collective-permute-done((f32[8,162]{1,0:T(8,128)S(1)}, f32[8,162]{1,0:T(8,128)S(1)}, u32[]{:S(2)}, u32[]{:S(2)}) %collective-permute-start.10) | collective-permute-done | bytes 5216 | tf_op jit(solution)/shard_map/ppermute | solution.py:764
  22.8 3.6 %collective-permute-start.12 = (f32[8,162]{1,0:T(8,128)S(1)}, f32[8,162]{1,0:T(8,128)S(1)}, u32[]{:S(2)}, u32[]{:S(2)}) collective-permute-start(f32[8,162]{1,0:T(8,128)S(1)} %shard_map.121), channel_id=1, source_target_pairs={{0,4},{4,8},{8,12},{12,0},{16,20},{20,16},{24,28},{28,24},{1,5},{5... | collective-permute-start | bytes 15560 | tf_op jit(solution)/shard_map/ppermute | solution.py:764
  26.4 0.0 collective-permute-start.13
  26.4 0.7 %collective-permute-start.11 = (f32[8,162]{1,0:T(8,128)S(1)}, f32[8,162]{1,0:T(8,128)S(1)}, u32[]{:S(2)}, u32[]{:S(2)}) collective-permute-start(f32[8,162]{1,0:T(8,128)S(1)} %get-tuple-element.103), channel_id=1, source_target_pairs={{0,4},{4,0},{8,12},{12,8},{16,20},{20,16},{24,28},{28,24},{1,5},{5... | collective-permute-start | bytes 15560 | tf_op jit(solution)/shard_map/ppermute | solution.py:582
  27.1 0.1 collective-permute-done.12.flow_ref.came_ref
  27.2 1.7 %collective-permute-done.13.wall_ref = f32[8,162]{1,0:T(8,128)S(1)} collective-permute-done((f32[8,162]{1,0:T(8,128)S(1)}, f32[8,162]{1,0:T(8,128)S(1)}, u32[]{:S(2)}, u32[]{:S(2)}) %collective-permute-start.13) | collective-permute-done | bytes 5216 | tf_op jit(solution)/shard_map/ppermute | solution.py:765
  28.9 0.0 collective-permute-done.11.met_ref
  28.9 1.1 %shard_map.124 = f32[2,8,162]{2,1,0:T(8,128)} custom-call(f32[8,162]{1,0:T(8,128)S(1)} %get-tuple-element.97.beyond_ref, f32[8,162]{1,0:T(8,128)S(1)} %collective-permute-done.11.met_ref, f32[8,162]{1,0:T(8,128)S(1)} %shard_map.123.middle_ref, f32[8,162]{1,0:T(8,128)S(1)} %collective-permute-done.13.wall_ref, ...), custom_call_target="tpu_custom_call" | custom-call | flops 1 | bytes 1 | tf_op jit(solution)/shard_map/pallas_call | solution.py:532
  (18 shorter events, 0.1 us)
Async XLA Ops:
  0.0 6.3 %collective-permute-start = (bf16[16,162]{1,0:T(8,128)(2,1)}, bf16[16,162]{1,0:T(8,128)(2,1)S(1)}, u32[]{:S(2)}, u32[]{:S(2)}) collective-permute-start(bf16[16,162]{1,0:T(8,128)(2,1)} %refs_5_.1), channel_id=1, source_target_pairs={{0,1},{1,2},{2,3},{3,0},{4,5},{5,6},{6,7},{7,4},{8,9},{9,10},{10,1... | collective-permute-start | bytes 15560 | tf_op jit(solution)/shard_map/ppermute | solution.py:621
  2.1 4.2 %collective-permute-start.1 = (bf16[16,162]{1,0:T(8,128)(2,1)}, bf16[16,162]{1,0:T(8,128)(2,1)S(1)}, u32[]{:S(2)}, u32[]{:S(2)}) collective-permute-start(bf16[16,162]{1,0:T(8,128)(2,1)} %refs_5_.1), channel_id=1, source_target_pairs={{1,0},{2,1},{3,2},{0,3},{5,4},{6,5},{7,6},{4,7},{9,8},{10,9},{11,1... | collective-permute-start | bytes 15560 | tf_op jit(solution)/shard_map/ppermute | solution.py:622
  7.5 2.3 %collective-permute-start.2 = (f32[8,162]{1,0:T(8,128)S(1)}, f32[8,162]{1,0:T(8,128)S(1)}, u32[]{:S(2)}, u32[]{:S(2)}) collective-permute-start(f32[8,162]{1,0:T(8,128)S(1)} %get-tuple-element.61), channel_id=1, source_target_pairs={{0,4},{4,0},{8,12},{12,8},{16,20},{20,16},{24,28},{28,24},{1,5},{5... | collective-permute-start | bytes 15560 | tf_op jit(solution)/shard_map/ppermute | solution.py:582
  9.9 3.8 %collective-permute-start.4 = (bf16[1408,384]{1,0:T(8,128)(2,1)S(1)}, bf16[1408,384]{1,0:T(8,128)(2,1)S(1)}, u32[]{:S(2)}, u32[]{:S(2)}) collective-permute-start(bf16[1408,384]{1,0:T(8,128)(2,1)S(1)} %get-tuple-element.73), channel_id=1, source_target_pairs={{0,4},{4,0},{8,12},{12,8},{16,20},{20,16},{24,28},{28,24},{1,5},{5... | collective-permute-start | bytes 3244040 | tf_op jit(solution)/shard_map/ppermute | solution.py:582
  11.0 2.6 %collective-permute-start.3 = (f32[8,162]{1,0:T(8,128)S(1)}, f32[8,162]{1,0:T(8,128)S(1)}, u32[]{:S(2)}, u32[]{:S(2)}) collective-permute-start(f32[8,162]{1,0:T(8,128)S(1)} %get-tuple-element.68), channel_id=1, source_target_pairs={{0,4},{4,12},{8,0},{12,8},{16,20},{20,16},{24,28},{28,24},{1,5},{5... | collective-permute-start | bytes 15560 | tf_op jit(solution)/shard_map/ppermute | solution.py:661
  13.6 2.8 %collective-permute-start.7 = (bf16[1408,384]{1,0:T(8,128)(2,1)S(1)}, bf16[1408,384]{1,0:T(8,128)(2,1)S(1)}, u32[]{:S(2)}, u32[]{:S(2)}) collective-permute-start(bf16[1408,384]{1,0:T(8,128)(2,1)S(1)} %get-tuple-element.77), channel_id=1, source_target_pairs={{0,4},{4,0},{8,12},{12,8},{16,20},{20,16},{24,28},{28,24},{1,5},{5... | collective-permute-start | bytes 3244040 | tf_op jit(solution)/shard_map/ppermute | solution.py:582
  14.2 2.3 %collective-permute-start.5 = (f32[8,162]{1,0:T(8,128)S(1)}, f32[8,162]{1,0:T(8,128)S(1)}, u32[]{:S(2)}, u32[]{:S(2)}) collective-permute-start(f32[8,162]{1,0:T(8,128)S(1)} %shard_map.106), channel_id=1, source_target_pairs={{0,4},{4,8},{8,12},{12,20},{16,0},{20,16},{24,28},{28,24},{1,5},{5... | collective-permute-start | bytes 15560 | tf_op jit(solution)/shard_map/ppermute | solution.py:713
  16.5 3.8 %collective-permute-start.8 = (bf16[1456,384]{1,0:T(8,128)(2,1)S(1)}, bf16[1456,384]{1,0:T(8,128)(2,1)S(1)}, u32[]{:S(2)}, u32[]{:S(2)}) collective-permute-start(bf16[1456,384]{1,0:T(8,128)(2,1)S(1)} %get-tuple-element.86), channel_id=1, source_target_pairs={{0,4},{4,0},{8,12},{12,8},{16,20},{20,16},{24,28},{28,24},{1,5},{5... | collective-permute-start | bytes 3354632 | tf_op jit(solution)/shard_map/ppermute | solution.py:582
  17.9 2.4 %collective-permute-start.6 = (f32[8,162]{1,0:T(8,128)S(1)}, f32[8,162]{1,0:T(8,128)S(1)}, u32[]{:S(2)}, u32[]{:S(2)}) collective-permute-start(f32[8,162]{1,0:T(8,128)S(1)} %shard_map.109), channel_id=1, source_target_pairs={{0,4},{4,0},{8,12},{12,8},{16,20},{20,28},{24,16},{28,24},{1,5},{5... | collective-permute-start | bytes 15560 | tf_op jit(solution)/shard_map/ppermute | solution.py:713
  20.4 1.3 %collective-permute-start.9 = (f32[8,162]{1,0:T(8,128)S(1)}, f32[8,162]{1,0:T(8,128)S(1)}, u32[]{:S(2)}, u32[]{:S(2)}) collective-permute-start(f32[8,162]{1,0:T(8,128)S(1)} %shard_map.114), channel_id=1, source_target_pairs={{0,4},{4,0},{8,12},{12,8},{16,24},{20,16},{24,28},{28,20},{1,5},{5... | collective-permute-start | bytes 15560 | tf_op jit(solution)/shard_map/ppermute | solution.py:750
  21.6 1.2 %collective-permute-start.10 = (f32[8,162]{1,0:T(8,128)S(1)}, f32[8,162]{1,0:T(8,128)S(1)}, u32[]{:S(2)}, u32[]{:S(2)}) collective-permute-start(f32[8,162]{1,0:T(8,128)S(1)} %shard_map.116), channel_id=1, source_target_pairs={{0,4},{4,0},{8,16},{12,8},{16,20},{20,12},{24,28},{28,24},{1,5},{5... | collective-permute-start | bytes 15560 | tf_op jit(solution)/shard_map/ppermute | solution.py:764
  22.8 4.4 %collective-permute-start.12 = (f32[8,162]{1,0:T(8,128)S(1)}, f32[8,162]{1,0:T(8,128)S(1)}, u32[]{:S(2)}, u32[]{:S(2)}) collective-permute-start(f32[8,162]{1,0:T(8,128)S(1)} %shard_map.121), channel_id=1, source_target_pairs={{0,4},{4,8},{8,12},{12,0},{16,20},{20,16},{24,28},{28,24},{1,5},{5... | collective-permute-start | bytes 15560 | tf_op jit(solution)/shard_map/ppermute | solution.py:764
  26.4 2.5 %collective-permute-start.13 = (f32[8,162]{1,0:T(8,128)S(1)}, f32[8,162]{1,0:T(8,128)S(1)}, u32[]{:S(2)}, u32[]{:S(2)}) collective-permute-start(f32[8,162]{1,0:T(8,128)S(1)} %shard_map.121), channel_id=1, source_target_pairs={{0,8},{4,0},{8,12},{12,4},{16,20},{20,16},{24,28},{28,24},{1,9},{5... | collective-permute-start | bytes 15560 | tf_op jit(solution)/shard_map/ppermute | solution.py:765
  26.4 2.5 %collective-permute-start.11 = (f32[8,162]{1,0:T(8,128)S(1)}, f32[8,162]{1,0:T(8,128)S(1)}, u32[]{:S(2)}, u32[]{:S(2)}) collective-permute-start(f32[8,162]{1,0:T(8,128)S(1)} %get-tuple-element.103), channel_id=1, source_target_pairs={{0,4},{4,0},{8,12},{12,8},{16,20},{20,16},{24,28},{28,24},{1,5},{5... | collective-permute-start | bytes 15560 | tf_op jit(solution)/shard_map/ppermute | solution.py:582
